TPU v7x, 32 devices: a whole 2x2x4 slice. The times are simulated.
32 devices in a mesh: dp: 2 (over core), zero: 16 (over z, y, x).
Axes of the slice: x: 2, y: 2, z: 4, core: 2. Of those that a mesh axis runs over, the one named last changes fastest.
Arguments:
- tokens: bfloat16 [32768, 768], P(('dp', 'zero')), may hold values from -6 to 6
- segments: int32 [32768], P(('dp', 'zero')), may hold values from 0 to 127, never falling along the last dimension, each value on 1 to 1024 neighbouring positions
- cotangent: bfloat16 [32768, 768], P(('dp', 'zero')), may hold values from -6.05 to 6.05
- master: float32 [9440256], P('zero'), may hold values from -1.8 to 1.8
- moment_one: float32 [9440256], P('zero'), may hold values from -4 to 4
- moment_two: float32 [9440256], P('zero'), may hold values from 0.003 to 0.3
Outputs:
- output: bfloat16 [32768, 768], P(('dp', 'zero'))
- input_grad: float32 [32768, 768], P(('dp', 'zero'))
- grad_shard: float32 [9440256], P('zero')
- moment_one_new: float32 [9440256], P('zero')
- moment_two_new: float32 [9440256], P('zero')
- master_new: float32 [9440256], P('zero')
- weight_new: bfloat16 [9440256], P('zero')
Inputs may be any that keep to these rules, and one draw needn't show every extreme that they name: `segments`: ids never fall along the tokens; each id covers 1 to 1024 consecutive tokens and some id covers exactly 1024.
All inputs are finite; a program needn't handle non-finite values.
Results may differ from a plain program's by a relative error of at most 0.012.
The roundings to bfloat16 on the way count: a program that leaves them out, or rounds other values in their place, can miss the bound.
Values may be sent and summed in bfloat16 or wider, within the bound.
A program may use at most 256 MiB of HBM per device.

v0:
```python
import jax
import jax.numpy as jnp
from jax import lax
from jax.sharding import PartitionSpec as P

D = 768
HEADS = 12
HEAD = 64
FF = 3072
LEN = 1024


learn_rate = 0.02
beta_one = 0.9
beta_two = 0.999
adam_eps = 1e-08
weight_decay = 0.01
correct_one = 1.0 - 0.9**10
correct_two = 1.0 - 0.999**10
norm_eps = 1e-06
inv_root_two = 0.7071067811865476
inv_root_tau = 0.3989422804014327


def split_flat(flat):
    dims_list = ((D, D), (D, D), (D, D), (D, D), (D, FF), (D, FF), (FF, D))
    pieces = []
    offset = 0
    for dims_pair in dims_list:
        length = dims_pair[0] * dims_pair[1]
        pieces.append(flat[offset : offset + length].reshape(dims_pair))
        offset = offset + length
    for number in range(4):
        pieces.append(flat[offset : offset + D].astype(jnp.float32))
        offset = offset + D
    return pieces


def head_slopes():
    return jnp.exp2(-8.0 * (jnp.arange(HEADS).astype(jnp.float32) + 1.0) / HEADS)


def layer_stats(value):
    centre = value - jnp.mean(value, -1, keepdims=True)
    inverse = lax.rsqrt(jnp.mean(centre * centre, -1, keepdims=True) + norm_eps)
    return (centre * inverse, inverse)


def norm_back(grad_normed, normed, inverse):
    centred = grad_normed - jnp.mean(grad_normed, -1, keepdims=True)
    return inverse * (centred - normed * jnp.mean(grad_normed * normed, -1, keepdims=True))


def project(left, right):
    return jnp.dot(left, right, preferred_element_type=jnp.float32)


def left_trans(left, right):
    return jnp.einsum("rd,re->de", left, right, preferred_element_type=jnp.float32)


def right_trans(left, right):
    return jnp.einsum("re,de->rd", left, right, preferred_element_type=jnp.float32)


def block_scores(q_block, keys_seq, seg_block, seg_seq, begin):
    width = q_block.shape[0]
    raw = jnp.einsum(
        "qhd,khd->hqk", q_block, keys_seq, preferred_element_type=jnp.float32
    ) * HEAD ** (-0.5)
    q_places = (begin + jnp.arange(width)).astype(jnp.float32)
    k_places = jnp.arange(keys_seq.shape[0]).astype(jnp.float32)
    distance = jnp.abs(q_places[:, None] - k_places[None, :])
    raw = raw - head_slopes()[:, None, None] * distance[None]
    same_doc = seg_block[:, None] == seg_seq[None, :]
    return jnp.where(same_doc[None], raw, -1e30)


def attend_forward(piece):
    queries, keys_seq, values_seq, seg_seq = piece
    span = min(512, LEN)
    outputs = []
    log_sums = []
    for begin in range(0, LEN, span):
        scores = block_scores(
            queries[begin : begin + span], keys_seq, seg_seq[begin : begin + span], seg_seq, begin
        )
        top = jnp.max(scores, -1, keepdims=True)
        expo = jnp.exp(scores - top)
        total = jnp.sum(expo, -1, keepdims=True)
        probs = (expo / total).astype(jnp.bfloat16)
        outputs.append(
            jnp.einsum("hqk,khd->qhd", probs, values_seq, preferred_element_type=jnp.float32)
        )
        log_sums.append(top[..., 0] + jnp.log(total[..., 0]))
    return (jnp.concatenate(outputs, 0), jnp.concatenate(log_sums, 1))


def attend_backward(piece):
    queries, keys_seq, values_seq, seg_seq, grad_out, log_sum = piece
    span = min(512, LEN)
    scale_factor = HEAD ** (-0.5)
    key_grad = jnp.zeros(keys_seq.shape, jnp.float32)
    value_grad = jnp.zeros(values_seq.shape, jnp.float32)
    query_grads = []
    for begin in range(0, LEN, span):
        q_block = queries[begin : begin + span]
        g_block = grad_out[begin : begin + span]
        scores = block_scores(q_block, keys_seq, seg_seq[begin : begin + span], seg_seq, begin)
        probs = jnp.exp(scores - log_sum[:, begin : begin + span, None])
        grad_probs = jnp.einsum(
            "qhd,khd->hqk", g_block, values_seq, preferred_element_type=jnp.float32
        )
        delta = jnp.sum(probs * grad_probs, -1, keepdims=True)
        grad_scores = (probs * (grad_probs - delta)).astype(jnp.bfloat16)
        query_grads.append(
            jnp.einsum("hqk,khd->qhd", grad_scores, keys_seq, preferred_element_type=jnp.float32)
            * scale_factor
        )
        key_grad = (
            key_grad
            + jnp.einsum("hqk,qhd->khd", grad_scores, q_block, preferred_element_type=jnp.float32)
            * scale_factor
        )
        value_grad = value_grad + jnp.einsum(
            "hqk,qhd->khd", probs.astype(jnp.bfloat16), g_block, preferred_element_type=jnp.float32
        )
    query_grad = jnp.concatenate(query_grads, 0)
    return (
        query_grad.astype(jnp.bfloat16),
        key_grad.astype(jnp.bfloat16),
        value_grad.astype(jnp.bfloat16),
    )


def local(tokens, segments, cotangent, master, moment_one, moment_two):
    flat_weights = lax.all_gather(master.astype(jnp.bfloat16), "zero", axis=0, tiled=True)
    (
        w_query,
        w_key,
        w_value,
        w_out,
        w_gate,
        w_up,
        w_down,
        gain_one,
        shift_one,
        gain_two,
        shift_two,
    ) = split_flat(flat_weights)
    height = tokens.shape[0]
    count = height // LEN

    def head_view(value):
        return value.reshape(count, LEN, HEADS, HEAD)

    queries = project(tokens, w_query).astype(jnp.bfloat16)
    keys_all = project(tokens, w_key).astype(jnp.bfloat16)
    values_all = project(tokens, w_value).astype(jnp.bfloat16)
    seg_view = segments.reshape(count, LEN)
    attended, log_sum = lax.map(
        attend_forward, (head_view(queries), head_view(keys_all), head_view(values_all), seg_view)
    )
    mixed = attended.reshape(height, D).astype(jnp.bfloat16)
    branch = project(mixed, w_out)
    normed_one, inverse_one = layer_stats(tokens.astype(jnp.float32) + branch)
    layer_one = normed_one * gain_one + shift_one
    inner = layer_one.astype(jnp.bfloat16)
    gate = project(inner, w_gate)
    up_part = project(inner, w_up)
    cumulative = 0.5 * (1.0 + lax.erf(gate * inv_root_two))
    gelu_gate = gate * cumulative
    hidden = (gelu_gate * up_part).astype(jnp.bfloat16)
    ffn = project(hidden, w_down)
    normed_two, inverse_two = layer_stats(layer_one + ffn)
    output = normed_two * gain_two + shift_two
    grad_output = cotangent.astype(jnp.float32)
    grad_gain_two = jnp.sum(grad_output * normed_two, 0)
    grad_shift_two = jnp.sum(grad_output, 0)
    grad_mid = norm_back(grad_output * gain_two, normed_two, inverse_two)
    grad_ffn = grad_mid.astype(jnp.bfloat16)
    grad_w_down = left_trans(hidden, grad_ffn)
    grad_hidden = right_trans(grad_ffn, w_down)
    density = jnp.exp(-0.5 * gate * gate) * inv_root_tau
    grad_gate = (grad_hidden * up_part * (cumulative + gate * density)).astype(jnp.bfloat16)
    grad_up = (grad_hidden * gelu_gate).astype(jnp.bfloat16)
    grad_w_gate = left_trans(inner, grad_gate)
    grad_w_up = left_trans(inner, grad_up)
    grad_layer_one = grad_mid + right_trans(grad_gate, w_gate) + right_trans(grad_up, w_up)
    grad_gain_one = jnp.sum(grad_layer_one * normed_one, 0)
    grad_shift_one = jnp.sum(grad_layer_one, 0)
    grad_first = norm_back(grad_layer_one * gain_one, normed_one, inverse_one)
    grad_branch = grad_first.astype(jnp.bfloat16)
    grad_w_out = left_trans(mixed, grad_branch)
    grad_mixed = right_trans(grad_branch, w_out).astype(jnp.bfloat16)
    grad_query, grad_key, grad_value = lax.map(
        attend_backward,
        (
            head_view(queries),
            head_view(keys_all),
            head_view(values_all),
            seg_view,
            head_view(grad_mixed),
            log_sum,
        ),
    )
    grad_query = grad_query.reshape(height, D)
    grad_key = grad_key.reshape(height, D)
    grad_value = grad_value.reshape(height, D)
    grad_w_query = left_trans(tokens, grad_query)
    grad_w_key = left_trans(tokens, grad_key)
    grad_w_value = left_trans(tokens, grad_value)
    input_grad = (
        grad_first
        + right_trans(grad_query, w_query)
        + right_trans(grad_key, w_key)
        + right_trans(grad_value, w_value)
    )
    flat_local = jnp.concatenate(
        [
            grad_w_query.reshape(-1),
            grad_w_key.reshape(-1),
            grad_w_value.reshape(-1),
            grad_w_out.reshape(-1),
            grad_w_gate.reshape(-1),
            grad_w_up.reshape(-1),
            grad_w_down.reshape(-1),
            grad_gain_one,
            grad_shift_one,
            grad_gain_two,
            grad_shift_two,
        ]
    )
    groups = lax.axis_size("zero")
    replicas = lax.axis_size("dp")
    partial_sum = lax.psum_scatter(flat_local, "zero", scatter_dimension=0, tiled=True)
    piece_sum = lax.psum_scatter(
        partial_sum.astype(jnp.bfloat16), "dp", scatter_dimension=0, tiled=True
    ).astype(jnp.float32)
    summed = lax.all_gather(piece_sum.astype(jnp.bfloat16), "dp", axis=0, tiled=True).astype(
        piece_sum.dtype
    )
    grad_shard = summed / (count * groups * replicas)
    first = beta_one * moment_one + (1.0 - beta_one) * grad_shard
    second = beta_two * moment_two + (1.0 - beta_two) * grad_shard * grad_shard
    update = first / correct_one / (jnp.sqrt(second / correct_two) + adam_eps)
    master_new = master - learn_rate * (update + weight_decay * master)
    return (
        output.astype(jnp.bfloat16),
        input_grad,
        grad_shard,
        first,
        second,
        master_new,
        master_new.astype(jnp.bfloat16),
    )


def solution(mesh):
    return jax.shard_map(
        local,
        mesh=mesh,
        in_specs=(
            P(("dp", "zero"), None),
            P(("dp", "zero")),
            P(("dp", "zero"), None),
            P("zero"),
            P("zero"),
            P("zero"),
        ),
        out_specs=(
            P(("dp", "zero"), None),
            P(("dp", "zero"), None),
            P("zero"),
            P("zero"),
            P("zero"),
            P("zero"),
            P("zero"),
        ),
        check_vma=False,
    )
```

profile of v0, /device:TPU:8, one launch (start us, length us, event | category | flops | bytes accessed | tf_op | source)
XLA Modules:
  0.0 2674.3 jit_solution(15234901383597866105)
XLA Ops:
  17.0 19.0 dynamic-update-slice
  45.4 498.0 %all-reduce.9.cloned.1.call-done = bf16[9440256]{0:T(1024)(128)(2,1)} async-done(((bf16[9440256]{0:T(1024)(128)(2,1)}), bf16[9440256]{0:T(1024)(128)(2,1)}) %all-reduce.9.cloned.1.call-update) | async-done | bytes 18880528
  567.5 12.5 fusion.62
  580.0 11.1 fusion
  591.7 11.7 fusion.35
  603.4 12.5 fusion.61
  615.9 10.9 fusion.1
  626.9 11.3 fusion.36
  646.0 10.8 fusion.54
  684.0 10.9 fusion.65
  695.0 18.2 multiply_convert_fusion.3
  728.0 25.3 multiply_convert_fusion.2
  776.6 20.0 multiply_reduce_fusion.1
  796.5 16.6 multiply_convert_fusion.1
  823.4 16.5 multiply_reduce_fusion
  839.9 12.5 fusion.10
  855.3 10.3 convolution_bitcast_fusion.1
  873.4 11.7 fusion.41
  885.2 15.2 multiply_convert_fusion
  900.4 10.0 multiply_convert_fusion.5
  916.1 12.9 add_convert_fusion
  974.3 10.8 reshape.330
  1014.6 1592.4 %all-reduce.14 = bf16[9440256]{0:T(1024)(128)(2,1)} all-reduce(f32[9440256]{0:T(1024)} %constant_dynamic-update-slice_fusion), channel_id=2, replica_groups=mesh['dp'=2,'zero'=16] {'zero'}, use_global_device_ids=true, to_apply=%region_18.19.clone | all-reduce | flops 9440256 | bytes 56641536
  2611.4 17.0 all-reduce.13.cloned.1.call-done
  (238 shorter events, 258.7 us)
Async XLA Ops:
  7.2 536.1 %all-reduce.9.cloned.1.call-start = ((), (), s32[]{:S(2)}) async-start(), calls=%async_computation | async-start | bytes 37761024
  36.1 2592.4 %all-reduce.13.cloned.1.call-start = ((), (), s32[]{:S(2)}) async-start(), calls=%async_computation.2 | async-start | bytes 2363392
  552.4 74.4 %copy-start.13 = (bf16[768,1024]{1,0:T(8,128)(2,1)}, bf16[768,1024]{1,0:T(8,128)(2,1)S(1)}, u32[]{:S(2)}) copy-start(bf16[768,1024]{1,0:T(8,128)(2,1)S(1)} %convolution_convert_fusion.3) | copy-start | bytes 4718596
  560.4 43.0 %copy-start.20 = (bf16[512,768]{0,1:T(8,128)(2,1)}, bf16[512,768]{0,1:T(8,128)(2,1)S(1)}, u32[]{:S(2)}) copy-start(bf16[512,768]{0,1:T(8,128)(2,1)S(1)} %get-tuple-element.111) | copy-start | bytes 2359300
  567.4 36.0 %copy-start.16 = (bf16[768,1024]{1,0:T(8,128)(2,1)}, bf16[768,1024]{1,0:T(8,128)(2,1)S(1)}, u32[]{:S(2)}) copy-start(bf16[768,1024]{1,0:T(8,128)(2,1)S(1)} %convolution_convert_fusion.1) | copy-start | bytes 4718596
  626.8 13.8 copy-start.41
  775.9 20.7 copy-start.10
  796.5 16.6 copy-start.24
  823.4 16.5 copy-start.12
  839.9 12.5 copy-start.7
  839.9 12.5 copy-start.35
  852.4 13.2 slice-start.15
  865.6 19.5 slice-start
  865.7 19.5 slice-start.1
  865.7 19.5 slice-start.2
  916.1 12.9 copy-start.32
  916.1 12.9 copy-start.39
  916.1 12.9 copy-start.40
  955.4 13.2 slice-start.12
  985.0 16.5 slice-start.9
  992.0 13.4 slice-start.6
  992.0 13.4 slice-start.7
  2610.0 26.8 %copy-start.36 = (bf16[768,768]{1,0:T(8,128)(2,1)S(1)}, bf16[768,768]{1,0:T(8,128)(2,1)}, u32[]{:S(2)}) copy-start(bf16[768,768]{1,0:T(8,128)(2,1)} %slice.156) | copy-start | bytes 3538948
  2610.0 48.0 %all-reduce.11.cloned.1.call-start = ((), (), s32[]{:S(2)}) async-start(), calls=%async_computation.1 | async-start | bytes 2363392
  (50 other events, 280.8 us)
Sparse Core Ops, SparseCore 0:
  36.2 507.0 all-reduce.8
  2610.1 18.2 all-reduce.12
  2636.9 21.0 all-reduce.10
where the time goes:
time: 2690 us; the launch traced here: 2670 us
  blocking collectives  1590 us (59%)
  waiting for transfers between devices  522 us (19%)
  matrix products  283 us (11%)
  local copies, waits for them, and re-layouts  182 us (7%)
  other arithmetic  77.8 us (3%)
    unnamed x1, blocking collectives  1590 us
    unnamed x6, waiting for transfers between devices  522 us
    unnamed x165, local copies, waits for them, and re-layouts  98.4 us
    dot_general x7, matrix products, right_trans(): jnp.einsum('re,de->rd', left, right, preferred_element_type=jnp.float32)  54.3 us
  transfers between devices with their start and end apart: 3, of which 3 were waited for; matrix products, arithmetic and copies ran while one was open for 1% of the time, Pallas kernels for 0%

commit v1 on v0

--- a/solution.py
+++ b/solution.py
@@ -1,7 +1,11 @@
+import functools
+
 import jax
 import jax.numpy as jnp
 from jax import lax
 from jax.sharding import PartitionSpec as P
+import jax.experimental.pallas as pl
+import jax.experimental.pallas.tpu as pltpu
 
 D = 768
 HEADS = 12
@@ -20,20 +24,6 @@
 norm_eps = 1e-06
 inv_root_two = 0.7071067811865476
 inv_root_tau = 0.3989422804014327
-
-
-def split_flat(flat):
-    dims_list = ((D, D), (D, D), (D, D), (D, D), (D, FF), (D, FF), (FF, D))
-    pieces = []
-    offset = 0
-    for dims_pair in dims_list:
-        length = dims_pair[0] * dims_pair[1]
-        pieces.append(flat[offset : offset + length].reshape(dims_pair))
-        offset = offset + length
-    for number in range(4):
-        pieces.append(flat[offset : offset + D].astype(jnp.float32))
-        offset = offset + D
-    return pieces
 
 
 def head_slopes():
@@ -133,21 +123,309 @@
     )
 
 
+MESH=pl.DeviceIdType.MESH
+RA,RB,RC=48,128,208
+OFFS=(0,RA,RA+RB)
+LENS=(RA,RB,RC)
+HALF=384
+
+def place():
+    i=lax.axis_index("zero"); c=lax.axis_index("dp")
+    z=i//4; y=(i//2)%2; x=i%2
+    return i,c,z,y,x
+
+def enter_barrier(i,c,z):
+    bar=pltpu.get_barrier_semaphore()
+    for dev in ((c,i+1-2*(i%2)),(c,i+2-4*((i//2)%2)),(1-c,i)):
+        pl.semaphore_signal(bar,inc=1,device_id=dev,device_id_type=MESH)
+    @pl.when(z>0)
+    def _(): pl.semaphore_signal(bar,inc=1,device_id=(c,i-4),device_id_type=MESH)
+    @pl.when(z<3)
+    def _(): pl.semaphore_signal(bar,inc=1,device_id=(c,i+4),device_id_type=MESH)
+    pl.semaphore_wait(bar,3+jnp.minimum(z,1)+jnp.minimum(3-z,1))
+
+def ag_kernel(blk,result,out,own_sem,out_sem,rx,ry,rz,sx,sy,szr,szl,rs,ss):
+    i,c,z,y,x=place()
+    xp=(c,i+1-2*x); yp=(c,i+2-4*y); sib=(1-c,i); zr=(c,i+4); zl=(c,i-4)
+    enter_barrier(i,c,z)
+    own=pltpu.make_async_copy(blk,out.at[z,y,x],own_sem)
+    own.start(); own.wait()
+    rows=[pl.ds(pl.multiple_of(c*HALF+OFFS[k],16),LENS[k]) for k in range(3)]
+    orow=[pl.ds(pl.multiple_of((1-c)*HALF+OFFS[k],16),LENS[k]) for k in range(3)]
+    def cp(sl,dev,s,r):
+        return pltpu.make_async_remote_copy(src_ref=out.at[sl],dst_ref=out.at[sl],send_sem=s,recv_sem=r,device_id=dev,device_id_type=MESH)
+    al=slice(None)
+    pend=[]
+    def A1(xx,R=rows): return (z,y,xx,R[0])
+    def A2(yy,R=rows): return (z,yy,al,R[0])
+    def A3(zs,R=rows): return (zs,al,al,R[0])
+    def B1(yy,R=rows): return (z,yy,x,R[1])
+    def B2(zs,xx,R=rows): return (zs,al,xx,R[1])
+    def C1(zs,R=rows): return (zs,y,x,R[2])
+    def C2(zs,xx,R=rows): return (zs,y,xx,R[2])
+    def C3(zs,yy,R=rows): return (zs,yy,al,R[2])
+    def sibsend(sl,k):
+        cp(sl,sib,ss.at[k],rs.at[k]).start()
+    def sibwait(sl,k):
+        d=cp(sl,sib,ss.at[k],rs.at[k]); d.wait_send(); d.wait_recv()
+    def zsend(sl,zs,base):
+        @pl.when(jnp.logical_and(zs<=z,z<3))
+        def _(): cp(sl,zr,szr.at[base+zs],rz.at[base+zs]).start()
+        @pl.when(jnp.logical_and(zs>=z,z>0))
+        def _(): cp(sl,zl,szl.at[base+zs],rz.at[base+zs]).start()
+    def zsent(sl,zs,base):
+        @pl.when(jnp.logical_and(zs<=z,z<3))
+        def _(): cp(sl,zr,szr.at[base+zs],rz.at[base+zs]).wait_send()
+        @pl.when(jnp.logical_and(zs>=z,z>0))
+        def _(): cp(sl,zl,szl.at[base+zs],rz.at[base+zs]).wait_send()
+    def zwait(sl,zs,base):
+        cp(sl,zr,szr.at[base+zs],rz.at[base+zs]).wait_recv()
+    A,B,C=0,4,8
+    def xs(sl,k): cp(sl,xp,sx.at[k],rx.at[k]).start()
+    def xw(sl,k): cp(sl,xp,sx.at[k],rx.at[k]).wait_recv()
+    def xd(sl,k): cp(sl,xp,sx.at[k],rx.at[k]).wait_send()
+    def ys(sl,k): cp(sl,yp,sy.at[k],ry.at[k]).start()
+    def yw(sl,k): cp(sl,yp,sy.at[k],ry.at[k]).wait_recv()
+    def yd(sl,k): cp(sl,yp,sy.at[k],ry.at[k]).wait_send()
+    xs(A1(x),0); ys(B1(y),1); zsend(C1(z),z,C); xs(C2(z,x),5+z)
+    xw(A1(1-x),0); ys(A2(y),0); sibsend(A1(1-x),0)
+    yw(B1(1-y),1); zsend(B2(z,x),z,B); xs(B2(z,x),1+z); sibsend(B1(1-y),6)
+    xw(C2(z,1-x),5+z); ys(C3(z,y),2+z); sibsend(C2(z,1-x),19+z)
+    def late(zs):
+        xw(C2(zs,1-x),5+zs); ys(C3(zs,y),2+zs); sibsend(C2(zs,1-x),19+zs)
+    def early(zs):
+        zwait(C1(zs),zs,C); zsend(C1(zs),zs,C); xs(C2(zs,x),5+zs); sibsend(C1(zs),15+zs)
+        zwait(B2(zs,x),zs,B); zsend(B2(zs,x),zs,B); xs(B2(zs,x),1+zs); sibsend(B2(zs,x),7+zs)
+    def both(s,f):
+        @pl.when(z-s>=0)
+        def _(): f(z-s)
+        @pl.when(z+s<=3)
+        def _(): f(z+s)
+    both(1,early)
+    yw(A2(1-y),0); zsend(A3(z),z,A); sibsend(A2(1-y),1)
+    both(1,late)
+    both(2,early)
+    def a3(zs):
+        zwait(A3(zs),zs,A); zsend(A3(zs),zs,A); sibsend(A3(zs),2+zs)
+    both(1,a3)
+    both(2,late)
+    both(3,early)
+    both(2,a3)
+    both(3,late)
+    both(3,a3)
+    for s in range(4):
+        def fin(zs):
+            xw(B2(zs,1-x),1+zs); sibsend(B2(zs,1-x),11+zs)
+            yw(C3(zs,1-y),2+zs); sibsend(C3(zs,1-y),23+zs)
+        if s==0: fin(z)
+        else: both(s,fin)
+    xd(A1(x),0); yd(A2(y),0); yd(B1(y),1)
+    sibwait(A1(1-x,orow),0) ; sibwait(A2(1-y,orow),1); sibwait(B1(1-y,orow),6)
+    for zs in range(4):
+        xd(B2(zs,x),1+zs); xd(C2(zs,x),5+zs); yd(C3(zs,y),2+zs)
+        zsent(A3(zs),zs,A); zsent(B2(zs,x),zs,B); zsent(C1(zs),zs,C)
+        sibwait(B2(zs,1-x,orow),11+zs); sibwait(C2(zs,1-x,orow),19+zs); sibwait(C3(zs,1-y,orow),23+zs)
+        @pl.when(zs!=z)
+        def _():
+            sibwait(A3(zs,orow),2+zs); sibwait(B2(zs,x,orow),7+zs); sibwait(C1(zs,orow),15+zs)
+    leave=[pltpu.make_async_copy(out.at[zs],result.at[zs],out_sem.at[zs]) for zs in range(4)]
+    for move in leave: move.start()
+    for move in leave: move.wait()
+
+def gather_blocks(blk):
+    D=pltpu.SemaphoreType.DMA
+    return pl.pallas_call(ag_kernel,out_shape=jax.ShapeDtypeStruct((4,2,2,768,768),jnp.bfloat16),
+        in_specs=[pl.BlockSpec(memory_space=pl.ANY)],out_specs=pl.BlockSpec(memory_space=pl.ANY),
+        scratch_shapes=[pltpu.VMEM((4,2,2,768,768),jnp.bfloat16),D,D((4,)),D((9,)),D((6,)),D((12,)),D((9,)),D((6,)),D((12,)),D((12,)),D((27,)),D((27,))],
+        compiler_params=pltpu.CompilerParams(collective_id=1,has_side_effects=True,vmem_limit_bytes=40<<20),name="gather_blocks")(blk)
+
+
+ALL = slice(None)
+
+def rs_kernel(g,out,own,sl,la1,la2,lafr,lafl,lb1,lb2r,lb2l,lb3,lc1r,lc1l,lc2,lc3,res,
+              own_sem,ss,rs,rx,ry,rzr,rzl,sx,sy,szr,szl,fs,fr,osem):
+    i,c,z,y,x=place()
+    xp=(c,i+1-2*x); yp=(c,i+2-4*y); sib=(1-c,i); zr=(c,i+4); zl=(c,i-4)
+    mine=pl.ds(pl.multiple_of(c*HALF,16),HALF); other=pl.ds(pl.multiple_of((1-c)*HALF,16),HALF)
+    locs=[pltpu.make_async_copy(g.at[zt,:,:,mine],own.at[zt],own_sem.at[zt]) for zt in range(4)]
+    for d in locs: d.start()
+    enter_barrier(i,c,z)
+    sibs=[pltpu.make_async_remote_copy(src_ref=g.at[zt,:,:,other],dst_ref=sl.at[zt],send_sem=ss.at[zt],recv_sem=rs.at[zt],device_id=sib,device_id_type=MESH) for zt in range(4)]
+    for d in sibs: d.start()
+    r=[pl.ds(OFFS[k],LENS[k]) for k in range(3)]
+    def rc(src,dst,dev,s,q):
+        return pltpu.make_async_remote_copy(src_ref=src,dst_ref=dst,send_sem=s,recv_sem=q,device_id=dev,device_id_type=MESH)
+    def add(dst,src,n,rows,step):
+        @pl.loop(0,rows//step)
+        def _(k):
+            q=pl.ds(pl.multiple_of(k*step,16),step)
+            dst(q)[...]=(dst(q)[...].astype(jnp.float32)+src(q)[...].astype(jnp.float32)).astype(jnp.bfloat16)
+    def sub(k,q): return pl.ds(pl.multiple_of(OFFS[k]+q.start,16),q.size)
+    def add2(ownidx,k,land):
+        add(lambda q: own.at[tuple(ownidx)+(sub(k,q),)], lambda q: land.at[tuple([ALL]*(len(land.shape)-2))+(q,)],0,LENS[k],16)
+    def C3(zt): return rc(own.at[zt,1-y,:,r[2]],lc3.at[zt],yp,sy.at[zt],ry.at[zt])
+    def B3(zt): return rc(own.at[zt,:,1-x,r[1]],lb3.at[zt],xp,sx.at[zt],rx.at[zt])
+    def C2(zt): return rc(own.at[zt,y,1-x,r[2]],lc2.at[zt],xp,sx.at[4+zt],rx.at[4+zt])
+    A2=rc(own.at[z,1-y,:,r[0]],la2,yp,sy.at[4],ry.at[4])
+    A1=rc(own.at[z,y,1-x,r[0]],la1,xp,sx.at[8],rx.at[8])
+    B1=rc(own.at[z,1-y,x,r[1]],lb1,yp,sy.at[5],ry.at[5])
+    def zline(src,landr,landl,base):
+        def R(zt): return rc(src(zt),landr.at[zt],zr,szr.at[base+zt],rzr.at[base+zt])
+        def L(zt): return rc(src(zt),landl.at[zt],zl,szl.at[base+zt],rzl.at[base+zt])
+        return R,L
+    AR,AL=zline(lambda zt: own.at[zt,:,:,r[0]],lafr,lafl,0)
+    BR,BL=zline(lambda zt: own.at[zt,:,x,r[1]],lb2r,lb2l,4)
+    CR,CL=zline(lambda zt: own.at[zt,y,x,r[2]],lc1r,lc1l,8)
+    def zgo(zt,idx,k,R,L,landr,landl):
+        @pl.when(zt>z)
+        def _():
+            @pl.when(z>0)
+            def _():
+                R(zt).wait_recv(); add2(idx,k,landr.at[zt])
+            R(zt).start()
+        @pl.when(zt<z)
+        def _():
+            @pl.when(z<3)
+            def _():
+                L(zt).wait_recv(); add2(idx,k,landl.at[zt])
+            L(zt).start()
+    def zfin(idx,k,R,L,landr,landl):
+        @pl.when(z>0)
+        def _(): R(z).wait_recv(); add2(idx,k,landr.at[z])
+        @pl.when(z<3)
+        def _(): L(z).wait_recv(); add2(idx,k,landl.at[z])
+    def far(s):
+        return s
+    def sumsib(zt):
+        locs[zt].wait(); sibs[zt].wait_recv()
+        @pl.loop(0,HALF//16)
+        def _(k):
+            q=pl.ds(pl.multiple_of(k*16,16),16)
+            own[zt,:,:,q]=(own[zt,:,:,q].astype(jnp.float32)+sl[zt,:,:,q].astype(jnp.float32)).astype(jnp.bfloat16)
+    order=[3,0,2,1]
+    for zt in order:
+        sumsib(zt)
+        C3(zt).start(); B3(zt).start()
+        zgo(zt,(zt,ALL,ALL),0,AR,AL,lafr,lafl)
+    def c3done(zt):
+        C3(zt).wait_recv(); add2((zt,y,ALL),2,lc3.at[zt]); C2(zt).start()
+    def b3done(zt):
+        B3(zt).wait_recv(); add2((zt,ALL,x),1,lb3.at[zt])
+        zgo(zt,(zt,ALL,x),1,BR,BL,lb2r,lb2l)
+    def c2done(zt):
+        C2(zt).wait_recv(); add2((zt,y,x),2,lc2.at[zt])
+        zgo(zt,(zt,y,x),2,CR,CL,lc1r,lc1l)
+    c3done(3); b3done(3); c3done(0); b3done(0); c2done(3); c3done(2); b3done(2); c2done(0); c3done(1); b3done(1); c2done(2); c2done(1)
+    zfin((z,ALL,ALL),0,AR,AL,lafr,lafl)
+    A2.start()
+    zfin((z,ALL,x),1,BR,BL,lb2r,lb2l)
+    B1.start()
+    A2.wait_recv(); add2((z,y,ALL),0,la2)
+    A1.start()
+    zfin((z,y,x),2,CR,CL,lc1r,lc1l)
+    def final(k,land):
+        @pl.loop(0,LENS[k]//16)
+        def _(t):
+            q=pl.ds(pl.multiple_of(t*16,16),16)
+            o=pl.ds(pl.multiple_of(OFFS[k]+t*16,16),16)
+            v=own[z,y,x,o].astype(jnp.float32)
+            if land is not None: v=v+land[q].astype(jnp.float32)
+            res[o]=v
+    final(2,None)
+    B1.wait_recv(); final(1,lb1)
+    A1.wait_recv(); final(0,la1)
+    fin=rc(res,out.at[mine],sib,fs,fr)
+    fin.start()
+    loc=pltpu.make_async_copy(res,out.at[mine],osem)
+    loc.start()
+    for zt in range(4):
+        sibs[zt].wait_send(); C3(zt).wait_send(); B3(zt).wait_send(); C2(zt).wait_send()
+        for R,L in ((AR,AL),(BR,BL),(CR,CL)):
+            @pl.when(zt>z)
+            def _(): R(zt).wait_send()
+            @pl.when(zt<z)
+            def _(): L(zt).wait_send()
+    A2.wait_send(); A1.wait_send(); B1.wait_send()
+    loc.wait(); fin.wait_send()
+    rc(res,out.at[other],sib,fs,fr).wait_recv()
+
+def reduce_blocks(g):
+    D=pltpu.SemaphoreType.DMA
+    bf=jnp.bfloat16
+    V=lambda *s: pltpu.VMEM(s,bf)
+    return pl.pallas_call(rs_kernel,out_shape=jax.ShapeDtypeStruct((768,768),jnp.float32),
+        in_specs=[pl.BlockSpec(memory_space=pl.ANY)],out_specs=pl.BlockSpec(memory_space=pl.ANY),
+        scratch_shapes=[V(4,2,2,HALF,768),V(4,2,2,HALF,768),V(RA,768),V(2,RA,768),V(4,2,2,RA,768),V(4,2,2,RA,768),
+            V(RB,768),V(4,2,RB,768),V(4,2,RB,768),V(4,2,RB,768),V(4,RC,768),V(4,RC,768),V(4,RC,768),V(4,2,RC,768),pltpu.VMEM((HALF,768),jnp.float32),
+            D((4,)),D((4,)),D((4,)),D((9,)),D((6,)),D((12,)),D((12,)),D((9,)),D((6,)),D((12,)),D((12,)),D,D,D],
+        compiler_params=pltpu.CompilerParams(collective_id=2,has_side_effects=True,vmem_limit_bytes=58<<20),name="reduce_blocks")(g)
+
+SQUARE = D * D
+TAIL = 4 * D
+
+
+def from_wide(blocks):
+    return blocks.reshape(4, 4, D // 4, D).transpose(0, 2, 1, 3).reshape(D, FF)
+
+
+def to_wide(value):
+    return value.reshape(4, D // 4, 4, D).transpose(0, 2, 1, 3).reshape(2, 2, D, D)
+
+
+def swap_wide(block, index, inverse):
+    dims = (4, D // 4, D) if inverse else (D // 4, 4, D)
+    swapped = block.reshape(dims).transpose(1, 0, 2).reshape(D, D)
+    wide = jnp.logical_and(index >= 4, index < 12)
+    return jnp.where(wide, swapped, block)
+
+
+def gather_weights(master):
+    count = lax.axis_size("zero")
+    index = lax.axis_index("zero")
+    size = 16 * SQUARE // count
+    weights = master.astype(jnp.bfloat16)
+    last = weights[-TAIL:]
+    before = lax.ppermute(last, "zero", [(k, k + 1) for k in range(count - 1)])
+    joined = jnp.concatenate([before, weights])
+    block = lax.dynamic_slice(joined, (TAIL - TAIL // count * index,), (size,))
+    norms = lax.psum(jnp.where(index == count - 1, last.astype(jnp.float32), 0.0), "zero")
+    if count == 16:
+        blocks = gather_blocks(swap_wide(block.reshape(D, D), index, False))
+    else:
+        natural = lax.all_gather(block.reshape(-1, D), "zero", axis=0, tiled=True)
+        parts = natural.reshape(4, 4 * D, D)
+        wide = [to_wide(parts[k].reshape(D, FF)) for k in (1, 2)]
+        blocks = jnp.stack([parts[0].reshape(2, 2, D, D), *wide, parts[3].reshape(2, 2, D, D)])
+    return blocks, norms.reshape(4, D)
+
+
+def scatter_grads(grads, norm_grads):
+    count = lax.axis_size("zero")
+    index = lax.axis_index("zero")
+    if count == 16:
+        block = swap_wide(reduce_blocks(grads), index, True)
+    else:
+        wide = [from_wide(grads[k]).reshape(4 * D, D) for k in (1, 2)]
+        natural = jnp.concatenate(
+            [grads[0].reshape(4 * D, D), *wide, grads[3].reshape(4 * D, D)]
+        )
+        block = lax.psum_scatter(natural, "zero", scatter_dimension=0, tiled=True)
+        block = lax.psum(block.astype(jnp.float32), "dp")
+    tail = lax.psum(norm_grads.reshape(-1), ("dp", "zero"))
+    flat = block.reshape(-1)
+    after = lax.ppermute(flat[:TAIL], "zero", [(k + 1, k) for k in range(count - 1)])
+    joined = jnp.concatenate([flat, jnp.where(index == count - 1, tail, after)])
+    shard = flat.shape[0] + TAIL // count
+    return lax.dynamic_slice(joined, (TAIL // count * index,), (shard,))
+
+
 def local(tokens, segments, cotangent, master, moment_one, moment_two):
-    flat_weights = lax.all_gather(master.astype(jnp.bfloat16), "zero", axis=0, tiled=True)
-    (
-        w_query,
-        w_key,
-        w_value,
-        w_out,
-        w_gate,
-        w_up,
-        w_down,
-        gain_one,
-        shift_one,
-        gain_two,
-        shift_two,
-    ) = split_flat(flat_weights)
+    blocks, norms = gather_weights(master)
+    w_query, w_key, w_value, w_out = blocks[0].reshape(4, D, D)
+    w_gate = from_wide(blocks[1])
+    w_up = from_wide(blocks[2])
+    w_down = blocks[3].reshape(FF, D)
+    gain_one, shift_one, gain_two, shift_two = norms
     height = tokens.shape[0]
     count = height // LEN
 
@@ -216,31 +494,19 @@
         + right_trans(grad_key, w_key)
         + right_trans(grad_value, w_value)
     )
-    flat_local = jnp.concatenate(
+    low = lambda value: value.astype(jnp.bfloat16)
+    grads = jnp.stack(
         [
-            grad_w_query.reshape(-1),
-            grad_w_key.reshape(-1),
-            grad_w_value.reshape(-1),
-            grad_w_out.reshape(-1),
-            grad_w_gate.reshape(-1),
-            grad_w_up.reshape(-1),
-            grad_w_down.reshape(-1),
-            grad_gain_one,
-            grad_shift_one,
-            grad_gain_two,
-            grad_shift_two,
+            low(jnp.stack([grad_w_query, grad_w_key, grad_w_value, grad_w_out])).reshape(2, 2, D, D),
+            to_wide(low(grad_w_gate)),
+            to_wide(low(grad_w_up)),
+            low(grad_w_down).reshape(2, 2, D, D),
         ]
     )
+    norm_grads = jnp.stack([grad_gain_one, grad_shift_one, grad_gain_two, grad_shift_two])
     groups = lax.axis_size("zero")
     replicas = lax.axis_size("dp")
-    partial_sum = lax.psum_scatter(flat_local, "zero", scatter_dimension=0, tiled=True)
-    piece_sum = lax.psum_scatter(
-        partial_sum.astype(jnp.bfloat16), "dp", scatter_dimension=0, tiled=True
-    ).astype(jnp.float32)
-    summed = lax.all_gather(piece_sum.astype(jnp.bfloat16), "dp", axis=0, tiled=True).astype(
-        piece_sum.dtype
-    )
-    grad_shard = summed / (count * groups * replicas)
+    grad_shard = scatter_grads(grads, norm_grads) / (count * groups * replicas)
     first = beta_one * moment_one + (1.0 - beta_one) * grad_shard
     second = beta_two * moment_two + (1.0 - beta_two) * grad_shard * grad_shard
     update = first / correct_one / (jnp.sqrt(second / correct_two) + adam_eps)

time: 2690 us -> 780 us (0.29)
  blocking collectives: 1590 us -> 109 us
  waiting for transfers between devices: 522 us -> 0.01 us
  Pallas kernels: 0 us -> 197 us
  local copies, waits for them, and re-layouts: 182 us -> 93.5 us
    unnamed x1 -> x0, blocking collectives: 1590 us -> none
    unnamed x6 -> x0, waiting for transfers between devices: 522 us -> none
    pallas_call x0 -> x2, Pallas kernels: none -> 197 us  [the longest x1 116 us: reduce_blocks(): pl.pallas_call(rs_kernel, out_shape=jax.ShapeDtypeStruct((768, 768), jnp....]
    psum x0 -> x2, blocking collectives: none -> 109 us  [the longest x1 68.6 us: gather_weights(): lax.psum(jnp.where(index == count - 1, last.astype(jnp.float32), 0.0), 'z...]
    unnamed x165 -> x100, local copies, waits for them, and re-layouts: 98.4 us -> 23.3 us
    slice x9 -> x4, local copies, waits for them, and re-layouts: 52 us -> 9.62 us  [the longest x1 9.53 us: local(): w_down = blocks[3].reshape(FF, D)]
  transfers between devices with their start and end apart: 3 -> 2, of which waited for: 3 -> 0; matrix products, arithmetic and copies ran while one was open for 1% -> 3% of each run, Pallas kernels for 0% -> 0%
where the time goes in v1:
time: 780 us; the launch traced here: 771 us
  matrix products  266 us (34%)
  Pallas kernels  197 us (25%)
  blocking collectives  109 us (14%)
  other arithmetic  98.6 us (13%)
  local copies, waits for them, and re-layouts  93.5 us (12%)
    pallas_call x1, Pallas kernels, reduce_blocks(): pl.pallas_call(rs_kernel, out_shape=jax.ShapeDtypeStruct((768, 768), jnp....  116 us
    pallas_call x1, Pallas kernels, gather_blocks(): pl.pallas_call(ag_kernel, out_shape=jax.ShapeDtypeStruct((4, 2, 2, 768, 7...  81.2 us
    psum x1, blocking collectives, gather_weights(): lax.psum(jnp.where(index == count - 1, last.astype(jnp.float32), 0.0), 'z...  68.6 us
    dot_general x7, matrix products, right_trans(): jnp.einsum('re,de->rd', left, right, preferred_element_type=jnp.float32)  59.3 us
    dot_general x7, matrix products, project(): return jnp.dot(left, right, preferred_element_type=jnp.float32)  44.4 us
    psum x1, blocking collectives, scatter_grads(): tail = lax.psum(norm_grads.reshape(-1), ('dp', 'zero'))  39.9 us
    dot_general x2, matrix products, attend_backward(): jnp.einsum('qhd,khd->hqk', g_block, values_seq, preferred_element_type=jn...  39.4 us
    convert_element_type x2, other arithmetic, attend_backward(): grad_scores = (probs * (grad_probs - delta)).astype(jnp.bfloat16)  33.4 us
  transfers between devices with their start and end apart: 2, of which 0 were waited for; matrix products, arithmetic and copies ran while one was open for 3% of the time, Pallas kernels for 0%

profile of v1, /device:TPU:8, one launch (start us, length us, event | category | flops | bytes accessed | tf_op | source)
XLA Modules:
  0.0 771.0 jit_solution(8261724684437397059)
XLA Ops:
  6.0 68.6 %psum.14 = f32[3072]{0:T(1024)S(1)} all-reduce(f32[3072]{0:T(1024)S(1)} %convert_select_fusion), channel_id=1, replica_groups=mesh['dp'=2,'zero'=16] {'zero'}, use_global_device_ids=true, to_apply=%region_6.7 | all-reduce | flops 3072 | bytes 24576 | tf_op jit(solution)/shard_map/psum | solution.py:391
  87.3 81.2 %gather_blocks.1 = bf16[4,2,2,768,768]{4,3,2,1,0:T(8,128)(2,1)} custom-call(bf16[768,768]{1,0:T(8,128)(2,1)S(1)} %bitcast_select_fusion.blk), custom_call_target="tpu_custom_call" | custom-call | tf_op jit(solution)/shard_map/gather_blocks/pallas_call | solution.py:237
  168.5 9.5 %fusion.56 = (bf16[1,2,2,768,768]{4,3,2,1,0:T(8,128)(2,1)}, bf16[1,2,2,768,768]{4,3,2,1,0:T(8,128)(2,1)S(1)}, bf16[1,2,2,768,768]{4,3,2,1,0:T(8,128)(2,1)S(1)}, bf16[1,2,2,768,768]{4,3,2,1,0:T(8,128)(2,1)S(1)}) fusion(bf16[4,2,2,768,768]{4,3,2,1,0:T(8,128)(2,1)} %gather_blocks.1), kind=kLoop, calls=%fused_computation.136 | loop fusion | bytes 37748736 | tf_op jit(solution)/shard_map/slice | solution.py:427
  185.6 12.3 %fusion.61 = (f32[12,512]{1,0:T(8,128)S(1)}, f32[12,512,1024]{2,1,0:T(8,128)}) fusion(f32[512,1024]{1,0:T(8,128)S(1)} %copy-done.23, f32[12]{0:T(128)S(1)} %multiply_exponential_fusion, bf16[512,12,64]{0,2,1:T(8,128)(2,1)S(1)} %bitcast.174, bf16[1024,12,64]{0,2,1:T(8,128)(2,1)S(1)} %bitcast.170, pred[512,1024]{1,0:T(8,128)(4,1)S(1)} %copy-done.36), kind=kOutput, calls=%fused_computation.141 | convolution fusion | flops 836757504 | bytes 30171184 | tf_op jit(solution)/shard_map/while/body/eval_jaxpr/qhd,khd->hqk/dot_general | solution.py:58
  198.0 10.9 %fusion.1 = f32[12,512]{1,0:T(8,128)S(1)} fusion(f32[12,512,1024]{2,1,0:T(8,128)} %get-tuple-element.109, f32[12,512]{1,0:T(8,128)S(1)} %get-tuple-element.108), kind=kLoop, calls=%fused_computation.13 | loop fusion | flops 12576768 | bytes 25214976 | tf_op jit(solution)/shard_map/while/body/eval_jaxpr/reduce_sum | solution.py:80
  209.5 12.0 %fusion.38 = bf16[12,64,512]{2,1,0:T(8,128)(2,1)} fusion(bf16[1024,12,64]{0,2,1:T(8,128)(2,1)} %bitcast.164, f32[12,512,1024]{2,1,0:T(8,128)} %get-tuple-element.109, f32[12,512]{1,0:T(8,128)S(1)} %fusion.1, f32[12,512]{1,0:T(8,128)S(1)} %get-tuple-element.108), kind=kOutput, calls=%fused_computation.93 | convolution fusion | flops 824573952 | bytes 27574272 | tf_op jit(solution)/shard_map/while/body/eval_jaxpr/hqk,khd->qhd/dot_general | solution.py:83
  221.5 13.8 %fusion.62 = (f32[12,512]{1,0:T(8,128)S(1)}, f32[12,512,1024]{2,1,0:T(8,128)}) fusion(f32[512,1024]{1,0:T(8,128)} %get-tuple-element.106, f32[12]{0:T(128)S(1)} %multiply_exponential_fusion, bf16[512,12,64]{0,2,1:T(8,128)(2,1)} %bitcast.180, bf16[1024,12,64]{0,2,1:T(8,128)(2,1)} %bitcast.171, pred[512,1024]{1,0:T(8,128)(4,1)} %get-tuple-element.102), kind=kOutput, calls=%fused_computation.142 | convolution fusion | flops 836757504 | bytes 30171184 | tf_op jit(solution)/shard_map/while/body/eval_jaxpr/qhd,khd->hqk/dot_general | solution.py:58
  235.3 10.9 %fusion = f32[12,512]{1,0:T(8,128)S(1)} fusion(f32[12,512,1024]{2,1,0:T(8,128)} %get-tuple-element.111, f32[12,512]{1,0:T(8,128)S(1)} %get-tuple-element.110), kind=kLoop, calls=%fused_computation.12 | loop fusion | flops 12576768 | bytes 25214976 | tf_op jit(solution)/shard_map/while/body/eval_jaxpr/reduce_sum | solution.py:80
  246.8 12.0 %fusion.39 = bf16[12,64,512]{2,1,0:T(8,128)(2,1)} fusion(bf16[1024,12,64]{0,2,1:T(8,128)(2,1)} %bitcast.165, f32[12,512,1024]{2,1,0:T(8,128)} %get-tuple-element.111, f32[12,512]{1,0:T(8,128)S(1)} %fusion, f32[12,512]{1,0:T(8,128)S(1)} %get-tuple-element.110), kind=kOutput, calls=%fused_computation.94 | convolution fusion | flops 824573952 | bytes 27574272 | tf_op jit(solution)/shard_map/while/body/eval_jaxpr/hqk,khd->qhd/dot_general | solution.py:83
  283.9 18.2 %multiply_convert_fusion.3 = (bf16[1024,3072]{1,0:T(8,128)(2,1)}, f32[1024,3072]{1,0:T(8,128)}, f32[1024,3072]{1,0:T(8,128)}) fusion(f32[1024,3072]{1,0:T(8,128)} %fusion.65, bf16[1024,768]{0,1:T(8,128)(2,1)S(1)} %fusion.26, bf16[768,3072]{1,0:T(8,128)(2,1)} %bitcast.138), kind=kOutput, calls=%fused_computation.29 | convolution fusion | flops 4850712576 | bytes 50331648 | tf_op jit(solution)/shard_map/dot_general | solution.py:45
  302.1 8.9 %fusion.64 = (f32[1024]{0:T(1024)S(1)}, f32[1024,768]{0,1:T(8,128)S(1)}) fusion(bf16[1024,3072]{1,0:T(8,128)(2,1)} %get-tuple-element.85, bf16[3072,768]{1,0:T(8,128)(2,1)} %bitcast.177, f32[768]{0:T(1024)S(1)} %get-tuple-element.100, f32[768]{0:T(1024)S(1)} %get-tuple-element.101, f32[1024]{0:T(1024)S(1)} %add_rsqrt_fusion.1, ...), kind=kOutput, calls=%fused_computation.144 | convolution fusion | flops 4836555776 | bytes 17319936 | tf_op jit(solution)/shard_map/dot_general | solution.py:45
  324.8 25.4 %multiply_convert_fusion.2 = (bf16[1024,3072]{1,0:T(8,128)(2,1)}, bf16[1024,3072]{1,0:T(8,128)(2,1)}) fusion(f32[1024,3072]{1,0:T(8,128)} %get-tuple-element.86, f32[1024,3072]{1,0:T(8,128)} %fusion.65, f32[1024,3072]{1,0:T(8,128)} %get-tuple-element.114, bf16[3072,768]{1,0:T(8,128)(2,1)} %bitcast.178, f32[1024]{0:T(1024)S(1)} %broadcast_multiply_fusion.3, ...), kind=kOutput, calls=%fused_computation.28 | convolution fusion | flops 4879810560 | bytes 59788288 | tf_op jit(solution)/shard_map/re,de->rd/dot_general | solution.py:53
  350.3 8.7 %fusion.66 = f32[1024,768]{0,1:T(8,128)S(1)} fusion(bf16[1024,3072]{1,0:T(8,128)(2,1)} %get-tuple-element.92, bf16[768,3072]{1,0:T(8,128)(2,1)} %bitcast.150), kind=kOutput, calls=%fused_computation.146 | convolution fusion | flops 4831838208 | bytes 14155776 | tf_op jit(solution)/shard_map/re,de->rd/dot_general | solution.py:53
  386.0 19.7 %multiply_reduce_fusion.1 = (f32[12,512]{1,0:T(8,128)S(1)}, f32[12,512,1024]{2,1,0:T(8,128)}) fusion(f32[12,512,1024]{2,1,0:T(8,128)} %get-tuple-element.111, f32[12,512]{1,0:T(8,128)S(1)} %copy-done.35, bf16[512,12,64]{0,2,1:T(8,128)(2,1)S(1)} %bitcast.160, bf16[1024,12,64]{0,2,1:T(8,128)(2,1)S(1)} %bitcast.166), kind=kOutput, calls=%fused_computation.4 | convolution fusion | flops 824174592 | bytes 52740096 | tf_op jit(solution)/shard_map/while/body/eval_jaxpr/qhd,khd->hqk/dot_general | solution.py:101
  405.7 16.7 %multiply_convert_fusion.1 = bf16[12,512,1024]{2,1,0:T(8,128)(2,1)S(1)} fusion(f32[12,512,1024]{2,1,0:T(8,128)} %get-tuple-element.119, f32[12,512,1024]{2,1,0:T(8,128)} %get-tuple-element.111, f32[12,512]{1,0:T(8,128)S(1)} %get-tuple-element.118, f32[12,512]{1,0:T(8,128)S(1)} %copy-done.35), kind=kLoop, calls=%fused_computation.3 | loop fusion | flops 25165824 | bytes 62963712 | tf_op jit(solution)/shard_map/while/body/eval_jaxpr/convert_element_type | solution.py:105
  433.8 12.1 %fusion.10 = f32[12,64,1024]{2,1,0:T(8,128)} fusion(bf16[512,12,64]{0,2,1:T(8,128)(2,1)S(1)} %bitcast.162, f32[12,512,1024]{2,1,0:T(8,128)} %get-tuple-element.109, f32[12,512]{1,0:T(8,128)S(1)} %copy-done.37), kind=kOutput, calls=%fused_computation.24 | convolution fusion | flops 817889280 | bytes 29122560 | tf_op jit(solution)/shard_map/while/body/eval_jaxpr/hqk,qhd->khd/dot_general | solution.py:115
  445.9 19.7 %multiply_reduce_fusion = (f32[12,512]{1,0:T(8,128)S(1)}, f32[12,512,1024]{2,1,0:T(8,128)}) fusion(f32[12,512,1024]{2,1,0:T(8,128)} %get-tuple-element.109, f32[12,512]{1,0:T(8,128)S(1)} %copy-done.37, bf16[512,12,64]{0,2,1:T(8,128)(2,1)S(1)} %bitcast.163, bf16[1024,12,64]{0,2,1:T(8,128)(2,1)S(1)} %bitcast.167), kind=kOutput, calls=%fused_computation.1 | convolution fusion | flops 824174592 | bytes 52740096 | tf_op jit(solution)/shard_map/while/body/eval_jaxpr/qhd,khd->hqk/dot_general | solution.py:101
  465.6 16.7 %multiply_convert_fusion = bf16[12,512,1024]{2,1,0:T(8,128)(2,1)S(1)} fusion(f32[12,512,1024]{2,1,0:T(8,128)} %get-tuple-element.121, f32[12,512,1024]{2,1,0:T(8,128)} %get-tuple-element.109, f32[12,512]{1,0:T(8,128)S(1)} %get-tuple-element.120, f32[12,512]{1,0:T(8,128)S(1)} %copy-done.37), kind=kLoop, calls=%fused_computation | loop fusion | flops 25165824 | bytes 62963712 | tf_op jit(solution)/shard_map/while/body/eval_jaxpr/convert_element_type | solution.py:105
  505.7 9.8 %reshape.296 = bf16[4,192,4,768]{3,2,1,0:T(4,128)(2,1)} reshape(bf16[768,3072]{1,0:T(8,128)(2,1)} %convolution_convert_fusion.2) | data formatting | bytes 9437184 | tf_op jit(solution)/shard_map/reshape | solution.py:372
  520.9 10.0 %reshape.297 = bf16[4,192,4,768]{3,2,1,0:T(4,128)(2,1)} reshape(bf16[768,3072]{1,0:T(8,128)(2,1)} %convolution_convert_fusion.1) | data formatting | bytes 9437184 | tf_op jit(solution)/shard_map/reshape | solution.py:372
  540.2 10.7 %add_convert_fusion = bf16[12,64,1024]{2,1,0:T(8,128)(2,1)S(1)} fusion(f32[12,64,1024]{2,1,0:T(8,128)S(1)} %copy-done.6, bf16[512,12,64]{0,2,1:T(8,128)(2,1)S(1)} %bitcast.161, f32[12,512,1024]{2,1,0:T(8,128)} %get-tuple-element.111, f32[12,512]{1,0:T(8,128)S(1)} %copy-done.35), kind=kOutput, calls=%fused_computation.48 | convolution fusion | flops 819462144 | bytes 30695424 | tf_op jit(solution)/shard_map/while/body/eval_jaxpr/hqk,qhd->khd/dot_general | solution.py:115
  561.9 17.1 %pad_maximum_fusion.g = bf16[4,2,2,768,768]{4,3,2,1,0:T(8,128)(2,1)} fusion(bf16[1,2,2,768,768]{4,3,2,1,0:T(8,128)(2,1)} %bitcast.176, bf16[1,2,2,768,768]{4,3,2,1,0:T(8,128)(2,1)} %bitcast.145, bf16[1,2,2,768,768]{4,3,2,1,0:T(8,128)(2,1)} %bitcast.144, bf16[1,2,2,768,768]{4,3,2,1,0:T(8,128)(2,1)} %bitcast.146), kind=kLoop, calls=%fused_computation.17 | loop fusion | flops 28311552 | bytes 37748736 | tf_op jit(solution)/shard_map/stack | solution.py:498
  579.0 115.6 %reduce_blocks.1 = f32[768,768]{1,0:T(8,128)} custom-call(bf16[4,2,2,768,768]{4,3,2,1,0:T(8,128)(2,1)} %pad_maximum_fusion.g), custom_call_target="tpu_custom_call" | custom-call | tf_op jit(solution)/shard_map/reduce_blocks/pallas_call | solution.py:356
  722.8 39.9 %psum.15 = f32[3072]{0:T(1024)S(1)} all-reduce(f32[3072]{0:T(1024)S(1)} %reshape.301), channel_id=1, replica_groups=mesh['dp'=2,'zero'=16] {'dp','zero'}, use_global_device_ids=true, to_apply=%region_19.20 | all-reduce | flops 3072 | bytes 24576 | tf_op jit(solution)/shard_map/psum | solution.py:414
  (179 shorter events, 188.8 us)
Async XLA Ops:
  0.6 5.3 copy-start.40
  2.5 81.9 %collective-permute-start = (bf16[3072]{0:T(1024)(128)(2,1)S(1)}, bf16[3072]{0:T(1024)(128)(2,1)S(1)}, u32[]{:S(2)}, u32[]{:S(2)}) collective-permute-start(bf16[3072]{0:T(1024)(128)(2,1)S(1)} %slice.91), channel_id=1, source_target_pairs={{0,1},{1,2},{2,3},{3,4},{4,5},{5,6},{6,7},{7,8},{8,9},{9,10},{10,1... | collective-permute-start | bytes 18440 | tf_op jit(solution)/shard_map/ppermute | solution.py:388
  168.5 9.5 %copy-start.24 = (bf16[1024,768]{1,0:T(8,128)(2,1)S(1)}, bf16[1024,768]{1,0:T(8,128)(2,1)}, u32[]{:S(2)}) copy-start(bf16[1024,768]{1,0:T(8,128)(2,1)} %param.6) | copy-start | bytes 4718596
  179.5 5.0 copy-start.18
  184.5 13.5 %copy-start.21 = (bf16[512,768]{0,1:T(8,128)(2,1)}, bf16[512,768]{0,1:T(8,128)(2,1)S(1)}, u32[]{:S(2)}) copy-start(bf16[512,768]{0,1:T(8,128)(2,1)S(1)} %get-tuple-element.97) | copy-start | bytes 2359300
  270.3 5.4 copy-start.3
  311.0 6.0 copy-start.4
  350.3 8.7 %copy-start.44 = (bf16[1024,3072]{1,0:T(8,128)(2,1)S(1)}, bf16[1024,3072]{1,0:T(8,128)(2,1)}, u32[]{:S(2)}) copy-start(bf16[1024,3072]{1,0:T(8,128)(2,1)} %get-tuple-element.92) | copy-start | bytes 18874372
  359.0 7.0 copy-start.43
  359.0 14.1 %slice-start = ((s8[4718592]{0:T(1024)(128)(4,1)}), s8[4194304]{0:T(1024)(128)(4,1)S(1)}, s32[]{:S(2)}) async-start(s8[4718592]{0:T(1024)(128)(4,1)} %bitcast.139), calls=%async_computation | async-start | bytes 8388608
  366.0 7.1 slice-start.1
  366.0 7.1 copy-start.5
  366.0 7.2 copy-start.20
  385.3 20.4 %copy-start.11 = (bf16[512,768]{0,1:T(8,128)(2,1)}, bf16[512,768]{0,1:T(8,128)(2,1)S(1)}, u32[]{:S(2)}) copy-start(bf16[512,768]{0,1:T(8,128)(2,1)S(1)} %get-tuple-element.95) | copy-start | bytes 2359300
  428.6 5.2 copy-start.13
  428.6 5.2 copy-start.37
  433.8 12.1 %copy-start.14 = (bf16[512,768]{0,1:T(8,128)(2,1)S(1)}, bf16[512,768]{0,1:T(8,128)(2,1)}, u32[]{:S(2)}) copy-start(bf16[512,768]{0,1:T(8,128)(2,1)} %get-tuple-element.94) | copy-start | bytes 2359300
  433.8 12.1 %copy-start.16 = (bf16[768,1024]{1,0:T(8,128)(2,1)S(1)}, bf16[768,1024]{1,0:T(8,128)(2,1)}, u32[]{:S(2)}) copy-start(bf16[768,1024]{1,0:T(8,128)(2,1)} %convolution_convert_fusion.6) | copy-start | bytes 4718596
  493.0 4.6 copy-start
  493.0 4.6 copy-start.22
  530.9 5.4 copy-start.32
  530.9 5.4 copy-start.34
  540.2 10.7 %copy-start.26 = (bf16[1024,768]{1,0:T(8,128)(2,1)S(1)}, bf16[1024,768]{1,0:T(8,128)(2,1)}, u32[]{:S(2)}) copy-start(bf16[1024,768]{1,0:T(8,128)(2,1)} %param.6) | copy-start | bytes 4718596
  706.3 56.4 %collective-permute-start.1 = (f32[3072]{0:T(1024)S(1)}, f32[3072]{0:T(1024)S(1)}, u32[]{:S(2)}, u32[]{:S(2)}) collective-permute-start(f32[3072]{0:T(1024)S(1)} %slice.90), channel_id=1, source_target_pairs={{1,0},{2,1},{3,2},{4,3},{5,4},{6,5},{7,6},{8,7},{9,8},{10,9},{11,1... | collective-permute-start | bytes 36872 | tf_op jit(solution)/shard_map/ppermute | solution.py:416
  (25 other events, 63.9 us)

commit v2 on v1

v2 whole, which is shorter than its diff:
```python
import functools

import jax
import jax.numpy as jnp
from jax import lax
from jax.sharding import PartitionSpec as P
import jax.experimental.pallas as pl
import jax.experimental.pallas.tpu as pltpu

D = 768
HEADS = 12
HEAD = 64
FF = 3072
LEN = 1024


learn_rate = 0.02
beta_one = 0.9
beta_two = 0.999
adam_eps = 1e-08
weight_decay = 0.01
correct_one = 1.0 - 0.9**10
correct_two = 1.0 - 0.999**10
norm_eps = 1e-06
inv_root_two = 0.7071067811865476
inv_root_tau = 0.3989422804014327


MESH=pl.DeviceIdType.MESH
RA,RB,RC=48,128,208
OFFS=(0,RA,RA+RB)
LENS=(RA,RB,RC)
HALF=384

def place():
    i=lax.axis_index("zero"); c=lax.axis_index("dp")
    z=i//4; y=(i//2)%2; x=i%2
    return i,c,z,y,x

def enter_barrier(i,c,z):
    bar=pltpu.get_barrier_semaphore()
    for dev in ((c,i+1-2*(i%2)),(c,i+2-4*((i//2)%2)),(1-c,i)):
        pl.semaphore_signal(bar,inc=1,device_id=dev,device_id_type=MESH)
    @pl.when(z>0)
    def _(): pl.semaphore_signal(bar,inc=1,device_id=(c,i-4),device_id_type=MESH)
    @pl.when(z<3)
    def _(): pl.semaphore_signal(bar,inc=1,device_id=(c,i+4),device_id_type=MESH)
    pl.semaphore_wait(bar,3+jnp.minimum(z,1)+jnp.minimum(3-z,1))

def ag_kernel(blk,last,result,tail,out,own_sem,out_sem,tr,tz,ty,tx,rx,ry,rz,sx,sy,szr,szl,rs,ss):
    i,c,z,y,x=place()
    xp=(c,i+1-2*x); yp=(c,i+2-4*y); sib=(1-c,i); zr=(c,i+4); zl=(c,i-4)
    enter_barrier(i,c,z)
    own=pltpu.make_async_copy(blk,out.at[z,y,x],own_sem)
    own.start()
    source=jnp.logical_and(z==3,jnp.logical_and(y==1,x==1))
    line=jnp.logical_and(y==1,x==1)
    @pl.when(source)
    def _(): tail[...]=last[...]
    def tcp(dev,s): return pltpu.make_async_remote_copy(src_ref=tail,dst_ref=tail,send_sem=s,recv_sem=tr,device_id=dev,device_id_type=MESH)
    def tail_along_z(first):
        @pl.when(jnp.logical_and(line,source if first else jnp.logical_not(source)))
        def _():
            if not first: tcp(zl,tz).wait_recv()
            @pl.when(z>0)
            def _(): tcp(zl,tz).start()
            tcp(yp,ty).start()
    def tail_along_x():
        @pl.when(x==1)
        def _():
            @pl.when(y==0)
            def _(): tcp(yp,ty).wait_recv()
            tcp(xp,tx).start()
    def tail_end():
        @pl.when(x==0)
        def _(): tcp(xp,tx).wait_recv()
        @pl.when(x==1)
        def _(): tcp(xp,tx).wait_send()
        @pl.when(line)
        def _():
            tcp(yp,ty).wait_send()
            @pl.when(z>0)
            def _(): tcp(zl,tz).wait_send()
    tail_along_z(True)
    own.wait()
    rows=[pl.ds(pl.multiple_of(c*HALF+OFFS[k],16),LENS[k]) for k in range(3)]
    orow=[pl.ds(pl.multiple_of((1-c)*HALF+OFFS[k],16),LENS[k]) for k in range(3)]
    def cp(sl,dev,s,r):
        return pltpu.make_async_remote_copy(src_ref=out.at[sl],dst_ref=out.at[sl],send_sem=s,recv_sem=r,device_id=dev,device_id_type=MESH)
    al=slice(None)
    pend=[]
    def A1(xx,R=rows): return (z,y,xx,R[0])
    def A2(yy,R=rows): return (z,yy,al,R[0])
    def A3(zs,R=rows): return (zs,al,al,R[0])
    def B1(yy,R=rows): return (z,yy,x,R[1])
    def B2(zs,xx,R=rows): return (zs,al,xx,R[1])
    def C1(zs,R=rows): return (zs,y,x,R[2])
    def C2(zs,xx,R=rows): return (zs,y,xx,R[2])
    def C3(zs,yy,R=rows): return (zs,yy,al,R[2])
    def sibsend(sl,k):
        cp(sl,sib,ss.at[k],rs.at[k]).start()
    def sibwait(sl,k):
        d=cp(sl,sib,ss.at[k],rs.at[k]); d.wait_send(); d.wait_recv()
    def zsend(sl,zs,base):
        @pl.when(jnp.logical_and(zs<=z,z<3))
        def _(): cp(sl,zr,szr.at[base+zs],rz.at[base+zs]).start()
        @pl.when(jnp.logical_and(zs>=z,z>0))
        def _(): cp(sl,zl,szl.at[base+zs],rz.at[base+zs]).start()
    def zsent(sl,zs,base):
        @pl.when(jnp.logical_and(zs<=z,z<3))
        def _(): cp(sl,zr,szr.at[base+zs],rz.at[base+zs]).wait_send()
        @pl.when(jnp.logical_and(zs>=z,z>0))
        def _(): cp(sl,zl,szl.at[base+zs],rz.at[base+zs]).wait_send()
    def zwait(sl,zs,base):
        cp(sl,zr,szr.at[base+zs],rz.at[base+zs]).wait_recv()
    A,B,C=0,4,8
    def xs(sl,k): cp(sl,xp,sx.at[k],rx.at[k]).start()
    def xw(sl,k): cp(sl,xp,sx.at[k],rx.at[k]).wait_recv()
    def xd(sl,k): cp(sl,xp,sx.at[k],rx.at[k]).wait_send()
    def ys(sl,k): cp(sl,yp,sy.at[k],ry.at[k]).start()
    def yw(sl,k): cp(sl,yp,sy.at[k],ry.at[k]).wait_recv()
    def yd(sl,k): cp(sl,yp,sy.at[k],ry.at[k]).wait_send()
    xs(A1(x),0); ys(B1(y),1); zsend(C1(z),z,C); xs(C2(z,x),5+z)
    xw(A1(1-x),0); ys(A2(y),0); sibsend(A1(1-x),0)
    yw(B1(1-y),1); zsend(B2(z,x),z,B); xs(B2(z,x),1+z); sibsend(B1(1-y),6)
    xw(C2(z,1-x),5+z); ys(C3(z,y),2+z); sibsend(C2(z,1-x),19+z)
    def late(zs):
        xw(C2(zs,1-x),5+zs); ys(C3(zs,y),2+zs); sibsend(C2(zs,1-x),19+zs)
    def early(zs):
        zwait(C1(zs),zs,C); zsend(C1(zs),zs,C); xs(C2(zs,x),5+zs); sibsend(C1(zs),15+zs)
        zwait(B2(zs,x),zs,B); zsend(B2(zs,x),zs,B); xs(B2(zs,x),1+zs); sibsend(B2(zs,x),7+zs)
    def both(s,f):
        @pl.when(z-s>=0)
        def _(): f(z-s)
        @pl.when(z+s<=3)
        def _(): f(z+s)
    both(1,early)
    yw(A2(1-y),0); zsend(A3(z),z,A); sibsend(A2(1-y),1)
    both(1,late)
    tail_along_z(False)
    both(2,early)
    def a3(zs):
        zwait(A3(zs),zs,A); zsend(A3(zs),zs,A); sibsend(A3(zs),2+zs)
    both(1,a3)
    both(2,late)
    tail_along_x()
    both(3,early)
    both(2,a3)
    both(3,late)
    both(3,a3)
    for s in range(4):
        def fin(zs):
            xw(B2(zs,1-x),1+zs); sibsend(B2(zs,1-x),11+zs)
            yw(C3(zs,1-y),2+zs); sibsend(C3(zs,1-y),23+zs)
        if s==0: fin(z)
        else: both(s,fin)
    xd(A1(x),0); yd(A2(y),0); yd(B1(y),1)
    sibwait(A1(1-x,orow),0) ; sibwait(A2(1-y,orow),1); sibwait(B1(1-y,orow),6)
    for zs in range(4):
        xd(B2(zs,x),1+zs); xd(C2(zs,x),5+zs); yd(C3(zs,y),2+zs)
        zsent(A3(zs),zs,A); zsent(B2(zs,x),zs,B); zsent(C1(zs),zs,C)
        sibwait(B2(zs,1-x,orow),11+zs); sibwait(C2(zs,1-x,orow),19+zs); sibwait(C3(zs,1-y,orow),23+zs)
        @pl.when(zs!=z)
        def _():
            sibwait(A3(zs,orow),2+zs); sibwait(B2(zs,x,orow),7+zs); sibwait(C1(zs,orow),15+zs)
    tail_end()
    leave=[pltpu.make_async_copy(out.at[zs],result.at[zs],out_sem.at[zs]) for zs in range(4)]
    for move in leave: move.start()
    for move in leave: move.wait()

def gather_blocks(blk,last):
    D=pltpu.SemaphoreType.DMA
    return pl.pallas_call(ag_kernel,out_shape=[jax.ShapeDtypeStruct((4,2,2,768,768),jnp.bfloat16),jax.ShapeDtypeStruct((16,768),jnp.bfloat16)],
        in_specs=[pl.BlockSpec(memory_space=pl.ANY),pl.BlockSpec(memory_space=pltpu.VMEM)],out_specs=[pl.BlockSpec(memory_space=pl.ANY),pl.BlockSpec(memory_space=pltpu.VMEM)],
        scratch_shapes=[pltpu.VMEM((4,2,2,768,768),jnp.bfloat16),D,D((4,)),D,D,D,D,D((9,)),D((6,)),D((12,)),D((9,)),D((6,)),D((12,)),D((12,)),D((27,)),D((27,))],
        compiler_params=pltpu.CompilerParams(collective_id=1,has_side_effects=True,vmem_limit_bytes=40<<20),name="gather_blocks")(blk,last)


ALL = slice(None)

def rs_kernel(g0,gwide,gdown,norm_in,out,norm_out,nx,ny,nz,nc,nacc,nrx,nry,nrz,nrc,nsx,nsy,nsz,nsc,own,sl,la1,la2,lafr,lafl,lb1,lb2r,lb2l,lb3,lc1r,lc1l,lc2,lc3,res,
              own_sem,ss,rs,rx,ry,rzr,rzl,sx,sy,szr,szl,fs,fr,osem):
    i,c,z,y,x=place()
    xp=(c,i+1-2*x); yp=(c,i+2-4*y); sib=(1-c,i); zr=(c,i+4); zl=(c,i-4)
    mine=pl.ds(pl.multiple_of(c*HALF,16),HALF); other=pl.ds(pl.multiple_of((1-c)*HALF,16),HALF)
    planes=[g0,gwide.at[0],gwide.at[1],gdown]
    locs=[pltpu.make_async_copy(planes[zt].at[:,:,mine],own.at[zt],own_sem.at[zt]) for zt in range(4)]
    for d in locs: d.start()
    enter_barrier(i,c,z)
    sibs=[pltpu.make_async_remote_copy(src_ref=planes[zt].at[:,:,other],dst_ref=sl.at[zt],send_sem=ss.at[zt],recv_sem=rs.at[zt],device_id=sib,device_id_type=MESH) for zt in range(4)]
    for d in sibs: d.start()
    r=[pl.ds(OFFS[k],LENS[k]) for k in range(3)]
    def rc(src,dst,dev,s,q):
        return pltpu.make_async_remote_copy(src_ref=src,dst_ref=dst,send_sem=s,recv_sem=q,device_id=dev,device_id_type=MESH)
    def add(dst,src,n,rows,step):
        @pl.loop(0,rows//step)
        def _(k):
            q=pl.ds(pl.multiple_of(k*step,16),step)
            dst(q)[...]=(dst(q)[...].astype(jnp.float32)+src(q)[...].astype(jnp.float32)).astype(jnp.bfloat16)
    def sub(k,q): return pl.ds(pl.multiple_of(OFFS[k]+q.start,16),q.size)
    def add2(ownidx,k,land):
        add(lambda q: own.at[tuple(ownidx)+(sub(k,q),)], lambda q: land.at[tuple([ALL]*(len(land.shape)-2))+(q,)],0,LENS[k],16)
    def C3(zt): return rc(own.at[zt,1-y,:,r[2]],lc3.at[zt],yp,sy.at[zt],ry.at[zt])
    def B3(zt): return rc(own.at[zt,:,1-x,r[1]],lb3.at[zt],xp,sx.at[zt],rx.at[zt])
    def C2(zt): return rc(own.at[zt,y,1-x,r[2]],lc2.at[zt],xp,sx.at[4+zt],rx.at[4+zt])
    A2=rc(own.at[z,1-y,:,r[0]],la2,yp,sy.at[4],ry.at[4])
    A1=rc(own.at[z,y,1-x,r[0]],la1,xp,sx.at[8],rx.at[8])
    B1=rc(own.at[z,1-y,x,r[1]],lb1,yp,sy.at[5],ry.at[5])
    def zline(src,landr,landl,base):
        def R(zt): return rc(src(zt),landr.at[zt],zr,szr.at[base+zt],rzr.at[base+zt])
        def L(zt): return rc(src(zt),landl.at[zt],zl,szl.at[base+zt],rzl.at[base+zt])
        return R,L
    AR,AL=zline(lambda zt: own.at[zt,:,:,r[0]],lafr,lafl,0)
    BR,BL=zline(lambda zt: own.at[zt,:,x,r[1]],lb2r,lb2l,4)
    CR,CL=zline(lambda zt: own.at[zt,y,x,r[2]],lc1r,lc1l,8)
    def zgo(zt,idx,k,R,L,landr,landl):
        @pl.when(zt>z)
        def _():
            @pl.when(z>0)
            def _():
                R(zt).wait_recv(); add2(idx,k,landr.at[zt])
            R(zt).start()
        @pl.when(zt<z)
        def _():
            @pl.when(z<3)
            def _():
                L(zt).wait_recv(); add2(idx,k,landl.at[zt])
            L(zt).start()
    def zfin(idx,k,R,L,landr,landl):
        @pl.when(z>0)
        def _(): R(z).wait_recv(); add2(idx,k,landr.at[z])
        @pl.when(z<3)
        def _(): L(z).wait_recv(); add2(idx,k,landl.at[z])
    def far(s):
        return s
    def sumsib(zt):
        locs[zt].wait(); sibs[zt].wait_recv()
        @pl.loop(0,HALF//16)
        def _(k):
            q=pl.ds(pl.multiple_of(k*16,16),16)
            own[zt,:,:,q]=(own[zt,:,:,q].astype(jnp.float32)+sl[zt,:,:,q].astype(jnp.float32)).astype(jnp.bfloat16)
    order=[3,0,2,1]
    nacc[...]=norm_in[...]
    NX=rc(nacc,nx,xp,nsx,nrx); NY=rc(nacc,ny,yp,nsy,nry); NZ=rc(nacc,nz,zr,nsz,nrz); NC=rc(nacc,nc,sib,nsc,nrc)
    line=jnp.logical_and(x==1,y==1)
    end=jnp.logical_and(line,z==3)
    @pl.when(x==0)
    def _(): NX.start()
    def norm_y():
        @pl.when(x==1)
        def _():
            NX.wait_recv(); nacc[...]+=nx[...]
            @pl.when(y==0)
            def _(): NY.start()
    def norm_z(k):
        @pl.when(jnp.logical_and(line,z==k))
        def _():
            NY.wait_recv(); nacc[...]+=ny[...]
            if k>0:
                NZ.wait_recv(); nacc[...]+=nz[...]
            if k<3: NZ.start()
            else: NC.start()
    def norm_end():
        @pl.when(x==0)
        def _(): NX.wait_send()
        @pl.when(jnp.logical_and(x==1,y==0))
        def _(): NY.wait_send()
        @pl.when(jnp.logical_and(line,z<3))
        def _(): NZ.wait_send()
        @pl.when(end)
        def _():
            NC.wait_recv(); NC.wait_send()
            nacc[...]+=nc[...]
        norm_out[...]=nacc[...]
    for zt in order:
        sumsib(zt)
        C3(zt).start(); B3(zt).start()
        zgo(zt,(zt,ALL,ALL),0,AR,AL,lafr,lafl)
    def c3done(zt):
        C3(zt).wait_recv(); add2((zt,y,ALL),2,lc3.at[zt]); C2(zt).start()
    def b3done(zt):
        B3(zt).wait_recv(); add2((zt,ALL,x),1,lb3.at[zt])
        zgo(zt,(zt,ALL,x),1,BR,BL,lb2r,lb2l)
    def c2done(zt):
        C2(zt).wait_recv(); add2((zt,y,x),2,lc2.at[zt])
        zgo(zt,(zt,y,x),2,CR,CL,lc1r,lc1l)
    c3done(3); b3done(3); norm_y(); c3done(0); b3done(0); norm_z(0); c2done(3); c3done(2); b3done(2); norm_z(1); c2done(0); c3done(1); b3done(1); norm_z(2); c2done(2); c2done(1); norm_z(3)
    zfin((z,ALL,ALL),0,AR,AL,lafr,lafl)
    A2.start()
    zfin((z,ALL,x),1,BR,BL,lb2r,lb2l)
    B1.start()
    A2.wait_recv(); add2((z,y,ALL),0,la2)
    A1.start()
    zfin((z,y,x),2,CR,CL,lc1r,lc1l)
    def final(k,land):
        @pl.loop(0,LENS[k]//16)
        def _(t):
            q=pl.ds(pl.multiple_of(t*16,16),16)
            o=pl.ds(pl.multiple_of(OFFS[k]+t*16,16),16)
            v=own[z,y,x,o].astype(jnp.float32)
            if land is not None: v=v+land[q].astype(jnp.float32)
            res[o]=v
    final(2,None)
    B1.wait_recv(); final(1,lb1)
    A1.wait_recv(); final(0,la1)
    fin=rc(res,out.at[mine],sib,fs,fr)
    fin.start()
    loc=pltpu.make_async_copy(res,out.at[mine],osem)
    loc.start()
    for zt in range(4):
        sibs[zt].wait_send(); C3(zt).wait_send(); B3(zt).wait_send(); C2(zt).wait_send()
        for R,L in ((AR,AL),(BR,BL),(CR,CL)):
            @pl.when(zt>z)
            def _(): R(zt).wait_send()
            @pl.when(zt<z)
            def _(): L(zt).wait_send()
    A2.wait_send(); A1.wait_send(); B1.wait_send()
    norm_end()
    loc.wait(); fin.wait_send()
    rc(res,out.at[other],sib,fs,fr).wait_recv()

def reduce_blocks(g0,gwide,gdown,norms):
    D=pltpu.SemaphoreType.DMA
    bf=jnp.bfloat16
    V=lambda *s: pltpu.VMEM(s,bf)
    return pl.pallas_call(rs_kernel,out_shape=[jax.ShapeDtypeStruct((768,768),jnp.float32),jax.ShapeDtypeStruct((4,768),jnp.float32)],
        in_specs=[pl.BlockSpec(memory_space=pl.ANY)]*3+[pl.BlockSpec(memory_space=pltpu.VMEM)],out_specs=[pl.BlockSpec(memory_space=pl.ANY),pl.BlockSpec(memory_space=pltpu.VMEM)],
        scratch_shapes=[*[pltpu.VMEM((4,768),jnp.float32)]*5,*[D]*8,V(4,2,2,HALF,768),V(4,2,2,HALF,768),V(RA,768),V(2,RA,768),V(4,2,2,RA,768),V(4,2,2,RA,768),
            V(RB,768),V(4,2,RB,768),V(4,2,RB,768),V(4,2,RB,768),V(4,RC,768),V(4,RC,768),V(4,RC,768),V(4,2,RC,768),pltpu.VMEM((HALF,768),jnp.float32),
            D((4,)),D((4,)),D((4,)),D((9,)),D((6,)),D((12,)),D((12,)),D((9,)),D((6,)),D((12,)),D((12,)),D,D,D],
        compiler_params=pltpu.CompilerParams(collective_id=2,has_side_effects=True,vmem_limit_bytes=58<<20),name="reduce_blocks")(g0,gwide,gdown,norms)

bf16=jnp.bfloat16; f32=jnp.float32
FAR=1e33
VM=pl.BlockSpec(memory_space=pltpu.VMEM)

def dot(a,b): return lax.dot_general(a,b,(((1,),(0,)),((),())),preferred_element_type=f32)
def dot_tn(a,b): return lax.dot_general(a,b,(((0,),(0,)),((),())),preferred_element_type=f32)
def dot_nt(a,b): return lax.dot_general(a,b,(((1,),(1,)),((),())),preferred_element_type=f32)

def slope(h):
    return jnp.exp2(-8.0/HEADS*(jnp.full((1,1),h,jnp.int32).astype(f32)+1.0))

def fill_distance(dist,seg_col,seg_row):
    @pl.loop(0,LEN//128)
    def _(k):
        r=pl.ds(pl.multiple_of(k*128,128),128)
        kk=(lax.broadcasted_iota(jnp.int32,(128,LEN),0)+k*128)
        qq=lax.broadcasted_iota(jnp.int32,(128,LEN),1)
        d=jnp.abs(kk-qq).astype(f32)
        dist[r]=jnp.where(seg_col[r]==seg_row[...],d,FAR)

QB=256
def attend_kernel(tokens,w,seg_col,seg_row,tokT,qT,kT,vT,mixT,lse,dist,kn):
    tokT[...]=tokens[...].astype(f32).T.astype(bf16)
    fill_distance(dist,seg_col,seg_row)
    for n,(o,s) in enumerate(((qT,0.125),(kT,1.0),(vT,1.0))):
        @pl.loop(0,3)
        def _(t):
            c=pl.ds(pl.multiple_of(t*256,256),256)
            r=dot_tn(w[0,n//2,n%2,:,c],tokT[...])
            o[c]=r.astype(bf16)
    @pl.loop(0,HEADS)
    def _(h):
        rows=pl.ds(pl.multiple_of(h*HEAD,HEAD),HEAD)
        kn[...]=kT[rows].astype(f32).T.astype(bf16)
        m=slope(h)
        for b in range(LEN//QB):
            cols=pl.ds(b*QB,QB)
            q=(qT[rows,cols]*bf16(0.125))
            s=dot(kn[...],q)-m*dist[:,cols]
            top=jnp.max(s,0,keepdims=True)
            e=jnp.exp(s-top)
            total=jnp.sum(e,0,keepdims=True)
            o=dot(vT[rows],e.astype(bf16))/total
            mixT[rows,cols]=o
            lse[h,:,cols]=top+jnp.log(total)

def attend(tokens,w,seg):
    T=jax.ShapeDtypeStruct((D,LEN),bf16)
    tokT,qT,kT,vT,mixT,lse=pl.pallas_call(attend_kernel,grid=(1,),
        in_specs=[VM,pl.BlockSpec((1,2,2,D,D),lambda i:(0,0,0,0,0)),VM,VM],out_specs=[VM]*6,
        out_shape=[T,T,T,T,jax.ShapeDtypeStruct((D,LEN),f32),jax.ShapeDtypeStruct((HEADS,1,LEN),f32)],
        scratch_shapes=[pltpu.VMEM((LEN,LEN),f32),pltpu.VMEM((LEN,HEAD),bf16)],
        compiler_params=pltpu.CompilerParams(vmem_limit_bytes=58<<20),name="attend")(tokens,w,seg.reshape(LEN,1),seg.reshape(1,LEN))
    return (tokT,qT,kT,vT),mixT,lse

def attend_back_kernel(w,seg_col,seg_row,tokT,qT,kT,vT,mixT,lse,dO,first,gout,g0,grad_in,dist,kn,vn,p_all,ds_all,dqT,dkT,dvT):
    fill_distance(dist,seg_col,seg_row)
    @pl.loop(0,HEADS)
    def _(h):
        rows=pl.ds(pl.multiple_of(h*HEAD,HEAD),HEAD)
        kn[...]=kT[rows].astype(f32).T.astype(bf16)
        vn[...]=vT[rows].astype(f32).T.astype(bf16)
        m=slope(h)
        for b in range(LEN//QB):
            cols=pl.ds(b*QB,QB)
            q=(qT[rows,cols]*bf16(0.125))
            s=dot(kn[...],q)-m*dist[:,cols]
            p=jnp.exp(s-lse[h,:,cols])
            do=dO[rows,cols]
            delta=jnp.sum(do.astype(f32)*mixT[rows,cols],0,keepdims=True)
            dp=dot(vn[...],do)
            p_all[:,cols]=p.astype(bf16)
            ds=(p*(dp-delta)).astype(bf16)
            ds_all[:,cols]=ds
            dqT[rows,cols]=(dot(kT[rows],ds)*0.125).astype(bf16)
        dvT[rows]=dot_nt(dO[rows],p_all[...]).astype(bf16)
        dkT[rows]=(dot_nt(qT[rows],ds_all[...])*0.125).astype(bf16)
    g0[1,1]=gout[...]
    for n,g in enumerate((dqT,dkT,dvT)):
        g0[n//2,n%2]=dot_nt(tokT[...],g[...]).astype(bf16)
    @pl.loop(0,4)
    def _(t):
        c=pl.ds(pl.multiple_of(t*256,256),256)
        acc=dot(w[0,0,0],dqT[:,c])+dot(w[0,0,1],dkT[:,c])+dot(w[0,1,0],dvT[:,c])
        grad_in[c]=first[c]+acc.T

def attend_back(w,seg,tokT,qT,kT,vT,mixT,lse,dO,first,gout):
    B=lambda: pltpu.VMEM((D,LEN),bf16)
    return pl.pallas_call(attend_back_kernel,grid=(1,),
        in_specs=[pl.BlockSpec((1,2,2,D,D),lambda i:(0,0,0,0,0))]+[VM]*11,out_specs=[VM]*2,
        out_shape=[jax.ShapeDtypeStruct((2,2,D,D),bf16),jax.ShapeDtypeStruct((LEN,D),f32)],
        scratch_shapes=[pltpu.VMEM((LEN,LEN),f32),pltpu.VMEM((LEN,HEAD),bf16),pltpu.VMEM((LEN,HEAD),bf16),pltpu.VMEM((LEN,LEN),bf16),pltpu.VMEM((LEN,LEN),bf16),B(),B(),B()],
        compiler_params=pltpu.CompilerParams(vmem_limit_bytes=60<<20),name="attend_back")(w,seg.reshape(LEN,1),seg.reshape(1,LEN),tokT,qT,kT,vT,mixT,lse,dO,first,gout)

TB=256
def feed_kernel(tokens,cot,mixT,wo,w1,w2,w3,norms,output,first,dO,ng,gout,gdown,gwide,inner,hidden,gg,gu,gffn,gbranch,fa,fb,mixb):
    step=pl.program_id(0)
    gain1=norms[0:1]; shift1=norms[1:2]; gain2=norms[2:3]; shift2=norms[3:4]
    def stats(v):
        c=v-jnp.mean(v,-1,keepdims=True)
        r=lax.rsqrt(jnp.mean(c*c,-1,keepdims=True)+norm_eps)
        return c*r,r
    def back(e,n,r):
        return r*(e-jnp.mean(e,-1,keepdims=True)-n*jnp.mean(e*n,-1,keepdims=True))
    W=lambda p,j: (w1,w2)[p-1][0,:,j].reshape(D,D)
    WD=lambda j: w3[0,j].reshape(D,D)
    WO=lambda: wo[0,0].reshape(D,D)
    @pl.when(step==0)
    def _(): ng[...]=jnp.zeros_like(ng)
    @pl.when(step<LEN//TB)
    def _():
        rows=pl.ds(pl.multiple_of(step*TB,TB),TB)
        mb=mixT[...].astype(bf16)
        mixb[:,rows]=mb
        branch=dot_tn(mb,WO())
        n1,r1=stats(tokens[...].astype(f32)+branch)
        l1=n1*gain1+shift1
        inn=l1.astype(bf16)
        inner[rows]=inn
        ffn=None
        for j in range(4):
            cols=pl.ds(j*D,D)
            ga=dot(inn,W(1,j)); up=dot(inn,W(2,j))
            cum=0.5*(1.0+lax.erf(ga*inv_root_two))
            gel=ga*cum
            fb[j]=gel
            fa[j]=up*(cum+ga*(jnp.exp(-0.5*ga*ga)*inv_root_tau))
            hid=(gel*up).astype(bf16)
            hidden[rows,cols]=hid
            t=dot(hid,WD(j))
            ffn=t if ffn is None else ffn+t
        n2,r2=stats(l1+ffn)
        output[...]=(n2*gain2+shift2).astype(bf16)
        c=cot[...].astype(f32)
        ng[2:3]+=jnp.sum(c*n2,0,keepdims=True)
        ng[3:4]+=jnp.sum(c,0,keepdims=True)
        mid=back(c*gain2,n2,r2)
        gf=mid.astype(bf16)
        gffn[rows]=gf
        gl=mid
        for j in range(4):
            cols=pl.ds(j*D,D)
            gh=dot_nt(gf,WD(j))
            a=(gh*fa[j]).astype(bf16); b=(gh*fb[j]).astype(bf16)
            gg[rows,cols]=a; gu[rows,cols]=b
            gl=gl+dot_nt(a,W(1,j))+dot_nt(b,W(2,j))
        ng[0:1]+=jnp.sum(gl*n1,0,keepdims=True)
        ng[1:2]+=jnp.sum(gl,0,keepdims=True)
        gfirst=back(gl*gain1,n1,r1)
        first[...]=gfirst
        gb=gfirst.astype(bf16)
        gbranch[rows]=gb
        dO[...]=dot_nt(WO(),gb).astype(bf16)
    def put(g,v):
        g[...]=v.astype(bf16).reshape(g.shape)
    base=LEN//TB
    for j in range(4):
        cols=pl.ds(j*D,D)
        @pl.when(step==base+j)
        def _(): put(gdown,dot_tn(hidden[:,cols],gffn[...]))
        @pl.when(step==base+4+j)
        def _(): put(gwide,dot_tn(inner[...],gg[:,cols]))
        @pl.when(step==base+8+j)
        def _(): put(gwide,dot_tn(inner[...],gu[:,cols]))
    @pl.when(step==base+12)
    def _(): put(gout,dot(mixb[...],gbranch[...]))

def feed(tokens,cot,mixT,w,norms):
    n=LEN//TB
    last=n-1
    row=lambda i:(jnp.minimum(i,last),0)
    col=lambda i:(0,jnp.minimum(i,last))
    one=pl.Buffered(1)
    S=jax.ShapeDtypeStruct
    V=lambda s,d=bf16: pltpu.VMEM(s,d)
    clip=lambda v,a,b: jnp.minimum(jnp.maximum(v,a),b)
    return pl.pallas_call(feed_kernel,grid=(n+13,),
        in_specs=[pl.BlockSpec((TB,D),row),pl.BlockSpec((TB,D),row),pl.BlockSpec((D,TB),col),
            pl.BlockSpec((1,1,4,D//4,D),lambda i:(0,3,0,0,0),pipeline_mode=one),*[pl.BlockSpec((1,4,4,D//4,D),lambda i,p=p:(p,0,0,0,0),pipeline_mode=one) for p in (1,2,3)],pl.BlockSpec((4,D),lambda i:(0,0))],
        out_specs=[pl.BlockSpec((TB,D),row),pl.BlockSpec((TB,D),row),pl.BlockSpec((D,TB),col),
            pl.BlockSpec((4,D),lambda i:(0,0)),
            pl.BlockSpec((D,D),lambda i:(0,0)),
            pl.BlockSpec((1,D,D),lambda i:(clip(i-n,0,3),0,0)),
            pl.BlockSpec((1,4,1,D//4,D),lambda i:(clip((i-n-4)//4,0,1),0,clip(i-n-4,0,7)%4,0,0))],
        out_shape=[S((LEN,D),bf16),S((LEN,D),f32),S((D,LEN),bf16),S((4,D),f32),S((D,D),bf16),S((4,D,D),bf16),S((2,4,4,D//4,D),bf16)],
        scratch_shapes=[V((LEN,D)),V((LEN,FF)),V((LEN,FF)),V((LEN,FF)),V((LEN,D)),V((LEN,D)),V((4,TB,D),f32),V((4,TB,D),f32),V((D,LEN))],
        compiler_params=pltpu.CompilerParams(vmem_limit_bytes=62<<20),name="feed")(tokens,cot,mixT,*[w.reshape(4,4,4,D//4,D)]*4,norms)

SQUARE = D * D
TAIL = 4 * D


def from_wide(blocks):
    return blocks.reshape(4, 4, D // 4, D).transpose(0, 2, 1, 3).reshape(D, FF)


def to_wide(value):
    return value.reshape(4, D // 4, 4, D).transpose(0, 2, 1, 3).reshape(2, 2, D, D)


def swap_wide(block, index, inverse):
    dims = (4, D // 4, D) if inverse else (D // 4, 4, D)
    swapped = block.reshape(dims).transpose(1, 0, 2).reshape(D, D)
    wide = jnp.logical_and(index >= 4, index < 12)
    return jnp.where(wide, swapped, block)


def gather_weights(master):
    count = lax.axis_size("zero")
    index = lax.axis_index("zero")
    size = 16 * SQUARE // count
    weights = master.astype(bf16)
    last = weights[-TAIL:]
    before = lax.ppermute(last, "zero", [(k, k + 1) for k in range(count - 1)])
    joined = jnp.concatenate([before, weights])
    block = lax.dynamic_slice(joined, (TAIL - TAIL // count * index,), (size,))
    if count == 16:
        padded = jnp.pad(last.reshape(4, D), ((0, 12), (0, 0)))
        blocks, tail = gather_blocks(swap_wide(block.reshape(D, D), index, False), padded)
        norms = tail[:4].astype(f32)
    else:
        natural = lax.all_gather(block.reshape(-1, D), "zero", axis=0, tiled=True)
        parts = natural.reshape(4, 4 * D, D)
        wide = [to_wide(parts[k].reshape(D, FF)) for k in (1, 2)]
        blocks = jnp.stack([parts[0].reshape(2, 2, D, D), *wide, parts[3].reshape(2, 2, D, D)])
        norms = lax.psum(jnp.where(index == count - 1, last.astype(f32), 0.0), "zero").reshape(4, D)
    return blocks, norms


def scatter_grads(square, wide, down, norm_grads):
    count = lax.axis_size("zero")
    index = lax.axis_index("zero")
    if count == 16:
        block, tail = reduce_blocks(square, wide, down, norm_grads)
        block = swap_wide(block, index, True)
    else:
        natural = [from_wide(wide[k]).reshape(4 * D, D) for k in (0, 1)]
        natural = jnp.concatenate([square.reshape(4 * D, D), *natural, down.reshape(4 * D, D)])
        block = lax.psum_scatter(natural, "zero", scatter_dimension=0, tiled=True)
        block = lax.psum(block.astype(f32), "dp")
        tail = lax.psum(norm_grads, ("dp", "zero"))
    flat = block.reshape(-1)
    after = lax.ppermute(flat[:TAIL], "zero", [(k + 1, k) for k in range(count - 1)])
    joined = jnp.concatenate([flat, jnp.where(index == count - 1, tail.reshape(-1), after)])
    shard = flat.shape[0] + TAIL // count
    return lax.dynamic_slice(joined, (TAIL // count * index,), (shard,))


def local(tokens, segments, cotangent, master, moment_one, moment_two):
    blocks, norms = gather_weights(master)
    kept, mixed, log_sum = attend(tokens, blocks, segments)
    output, first_grad, grad_mixed, norm_grads, out_grad, down_grad, wide_grad = feed(
        tokens, cotangent, mixed, blocks, norms
    )
    square_grad, input_grad = attend_back(
        blocks, segments, *kept, mixed, log_sum, grad_mixed, first_grad, out_grad
    )
    grad_shard = scatter_grads(
        square_grad, wide_grad.reshape(2, 2, 2, D, D), down_grad.reshape(2, 2, D, D), norm_grads
    )
    grad_shard = grad_shard / (lax.axis_size("zero") * lax.axis_size("dp"))
    first = beta_one * moment_one + (1.0 - beta_one) * grad_shard
    second = beta_two * moment_two + (1.0 - beta_two) * grad_shard * grad_shard
    update = first / correct_one / (jnp.sqrt(second / correct_two) + adam_eps)
    master_new = master - learn_rate * (update + weight_decay * master)
    return (
        output,
        input_grad,
        grad_shard,
        first,
        second,
        master_new,
        master_new.astype(jnp.bfloat16),
    )


def solution(mesh):
    return jax.shard_map(
        local,
        mesh=mesh,
        in_specs=(
            P(("dp", "zero"), None),
            P(("dp", "zero")),
            P(("dp", "zero"), None),
            P("zero"),
            P("zero"),
            P("zero"),
        ),
        out_specs=(
            P(("dp", "zero"), None),
            P(("dp", "zero"), None),
            P("zero"),
            P("zero"),
            P("zero"),
            P("zero"),
            P("zero"),
        ),
        check_vma=False,
    )
```

time: 780 us -> 458 us (0.59)
  matrix products: 266 us -> 0 us
  Pallas kernels: 197 us -> 416 us
  blocking collectives: 109 us -> 0 us
  other arithmetic: 98.6 us -> 13.4 us
  local copies, waits for them, and re-layouts: 93.5 us -> 11.4 us
    dot_general x33 -> x0, matrix products: 266 us -> none  [the longest x7 59.3 us: right_trans(): jnp.einsum('re,de->rd', left, right, preferred_element_type=jnp.float32)]
    pallas_call x2 -> x5, Pallas kernels: 197 us -> 416 us  [the longest x1 134 us: reduce_blocks(): pl.pallas_call(rs_kernel, out_shape=[jax.ShapeDtypeStruct((768, 768), jnp...]
    psum x2 -> x0, blocking collectives: 109 us -> none  [the longest x1 68.6 us: gather_weights(): lax.psum(jnp.where(index == count - 1, last.astype(jnp.float32), 0.0), 'z...]
    convert_element_type x6 -> x2, other arithmetic: 35.7 us -> 2.39 us  [the longest x1 1.79 us: gather_weights(): weights = master.astype(bf16)]
    reshape x6 -> x4, local copies, waits for them, and re-layouts: 31.6 us -> 2.91 us  [the longest x1 1.87 us: gather_weights(): block.reshape(D, D)]
    reduce_sum x5 -> x0, other arithmetic: 26 us -> none  [the longest x2 21.8 us: attend_forward(): total = jnp.sum(expo, -1, keepdims=True)]
    unnamed x100 -> x6, local copies, waits for them, and re-layouts: 23.3 us -> 1.16 us
    another operation x3 -> x0, other arithmetic: 19.5 us -> none  [the longest x1 17.1 us: local(): jnp.stack([low(jnp.stack([grad_w_query, grad_w_key, grad_w_value, grad_w_...]
  transfers between devices with their start and end apart: 2 -> 2, of which waited for: 0 -> 2; matrix products, arithmetic and copies ran while one was open for 3% -> 1% of each run, Pallas kernels for 0% -> 0%
where the time goes in v2:
time: 458 us; the launch traced here: 451 us
  Pallas kernels  416 us (91%)
  other arithmetic  13.4 us (3%)
  local copies, waits for them, and re-layouts  11.4 us (2%)
  starting transfers between devices  5.31 us (1%)
  waiting for transfers between devices  4.94 us (1%)
    pallas_call x1, Pallas kernels, reduce_blocks(): pl.pallas_call(rs_kernel, out_shape=[jax.ShapeDtypeStruct((768, 768), jnp...  134 us
    pallas_call x1, Pallas kernels, feed(): pl.pallas_call(feed_kernel, grid=(n + 13,), in_specs=[pl.BlockSpec((TB, D...  99.4 us
    pallas_call x1, Pallas kernels, gather_blocks(): pl.pallas_call(ag_kernel, out_shape=[jax.ShapeDtypeStruct((4, 2, 2, 768,...  79.3 us
    pallas_call x1, Pallas kernels, attend_back(): pl.pallas_call(attend_back_kernel, grid=(1,), in_specs=[pl.BlockSpec((1,...  55.4 us
    pallas_call x1, Pallas kernels, attend(): pl.pallas_call(attend_kernel, grid=(1,), in_specs=[VM, pl.BlockSpec((1, 2...  47.4 us
  transfers between devices with their start and end apart: 2, of which 2 were waited for; matrix products, arithmetic and copies ran while one was open for 1% of the time, Pallas kernels for 0%

profile of v2, /device:TPU:8, one launch (start us, length us, event | category | flops | bytes accessed | tf_op | source)
XLA Modules:
  0.0 451.5 jit_solution(9143226698356240006)
XLA Ops:
  0.6 1.8 convert_element_type.11
  2.4 0.1 slice.16
  2.5 3.4 collective-permute-start
  5.9 1.0 copy.15.seg_col
  7.0 2.9 collective-permute-done
  9.8 1.0 fusion.1
  10.8 0.5 reshape_reshape.3
  11.3 1.9 reshape.54
  13.2 0.1 copy.14
  13.3 1.1 copy-done
  14.4 0.2 bitcast_select_fusion.blk
  14.7 79.3 %gather_blocks.1 = (bf16[4,2,2,768,768]{4,3,2,1,0:T(8,128)(2,1)}, bf16[16,768]{1,0:T(8,128)(2,1)S(1)}) custom-call(bf16[768,768]{1,0:T(8,128)(2,1)S(1)} %bitcast_select_fusion.blk, bf16[16,768]{1,0:T(8,128)(2,1)S(1)} %pad.4.last), custom_call_target="tpu_custom_call" | custom-call | tf_op jit(solution)/shard_map/gather_blocks/pallas_call | solution.py:173
  94.0 0.6 slice_convert_fusion.norms
  94.6 47.4 %attend.1 = (bf16[768,1024]{1,0:T(8,128)(2,1)}, bf16[768,1024]{1,0:T(8,128)(2,1)}, bf16[768,1024]{1,0:T(8,128)(2,1)}, bf16[768,1024]{1,0:T(8,128)(2,1)}, f32[768,1024]{1,0:T(8,128)}, /*index=5*/f32[12,1,1024]{2,1,0:T(1,128)}) custom-call(bf16[1024,768]{1,0:T(8,128)(2,1)} %tokens.3, bf16[4,2,2,768,768]{4,3,2,1,0:T(8,128)(2,1)} %get-tuple-element.26.w, ...), custom_call_target="tpu_custom_call" | custom-call | tf_op jit(solution)/shard_map/attend/pallas_call | solution.py:381
  142.0 99.4 %feed.1 = (bf16[1024,768]{1,0:T(8,128)(2,1)}, f32[1024,768]{1,0:T(8,128)}, bf16[768,1024]{1,0:T(8,128)(2,1)}, f32[4,768]{1,0:T(4,128)}, bf16[768,768]{1,0:T(8,12...) custom-call(bf16[1024,768]{1,0:T(8,128)(2,1)} %tokens.3, bf16[1024,768]{1,0:T(8,128)(2,1)} %cot.1, ...), custom_call_target="tpu_custom_call" | custom-call | tf_op jit(solution)/shard_map/feed/pallas_call | solution.py:509
  241.4 55.4 %attend_back.1 = (bf16[2,2,768,768]{3,2,1,0:T(8,128)(2,1)}, f32[1024,768]{1,0:T(8,128)}) custom-call(bf16[4,2,2,768,768]{4,3,2,1,0:T(8,128)(2,1)} %get-tuple-element.26.w, s32[1024,1]{1,0:T(8,128)} %copy.15.seg_col, s32[1,1024]{1,0:T(1,128)} %bitcast.22, bf16[768,1024]{1,0:T(8,128)(2,1)} %get-tuple-element.30.tokT, bf16[768,1024]{1,0:T(8,128)(2,1)} %get-tuple-element.31.qT, ...), custom_call_target="tpu_custom_call" | custom-call | tf_op jit(solution)/shard_map/attend_back/pallas_call | solution.py:421
  296.8 134.0 %reduce_blocks.1 = (f32[768,768]{1,0:T(8,128)}, f32[4,768]{1,0:T(4,128)}) custom-call(bf16[2,2,768,768]{3,2,1,0:T(8,128)(2,1)} %get-tuple-element.39.g0, bf16[2,2,2,768,768]{4,3,2,1,0:T(8,128)(2,1)} %bitcast.17, bf16[2,2,768,768]{3,2,1,0:T(8,128)(2,1)} %bitcast.20, f32[4,768]{1,0:T(4,128)} %get-tuple-element.42.norm_in), custom_call_target="tpu_custom_call" | custom-call | tf_op jit(solution)/shard_map/reduce_blocks/pallas_call | solution.py:326
  430.8 3.2 copy.19
  434.0 1.9 reshape.62
  435.9 2.0 broadcast_select_fusion
  437.9 1.9 collective-permute-start.1
  439.8 1.6 reshape.63
  441.4 2.1 collective-permute-done.1
  443.5 7.8 %fusion.2 = (bf16[590016]{0:T(1024)(128)(2,1)}, f32[590016]{0:T(1024)}, f32[590016]{0:T(1024)}, f32[590016]{0:T(1024)}, f32[590016]{0:T(1024)}) fusion(f32[590016]{0:T(1024)} %param.9, f32[590016]{0:T(1024)} %param.11, f32[590016]{0:T(1024)} %param.10, s32[]{:T(128)S(6)} %select_n.34, f32[3072]{0:T(1024)S(1)} %broadcast_select_fusion.1, f32[589824]{0:T(1024)} %reshape.63), kind=kLoop, calls=%fused_computation.15 | loop fusion | flops 10620288 | bytes 20072068 | tf_op jit(solution)/shard_map/convert_element_type | solution.py:605
  (11 shorter events, 0.1 us)
Async XLA Ops:
  0.6 5.3 %copy-start.1 = (s32[1024]{0:T(1024)S(1)}, s32[1024]{0:T(1024)}, u32[]{:S(2)}) copy-start(s32[1024]{0:T(1024)} %param.7) | copy-start | bytes 12292
  2.5 7.3 %collective-permute-start = (bf16[3072]{0:T(1024)(128)(2,1)S(1)}, bf16[3072]{0:T(1024)(128)(2,1)S(1)}, u32[]{:S(2)}, u32[]{:S(2)}) collective-permute-start(bf16[3072]{0:T(1024)(128)(2,1)S(1)} %slice.16), channel_id=1, source_target_pairs={{0,1},{1,2},{2,3},{3,4},{4,5},{5,6},{6,7},{7,8},{8,9},{9,10},{10,1... | collective-permute-start | bytes 18440 | tf_op jit(solution)/shard_map/ppermute | solution.py:546
  13.2 1.3 copy-start
  437.9 5.6 %collective-permute-start.1 = (f32[3072]{0:T(1024)S(1)}, f32[3072]{0:T(1024)S(1)}, u32[]{:S(2)}, u32[]{:S(2)}) collective-permute-start(f32[3072]{0:T(1024)S(1)} %slice.15), channel_id=1, source_target_pairs={{1,0},{2,1},{3,2},{4,3},{5,4},{6,5},{7,6},{8,7},{9,8},{10,9},{11,1... | collective-permute-start | bytes 36872 | tf_op jit(solution)/shard_map/ppermute | solution.py:575
  439.8 1.6 copy-start.2

commit v3 on v2

--- a/solution.py
+++ b/solution.py
@@ -351,7 +351,7 @@
         dist[r]=jnp.where(seg_col[r]==seg_row[...],d,FAR)
 
 QB=256
-def attend_kernel(tokens,w,seg_col,seg_row,tokT,qT,kT,vT,mixT,lse,dist,kn):
+def attend_kernel(tokens,w,seg_col,seg_row,tokT,qT,kT,vT,mixT,mixb,lse,dist,kn):
     tokT[...]=tokens[...].astype(f32).T.astype(bf16)
     fill_distance(dist,seg_col,seg_row)
     for n,(o,s) in enumerate(((qT,0.125),(kT,1.0),(vT,1.0))):
@@ -374,18 +374,19 @@
             total=jnp.sum(e,0,keepdims=True)
             o=dot(vT[rows],e.astype(bf16))/total
             mixT[rows,cols]=o
+            mixb[rows,cols]=o.astype(bf16)
             lse[h,:,cols]=top+jnp.log(total)
 
 def attend(tokens,w,seg):
     T=jax.ShapeDtypeStruct((D,LEN),bf16)
-    tokT,qT,kT,vT,mixT,lse=pl.pallas_call(attend_kernel,grid=(1,),
-        in_specs=[VM,pl.BlockSpec((1,2,2,D,D),lambda i:(0,0,0,0,0)),VM,VM],out_specs=[VM]*6,
-        out_shape=[T,T,T,T,jax.ShapeDtypeStruct((D,LEN),f32),jax.ShapeDtypeStruct((HEADS,1,LEN),f32)],
+    tokT,qT,kT,vT,mixT,mixb,lse=pl.pallas_call(attend_kernel,grid=(1,),
+        in_specs=[VM,pl.BlockSpec((1,2,2,D,D),lambda i:(0,0,0,0,0)),VM,VM],out_specs=[VM]*7,
+        out_shape=[T,T,T,T,jax.ShapeDtypeStruct((D,LEN),f32),T,jax.ShapeDtypeStruct((HEADS,1,LEN),f32)],
         scratch_shapes=[pltpu.VMEM((LEN,LEN),f32),pltpu.VMEM((LEN,HEAD),bf16)],
         compiler_params=pltpu.CompilerParams(vmem_limit_bytes=58<<20),name="attend")(tokens,w,seg.reshape(LEN,1),seg.reshape(1,LEN))
-    return (tokT,qT,kT,vT),mixT,lse
-
-def attend_back_kernel(w,seg_col,seg_row,tokT,qT,kT,vT,mixT,lse,dO,first,gout,g0,grad_in,dist,kn,vn,p_all,ds_all,dqT,dkT,dvT):
+    return (tokT,qT,kT,vT,mixT),mixb,lse
+
+def attend_back_kernel(w,seg_col,seg_row,tokT,qT,kT,vT,mixT,lse,dO,first,gbranch,g0,grad_in,dist,kn,vn,p_all,ds_all,dqT,dkT,dvT):
     fill_distance(dist,seg_col,seg_row)
     @pl.loop(0,HEADS)
     def _(h):
@@ -407,7 +408,7 @@
             dqT[rows,cols]=(dot(kT[rows],ds)*0.125).astype(bf16)
         dvT[rows]=dot_nt(dO[rows],p_all[...]).astype(bf16)
         dkT[rows]=(dot_nt(qT[rows],ds_all[...])*0.125).astype(bf16)
-    g0[1,1]=gout[...]
+    g0[1,1]=dot(mixT[...].astype(bf16),gbranch[...]).astype(bf16)
     for n,g in enumerate((dqT,dkT,dvT)):
         g0[n//2,n%2]=dot_nt(tokT[...],g[...]).astype(bf16)
     @pl.loop(0,4)
@@ -416,16 +417,16 @@
         acc=dot(w[0,0,0],dqT[:,c])+dot(w[0,0,1],dkT[:,c])+dot(w[0,1,0],dvT[:,c])
         grad_in[c]=first[c]+acc.T
 
-def attend_back(w,seg,tokT,qT,kT,vT,mixT,lse,dO,first,gout):
+def attend_back(w,seg,tokT,qT,kT,vT,mixT,lse,dO,first,gbranch):
     B=lambda: pltpu.VMEM((D,LEN),bf16)
     return pl.pallas_call(attend_back_kernel,grid=(1,),
         in_specs=[pl.BlockSpec((1,2,2,D,D),lambda i:(0,0,0,0,0))]+[VM]*11,out_specs=[VM]*2,
         out_shape=[jax.ShapeDtypeStruct((2,2,D,D),bf16),jax.ShapeDtypeStruct((LEN,D),f32)],
         scratch_shapes=[pltpu.VMEM((LEN,LEN),f32),pltpu.VMEM((LEN,HEAD),bf16),pltpu.VMEM((LEN,HEAD),bf16),pltpu.VMEM((LEN,LEN),bf16),pltpu.VMEM((LEN,LEN),bf16),B(),B(),B()],
-        compiler_params=pltpu.CompilerParams(vmem_limit_bytes=60<<20),name="attend_back")(w,seg.reshape(LEN,1),seg.reshape(1,LEN),tokT,qT,kT,vT,mixT,lse,dO,first,gout)
+        compiler_params=pltpu.CompilerParams(vmem_limit_bytes=60<<20),name="attend_back")(w,seg.reshape(LEN,1),seg.reshape(1,LEN),tokT,qT,kT,vT,mixT,lse,dO,first,gbranch)
 
 TB=256
-def feed_kernel(tokens,cot,mixT,wo,w1,w2,w3,norms,output,first,dO,ng,gout,gdown,gwide,inner,hidden,gg,gu,gffn,gbranch,fa,fb,mixb):
+def feed_kernel(tokens,cot,mixb,wo,w1,w2,w3,norms,output,first,dO,gbranch,ng,gdown,gwide,inner,wide,gffn,fa,fb,acc,hid):
     step=pl.program_id(0)
     gain1=norms[0:1]; shift1=norms[1:2]; gain2=norms[2:3]; shift2=norms[3:4]
     def stats(v):
@@ -442,62 +443,53 @@
     @pl.when(step<LEN//TB)
     def _():
         rows=pl.ds(pl.multiple_of(step*TB,TB),TB)
-        mb=mixT[...].astype(bf16)
-        mixb[:,rows]=mb
-        branch=dot_tn(mb,WO())
+        branch=dot_tn(mixb[...],WO())
         n1,r1=stats(tokens[...].astype(f32)+branch)
         l1=n1*gain1+shift1
-        inn=l1.astype(bf16)
-        inner[rows]=inn
-        ffn=None
-        for j in range(4):
-            cols=pl.ds(j*D,D)
+        inner[rows]=l1.astype(bf16)
+        acc[...]=l1
+        @pl.loop(0,4,unroll=2)
+        def _(j):
+            inn=inner[rows]
             ga=dot(inn,W(1,j)); up=dot(inn,W(2,j))
             cum=0.5*(1.0+lax.erf(ga*inv_root_two))
             gel=ga*cum
             fb[j]=gel
             fa[j]=up*(cum+ga*(jnp.exp(-0.5*ga*ga)*inv_root_tau))
-            hid=(gel*up).astype(bf16)
-            hidden[rows,cols]=hid
-            t=dot(hid,WD(j))
-            ffn=t if ffn is None else ffn+t
-        n2,r2=stats(l1+ffn)
+            h=(gel*up).astype(bf16)
+            hid[j,rows]=h
+            acc[...]+=dot(h,WD(j))
+        n2,r2=stats(acc[...])
         output[...]=(n2*gain2+shift2).astype(bf16)
         c=cot[...].astype(f32)
         ng[2:3]+=jnp.sum(c*n2,0,keepdims=True)
         ng[3:4]+=jnp.sum(c,0,keepdims=True)
         mid=back(c*gain2,n2,r2)
-        gf=mid.astype(bf16)
-        gffn[rows]=gf
-        gl=mid
-        for j in range(4):
-            cols=pl.ds(j*D,D)
-            gh=dot_nt(gf,WD(j))
+        gffn[rows]=mid.astype(bf16)
+        acc[...]=mid
+        @pl.loop(0,4,unroll=2)
+        def _(j):
+            gh=dot_nt(gffn[rows],WD(j))
             a=(gh*fa[j]).astype(bf16); b=(gh*fb[j]).astype(bf16)
-            gg[rows,cols]=a; gu[rows,cols]=b
-            gl=gl+dot_nt(a,W(1,j))+dot_nt(b,W(2,j))
+            wide[j,rows]=a; wide[4+j,rows]=b
+            acc[...]+=dot_nt(a,W(1,j))+dot_nt(b,W(2,j))
+        gl=acc[...]
         ng[0:1]+=jnp.sum(gl*n1,0,keepdims=True)
         ng[1:2]+=jnp.sum(gl,0,keepdims=True)
         gfirst=back(gl*gain1,n1,r1)
         first[...]=gfirst
         gb=gfirst.astype(bf16)
-        gbranch[rows]=gb
+        gbranch[...]=gb
         dO[...]=dot_nt(WO(),gb).astype(bf16)
     def put(g,v):
         g[...]=v.astype(bf16).reshape(g.shape)
     base=LEN//TB
-    for j in range(4):
-        cols=pl.ds(j*D,D)
-        @pl.when(step==base+j)
-        def _(): put(gdown,dot_tn(hidden[:,cols],gffn[...]))
-        @pl.when(step==base+4+j)
-        def _(): put(gwide,dot_tn(inner[...],gg[:,cols]))
-        @pl.when(step==base+8+j)
-        def _(): put(gwide,dot_tn(inner[...],gu[:,cols]))
-    @pl.when(step==base+12)
-    def _(): put(gout,dot(mixb[...],gbranch[...]))
-
-def feed(tokens,cot,mixT,w,norms):
+    @pl.when(jnp.logical_and(step>=base,step<base+4))
+    def _(): put(gdown,dot_tn(hid[step-base],gffn[...]))
+    @pl.when(jnp.logical_and(step>=base+4,step<base+12))
+    def _(): put(gwide,dot_tn(inner[...],wide[step-base-4]))
+
+def feed(tokens,cot,mixb,w,norms):
     n=LEN//TB
     last=n-1
     row=lambda i:(jnp.minimum(i,last),0)
@@ -506,17 +498,16 @@
     S=jax.ShapeDtypeStruct
     V=lambda s,d=bf16: pltpu.VMEM(s,d)
     clip=lambda v,a,b: jnp.minimum(jnp.maximum(v,a),b)
-    return pl.pallas_call(feed_kernel,grid=(n+13,),
+    return pl.pallas_call(feed_kernel,grid=(n+12,),
         in_specs=[pl.BlockSpec((TB,D),row),pl.BlockSpec((TB,D),row),pl.BlockSpec((D,TB),col),
             pl.BlockSpec((1,1,4,D//4,D),lambda i:(0,3,0,0,0),pipeline_mode=one),*[pl.BlockSpec((1,4,4,D//4,D),lambda i,p=p:(p,0,0,0,0),pipeline_mode=one) for p in (1,2,3)],pl.BlockSpec((4,D),lambda i:(0,0))],
-        out_specs=[pl.BlockSpec((TB,D),row),pl.BlockSpec((TB,D),row),pl.BlockSpec((D,TB),col),
+        out_specs=[pl.BlockSpec((TB,D),row),pl.BlockSpec((TB,D),row),pl.BlockSpec((D,TB),col),pl.BlockSpec((TB,D),row),
             pl.BlockSpec((4,D),lambda i:(0,0)),
-            pl.BlockSpec((D,D),lambda i:(0,0)),
             pl.BlockSpec((1,D,D),lambda i:(clip(i-n,0,3),0,0)),
             pl.BlockSpec((1,4,1,D//4,D),lambda i:(clip((i-n-4)//4,0,1),0,clip(i-n-4,0,7)%4,0,0))],
-        out_shape=[S((LEN,D),bf16),S((LEN,D),f32),S((D,LEN),bf16),S((4,D),f32),S((D,D),bf16),S((4,D,D),bf16),S((2,4,4,D//4,D),bf16)],
-        scratch_shapes=[V((LEN,D)),V((LEN,FF)),V((LEN,FF)),V((LEN,FF)),V((LEN,D)),V((LEN,D)),V((4,TB,D),f32),V((4,TB,D),f32),V((D,LEN))],
-        compiler_params=pltpu.CompilerParams(vmem_limit_bytes=62<<20),name="feed")(tokens,cot,mixT,*[w.reshape(4,4,4,D//4,D)]*4,norms)
+        out_shape=[S((LEN,D),bf16),S((LEN,D),f32),S((D,LEN),bf16),S((LEN,D),bf16),S((4,D),f32),S((4,D,D),bf16),S((2,4,4,D//4,D),bf16)],
+        scratch_shapes=[V((LEN,D)),V((8,LEN,D)),V((LEN,D)),V((4,TB,D),f32),V((4,TB,D),f32),V((TB,D),f32),V((4,LEN,D))],
+        compiler_params=pltpu.CompilerParams(vmem_limit_bytes=62<<20),name="feed")(tokens,cot,mixb,*[w.reshape(4,4,4,D//4,D)]*4,norms)
 
 SQUARE = D * D
 TAIL = 4 * D
@@ -581,11 +572,11 @@
 def local(tokens, segments, cotangent, master, moment_one, moment_two):
     blocks, norms = gather_weights(master)
     kept, mixed, log_sum = attend(tokens, blocks, segments)
-    output, first_grad, grad_mixed, norm_grads, out_grad, down_grad, wide_grad = feed(
+    output, first_grad, grad_mixed, branch_grad, norm_grads, down_grad, wide_grad = feed(
         tokens, cotangent, mixed, blocks, norms
     )
     square_grad, input_grad = attend_back(
-        blocks, segments, *kept, mixed, log_sum, grad_mixed, first_grad, out_grad
+        blocks, segments, *kept, log_sum, grad_mixed, first_grad, branch_grad
     )
     grad_shard = scatter_grads(
         square_grad, wide_grad.reshape(2, 2, 2, D, D), down_grad.reshape(2, 2, D, D), norm_grads

time: 458 us -> 431 us (0.941); the launches traced: 451 us -> 430 us
  Pallas kernels: 416 us -> 394 us
    pallas_call x1, Pallas kernels: 99.4 us -> 75.9 us  [feed(): pl.pallas_call(feed_kernel, grid=(n + 12,), in_specs=[pl.BlockSpec((TB, D...]
where the time goes in v3:
time: 431 us; the launch traced here: 430 us
  Pallas kernels  394 us (91%)
  other arithmetic  13.4 us (3%)
  local copies, waits for them, and re-layouts  11.4 us (3%)
  starting transfers between devices  5.31 us (1%)
  waiting for transfers between devices  4.9 us (1%)
    pallas_call x1, Pallas kernels, reduce_blocks(): pl.pallas_call(rs_kernel, out_shape=[jax.ShapeDtypeStruct((768, 768), jnp...  134 us
    pallas_call x1, Pallas kernels, gather_blocks(): pl.pallas_call(ag_kernel, out_shape=[jax.ShapeDtypeStruct((4, 2, 2, 768,...  79.3 us
    pallas_call x1, Pallas kernels, feed(): pl.pallas_call(feed_kernel, grid=(n + 12,), in_specs=[pl.BlockSpec((TB, D...  75.9 us
    pallas_call x1, Pallas kernels, attend_back(): pl.pallas_call(attend_back_kernel, grid=(1,), in_specs=[pl.BlockSpec((1,...  56.6 us
    pallas_call x1, Pallas kernels, attend(): pl.pallas_call(attend_kernel, grid=(1,), in_specs=[VM, pl.BlockSpec((1, 2...  48.6 us
  transfers between devices with their start and end apart: 2, of which 2 were waited for; matrix products, arithmetic and copies ran while one was open for 1% of the time, Pallas kernels for 0%

profile of v3, /device:TPU:8, one launch (start us, length us, event | category | flops | bytes accessed | tf_op | source)
XLA Modules:
  0.0 430.2 jit_solution(5209448103570171307)
XLA Ops:
  0.6 1.8 convert_element_type.11
  2.4 0.1 slice.16
  2.5 3.4 collective-permute-start
  5.9 1.1 copy.15.seg_col
  7.0 2.8 collective-permute-done
  9.8 1.0 fusion.1
  10.8 0.5 reshape_reshape.3
  11.3 1.9 reshape.54
  13.2 0.1 copy.14
  13.3 1.1 copy-done
  14.4 0.2 bitcast_select_fusion.blk
  14.7 79.3 %gather_blocks.1 = (bf16[4,2,2,768,768]{4,3,2,1,0:T(8,128)(2,1)}, bf16[16,768]{1,0:T(8,128)(2,1)S(1)}) custom-call(bf16[768,768]{1,0:T(8,128)(2,1)S(1)} %bitcast_select_fusion.blk, bf16[16,768]{1,0:T(8,128)(2,1)S(1)} %pad.4.last), custom_call_target="tpu_custom_call" | custom-call | tf_op jit(solution)/shard_map/gather_blocks/pallas_call | solution.py:173
  94.0 0.6 slice_convert_fusion.norms
  94.6 48.6 %attend.1 = (bf16[768,1024]{1,0:T(8,128)(2,1)}, bf16[768,1024]{1,0:T(8,128)(2,1)}, bf16[768,1024]{1,0:T(8,128)(2,1)}, bf16[768,1024]{1,0:T(8,128)(2,1)}, f32[768...) custom-call(bf16[1024,768]{1,0:T(8,128)(2,1)} %tokens.3, ...), custom_call_target="tpu_custom_call" | custom-call | tf_op jit(solution)/shard_map/attend/pallas_call | solution.py:382
  143.1 75.9 %feed.1 = (bf16[1024,768]{1,0:T(8,128)(2,1)}, f32[1024,768]{1,0:T(8,128)}, bf16[768,1024]{1,0:T(8,128)(2,1)}, bf16[1024,768]{1,0:T(8,128)(2,1)}, f32[4,768]{1,0:...) custom-call(bf16[1024,768]{1,0:T(8,128)(2,1)} %tokens.3, bf16[1024,768]{1,0:T(8,128)(2,1)} %cot.1, ...), custom_call_target="tpu_custom_call" | custom-call | tf_op jit(solution)/shard_map/feed/pallas_call | solution.py:501
  219.1 56.6 %attend_back.1 = (bf16[2,2,768,768]{3,2,1,0:T(8,128)(2,1)}, f32[1024,768]{1,0:T(8,128)}) custom-call(bf16[4,2,2,768,768]{4,3,2,1,0:T(8,128)(2,1)} %get-tuple-element.27.w, s32[1024,1]{1,0:T(8,128)} %copy.15.seg_col, s32[1,1024]{1,0:T(1,128)} %bitcast.22, bf16[768,1024]{1,0:T(8,128)(2,1)} %get-tuple-element.31.tokT, bf16[768,1024]{1,0:T(8,128)(2,1)} %get-tuple-element.32.qT, ...), custom_call_target="tpu_custom_call" | custom-call | tf_op jit(solution)/shard_map/attend_back/pallas_call | solution.py:422
  275.7 134.0 %reduce_blocks.1 = (f32[768,768]{1,0:T(8,128)}, f32[4,768]{1,0:T(4,128)}) custom-call(bf16[2,2,768,768]{3,2,1,0:T(8,128)(2,1)} %get-tuple-element.41.g0, bf16[2,2,2,768,768]{4,3,2,1,0:T(8,128)(2,1)} %bitcast.17, bf16[2,2,768,768]{3,2,1,0:T(8,128)(2,1)} %bitcast.20, f32[4,768]{1,0:T(4,128)} %get-tuple-element.44.norm_in), custom_call_target="tpu_custom_call" | custom-call | tf_op jit(solution)/shard_map/reduce_blocks/pallas_call | solution.py:326
  409.7 3.2 copy.19
  412.9 1.9 reshape.62
  414.8 2.0 broadcast_select_fusion
  416.8 1.9 collective-permute-start.1
  418.7 1.6 reshape.63
  420.3 2.1 collective-permute-done.1
  422.4 7.8 %fusion.2 = (bf16[590016]{0:T(1024)(128)(2,1)}, f32[590016]{0:T(1024)}, f32[590016]{0:T(1024)}, f32[590016]{0:T(1024)}, f32[590016]{0:T(1024)}) fusion(f32[590016]{0:T(1024)} %param.9, f32[590016]{0:T(1024)} %param.11, f32[590016]{0:T(1024)} %param.10, s32[]{:T(128)S(6)} %select_n.34, f32[3072]{0:T(1024)S(1)} %broadcast_select_fusion.1, f32[589824]{0:T(1024)} %reshape.63), kind=kLoop, calls=%fused_computation.15 | loop fusion | flops 10620288 | bytes 20072068 | tf_op jit(solution)/shard_map/convert_element_type | solution.py:596
  (11 shorter events, 0.1 us)
Async XLA Ops:
  0.6 5.3 %copy-start.1 = (s32[1024]{0:T(1024)S(1)}, s32[1024]{0:T(1024)}, u32[]{:S(2)}) copy-start(s32[1024]{0:T(1024)} %param.7) | copy-start | bytes 12292
  2.5 7.3 %collective-permute-start = (bf16[3072]{0:T(1024)(128)(2,1)S(1)}, bf16[3072]{0:T(1024)(128)(2,1)S(1)}, u32[]{:S(2)}, u32[]{:S(2)}) collective-permute-start(bf16[3072]{0:T(1024)(128)(2,1)S(1)} %slice.16), channel_id=1, source_target_pairs={{0,1},{1,2},{2,3},{3,4},{4,5},{5,6},{6,7},{7,8},{8,9},{9,10},{10,1... | collective-permute-start | bytes 18440 | tf_op jit(solution)/shard_map/ppermute | solution.py:537
  13.2 1.3 copy-start
  416.8 5.6 %collective-permute-start.1 = (f32[3072]{0:T(1024)S(1)}, f32[3072]{0:T(1024)S(1)}, u32[]{:S(2)}, u32[]{:S(2)}) collective-permute-start(f32[3072]{0:T(1024)S(1)} %slice.15), channel_id=1, source_target_pairs={{1,0},{2,1},{3,2},{4,3},{5,4},{6,5},{7,6},{8,7},{9,8},{10,9},{11,1... | collective-permute-start | bytes 36872 | tf_op jit(solution)/shard_map/ppermute | solution.py:566
  418.7 1.6 copy-start.2

commit v4 on v3

--- a/solution.py
+++ b/solution.py
@@ -26,16 +26,9 @@
 inv_root_tau = 0.3989422804014327
 
 
-MESH=pl.DeviceIdType.MESH
 RA,RB,RC=48,128,208
 OFFS=(0,RA,RA+RB)
 LENS=(RA,RB,RC)
-HALF=384
-
-def place():
-    i=lax.axis_index("zero"); c=lax.axis_index("dp")
-    z=i//4; y=(i//2)%2; x=i%2
-    return i,c,z,y,x
 
 def enter_barrier(i,c,z):
     bar=pltpu.get_barrier_semaphore()
@@ -46,137 +39,6 @@
     @pl.when(z<3)
     def _(): pl.semaphore_signal(bar,inc=1,device_id=(c,i+4),device_id_type=MESH)
     pl.semaphore_wait(bar,3+jnp.minimum(z,1)+jnp.minimum(3-z,1))
-
-def ag_kernel(blk,last,result,tail,out,own_sem,out_sem,tr,tz,ty,tx,rx,ry,rz,sx,sy,szr,szl,rs,ss):
-    i,c,z,y,x=place()
-    xp=(c,i+1-2*x); yp=(c,i+2-4*y); sib=(1-c,i); zr=(c,i+4); zl=(c,i-4)
-    enter_barrier(i,c,z)
-    own=pltpu.make_async_copy(blk,out.at[z,y,x],own_sem)
-    own.start()
-    source=jnp.logical_and(z==3,jnp.logical_and(y==1,x==1))
-    line=jnp.logical_and(y==1,x==1)
-    @pl.when(source)
-    def _(): tail[...]=last[...]
-    def tcp(dev,s): return pltpu.make_async_remote_copy(src_ref=tail,dst_ref=tail,send_sem=s,recv_sem=tr,device_id=dev,device_id_type=MESH)
-    def tail_along_z(first):
-        @pl.when(jnp.logical_and(line,source if first else jnp.logical_not(source)))
-        def _():
-            if not first: tcp(zl,tz).wait_recv()
-            @pl.when(z>0)
-            def _(): tcp(zl,tz).start()
-            tcp(yp,ty).start()
-    def tail_along_x():
-        @pl.when(x==1)
-        def _():
-            @pl.when(y==0)
-            def _(): tcp(yp,ty).wait_recv()
-            tcp(xp,tx).start()
-    def tail_end():
-        @pl.when(x==0)
-        def _(): tcp(xp,tx).wait_recv()
-        @pl.when(x==1)
-        def _(): tcp(xp,tx).wait_send()
-        @pl.when(line)
-        def _():
-            tcp(yp,ty).wait_send()
-            @pl.when(z>0)
-            def _(): tcp(zl,tz).wait_send()
-    tail_along_z(True)
-    own.wait()
-    rows=[pl.ds(pl.multiple_of(c*HALF+OFFS[k],16),LENS[k]) for k in range(3)]
-    orow=[pl.ds(pl.multiple_of((1-c)*HALF+OFFS[k],16),LENS[k]) for k in range(3)]
-    def cp(sl,dev,s,r):
-        return pltpu.make_async_remote_copy(src_ref=out.at[sl],dst_ref=out.at[sl],send_sem=s,recv_sem=r,device_id=dev,device_id_type=MESH)
-    al=slice(None)
-    pend=[]
-    def A1(xx,R=rows): return (z,y,xx,R[0])
-    def A2(yy,R=rows): return (z,yy,al,R[0])
-    def A3(zs,R=rows): return (zs,al,al,R[0])
-    def B1(yy,R=rows): return (z,yy,x,R[1])
-    def B2(zs,xx,R=rows): return (zs,al,xx,R[1])
-    def C1(zs,R=rows): return (zs,y,x,R[2])
-    def C2(zs,xx,R=rows): return (zs,y,xx,R[2])
-    def C3(zs,yy,R=rows): return (zs,yy,al,R[2])
-    def sibsend(sl,k):
-        cp(sl,sib,ss.at[k],rs.at[k]).start()
-    def sibwait(sl,k):
-        d=cp(sl,sib,ss.at[k],rs.at[k]); d.wait_send(); d.wait_recv()
-    def zsend(sl,zs,base):
-        @pl.when(jnp.logical_and(zs<=z,z<3))
-        def _(): cp(sl,zr,szr.at[base+zs],rz.at[base+zs]).start()
-        @pl.when(jnp.logical_and(zs>=z,z>0))
-        def _(): cp(sl,zl,szl.at[base+zs],rz.at[base+zs]).start()
-    def zsent(sl,zs,base):
-        @pl.when(jnp.logical_and(zs<=z,z<3))
-        def _(): cp(sl,zr,szr.at[base+zs],rz.at[base+zs]).wait_send()
-        @pl.when(jnp.logical_and(zs>=z,z>0))
-        def _(): cp(sl,zl,szl.at[base+zs],rz.at[base+zs]).wait_send()
-    def zwait(sl,zs,base):
-        cp(sl,zr,szr.at[base+zs],rz.at[base+zs]).wait_recv()
-    A,B,C=0,4,8
-    def xs(sl,k): cp(sl,xp,sx.at[k],rx.at[k]).start()
-    def xw(sl,k): cp(sl,xp,sx.at[k],rx.at[k]).wait_recv()
-    def xd(sl,k): cp(sl,xp,sx.at[k],rx.at[k]).wait_send()
-    def ys(sl,k): cp(sl,yp,sy.at[k],ry.at[k]).start()
-    def yw(sl,k): cp(sl,yp,sy.at[k],ry.at[k]).wait_recv()
-    def yd(sl,k): cp(sl,yp,sy.at[k],ry.at[k]).wait_send()
-    xs(A1(x),0); ys(B1(y),1); zsend(C1(z),z,C); xs(C2(z,x),5+z)
-    xw(A1(1-x),0); ys(A2(y),0); sibsend(A1(1-x),0)
-    yw(B1(1-y),1); zsend(B2(z,x),z,B); xs(B2(z,x),1+z); sibsend(B1(1-y),6)
-    xw(C2(z,1-x),5+z); ys(C3(z,y),2+z); sibsend(C2(z,1-x),19+z)
-    def late(zs):
-        xw(C2(zs,1-x),5+zs); ys(C3(zs,y),2+zs); sibsend(C2(zs,1-x),19+zs)
-    def early(zs):
-        zwait(C1(zs),zs,C); zsend(C1(zs),zs,C); xs(C2(zs,x),5+zs); sibsend(C1(zs),15+zs)
-        zwait(B2(zs,x),zs,B); zsend(B2(zs,x),zs,B); xs(B2(zs,x),1+zs); sibsend(B2(zs,x),7+zs)
-    def both(s,f):
-        @pl.when(z-s>=0)
-        def _(): f(z-s)
-        @pl.when(z+s<=3)
-        def _(): f(z+s)
-    both(1,early)
-    yw(A2(1-y),0); zsend(A3(z),z,A); sibsend(A2(1-y),1)
-    both(1,late)
-    tail_along_z(False)
-    both(2,early)
-    def a3(zs):
-        zwait(A3(zs),zs,A); zsend(A3(zs),zs,A); sibsend(A3(zs),2+zs)
-    both(1,a3)
-    both(2,late)
-    tail_along_x()
-    both(3,early)
-    both(2,a3)
-    both(3,late)
-    both(3,a3)
-    for s in range(4):
-        def fin(zs):
-            xw(B2(zs,1-x),1+zs); sibsend(B2(zs,1-x),11+zs)
-            yw(C3(zs,1-y),2+zs); sibsend(C3(zs,1-y),23+zs)
-        if s==0: fin(z)
-        else: both(s,fin)
-    xd(A1(x),0); yd(A2(y),0); yd(B1(y),1)
-    sibwait(A1(1-x,orow),0) ; sibwait(A2(1-y,orow),1); sibwait(B1(1-y,orow),6)
-    for zs in range(4):
-        xd(B2(zs,x),1+zs); xd(C2(zs,x),5+zs); yd(C3(zs,y),2+zs)
-        zsent(A3(zs),zs,A); zsent(B2(zs,x),zs,B); zsent(C1(zs),zs,C)
-        sibwait(B2(zs,1-x,orow),11+zs); sibwait(C2(zs,1-x,orow),19+zs); sibwait(C3(zs,1-y,orow),23+zs)
-        @pl.when(zs!=z)
-        def _():
-            sibwait(A3(zs,orow),2+zs); sibwait(B2(zs,x,orow),7+zs); sibwait(C1(zs,orow),15+zs)
-    tail_end()
-    leave=[pltpu.make_async_copy(out.at[zs],result.at[zs],out_sem.at[zs]) for zs in range(4)]
-    for move in leave: move.start()
-    for move in leave: move.wait()
-
-def gather_blocks(blk,last):
-    D=pltpu.SemaphoreType.DMA
-    return pl.pallas_call(ag_kernel,out_shape=[jax.ShapeDtypeStruct((4,2,2,768,768),jnp.bfloat16),jax.ShapeDtypeStruct((16,768),jnp.bfloat16)],
-        in_specs=[pl.BlockSpec(memory_space=pl.ANY),pl.BlockSpec(memory_space=pltpu.VMEM)],out_specs=[pl.BlockSpec(memory_space=pl.ANY),pl.BlockSpec(memory_space=pltpu.VMEM)],
-        scratch_shapes=[pltpu.VMEM((4,2,2,768,768),jnp.bfloat16),D,D((4,)),D,D,D,D,D((9,)),D((6,)),D((12,)),D((9,)),D((6,)),D((12,)),D((12,)),D((27,)),D((27,))],
-        compiler_params=pltpu.CompilerParams(collective_id=1,has_side_effects=True,vmem_limit_bytes=40<<20),name="gather_blocks")(blk,last)
-
-
-ALL = slice(None)
 
 def rs_kernel(g0,gwide,gdown,norm_in,out,norm_out,nx,ny,nz,nc,nacc,nrx,nry,nrz,nrc,nsx,nsy,nsz,nsc,own,sl,la1,la2,lafr,lafl,lb1,lb2r,lb2l,lb3,lc1r,lc1l,lc2,lc3,res,
               own_sem,ss,rs,rx,ry,rzr,rzl,sx,sy,szr,szl,fs,fr,osem):
@@ -351,31 +213,36 @@
         dist[r]=jnp.where(seg_col[r]==seg_row[...],d,FAR)
 
 QB=256
+def project_all(w,tokT,qT,kT,vT):
+    for n,o in enumerate((qT,kT,vT)):
+        @pl.loop(0,3)
+        def _(t):
+            c=pl.ds(pl.multiple_of(t*256,256),256)
+            o[c]=dot_tn(w[0,n//2,n%2,:,c],tokT[...]).astype(bf16)
+
+def attend_head(h,dist,kn,qT,kT,vT,mixT,mixb,lse):
+    rows=pl.ds(pl.multiple_of(h*HEAD,HEAD),HEAD)
+    kn[...]=kT[rows].astype(f32).T.astype(bf16)
+    m=slope(h)
+    for b in range(LEN//QB):
+        cols=pl.ds(b*QB,QB)
+        q=(qT[rows,cols]*bf16(0.125))
+        s=dot(kn[...],q)-m*dist[:,cols]
+        top=jnp.max(s,0,keepdims=True)
+        e=jnp.exp(s-top)
+        total=jnp.sum(e,0,keepdims=True)
+        o=dot(vT[rows],e.astype(bf16))/total
+        mixT[rows,cols]=o
+        mixb[rows,cols]=o.astype(bf16)
+        lse[h,:,cols]=top+jnp.log(total)
+
 def attend_kernel(tokens,w,seg_col,seg_row,tokT,qT,kT,vT,mixT,mixb,lse,dist,kn):
     tokT[...]=tokens[...].astype(f32).T.astype(bf16)
     fill_distance(dist,seg_col,seg_row)
-    for n,(o,s) in enumerate(((qT,0.125),(kT,1.0),(vT,1.0))):
-        @pl.loop(0,3)
-        def _(t):
-            c=pl.ds(pl.multiple_of(t*256,256),256)
-            r=dot_tn(w[0,n//2,n%2,:,c],tokT[...])
-            o[c]=r.astype(bf16)
+    project_all(w,tokT,qT,kT,vT)
     @pl.loop(0,HEADS)
     def _(h):
-        rows=pl.ds(pl.multiple_of(h*HEAD,HEAD),HEAD)
-        kn[...]=kT[rows].astype(f32).T.astype(bf16)
-        m=slope(h)
-        for b in range(LEN//QB):
-            cols=pl.ds(b*QB,QB)
-            q=(qT[rows,cols]*bf16(0.125))
-            s=dot(kn[...],q)-m*dist[:,cols]
-            top=jnp.max(s,0,keepdims=True)
-            e=jnp.exp(s-top)
-            total=jnp.sum(e,0,keepdims=True)
-            o=dot(vT[rows],e.astype(bf16))/total
-            mixT[rows,cols]=o
-            mixb[rows,cols]=o.astype(bf16)
-            lse[h,:,cols]=top+jnp.log(total)
+        attend_head(h,dist,kn,qT,kT,vT,mixT,mixb,lse)
 
 def attend(tokens,w,seg):
     T=jax.ShapeDtypeStruct((D,LEN),bf16)
@@ -508,6 +375,378 @@
         out_shape=[S((LEN,D),bf16),S((LEN,D),f32),S((D,LEN),bf16),S((LEN,D),bf16),S((4,D),f32),S((4,D,D),bf16),S((2,4,4,D//4,D),bf16)],
         scratch_shapes=[V((LEN,D)),V((8,LEN,D)),V((LEN,D)),V((4,TB,D),f32),V((4,TB,D),f32),V((TB,D),f32),V((4,LEN,D))],
         compiler_params=pltpu.CompilerParams(vmem_limit_bytes=62<<20),name="feed")(tokens,cot,mixb,*[w.reshape(4,4,4,D//4,D)]*4,norms)
+MESH = pl.DeviceIdType.MESH
+ALL = slice(None)
+HALF = D // 2
+B_ROWS, C_ROWS = 144, 240
+CHUNK = 96
+
+
+def place():
+    i = lax.axis_index("zero")
+    c = lax.axis_index("dp")
+    return i, c, i // 4, (i // 2) % 2, i % 2
+
+
+def partners(i, c, z, y, x):
+    return (c, i + 1 - 2 * x), (c, i + 2 - 4 * y), (1 - c, i), (c, i + 4), (c, i - 4)
+
+
+def enter(i, c, z, y, x):
+    barrier = pltpu.get_barrier_semaphore()
+    xp, yp, sib, up, down = partners(i, c, z, y, x)
+    for peer in (xp, yp, sib):
+        pl.semaphore_signal(barrier, inc=1, device_id=peer, device_id_type=MESH)
+
+    @pl.when(z > 0)
+    def _():
+        pl.semaphore_signal(barrier, inc=1, device_id=down, device_id_type=MESH)
+
+    @pl.when(z < 3)
+    def _():
+        pl.semaphore_signal(barrier, inc=1, device_id=up, device_id_type=MESH)
+
+    pl.semaphore_wait(barrier, 3 + jnp.minimum(z, 1) + jnp.minimum(3 - z, 1))
+
+
+class Lane:
+    def __init__(self, peer, sends, recvs):
+        self.peer, self.sends, self.recvs = peer, sends, recvs
+
+    def copy(self, ref, n):
+        return pltpu.make_async_remote_copy(
+            src_ref=ref, dst_ref=ref, send_sem=self.sends.at[n], recv_sem=self.recvs.at[n],
+            device_id=self.peer, device_id_type=MESH,
+        )
+
+    def go(self, ref, n):
+        self.copy(ref, n).start()
+
+    def got(self, ref, n):
+        self.copy(ref, n).wait_recv()
+
+    def gone(self, ref, n):
+        self.copy(ref, n).wait_send()
+
+
+def when(cond, fn):
+    @pl.when(cond)
+    def _():
+        fn()
+
+
+def gather_steps(out, tail, result, last, own_sem, out_sem, blk, sems):
+    i, c, z, y, x = place()
+    xp, yp, sib, up, down = partners(i, c, z, y, x)
+    (sp0z, rp0z, sp0f, rp0f, sp0g, rp0g, ssib0, rsib0, sx, rx, sy, ry, sup, sdown, rz, ssib, rsib,
+     st, rt) = sems
+    lane0z = Lane(up, sp0z, rp0z)
+    half = c * HALF
+    other = (1 - c) * HALF
+
+    def rows(base, start, size):
+        return pl.ds(pl.multiple_of(base + start, 16), size)
+
+    def p0(k, kind, base, mine):
+        r = rows(base, k * CHUNK, CHUNK)
+        if kind == "z":
+            return out.at[0, y, x, r]
+        if k % 2 == 0:
+            if kind == "f":
+                return out.at[0, y, x if mine else 1 - x, r]
+            return out.at[0, y if mine else 1 - y, ALL, r]
+        if kind == "f":
+            return out.at[0, y if mine else 1 - y, x, r]
+        return out.at[0, ALL, x if mine else 1 - x, r]
+
+    def first(k):
+        return Lane(xp if k % 2 == 0 else yp, sp0f, rp0f)
+
+    def second(k):
+        return Lane(yp if k % 2 == 0 else xp, sp0g, rp0g)
+
+    lane0s = Lane(sib, ssib0, rsib0)
+    lx, ly, ls = Lane(xp, sx, rx), Lane(yp, sy, ry), Lane(sib, ssib, rsib)
+    lup, ldown = Lane(up, sup, rz), Lane(down, sdown, rz)
+
+    def b1(yy, base=half):
+        return out.at[z, yy, x, rows(base, 0, B_ROWS)]
+
+    def b2(zs, xx, base=half):
+        return out.at[zs, ALL, xx, rows(base, 0, B_ROWS)]
+
+    def c1(zs, base=half):
+        return out.at[zs, y, x, rows(base, B_ROWS, C_ROWS)]
+
+    def c2(zs, xx, base=half):
+        return out.at[zs, y, xx, rows(base, B_ROWS, C_ROWS)]
+
+    def c3(zs, yy, base=half):
+        return out.at[zs, yy, ALL, rows(base, B_ROWS, C_ROWS)]
+
+    B, C = 0, 4
+    SB1, SB2, SB3, SC1, SC2, SC3 = 0, 1, 5, 9, 13, 17
+
+    def z_up(ref, n):
+        when(z < 3, lambda: lup.go(ref, n))
+
+    def z_down(ref, n):
+        when(z > 0, lambda: ldown.go(ref, n))
+
+    def z_on(ref, zs, base):
+        when(jnp.logical_and(zs < z, z < 3), lambda: lup.go(ref, base + zs))
+        when(jnp.logical_and(zs > z, z > 0), lambda: ldown.go(ref, base + zs))
+
+    def own(fn):
+        when(z > 0, fn)
+
+    def both(s, fn):
+        when(z - s >= 1, lambda: fn(z - s))
+        when(z + s <= 3, lambda: fn(z + s))
+
+    line = jnp.logical_and(y == 1, x == 1)
+    source = jnp.logical_and(line, z == 3)
+    tz, ty, tx = Lane(down, st, rt), Lane(yp, st, rt), Lane(xp, st, rt)
+
+    def tail_z(at_source):
+        def send():
+            if not at_source:
+                tz.copy(tail, 0).wait_recv()
+            when(z > 0, lambda: tail_copy(down, 0).start())
+            tail_copy(yp, 1).start()
+
+        when(jnp.logical_and(line, source if at_source else jnp.logical_not(source)), send)
+
+    def tail_copy(peer, n):
+        return pltpu.make_async_remote_copy(
+            src_ref=tail, dst_ref=tail, send_sem=st.at[n], recv_sem=rt.at[0],
+            device_id=peer, device_id_type=MESH,
+        )
+
+    def tail_x():
+        def send():
+            when(y == 0, lambda: tail_copy(yp, 1).wait_recv())
+            tail_copy(xp, 2).start()
+
+        when(x == 1, send)
+
+    def tail_end():
+        when(x == 0, lambda: tail_copy(xp, 2).wait_recv())
+        when(x == 1, lambda: tail_copy(xp, 2).wait_send())
+
+        def sent():
+            tail_copy(yp, 1).wait_send()
+            when(z > 0, lambda: tail_copy(down, 0).wait_send())
+
+        when(line, sent)
+
+    def begin():
+        local = pltpu.make_async_copy(blk, out.at[z, y, x], own_sem)
+        local.start()
+        when(source, lambda: tail.__setitem__(Ellipsis, last[...]))
+        local.wait()
+        tail_z(True)
+
+        def at_zero():
+            for k in range(4):
+                lane0z.go(p0(k, "z", half, True), k)
+            for k in range(4):
+                first(k).go(p0(k, "f", half, True), k)
+
+        when(z == 0, at_zero)
+
+        def others():
+            ly.go(b1(y), 4)
+            lx.go(c2(z, x), C + z)
+            ldown.go(c1(z), C + z)
+
+        own(others)
+
+        def pass_on(k):
+            def there():
+                lane0z.got(p0(k, "z", half, True), k)
+                when(z < 3, lambda: lane0z.go(p0(k, "z", half, True), k))
+                lane0s.go(p0(k, "z", half, True), k)
+                first(k).go(p0(k, "f", half, True), k)
+
+            own(there)
+
+        def turn(k):
+            first(k).got(p0(k, "f", half, False), k)
+            second(k).go(p0(k, "g", half, True), k)
+            lane0s.go(p0(k, "f", half, False), 4 + k)
+
+        pass_on(0)
+        pass_on(1)
+        turn(0)
+        pass_on(2)
+        turn(1)
+        pass_on(3)
+        turn(2)
+
+        def own_b():
+            ly.got(b1(1 - y), 4)
+            ls.go(b1(1 - y), SB1)
+            z_up(c1(z), C + z)
+            z_down(b2(z, x), B + z)
+            z_up(b2(z, x), B + z)
+            lx.go(b2(z, x), B + z)
+
+        turn(3)
+        own(own_b)
+        for k in range(4):
+            second(k).got(p0(k, "g", half, False), k)
+            lane0s.go(p0(k, "g", half, False), 8 + k)
+        for k in range(4):
+            own(lambda k=k: lane0s.got(p0(k, "z", other, True), k))
+            lane0s.got(p0(k, "f", other, False), 4 + k)
+            lane0s.got(p0(k, "g", other, False), 8 + k)
+
+    def early_c(zs):
+        lup.got(c1(zs), C + zs)
+        z_on(c1(zs), zs, C)
+        lx.go(c2(zs, x), C + zs)
+        ls.go(c1(zs), SC1 + zs)
+
+    def early_b(zs):
+        lup.got(b2(zs, x), B + zs)
+        z_on(b2(zs, x), zs, B)
+        lx.go(b2(zs, x), B + zs)
+        ls.go(b2(zs, x), SB2 + zs)
+
+    def late(zs):
+        lx.got(c2(zs, 1 - x), C + zs)
+        ly.go(c3(zs, y), zs)
+        ls.go(c2(zs, 1 - x), SC2 + zs)
+
+    def fin(zs):
+        lx.got(b2(zs, 1 - x), B + zs)
+        ls.go(b2(zs, 1 - x), SB3 + zs)
+        ly.got(c3(zs, 1 - y), zs)
+        ls.go(c3(zs, 1 - y), SC3 + zs)
+
+    steps = [
+        lambda: (own(lambda: late(z)), both(1, early_c)),
+        lambda: (both(1, early_b), tail_z(False)),
+        lambda: (both(1, late), both(2, early_c)),
+        lambda: (both(2, early_b), tail_x()),
+        lambda: both(2, late),
+        lambda: (own(lambda: fin(z)), both(3, early_c)),
+        lambda: both(3, early_b),
+        lambda: (both(3, late), both(1, fin)),
+        lambda: both(2, fin),
+        lambda: both(3, fin),
+    ]
+
+    def leave(zs):
+        return pltpu.make_async_copy(out.at[zs], result.at[zs], out_sem.at[zs])
+
+    def sib_got(zs):
+        def own_items():
+            ls.got(b1(1 - y, other), SB1)
+
+        def their_items():
+            ls.got(c1(zs, other), SC1 + zs)
+            ls.got(b2(zs, x, other), SB2 + zs)
+
+        when(zs == z, own_items)
+        when(zs != z, their_items)
+        ls.got(c2(zs, 1 - x, other), SC2 + zs)
+        ls.got(b2(zs, 1 - x, other), SB3 + zs)
+        ls.got(c3(zs, 1 - y, other), SC3 + zs)
+
+    def end():
+        leave(0).start()
+        for zs in range(1, 4):
+            sib_got(zs)
+            leave(zs).start()
+        tail_end()
+        for k in range(4):
+            when(z < 3, lambda: lane0z.gone(p0(k, "z", half, True), k))
+            first(k).gone(p0(k, "f", half, True), k)
+            second(k).gone(p0(k, "g", half, True), k)
+            own(lambda: lane0s.gone(p0(k, "z", half, True), k))
+            lane0s.gone(p0(k, "f", half, False), 4 + k)
+            lane0s.gone(p0(k, "g", half, False), 8 + k)
+
+        def own_sent():
+            ly.gone(b1(y), 4)
+            ls.gone(b1(1 - y), SB1)
+
+        own(own_sent)
+        for zs in range(1, 4):
+            lx.gone(c2(zs, x), C + zs)
+            lx.gone(b2(zs, x), B + zs)
+            ly.gone(c3(zs, y), zs)
+            for ref, base in ((c1(zs), C), (b2(zs, x), B)):
+                when(jnp.logical_and(zs <= z, z < 3), lambda: lup.gone(ref, base + zs))
+                when(jnp.logical_and(zs >= z, z > 0), lambda: ldown.gone(ref, base + zs))
+
+            def theirs():
+                ls.gone(c1(zs), SC1 + zs)
+                ls.gone(b2(zs, x), SB2 + zs)
+
+            when(zs != z, theirs)
+            ls.gone(c2(zs, 1 - x), SC2 + zs)
+            ls.gone(b2(zs, 1 - x), SB3 + zs)
+            ls.gone(c3(zs, 1 - y), SC3 + zs)
+        for zs in range(4):
+            leave(zs).wait()
+
+    return begin, steps, end
+
+
+def gather_attend_kernel(blk, last, tokens, seg_col, seg_row, result, tail, tokT, qT, kT, vT, mixT, mixb,
+                         lse, held, dist, kn, own_sem, out_sem, *sems):
+    i, c, z, y, x = place()
+    with jax.named_scope("enter"):
+        enter(i, c, z, y, x)
+    begin, steps, end = gather_steps(held, tail, result, last, own_sem, out_sem, blk, sems)
+    with jax.named_scope("distance"):
+        tokT[...] = tokens[...].astype(f32).T.astype(bf16)
+        fill_distance(dist, seg_col, seg_row)
+    with jax.named_scope("begin"):
+        begin()
+    with jax.named_scope("project"):
+        project_all(held, tokT, qT, kT, vT)
+
+    @pl.loop(0, HEADS)
+    def _(h):
+        if True:
+            for n, step in enumerate(steps):
+                when(h == n + 1, step)
+        with jax.named_scope("head"):
+            attend_head(h, dist, kn, qT, kT, vT, mixT, mixb, lse)
+
+    with jax.named_scope("end"):
+        end()
+
+
+def gather_attend(blk, last, tokens, seg):
+    T = jax.ShapeDtypeStruct((D, LEN), bf16)
+    Q = pltpu.SemaphoreType.DMA
+    any_space = pl.BlockSpec(memory_space=pl.ANY)
+    counts = [4] * 6 + [12, 12, 8, 8, 5, 5, 8, 8, 8, 21, 21, 3, 1]
+    outs = pl.pallas_call(
+        gather_attend_kernel,
+        in_specs=[any_space, VM, VM, VM, VM],
+        out_specs=[any_space] + [VM] * 8,
+        out_shape=[
+            jax.ShapeDtypeStruct((4, 2, 2, D, D), bf16), jax.ShapeDtypeStruct((16, D), bf16), T, T, T, T,
+            jax.ShapeDtypeStruct((D, LEN), f32), T, jax.ShapeDtypeStruct((HEADS, 1, LEN), f32),
+        ],
+        scratch_shapes=[
+            pltpu.VMEM((4, 2, 2, D, D), bf16), pltpu.VMEM((LEN, LEN), f32), pltpu.VMEM((LEN, HEAD), bf16),
+            Q, Q((4,)), *[Q((n,)) for n in counts],
+        ],
+        compiler_params=pltpu.CompilerParams(
+            collective_id=1, has_side_effects=True, vmem_limit_bytes=58 << 20
+        ),
+        name="gather_attend",
+    )(blk, last, tokens, seg.reshape(LEN, 1), seg.reshape(1, LEN))
+    blocks, tail, tokT, qT, kT, vT, mixT, mixb, lse = outs
+    return blocks, tail, (tokT, qT, kT, vT, mixT), mixb, lse
+
 
 SQUARE = D * D
 TAIL = 4 * D
@@ -528,7 +767,7 @@
     return jnp.where(wide, swapped, block)
 
 
-def gather_weights(master):
+def gather_and_attend(master, tokens, segments):
     count = lax.axis_size("zero")
     index = lax.axis_index("zero")
     size = 16 * SQUARE // count
@@ -539,7 +778,8 @@
     block = lax.dynamic_slice(joined, (TAIL - TAIL // count * index,), (size,))
     if count == 16:
         padded = jnp.pad(last.reshape(4, D), ((0, 12), (0, 0)))
-        blocks, tail = gather_blocks(swap_wide(block.reshape(D, D), index, False), padded)
+        block = swap_wide(block.reshape(D, D), index, False)
+        blocks, tail, *attended = gather_attend(block, padded, tokens, segments)
         norms = tail[:4].astype(f32)
     else:
         natural = lax.all_gather(block.reshape(-1, D), "zero", axis=0, tiled=True)
@@ -547,7 +787,8 @@
         wide = [to_wide(parts[k].reshape(D, FF)) for k in (1, 2)]
         blocks = jnp.stack([parts[0].reshape(2, 2, D, D), *wide, parts[3].reshape(2, 2, D, D)])
         norms = lax.psum(jnp.where(index == count - 1, last.astype(f32), 0.0), "zero").reshape(4, D)
-    return blocks, norms
+        attended = attend(tokens, blocks, segments)
+    return blocks, norms, *attended
 
 
 def scatter_grads(square, wide, down, norm_grads):
@@ -570,8 +811,7 @@
 
 
 def local(tokens, segments, cotangent, master, moment_one, moment_two):
-    blocks, norms = gather_weights(master)
-    kept, mixed, log_sum = attend(tokens, blocks, segments)
+    blocks, norms, kept, mixed, log_sum = gather_and_attend(master, tokens, segments)
     output, first_grad, grad_mixed, branch_grad, norm_grads, down_grad, wide_grad = feed(
         tokens, cotangent, mixed, blocks, norms
     )

time: 431 us -> 432 us (level)
    pallas_call x1, Pallas kernels: 134 us -> 140 us  [reduce_blocks(): pl.pallas_call(rs_kernel, out_shape=[jax.ShapeDtypeStruct((768, 768), jnp...]
    pallas_call x2 -> x1, Pallas kernels: 128 us -> 123 us  [gather_attend(): pl.pallas_call(gather_attend_kernel, in_specs=[any_space, VM, VM, VM, VM]...]
where the time goes in v4:
time: 432 us
  Pallas kernels  396 us (92%)
  other arithmetic  15.1 us (3%)
  local copies, waits for them, and re-layouts  10 us (2%)
  starting transfers between devices  5.31 us (1%)
    pallas_call x1, Pallas kernels, reduce_blocks(): pl.pallas_call(rs_kernel, out_shape=[jax.ShapeDtypeStruct((768, 768), jnp...  140 us
    pallas_call x1, Pallas kernels, gather_attend(): pl.pallas_call(gather_attend_kernel, in_specs=[any_space, VM, VM, VM, VM]...  123 us
    pallas_call x1, Pallas kernels, feed(): pl.pallas_call(feed_kernel, grid=(n + 12,), in_specs=[pl.BlockSpec((TB, D...  76.1 us
    pallas_call x1, Pallas kernels, attend_back(): pl.pallas_call(attend_back_kernel, grid=(1,), in_specs=[pl.BlockSpec((1,...  56.9 us
  transfers between devices with their start and end apart: 2, of which 2 were waited for; matrix products, arithmetic and copies ran while one was open for 1% of the time, Pallas kernels for 0%

profile of v4, /device:TPU:8, one launch (start us, length us, event | category | flops | bytes accessed | tf_op | source)
XLA Modules:
  0.0 431.6 jit_solution(16229197520064482909)
XLA Ops:
  0.6 0.0 copy-start
  0.6 1.8 convert_element_type.11
  2.4 0.1 slice.16
  2.5 3.4 collective-permute-start
  5.9 1.0 copy.15.seg_col
  7.0 0.6 pad.4.last
  7.6 2.2 collective-permute-done
  9.8 1.0 fusion.1
  10.8 0.5 reshape_reshape.3
  11.3 1.1 reshape.54
  12.4 0.1 copy.14
  12.5 1.2 bitcast_select_fusion.blk
  13.7 123.0 %gather_attend.1 = (bf16[4,2,2,768,768]{4,3,2,1,0:T(8,128)(2,1)}, bf16[16,768]{1,0:T(8,128)(2,1)}, bf16[768,1024]{1,0:T(8,128)(2,1)}, bf16[768,1024]{1,0:T(8,128...) custom-call(bf16[768,768]{1,0:T(8,128)(2,1)} %bitcast_select_fusion., ...), custom_call_target="tpu_custom_call" | custom-call | tf_op jit(solution)/shard_map/gather_attend/pallas_call | solution.py:730
  136.7 1.3 slice_convert_fusion.norms
  138.0 76.1 %feed.1 = (bf16[1024,768]{1,0:T(8,128)(2,1)}, f32[1024,768]{1,0:T(8,128)}, bf16[768,1024]{1,0:T(8,128)(2,1)}, bf16[1024,768]{1,0:T(8,128)(2,1)}, f32[4,768]{1,0:...) custom-call(bf16[1024,768]{1,0:T(8,128)(2,1)} %tokens.3, bf16[1024,768]{1,0:T(8,128)(2,1)} %cot.1, ...), custom_call_target="tpu_custom_call" | custom-call | tf_op jit(solution)/shard_map/feed/pallas_call | solution.py:368
  214.1 56.9 %attend_back.1 = (bf16[2,2,768,768]{3,2,1,0:T(8,128)(2,1)}, f32[1024,768]{1,0:T(8,128)}) custom-call(bf16[4,2,2,768,768]{4,3,2,1,0:T(8,128)(2,1)} %get-tuple-element.28.w, s32[1024,1]{1,0:T(8,128)} %copy.15.seg_col, s32[1,1024]{1,0:T(1,128)} %bitcast.22, bf16[768,1024]{1,0:T(8,128)(2,1)} %get-tuple-element.31.tokT, bf16[768,1024]{1,0:T(8,128)(2,1)} %get-tuple-element.32.qT, ...), custom_call_target="tpu_custom_call" | custom-call | tf_op jit(solution)/shard_map/attend_back/pallas_call | solution.py:289
  271.0 140.2 %reduce_blocks.1 = (f32[768,768]{1,0:T(8,128)}, f32[4,768]{1,0:T(4,128)}) custom-call(bf16[2,2,768,768]{3,2,1,0:T(8,128)(2,1)} %get-tuple-element.41.g0, bf16[2,2,2,768,768]{4,3,2,1,0:T(8,128)(2,1)} %bitcast.17, bf16[2,2,768,768]{3,2,1,0:T(8,128)(2,1)} %bitcast.20, f32[4,768]{1,0:T(4,128)} %get-tuple-element.44.norm_in), custom_call_target="tpu_custom_call" | custom-call | tf_op jit(solution)/shard_map/reduce_blocks/pallas_call | solution.py:188
  411.1 3.2 copy.19
  414.3 1.9 reshape.62
  416.2 2.0 broadcast_select_fusion
  418.1 1.9 collective-permute-start.1
  420.1 1.6 reshape.63
  421.7 2.1 collective-permute-done.1
  423.8 7.8 %fusion.2 = (bf16[590016]{0:T(1024)(128)(2,1)}, f32[590016]{0:T(1024)}, f32[590016]{0:T(1024)}, f32[590016]{0:T(1024)}, f32[590016]{0:T(1024)}) fusion(f32[590016]{0:T(1024)} %param.9, f32[590016]{0:T(1024)} %param.11, f32[590016]{0:T(1024)} %param.10, s32[]{:T(128)S(6)} %select_n.34, f32[3072]{0:T(1024)S(1)} %broadcast_select_fusion.1, f32[589824]{0:T(1024)} %reshape.63), kind=kLoop, calls=%fused_computation.15 | loop fusion | flops 10620288 | bytes 20072068 | tf_op jit(solution)/shard_map/convert_element_type | solution.py:836
  (8 shorter events, 0.0 us)
Async XLA Ops:
  0.6 5.3 %copy-start = (s32[1024]{0:T(1024)S(1)}, s32[1024]{0:T(1024)}, u32[]{:S(2)}) copy-start(s32[1024]{0:T(1024)} %param.7) | copy-start | bytes 12292
  2.5 7.3 %collective-permute-start = (bf16[3072]{0:T(1024)(128)(2,1)S(1)}, bf16[3072]{0:T(1024)(128)(2,1)S(1)}, u32[]{:S(2)}, u32[]{:S(2)}) collective-permute-start(bf16[3072]{0:T(1024)(128)(2,1)S(1)} %slice.16), channel_id=1, source_target_pairs={{0,1},{1,2},{2,3},{3,4},{4,5},{5,6},{6,7},{7,8},{8,9},{9,10},{10,1... | collective-permute-start | bytes 18440 | tf_op jit(solution)/shard_map/ppermute | solution.py:776
  418.1 5.6 %collective-permute-start.1 = (f32[3072]{0:T(1024)S(1)}, f32[3072]{0:T(1024)S(1)}, u32[]{:S(2)}, u32[]{:S(2)}) collective-permute-start(f32[3072]{0:T(1024)S(1)} %slice.15), channel_id=1, source_target_pairs={{1,0},{2,1},{3,2},{4,3},{5,4},{6,5},{7,6},{8,7},{9,8},{10,9},{11,1... | collective-permute-start | bytes 36872 | tf_op jit(solution)/shard_map/ppermute | solution.py:807
  420.1 1.6 copy-start.1

commit v5 on v4

--- a/solution.py
+++ b/solution.py
@@ -26,172 +26,6 @@
 inv_root_tau = 0.3989422804014327
 
 
-RA,RB,RC=48,128,208
-OFFS=(0,RA,RA+RB)
-LENS=(RA,RB,RC)
-
-def enter_barrier(i,c,z):
-    bar=pltpu.get_barrier_semaphore()
-    for dev in ((c,i+1-2*(i%2)),(c,i+2-4*((i//2)%2)),(1-c,i)):
-        pl.semaphore_signal(bar,inc=1,device_id=dev,device_id_type=MESH)
-    @pl.when(z>0)
-    def _(): pl.semaphore_signal(bar,inc=1,device_id=(c,i-4),device_id_type=MESH)
-    @pl.when(z<3)
-    def _(): pl.semaphore_signal(bar,inc=1,device_id=(c,i+4),device_id_type=MESH)
-    pl.semaphore_wait(bar,3+jnp.minimum(z,1)+jnp.minimum(3-z,1))
-
-def rs_kernel(g0,gwide,gdown,norm_in,out,norm_out,nx,ny,nz,nc,nacc,nrx,nry,nrz,nrc,nsx,nsy,nsz,nsc,own,sl,la1,la2,lafr,lafl,lb1,lb2r,lb2l,lb3,lc1r,lc1l,lc2,lc3,res,
-              own_sem,ss,rs,rx,ry,rzr,rzl,sx,sy,szr,szl,fs,fr,osem):
-    i,c,z,y,x=place()
-    xp=(c,i+1-2*x); yp=(c,i+2-4*y); sib=(1-c,i); zr=(c,i+4); zl=(c,i-4)
-    mine=pl.ds(pl.multiple_of(c*HALF,16),HALF); other=pl.ds(pl.multiple_of((1-c)*HALF,16),HALF)
-    planes=[g0,gwide.at[0],gwide.at[1],gdown]
-    locs=[pltpu.make_async_copy(planes[zt].at[:,:,mine],own.at[zt],own_sem.at[zt]) for zt in range(4)]
-    for d in locs: d.start()
-    enter_barrier(i,c,z)
-    sibs=[pltpu.make_async_remote_copy(src_ref=planes[zt].at[:,:,other],dst_ref=sl.at[zt],send_sem=ss.at[zt],recv_sem=rs.at[zt],device_id=sib,device_id_type=MESH) for zt in range(4)]
-    for d in sibs: d.start()
-    r=[pl.ds(OFFS[k],LENS[k]) for k in range(3)]
-    def rc(src,dst,dev,s,q):
-        return pltpu.make_async_remote_copy(src_ref=src,dst_ref=dst,send_sem=s,recv_sem=q,device_id=dev,device_id_type=MESH)
-    def add(dst,src,n,rows,step):
-        @pl.loop(0,rows//step)
-        def _(k):
-            q=pl.ds(pl.multiple_of(k*step,16),step)
-            dst(q)[...]=(dst(q)[...].astype(jnp.float32)+src(q)[...].astype(jnp.float32)).astype(jnp.bfloat16)
-    def sub(k,q): return pl.ds(pl.multiple_of(OFFS[k]+q.start,16),q.size)
-    def add2(ownidx,k,land):
-        add(lambda q: own.at[tuple(ownidx)+(sub(k,q),)], lambda q: land.at[tuple([ALL]*(len(land.shape)-2))+(q,)],0,LENS[k],16)
-    def C3(zt): return rc(own.at[zt,1-y,:,r[2]],lc3.at[zt],yp,sy.at[zt],ry.at[zt])
-    def B3(zt): return rc(own.at[zt,:,1-x,r[1]],lb3.at[zt],xp,sx.at[zt],rx.at[zt])
-    def C2(zt): return rc(own.at[zt,y,1-x,r[2]],lc2.at[zt],xp,sx.at[4+zt],rx.at[4+zt])
-    A2=rc(own.at[z,1-y,:,r[0]],la2,yp,sy.at[4],ry.at[4])
-    A1=rc(own.at[z,y,1-x,r[0]],la1,xp,sx.at[8],rx.at[8])
-    B1=rc(own.at[z,1-y,x,r[1]],lb1,yp,sy.at[5],ry.at[5])
-    def zline(src,landr,landl,base):
-        def R(zt): return rc(src(zt),landr.at[zt],zr,szr.at[base+zt],rzr.at[base+zt])
-        def L(zt): return rc(src(zt),landl.at[zt],zl,szl.at[base+zt],rzl.at[base+zt])
-        return R,L
-    AR,AL=zline(lambda zt: own.at[zt,:,:,r[0]],lafr,lafl,0)
-    BR,BL=zline(lambda zt: own.at[zt,:,x,r[1]],lb2r,lb2l,4)
-    CR,CL=zline(lambda zt: own.at[zt,y,x,r[2]],lc1r,lc1l,8)
-    def zgo(zt,idx,k,R,L,landr,landl):
-        @pl.when(zt>z)
-        def _():
-            @pl.when(z>0)
-            def _():
-                R(zt).wait_recv(); add2(idx,k,landr.at[zt])
-            R(zt).start()
-        @pl.when(zt<z)
-        def _():
-            @pl.when(z<3)
-            def _():
-                L(zt).wait_recv(); add2(idx,k,landl.at[zt])
-            L(zt).start()
-    def zfin(idx,k,R,L,landr,landl):
-        @pl.when(z>0)
-        def _(): R(z).wait_recv(); add2(idx,k,landr.at[z])
-        @pl.when(z<3)
-        def _(): L(z).wait_recv(); add2(idx,k,landl.at[z])
-    def far(s):
-        return s
-    def sumsib(zt):
-        locs[zt].wait(); sibs[zt].wait_recv()
-        @pl.loop(0,HALF//16)
-        def _(k):
-            q=pl.ds(pl.multiple_of(k*16,16),16)
-            own[zt,:,:,q]=(own[zt,:,:,q].astype(jnp.float32)+sl[zt,:,:,q].astype(jnp.float32)).astype(jnp.bfloat16)
-    order=[3,0,2,1]
-    nacc[...]=norm_in[...]
-    NX=rc(nacc,nx,xp,nsx,nrx); NY=rc(nacc,ny,yp,nsy,nry); NZ=rc(nacc,nz,zr,nsz,nrz); NC=rc(nacc,nc,sib,nsc,nrc)
-    line=jnp.logical_and(x==1,y==1)
-    end=jnp.logical_and(line,z==3)
-    @pl.when(x==0)
-    def _(): NX.start()
-    def norm_y():
-        @pl.when(x==1)
-        def _():
-            NX.wait_recv(); nacc[...]+=nx[...]
-            @pl.when(y==0)
-            def _(): NY.start()
-    def norm_z(k):
-        @pl.when(jnp.logical_and(line,z==k))
-        def _():
-            NY.wait_recv(); nacc[...]+=ny[...]
-            if k>0:
-                NZ.wait_recv(); nacc[...]+=nz[...]
-            if k<3: NZ.start()
-            else: NC.start()
-    def norm_end():
-        @pl.when(x==0)
-        def _(): NX.wait_send()
-        @pl.when(jnp.logical_and(x==1,y==0))
-        def _(): NY.wait_send()
-        @pl.when(jnp.logical_and(line,z<3))
-        def _(): NZ.wait_send()
-        @pl.when(end)
-        def _():
-            NC.wait_recv(); NC.wait_send()
-            nacc[...]+=nc[...]
-        norm_out[...]=nacc[...]
-    for zt in order:
-        sumsib(zt)
-        C3(zt).start(); B3(zt).start()
-        zgo(zt,(zt,ALL,ALL),0,AR,AL,lafr,lafl)
-    def c3done(zt):
-        C3(zt).wait_recv(); add2((zt,y,ALL),2,lc3.at[zt]); C2(zt).start()
-    def b3done(zt):
-        B3(zt).wait_recv(); add2((zt,ALL,x),1,lb3.at[zt])
-        zgo(zt,(zt,ALL,x),1,BR,BL,lb2r,lb2l)
-    def c2done(zt):
-        C2(zt).wait_recv(); add2((zt,y,x),2,lc2.at[zt])
-        zgo(zt,(zt,y,x),2,CR,CL,lc1r,lc1l)
-    c3done(3); b3done(3); norm_y(); c3done(0); b3done(0); norm_z(0); c2done(3); c3done(2); b3done(2); norm_z(1); c2done(0); c3done(1); b3done(1); norm_z(2); c2done(2); c2done(1); norm_z(3)
-    zfin((z,ALL,ALL),0,AR,AL,lafr,lafl)
-    A2.start()
-    zfin((z,ALL,x),1,BR,BL,lb2r,lb2l)
-    B1.start()
-    A2.wait_recv(); add2((z,y,ALL),0,la2)
-    A1.start()
-    zfin((z,y,x),2,CR,CL,lc1r,lc1l)
-    def final(k,land):
-        @pl.loop(0,LENS[k]//16)
-        def _(t):
-            q=pl.ds(pl.multiple_of(t*16,16),16)
-            o=pl.ds(pl.multiple_of(OFFS[k]+t*16,16),16)
-            v=own[z,y,x,o].astype(jnp.float32)
-            if land is not None: v=v+land[q].astype(jnp.float32)
-            res[o]=v
-    final(2,None)
-    B1.wait_recv(); final(1,lb1)
-    A1.wait_recv(); final(0,la1)
-    fin=rc(res,out.at[mine],sib,fs,fr)
-    fin.start()
-    loc=pltpu.make_async_copy(res,out.at[mine],osem)
-    loc.start()
-    for zt in range(4):
-        sibs[zt].wait_send(); C3(zt).wait_send(); B3(zt).wait_send(); C2(zt).wait_send()
-        for R,L in ((AR,AL),(BR,BL),(CR,CL)):
-            @pl.when(zt>z)
-            def _(): R(zt).wait_send()
-            @pl.when(zt<z)
-            def _(): L(zt).wait_send()
-    A2.wait_send(); A1.wait_send(); B1.wait_send()
-    norm_end()
-    loc.wait(); fin.wait_send()
-    rc(res,out.at[other],sib,fs,fr).wait_recv()
-
-def reduce_blocks(g0,gwide,gdown,norms):
-    D=pltpu.SemaphoreType.DMA
-    bf=jnp.bfloat16
-    V=lambda *s: pltpu.VMEM(s,bf)
-    return pl.pallas_call(rs_kernel,out_shape=[jax.ShapeDtypeStruct((768,768),jnp.float32),jax.ShapeDtypeStruct((4,768),jnp.float32)],
-        in_specs=[pl.BlockSpec(memory_space=pl.ANY)]*3+[pl.BlockSpec(memory_space=pltpu.VMEM)],out_specs=[pl.BlockSpec(memory_space=pl.ANY),pl.BlockSpec(memory_space=pltpu.VMEM)],
-        scratch_shapes=[*[pltpu.VMEM((4,768),jnp.float32)]*5,*[D]*8,V(4,2,2,HALF,768),V(4,2,2,HALF,768),V(RA,768),V(2,RA,768),V(4,2,2,RA,768),V(4,2,2,RA,768),
-            V(RB,768),V(4,2,RB,768),V(4,2,RB,768),V(4,2,RB,768),V(4,RC,768),V(4,RC,768),V(4,RC,768),V(4,2,RC,768),pltpu.VMEM((HALF,768),jnp.float32),
-            D((4,)),D((4,)),D((4,)),D((9,)),D((6,)),D((12,)),D((12,)),D((9,)),D((6,)),D((12,)),D((12,)),D,D,D],
-        compiler_params=pltpu.CompilerParams(collective_id=2,has_side_effects=True,vmem_limit_bytes=58<<20),name="reduce_blocks")(g0,gwide,gdown,norms)
-
 bf16=jnp.bfloat16; f32=jnp.float32
 FAR=1e33
 VM=pl.BlockSpec(memory_space=pltpu.VMEM)
@@ -213,69 +47,71 @@
         dist[r]=jnp.where(seg_col[r]==seg_row[...],d,FAR)
 
 QB=256
-def project_all(w,tokT,qT,kT,vT):
-    for n,o in enumerate((qT,kT,vT)):
+def project_all(w,tokT,qkv):
+    @pl.loop(0,3)
+    def _(n):
         @pl.loop(0,3)
         def _(t):
             c=pl.ds(pl.multiple_of(t*256,256),256)
-            o[c]=dot_tn(w[0,n//2,n%2,:,c],tokT[...]).astype(bf16)
-
-def attend_head(h,dist,kn,qT,kT,vT,mixT,mixb,lse):
+            qkv[n,c]=dot_tn(w[0,n//2,n%2,:,c],tokT[...]).astype(bf16)
+
+def attend_head(h,dist,kn,qkv,mixb,lse):
     rows=pl.ds(pl.multiple_of(h*HEAD,HEAD),HEAD)
-    kn[...]=kT[rows].astype(f32).T.astype(bf16)
+    kn[...]=qkv[1,rows].astype(f32).T.astype(bf16)
     m=slope(h)
     for b in range(LEN//QB):
         cols=pl.ds(b*QB,QB)
-        q=(qT[rows,cols]*bf16(0.125))
+        q=qkv[0,rows,cols]*bf16(0.125)
         s=dot(kn[...],q)-m*dist[:,cols]
         top=jnp.max(s,0,keepdims=True)
         e=jnp.exp(s-top)
         total=jnp.sum(e,0,keepdims=True)
-        o=dot(vT[rows],e.astype(bf16))/total
-        mixT[rows,cols]=o
+        o=dot(qkv[2,rows],e.astype(bf16))/total
         mixb[rows,cols]=o.astype(bf16)
         lse[h,:,cols]=top+jnp.log(total)
 
-def attend_kernel(tokens,w,seg_col,seg_row,tokT,qT,kT,vT,mixT,mixb,lse,dist,kn):
+def attend_kernel(tokens,w,seg_col,seg_row,tokT,qkv,mixb,lse,dist,kn):
     tokT[...]=tokens[...].astype(f32).T.astype(bf16)
     fill_distance(dist,seg_col,seg_row)
-    project_all(w,tokT,qT,kT,vT)
+    project_all(w,tokT,qkv)
     @pl.loop(0,HEADS)
     def _(h):
-        attend_head(h,dist,kn,qT,kT,vT,mixT,mixb,lse)
+        attend_head(h,dist,kn,qkv,mixb,lse)
+
+def attend_shapes():
+    S=jax.ShapeDtypeStruct
+    return [S((D,LEN),bf16),S((3,D,LEN),bf16),S((D,LEN),bf16),S((HEADS,1,LEN),f32)]
 
 def attend(tokens,w,seg):
-    T=jax.ShapeDtypeStruct((D,LEN),bf16)
-    tokT,qT,kT,vT,mixT,mixb,lse=pl.pallas_call(attend_kernel,grid=(1,),
-        in_specs=[VM,pl.BlockSpec((1,2,2,D,D),lambda i:(0,0,0,0,0)),VM,VM],out_specs=[VM]*7,
-        out_shape=[T,T,T,T,jax.ShapeDtypeStruct((D,LEN),f32),T,jax.ShapeDtypeStruct((HEADS,1,LEN),f32)],
+    return pl.pallas_call(attend_kernel,grid=(1,),
+        in_specs=[VM,pl.BlockSpec((1,2,2,D,D),lambda i:(0,0,0,0,0)),VM,VM],out_specs=[VM]*4,
+        out_shape=attend_shapes(),
         scratch_shapes=[pltpu.VMEM((LEN,LEN),f32),pltpu.VMEM((LEN,HEAD),bf16)],
         compiler_params=pltpu.CompilerParams(vmem_limit_bytes=58<<20),name="attend")(tokens,w,seg.reshape(LEN,1),seg.reshape(1,LEN))
-    return (tokT,qT,kT,vT,mixT),mixb,lse
-
-def attend_back_kernel(w,seg_col,seg_row,tokT,qT,kT,vT,mixT,lse,dO,first,gbranch,g0,grad_in,dist,kn,vn,p_all,ds_all,dqT,dkT,dvT):
+
+def attend_back_kernel(w,seg_col,seg_row,tokT,qkv,mixb,lse,dO,first,gbranch,g0,grad_in,dist,kn,vn,p_all,ds_all,dqT,dkT,dvT):
     fill_distance(dist,seg_col,seg_row)
     @pl.loop(0,HEADS)
     def _(h):
         rows=pl.ds(pl.multiple_of(h*HEAD,HEAD),HEAD)
-        kn[...]=kT[rows].astype(f32).T.astype(bf16)
-        vn[...]=vT[rows].astype(f32).T.astype(bf16)
+        kn[...]=qkv[1,rows].astype(f32).T.astype(bf16)
+        vn[...]=qkv[2,rows].astype(f32).T.astype(bf16)
         m=slope(h)
         for b in range(LEN//QB):
             cols=pl.ds(b*QB,QB)
-            q=(qT[rows,cols]*bf16(0.125))
+            q=qkv[0,rows,cols]*bf16(0.125)
             s=dot(kn[...],q)-m*dist[:,cols]
             p=jnp.exp(s-lse[h,:,cols])
             do=dO[rows,cols]
-            delta=jnp.sum(do.astype(f32)*mixT[rows,cols],0,keepdims=True)
+            delta=jnp.sum(do.astype(f32)*mixb[rows,cols].astype(f32),0,keepdims=True)
             dp=dot(vn[...],do)
             p_all[:,cols]=p.astype(bf16)
             ds=(p*(dp-delta)).astype(bf16)
             ds_all[:,cols]=ds
-            dqT[rows,cols]=(dot(kT[rows],ds)*0.125).astype(bf16)
+            dqT[rows,cols]=(dot(qkv[1,rows],ds)*0.125).astype(bf16)
         dvT[rows]=dot_nt(dO[rows],p_all[...]).astype(bf16)
-        dkT[rows]=(dot_nt(qT[rows],ds_all[...])*0.125).astype(bf16)
-    g0[1,1]=dot(mixT[...].astype(bf16),gbranch[...]).astype(bf16)
+        dkT[rows]=(dot_nt(qkv[0,rows],ds_all[...])*0.125).astype(bf16)
+    g0[1,1]=dot(mixb[...],gbranch[...]).astype(bf16)
     for n,g in enumerate((dqT,dkT,dvT)):
         g0[n//2,n%2]=dot_nt(tokT[...],g[...]).astype(bf16)
     @pl.loop(0,4)
@@ -284,13 +120,13 @@
         acc=dot(w[0,0,0],dqT[:,c])+dot(w[0,0,1],dkT[:,c])+dot(w[0,1,0],dvT[:,c])
         grad_in[c]=first[c]+acc.T
 
-def attend_back(w,seg,tokT,qT,kT,vT,mixT,lse,dO,first,gbranch):
+def attend_back(w,seg,tokT,qkv,mixb,lse,dO,first,gbranch):
     B=lambda: pltpu.VMEM((D,LEN),bf16)
     return pl.pallas_call(attend_back_kernel,grid=(1,),
-        in_specs=[pl.BlockSpec((1,2,2,D,D),lambda i:(0,0,0,0,0))]+[VM]*11,out_specs=[VM]*2,
+        in_specs=[pl.BlockSpec((1,2,2,D,D),lambda i:(0,0,0,0,0))]+[VM]*9,out_specs=[VM]*2,
         out_shape=[jax.ShapeDtypeStruct((2,2,D,D),bf16),jax.ShapeDtypeStruct((LEN,D),f32)],
         scratch_shapes=[pltpu.VMEM((LEN,LEN),f32),pltpu.VMEM((LEN,HEAD),bf16),pltpu.VMEM((LEN,HEAD),bf16),pltpu.VMEM((LEN,LEN),bf16),pltpu.VMEM((LEN,LEN),bf16),B(),B(),B()],
-        compiler_params=pltpu.CompilerParams(vmem_limit_bytes=60<<20),name="attend_back")(w,seg.reshape(LEN,1),seg.reshape(1,LEN),tokT,qT,kT,vT,mixT,lse,dO,first,gbranch)
+        compiler_params=pltpu.CompilerParams(vmem_limit_bytes=60<<20),name="attend_back")(w,seg.reshape(LEN,1),seg.reshape(1,LEN),tokT,qkv,mixb,lse,dO,first,gbranch)
 
 TB=256
 def feed_kernel(tokens,cot,mixb,wo,w1,w2,w3,norms,output,first,dO,gbranch,ng,gdown,gwide,inner,wide,gffn,fa,fb,acc,hid):
@@ -375,6 +211,7 @@
         out_shape=[S((LEN,D),bf16),S((LEN,D),f32),S((D,LEN),bf16),S((LEN,D),bf16),S((4,D),f32),S((4,D,D),bf16),S((2,4,4,D//4,D),bf16)],
         scratch_shapes=[V((LEN,D)),V((8,LEN,D)),V((LEN,D)),V((4,TB,D),f32),V((4,TB,D),f32),V((TB,D),f32),V((4,LEN,D))],
         compiler_params=pltpu.CompilerParams(vmem_limit_bytes=62<<20),name="feed")(tokens,cot,mixb,*[w.reshape(4,4,4,D//4,D)]*4,norms)
+
 MESH = pl.DeviceIdType.MESH
 ALL = slice(None)
 HALF = D // 2
@@ -696,44 +533,43 @@
     return begin, steps, end
 
 
-def gather_attend_kernel(blk, last, tokens, seg_col, seg_row, result, tail, tokT, qT, kT, vT, mixT, mixb,
-                         lse, held, dist, kn, own_sem, out_sem, *sems):
+def gather_attend_kernel(blk, last, tokens, seg_col, seg_row, result, tail, tokT, qkv, mixb, lse,
+                          held, dist, kn, own_sem, out_sem, *sems):
     i, c, z, y, x = place()
-    with jax.named_scope("enter"):
+    if True:
         enter(i, c, z, y, x)
     begin, steps, end = gather_steps(held, tail, result, last, own_sem, out_sem, blk, sems)
-    with jax.named_scope("distance"):
+    if True:
         tokT[...] = tokens[...].astype(f32).T.astype(bf16)
         fill_distance(dist, seg_col, seg_row)
-    with jax.named_scope("begin"):
+    if True:
         begin()
-    with jax.named_scope("project"):
-        project_all(held, tokT, qT, kT, vT)
+    if True:
+        project_all(held, tokT, qkv)
 
     @pl.loop(0, HEADS)
     def _(h):
         if True:
             for n, step in enumerate(steps):
                 when(h == n + 1, step)
-        with jax.named_scope("head"):
-            attend_head(h, dist, kn, qT, kT, vT, mixT, mixb, lse)
-
-    with jax.named_scope("end"):
+        if True:
+            attend_head(h, dist, kn, qkv, mixb, lse)
+
+    if True:
         end()
 
 
 def gather_attend(blk, last, tokens, seg):
-    T = jax.ShapeDtypeStruct((D, LEN), bf16)
     Q = pltpu.SemaphoreType.DMA
     any_space = pl.BlockSpec(memory_space=pl.ANY)
     counts = [4] * 6 + [12, 12, 8, 8, 5, 5, 8, 8, 8, 21, 21, 3, 1]
-    outs = pl.pallas_call(
+    return pl.pallas_call(
         gather_attend_kernel,
         in_specs=[any_space, VM, VM, VM, VM],
-        out_specs=[any_space] + [VM] * 8,
+        out_specs=[any_space] + [VM] * 5,
         out_shape=[
-            jax.ShapeDtypeStruct((4, 2, 2, D, D), bf16), jax.ShapeDtypeStruct((16, D), bf16), T, T, T, T,
-            jax.ShapeDtypeStruct((D, LEN), f32), T, jax.ShapeDtypeStruct((HEADS, 1, LEN), f32),
+            jax.ShapeDtypeStruct((4, 2, 2, D, D), bf16), jax.ShapeDtypeStruct((16, D), bf16),
+            *attend_shapes(),
         ],
         scratch_shapes=[
             pltpu.VMEM((4, 2, 2, D, D), bf16), pltpu.VMEM((LEN, LEN), f32), pltpu.VMEM((LEN, HEAD), bf16),
@@ -744,9 +580,539 @@
         ),
         name="gather_attend",
     )(blk, last, tokens, seg.reshape(LEN, 1), seg.reshape(1, LEN))
-    blocks, tail, tokT, qT, kT, vT, mixT, mixb, lse = outs
-    return blocks, tail, (tokT, qT, kT, vT, mixT), mixb, lse
-
+
+
+PLANE_ORDER = (1, 3, 2)
+BACK_PLAN = (
+    (
+        14709104, 65761, 422402, 475168, 2192136, 200769, 4334084, 7606533, 7685670, 2639655,
+        8589896, 5255296, 8552726, 4399990, 9454628, 9671313, 3241751, 4531537, 3307544, 3543890,
+        10582358, 10713620, 10517269, 3692343, 8905304, 10638131, 11634052, 8803380, 3526835, 11587925,
+        9745106, 9934485, 10855635, 10987200, 11843009, 12761014, 12895683, 15779782, 15790320,
+    ),
+    (
+        14709104, 65761, 422402, 526112, 1057139, 328707, 4224034, 7672102, 8589863, 2639425,
+        3151488, 4358785, 4748871, 9446435, 9671313, 5273367, 3228453, 4487192, 7934770, 4535969,
+        5339668, 5667747, 6378080, 14825527, 6457109, 8750131, 5736096, 10670132, 13719605, 9744816,
+        9934485, 11776722, 5559123, 12625316, 10928469, 11842983, 12039874, 12895683, 15779782,
+    ),
+    (
+        14709104, 65761, 422402, 526112, 1057139, 262976, 7603490, 1123905, 2572917, 8595474,
+        3151488, 7766657, 2311760, 9539620, 1545106, 4749127, 3217445, 1258104, 5325689, 1324705,
+        4477562, 4553635, 3684256, 8852962, 3383940, 6510213, 13644934, 6599088, 3519441, 5747410,
+        9802853, 12621718, 5816787, 5481892, 12801218, 11904934, 11949492, 12895671, 15779782,
+    ),
+    (
+        14709104, 65761, 422402, 475168, 2192136, 200769, 4334084, 7606533, 2585894, 8595474,
+        3151488, 8552784, 4399990, 9454628, 9671313, 4618007, 3228965, 7870545, 5386823, 4732435,
+        1352057, 8102778, 3684256, 8852962, 3383940, 6718803, 5518470, 11587687, 13723840, 5685681,
+        9721141, 11703957, 12825538, 13882007, 5744036, 10987096, 11847093, 13022916, 15779767,
+    ),
+)
+
+
+B_PART, C_PART, PARTS = 48, 80, 3
+Q_PART = 96
+COLS = D // 2
+
+
+def pick(z, values):
+    out = jnp.int32(values[3])
+    for k in (2, 1, 0):
+        out = jnp.where(z == k, jnp.int32(values[k]), out)
+    return out
+
+
+def run_plan(z, words, ops):
+    count = len(words[0])
+    held = [pick(z, [words[k][n] for k in range(4)]) for n in range(count)]
+
+    @pl.loop(0, count)
+    def _(n):
+        word = held[0]
+        for k in range(1, count):
+            word = jnp.where(n == k, held[k], word)
+
+        @pl.loop(0, 3)
+        def _(m):
+            code = jnp.where(m == 0, word, jnp.where(m == 1, word // 256, word // 65536)) % 256
+            kind, e = code // 16, code % 16
+            for k, op in enumerate(ops):
+                when(kind == k, lambda op=op: op(e))
+
+
+def reduce_back_kernel(wide, down, w, qkv_in, dO, mixb, lse, tokT, gbranch, first, norm_in, seg_col, seg_row,
+                       grad_in, flat_out, own, sl, lc3, lc2, lcz, lczx, lb3, lbz, lbzx, lb1, lf, lg, lz, stage,
+                       dist, p_all, ds_all, wv, kn, vn, qkv, fchunk, flat, nacc, nx, ny, nz, nc,
+                       own_sem, qkv_sem, w_sem, f_sem, g_sem, o_sem, sib_s, sib_r, st_s, st_r,
+                       c3s, c3r, b3s, b3r, c2s, c2r, bus, bur, bds, bdr, cus, cur, cds, cdr, b1s, b1r,
+                       fs, fr, gs, gr, zs_, zr_, ns, nr, share_s, share_r, aft_s, aft_r):
+    i, c, z, y, x = place()
+    xp, yp, sib, up, down_peer = partners(i, c, z, y, x)
+    base = c * HALF
+    mine = pl.ds(pl.multiple_of(base, 16), HALF)
+    other = pl.ds(pl.multiple_of((1 - c) * HALF, 16), HALF)
+    planes = [wide.at[0], wide.at[1], down]
+
+    def remote(src, dst, peer, s, r):
+        return pltpu.make_async_remote_copy(
+            src_ref=src, dst_ref=dst, send_sem=s, recv_sem=r, device_id=peer, device_id_type=MESH
+        )
+
+    def local_in(t):
+        return pltpu.make_async_copy(planes[t - 1].at[:, :, mine], own.at[t], own_sem.at[t])
+
+    def sib_in(t):
+        return remote(planes[t - 1].at[:, :, other], sl.at[t], sib, sib_s.at[t], sib_r.at[t])
+
+    for t in PLANE_ORDER:
+        local_in(t).start()
+    qkv_copy = pltpu.make_async_copy(qkv_in, qkv, qkv_sem)
+    qkv_copy.start()
+    enter_more(i, c, z, y, x)
+    for t in PLANE_ORDER:
+        sib_in(t).start()
+    nacc[...] = norm_in[...]
+    NX = remote(nacc, nx, xp, ns.at[0], nr.at[0])
+    NY = remote(nacc, ny, yp, ns.at[1], nr.at[1])
+    NZ = remote(nacc, nz, up, ns.at[2], nr.at[2])
+    NC = remote(nacc, nc, sib, ns.at[3], nr.at[3])
+    line = jnp.logical_and(x == 1, y == 1)
+    last_line = jnp.logical_and(line, z == 3)
+    when(x == 0, lambda: NX.start())
+    fill_distance(dist, seg_col, seg_row)
+    qkv_copy.wait()
+
+    def rb(s, k=0, size=B_PART):
+        return pl.ds(pl.multiple_of(s * B_PART + k, 16), size)
+
+    def rc(s, k=0, size=C_PART):
+        return pl.ds(pl.multiple_of(3 * B_PART + s * C_PART + k, 16), size)
+
+    def add_rows(dst, src, rows):
+        @pl.loop(0, rows // 16)
+        def _(n):
+            k = pl.multiple_of(n * 16, 16)
+            a = dst(k)
+            a[...] = (a[...].astype(f32) + src(k)[...].astype(f32)).astype(bf16)
+
+    r16 = lambda k: pl.ds(k, 16)
+    split = lambda e: (e // 3 + 1, e % 3)
+
+    def C3(t, s, e):
+        return remote(own.at[t, 1 - y, :, rc(s)], lc3.at[e], yp, c3s.at[e], c3r.at[e])
+
+    def B3(t, s, e):
+        return remote(own.at[t, :, 1 - x, rb(s)], lb3.at[e], xp, b3s.at[e], b3r.at[e])
+
+    def C2(t, s, e):
+        return remote(own.at[t, y, 1 - x, rc(s)], lc2.at[e], xp, c2s.at[e], c2r.at[e])
+
+    def BU(t, s, e):
+        return remote(own.at[t, :, x, rb(s)], lbz.at[e], up, bus.at[e], bur.at[e])
+
+    def BD(t, s, e, extra=False):
+        return remote(own.at[t, :, x, rb(s)], lbzx.at[s] if extra else lbz.at[e], down_peer, bds.at[e], bdr.at[e])
+
+    def CU(t, s, e):
+        return remote(own.at[t, y, x, rc(s)], lcz.at[e], up, cus.at[e], cur.at[e])
+
+    def CD(t, s, e, extra=False):
+        return remote(own.at[t, y, x, rc(s)], lczx.at[s] if extra else lcz.at[e], down_peer, cds.at[e], cdr.at[e])
+
+    def B1(s):
+        return remote(own.at[z, 1 - y, x, rb(s)], lb1.at[s], yp, b1s.at[s], b1r.at[s])
+
+    def op_sum(e):
+        t, s = split(e)
+
+        def arrive():
+            for k in (1, 2, 3):
+                def both(k=k):
+                    local_in(k).wait()
+                    sib_in(k).wait_recv()
+
+                when(t == k, both)
+
+        when(s == 0, arrive)
+        add_rows(lambda k: own.at[t, :, :, rb(s, k, 16)], lambda k: sl.at[t, :, :, rb(s, k, 16)], B_PART)
+        add_rows(lambda k: own.at[t, :, :, rc(s, k, 16)], lambda k: sl.at[t, :, :, rc(s, k, 16)], C_PART)
+        C3(t, s, e).start()
+        B3(t, s, e).start()
+
+    def op_c3(e):
+        t, s = split(e)
+        C3(t, s, e).wait_recv()
+        add_rows(lambda k: own.at[t, y, :, rc(s, k, 16)], lambda k: lc3.at[e, :, r16(k)], C_PART)
+        C2(t, s, e).start()
+
+    def op_b3(e):
+        t, s = split(e)
+        B3(t, s, e).wait_recv()
+        add_rows(lambda k: own.at[t, :, x, rb(s, k, 16)], lambda k: lb3.at[e, :, r16(k)], B_PART)
+
+    def op_c2(e):
+        t, s = split(e)
+        C2(t, s, e).wait_recv()
+        add_rows(lambda k: own.at[t, y, x, rc(s, k, 16)], lambda k: lc2.at[e, r16(k)], C_PART)
+
+    def op_bz(e):
+        t, s = split(e)
+        dst = lambda k: own.at[t, :, x, rb(s, k, 16)]
+
+        def from_below():
+            BU(t, s, e).wait_recv()
+            add_rows(dst, lambda k: lbz.at[e, :, r16(k)], B_PART)
+
+        when(jnp.logical_and(t >= z, z > 0), from_below)
+
+        def from_above():
+            BD(t, s, e).wait_recv()
+            add_rows(dst, lambda k: lbz.at[e, :, r16(k)], B_PART)
+
+        when(t < z, lambda: when(z < 3, from_above))
+
+        def from_above_last():
+            BD(t, s, e).wait_recv()
+            add_rows(dst, lambda k: lbzx.at[s, :, r16(k)], B_PART)
+
+        when(jnp.logical_and(t == z, z < 3), from_above_last)
+        when(t > z, lambda: BU(t, s, e).start())
+        when(t == z - 1, lambda: BD(t, s, e, True).start())
+        when(t < z - 1, lambda: BD(t, s, e).start())
+        when(t == z, lambda: B1(s).start())
+
+    def res(rows):
+        return dist.at[rows, pl.ds(0, D)]
+
+    def op_cz(e):
+        t, s = split(e)
+        dst = lambda k: own.at[t, y, x, rc(s, k, 16)]
+
+        def from_below():
+            CU(t, s, e).wait_recv()
+            add_rows(dst, lambda k: lcz.at[e, r16(k)], C_PART)
+
+        when(jnp.logical_and(t >= z, z > 0), from_below)
+
+        def from_above():
+            CD(t, s, e).wait_recv()
+            add_rows(dst, lambda k: lcz.at[e, r16(k)], C_PART)
+
+        when(t < z, lambda: when(z < 3, from_above))
+
+        def from_above_last():
+            CD(t, s, e).wait_recv()
+            add_rows(dst, lambda k: lczx.at[s, r16(k)], C_PART)
+
+        when(jnp.logical_and(t == z, z < 3), from_above_last)
+        when(t > z, lambda: CU(t, s, e).start())
+        when(t == z - 1, lambda: CD(t, s, e, True).start())
+        when(t < z - 1, lambda: CD(t, s, e).start())
+
+    def op_b1(e):
+        t, s = split(e)
+        B1(s).wait_recv()
+        add_rows(lambda k: own.at[z, y, x, rb(s, k, 16)], lambda k: lb1.at[s, r16(k)], B_PART)
+
+    def op_head(h):
+        rows = pl.ds(pl.multiple_of(h * HEAD, HEAD), HEAD)
+        kn[...] = qkv[1, rows].astype(f32).T.astype(bf16)
+        vn[...] = qkv[2, rows].astype(f32).T.astype(bf16)
+        m = slope(h)
+        for b in range(LEN // QB):
+            cols = pl.ds(b * QB, QB)
+            q = qkv[0, rows, cols] * bf16(0.125)
+            s = dot(kn[...], q) - m * dist[:, cols]
+            p = jnp.exp(s - lse[h, :, cols])
+            do = dO[rows, cols]
+            delta = jnp.sum(do.astype(f32) * mixb[rows, cols].astype(f32), 0, keepdims=True)
+            dp = dot(vn[...], do)
+            p_all[:, cols] = p.astype(bf16)
+            ds_all[:, cols] = (p * (dp - delta)).astype(bf16)
+        grad_q = (dot(qkv[1, rows], ds_all[...]) * 0.125).astype(bf16)
+        grad_k = (dot_nt(qkv[0, rows], ds_all[...]) * 0.125).astype(bf16)
+        grad_v = dot_nt(dO[rows], p_all[...]).astype(bf16)
+        qkv[0, rows] = grad_q
+        qkv[1, rows] = grad_k
+        qkv[2, rows] = grad_v
+
+    def columns(g):
+        return pl.ds(pl.multiple_of(g * COLS, 128), COLS)
+
+    def stage_copy(e):
+        g, n = e // 4, e % 4
+        return remote(
+            stage.at[e], sl.at[0, n // 2, n % 2, :, columns(g)], sib, st_s.at[e], st_r.at[e]
+        )
+
+    def op_dw(e):
+        g, n = e // 4, e % 4
+        cols = columns(g)
+
+        def put(half, value):
+            if half == 0:
+                own[0, n // 2, n % 2, :, cols] = value.astype(bf16)
+            else:
+                stage[e] = value.astype(bf16)
+
+        def inputs():
+            right = qkv[n, pl.ds(pl.multiple_of(g * COLS, 128), COLS)]
+            for half, rows in ((0, mine), (1, other)):
+                put(half, dot_nt(tokT[rows], right))
+
+        def output():
+            right = gbranch[:, cols]
+            for half, rows in ((0, mine), (1, other)):
+                put(half, dot(mixb[rows], right))
+
+        when(n < 3, inputs)
+        when(n == 3, output)
+        stage_copy(e).start()
+
+    def rq(k, n=0, size=Q_PART):
+        return pl.ds(pl.multiple_of(k * Q_PART + n, 16), size)
+
+    def F0(e, g, k, odd):
+        src = own.at[0, :, 1 - x, rq(k), columns(g)] if odd else own.at[0, 1 - y, :, rq(k), columns(g)]
+        return remote(src, lf.at[e], xp if odd else yp, fs.at[e], fr.at[e])
+
+    def G0(e, g, k, odd):
+        if odd:
+            return remote(own.at[0, 1 - y, x, rq(k), columns(g)], lg.at[e], yp, gs.at[e], gr.at[e])
+        return remote(own.at[0, y, 1 - x, rq(k), columns(g)], lg.at[e], xp, gs.at[e], gr.at[e])
+
+    def Z0(e, g, k):
+        return remote(own.at[0, y, x, rq(k), columns(g)], lz.at[e], down_peer, zs_.at[e], zr_.at[e])
+
+    def by_parity(k, fn):
+        when(k % 2 == 0, lambda: fn(False))
+        when(k % 2 == 1, lambda: fn(True))
+
+    def op_sum0(e):
+        g, k = e // 4, e % 4
+
+        def arrive():
+            @pl.loop(0, 4)
+            def _(n):
+                stage_copy(g * 4 + n).wait_recv()
+
+        when(k == 0, arrive)
+        add_rows(
+            lambda n: own.at[0, :, :, rq(k, n, 16), columns(g)],
+            lambda n: sl.at[0, :, :, rq(k, n, 16), columns(g)], Q_PART,
+        )
+        by_parity(k, lambda odd: F0(e, g, k, odd).start())
+
+    def op_f0(e):
+        g, k = e // 4, e % 4
+
+        def turn(odd):
+            F0(e, g, k, odd).wait_recv()
+            if odd:
+                dst = lambda n: own.at[0, :, x, rq(k, n, 16), columns(g)]
+            else:
+                dst = lambda n: own.at[0, y, :, rq(k, n, 16), columns(g)]
+            add_rows(dst, lambda n: lf.at[e, :, r16(n)], Q_PART)
+            G0(e, g, k, odd).start()
+
+        by_parity(k, turn)
+
+    def op_g0(e):
+        g, k = e // 4, e % 4
+        by_parity(k, lambda odd: G0(e, g, k, odd).wait_recv())
+        add_rows(lambda n: own.at[0, y, x, rq(k, n, 16), columns(g)], lambda n: lg.at[e, r16(n)], Q_PART)
+
+    def op_z0(e):
+        g, k = e // 4, e % 4
+
+        def arrive():
+            Z0(e, g, k).wait_recv()
+            add_rows(lambda n: own.at[0, y, x, rq(k, n, 16), columns(g)], lambda n: lz.at[e, r16(n)], Q_PART)
+
+        when(z < 3, arrive)
+        when(z > 0, lambda: Z0(e, g, k).start())
+
+    def first_in(q):
+        return pltpu.make_async_copy(first.at[pl.ds(pl.multiple_of(q * 256, 256), 256)], fchunk, f_sem)
+
+    def grad_out(q):
+        return pltpu.make_async_copy(fchunk, grad_in.at[pl.ds(pl.multiple_of(q * 256, 256), 256)], g_sem)
+
+    def weight_in(n):
+        target = (p_all.at[pl.ds(0, D), pl.ds(0, D)], ds_all.at[pl.ds(0, D), pl.ds(0, D)], wv)[n]
+        return pltpu.make_async_copy(w.at[0, n // 2, n % 2], target, w_sem.at[n])
+
+    def op_gin(q):
+        def weights():
+            for n in range(3):
+                weight_in(n).wait()
+
+        when(q == 0, weights)
+        when(q > 0, lambda: grad_out(q - 1).wait())
+        first_in(q).start()
+        cols = pl.ds(pl.multiple_of(q * 256, 256), 256)
+        d = pl.ds(0, D)
+        acc = dot(p_all[d, d], qkv[0, :, cols]) + dot(ds_all[d, d], qkv[1, :, cols])
+        acc = (acc + dot(wv[...], qkv[2, :, cols])).T
+        first_in(q).wait()
+        fchunk[...] += acc
+        grad_out(q).start()
+
+    def op_other(e):
+        def norm_y():
+            def go():
+                NX.wait_recv()
+                nacc[...] += nx[...]
+                when(y == 0, lambda: NY.start())
+
+            when(x == 1, go)
+
+        def norm_z():
+            def go():
+                NY.wait_recv()
+                nacc[...] += ny[...]
+
+                def more():
+                    NZ.wait_recv()
+                    nacc[...] += nz[...]
+
+                when(z > 0, more)
+                when(z < 3, lambda: NZ.start())
+                when(z == 3, lambda: NC.start())
+
+            when(line, go)
+
+        def load():
+            for n in range(3):
+                weight_in(n).start()
+
+        when(e == 0, norm_y)
+        when(e == 1, norm_z)
+        when(e == 2, load)
+
+    run_plan(z, BACK_PLAN, [op_sum, op_c3, op_b3, op_c2, op_bz, op_cz, op_b1, op_head, op_dw, op_sum0, op_f0,
+                            op_g0, op_z0, op_gin, op_other])
+
+    half = pl.ds(pl.multiple_of(base, 16), HALF)
+    res(half)[...] = own[z, y, x].astype(f32)
+    share = remote(res(half), res(half), sib, share_s, share_r)
+    share.start()
+
+    @pl.loop(0, 9)
+    def _(e):
+        t, s = split(e)
+        C3(t, s, e).wait_send()
+        B3(t, s, e).wait_send()
+        C2(t, s, e).wait_send()
+
+        def went_up():
+            BU(t, s, e).wait_send()
+            CU(t, s, e).wait_send()
+
+        def went_down():
+            BD(t, s, e).wait_send()
+            CD(t, s, e).wait_send()
+
+        when(t > z, went_up)
+        when(t < z, went_down)
+        when(t == z, lambda: B1(s).wait_send())
+
+    @pl.loop(0, 8)
+    def _(e):
+        g, k = e // 4, e % 4
+        stage_copy(e).wait_send()
+
+        def gone(odd):
+            F0(e, g, k, odd).wait_send()
+            G0(e, g, k, odd).wait_send()
+
+        by_parity(k, gone)
+        when(z > 0, lambda: Z0(e, g, k).wait_send())
+
+    for t in (1, 2, 3):
+        sib_in(t).wait_send()
+    when(x == 0, lambda: NX.wait_send())
+    when(jnp.logical_and(x == 1, y == 0), lambda: NY.wait_send())
+    when(jnp.logical_and(line, z < 3), lambda: NZ.wait_send())
+
+    def norm_last():
+        NC.wait_recv()
+        NC.wait_send()
+        nacc[...] += nc[...]
+
+    when(last_line, norm_last)
+    grad_out(3).wait()
+    share.wait_send()
+    oth = pl.ds(pl.multiple_of((1 - c) * HALF, 16), HALF)
+    remote(res(oth), res(oth), sib, share_s, share_r).wait_recv()
+
+    spread = jnp.logical_or(z == 1, z == 2)
+    for n in range(6):
+        cols = pl.ds(n * 128, 128)
+
+        def plain():
+            flat[pl.ds(n, D, stride=6)] = dist[pl.ds(0, D), cols]
+
+        def swapped():
+            for j in range(4):
+                flat[pl.ds(j * 6 + n, D // 4, stride=24)] = dist[pl.ds(j * (D // 4), D // 4), cols]
+
+        when(jnp.logical_not(spread), plain)
+        when(spread, swapped)
+        when(i == 15, lambda: flat.__setitem__((pl.ds(6 * D + n, 4, stride=6), slice(None)), nacc[:, cols]))
+
+    head_rows, after = pl.ds(0, 24), pl.ds(6 * D, 24)
+    give = remote(flat.at[head_rows], flat.at[after], (c, i - 1), aft_s, aft_r)
+    when(i > 0, lambda: give.start())
+    when(i < 15, lambda: give.wait_recv())
+    leave = pltpu.make_async_copy(flat, flat_out, o_sem)
+    leave.start()
+    when(i > 0, lambda: give.wait_send())
+    leave.wait()
+
+
+def enter_more(i, c, z, y, x):
+    barrier = pltpu.get_barrier_semaphore()
+    xp, yp, sib, up, down = partners(i, c, z, y, x)
+
+    def signal(peer):
+        pl.semaphore_signal(barrier, inc=1, device_id=peer, device_id_type=MESH)
+
+    for peer in (xp, yp, sib):
+        signal(peer)
+    when(z > 0, lambda: signal(down))
+    when(z < 3, lambda: signal(up))
+    when(jnp.logical_and(x == 0, i > 0), lambda: signal((c, i - 1)))
+    when(jnp.logical_and(x == 1, i < 15), lambda: signal((c, i + 1)))
+    more = 1 - jnp.where(i == 0, 1, 0) - jnp.where(i == 15, 1, 0)
+    pl.semaphore_wait(barrier, 3 + jnp.minimum(z, 1) + jnp.minimum(3 - z, 1) + more)
+
+
+def reduce_back(wide, down, w, qkv, dO, mixb, lse, tokT, gbranch, first, norms, seg):
+    Q = pltpu.SemaphoreType.DMA
+    V = lambda *s: pltpu.VMEM(s, bf16)
+    F = lambda *s: pltpu.VMEM(s, f32)
+    A = pl.BlockSpec(memory_space=pl.ANY)
+    return pl.pallas_call(
+        reduce_back_kernel,
+        in_specs=[A, A, A, A, VM, VM, VM, VM, VM, A, VM, VM, VM],
+        out_specs=[A, A],
+        out_shape=[jax.ShapeDtypeStruct((LEN, D), f32), jax.ShapeDtypeStruct((6 * D + 24, 128), f32)],
+        scratch_shapes=[
+            V(4, 2, 2, HALF, D), V(4, 2, 2, HALF, D), V(9, 2, C_PART, D), V(9, C_PART, D), V(9, C_PART, D),
+            V(3, C_PART, D), V(9, 2, B_PART, D), V(9, 2, B_PART, D), V(3, 2, B_PART, D), V(3, B_PART, D),
+            V(8, 2, Q_PART, COLS), V(8, Q_PART, COLS), V(8, Q_PART, COLS), V(8, HALF, COLS),
+            F(LEN, LEN), V(LEN, LEN), V(LEN, LEN), V(D, D), V(LEN, HEAD), V(LEN, HEAD), V(3, D, LEN),
+            F(256, D), F(6 * D + 24, 128), F(4, D), F(4, D), F(4, D), F(4, D), F(4, D),
+            Q((4,)), Q, Q((3,)), Q, Q, Q, Q((4,)), Q((4,)), Q((8,)), Q((8,)),
+            *[Q((9,))] * 14, Q((3,)), Q((3,)), *[Q((8,))] * 6, Q((4,)), Q((4,)), Q, Q, Q, Q,
+        ],
+        compiler_params=pltpu.CompilerParams(
+            collective_id=2, has_side_effects=True, vmem_limit_bytes=62 << 20
+        ),
+        name="reduce_back",
+    )(wide, down, w, qkv, dO, mixb, lse, tokT, gbranch, first, norms, seg.reshape(LEN, 1), seg.reshape(1, LEN))
 
 SQUARE = D * D
 TAIL = 4 * D
@@ -760,9 +1126,8 @@
     return value.reshape(4, D // 4, 4, D).transpose(0, 2, 1, 3).reshape(2, 2, D, D)
 
 
-def swap_wide(block, index, inverse):
-    dims = (4, D // 4, D) if inverse else (D // 4, 4, D)
-    swapped = block.reshape(dims).transpose(1, 0, 2).reshape(D, D)
+def swap_wide(block, index):
+    swapped = block.reshape(D // 4, 4, D).transpose(1, 0, 2).reshape(D, D)
     wide = jnp.logical_and(index >= 4, index < 12)
     return jnp.where(wide, swapped, block)
 
@@ -778,7 +1143,7 @@
     block = lax.dynamic_slice(joined, (TAIL - TAIL // count * index,), (size,))
     if count == 16:
         padded = jnp.pad(last.reshape(4, D), ((0, 12), (0, 0)))
-        block = swap_wide(block.reshape(D, D), index, False)
+        block = swap_wide(block.reshape(D, D), index)
         blocks, tail, *attended = gather_attend(block, padded, tokens, segments)
         norms = tail[:4].astype(f32)
     else:
@@ -791,35 +1156,40 @@
     return blocks, norms, *attended
 
 
-def scatter_grads(square, wide, down, norm_grads):
+def back_and_scatter(blocks, segments, tokT, qkv, mixed, log_sum, grad_mixed, first_grad, branch_grad, norm_grads,
+                     down_grad, wide_grad):
     count = lax.axis_size("zero")
     index = lax.axis_index("zero")
     if count == 16:
-        block, tail = reduce_blocks(square, wide, down, norm_grads)
-        block = swap_wide(block, index, True)
+        input_grad, joined = reduce_back(
+            wide_grad, down_grad, blocks, qkv, grad_mixed, mixed, log_sum, tokT, branch_grad, first_grad,
+            norm_grads, segments,
+        )
+        joined = joined.reshape(-1)
     else:
-        natural = [from_wide(wide[k]).reshape(4 * D, D) for k in (0, 1)]
-        natural = jnp.concatenate([square.reshape(4 * D, D), *natural, down.reshape(4 * D, D)])
+        square, input_grad = attend_back(
+            blocks, segments, tokT, qkv, mixed, log_sum, grad_mixed, first_grad, branch_grad
+        )
+        natural = [from_wide(wide_grad[k]).reshape(4 * D, D) for k in (0, 1)]
+        natural = jnp.concatenate([square.reshape(4 * D, D), *natural, down_grad.reshape(4 * D, D)])
         block = lax.psum_scatter(natural, "zero", scatter_dimension=0, tiled=True)
         block = lax.psum(block.astype(f32), "dp")
         tail = lax.psum(norm_grads, ("dp", "zero"))
-    flat = block.reshape(-1)
-    after = lax.ppermute(flat[:TAIL], "zero", [(k + 1, k) for k in range(count - 1)])
-    joined = jnp.concatenate([flat, jnp.where(index == count - 1, tail.reshape(-1), after)])
-    shard = flat.shape[0] + TAIL // count
-    return lax.dynamic_slice(joined, (TAIL // count * index,), (shard,))
+        flat = block.reshape(-1)
+        after = lax.ppermute(flat[:TAIL], "zero", [(k + 1, k) for k in range(count - 1)])
+        joined = jnp.concatenate([flat, jnp.where(index == count - 1, tail.reshape(-1), after)])
+    shard = 16 * SQUARE // count + TAIL // count
+    return input_grad, lax.dynamic_slice(joined, (TAIL // count * index,), (shard,))
 
 
 def local(tokens, segments, cotangent, master, moment_one, moment_two):
-    blocks, norms, kept, mixed, log_sum = gather_and_attend(master, tokens, segments)
+    blocks, norms, tokT, qkv, mixed, log_sum = gather_and_attend(master, tokens, segments)
     output, first_grad, grad_mixed, branch_grad, norm_grads, down_grad, wide_grad = feed(
         tokens, cotangent, mixed, blocks, norms
     )
-    square_grad, input_grad = attend_back(
-        blocks, segments, *kept, log_sum, grad_mixed, first_grad, branch_grad
-    )
-    grad_shard = scatter_grads(
-        square_grad, wide_grad.reshape(2, 2, 2, D, D), down_grad.reshape(2, 2, D, D), norm_grads
+    input_grad, grad_shard = back_and_scatter(
+        blocks, segments, tokT, qkv, mixed, log_sum, grad_mixed, first_grad, branch_grad, norm_grads,
+        down_grad.reshape(2, 2, D, D), wide_grad.reshape(2, 2, 2, D, D),
     )
     grad_shard = grad_shard / (lax.axis_size("zero") * lax.axis_size("dp"))
     first = beta_one * moment_one + (1.0 - beta_one) * grad_shard

time: 432 us -> 365 us (0.84); the launches traced: 432 us -> 359 us
  Pallas kernels: 396 us -> 332 us
  local copies, waits for them, and re-layouts: 10 us -> 5.08 us
    pallas_call x2 -> x1, Pallas kernels: 197 us -> 135 us  [reduce_back(): pl.pallas_call(reduce_back_kernel, in_specs=[A, A, A, A, VM, VM, VM, VM,...]
    reshape x5 -> x1, local copies, waits for them, and re-layouts: 7.69 us -> 1.07 us  [gather_and_attend(): block = swap_wide(block.reshape(D, D), index)]
  transfers between devices with their start and end apart: 2 -> 1, of which waited for: 2 -> 1; matrix products, arithmetic and copies ran while one was open for 1% -> 0% of each run, Pallas kernels for 0% -> 0%
where the time goes in v5:
time: 365 us; the launch traced here: 359 us
  Pallas kernels  332 us (91%)
  other arithmetic  15.5 us (4%)
  local copies, waits for them, and re-layouts  5.08 us (1%)
    pallas_call x1, Pallas kernels, reduce_back(): pl.pallas_call(reduce_back_kernel, in_specs=[A, A, A, A, VM, VM, VM, VM,...  135 us
    pallas_call x1, Pallas kernels, gather_attend(): pl.pallas_call(gather_attend_kernel, in_specs=[any_space, VM, VM, VM, VM]...  121 us
    pallas_call x1, Pallas kernels, feed(): pl.pallas_call(feed_kernel, grid=(n + 12,), in_specs=[pl.BlockSpec((TB, D...  76.1 us
    convert_element_type x1, other arithmetic, local(): master_new.astype(jnp.bfloat16)  10.2 us
  transfers between devices with their start and end apart: 1, of which 1 were waited for; matrix products, arithmetic and copies ran while one was open for 0% of the time, Pallas kernels for 0%

profile of v5, /device:TPU:8, one launch (start us, length us, event | category | flops | bytes accessed | tf_op | source)
XLA Modules:
  0.0 359.1 jit_solution(9272152785016675842)
XLA Ops:
  0.6 0.0 copy-start.1
  0.6 1.8 convert_element_type.11
  2.4 0.1 slice.8
  2.5 3.4 collective-permute-start
  5.9 0.0 copy-done.1
  5.9 1.0 copy.14.seg_col
  7.0 0.6 pad.4.last
  7.6 2.2 collective-permute-done
  9.8 1.0 fusion
  10.8 0.5 reshape_reshape.3
  11.3 1.1 reshape.44
  12.4 0.1 copy.13
  12.5 1.2 bitcast_select_fusion.blk
  13.7 120.8 %gather_attend.1 = (bf16[4,2,2,768,768]{4,3,2,1,0:T(8,128)(2,1)}, bf16[16,768]{1,0:T(8,128)(2,1)}, bf16[768,1024]{1,0:T(8,128)(2,1)}, bf16[3,768,1024]{2,1,0:T(8...) custom-call(bf16[768,768]{1,0:T(8,128)(2,1)} %bitcast_select_fusion.blk, bf16[16,768]{1,0:T(8,128)(2,1)} %pad.4.last, ...), custom_call_target="tpu_custom_call" | custom-call | tf_op jit(solution)/shard_map/gather_attend/pallas_call | solution.py:566
  134.5 1.3 slice_convert_fusion.norms
  135.8 76.1 %feed.1 = (bf16[1024,768]{1,0:T(8,128)(2,1)}, f32[1024,768]{1,0:T(8,128)}, bf16[768,1024]{1,0:T(8,128)(2,1)}, bf16[1024,768]{1,0:T(8,128)(2,1)}, f32[4,768]{1,0:...) custom-call(bf16[1024,768]{1,0:T(8,128)(2,1)} %tokens.3, bf16[1024,768]{1,0:T(8,128)(2,1)} %cot.1, ...), custom_call_target="tpu_custom_call" | custom-call | tf_op jit(solution)/shard_map/feed/pallas_call | solution.py:204
  211.9 135.3 %reduce_back.1 = (f32[1024,768]{1,0:T(8,128)}, f32[4632,128]{1,0:T(8,128)}) custom-call(bf16[2,2,2,768,768]{4,3,2,1,0:T(8,128)(2,1)} %bitcast.13, bf16[2,2,768,768]{3,2,1,0:T(8,128)(2,1)} %bitcast.14, bf16[4,2,2,768,768]{4,3,2,1,0:T(8,128)(2,1)} %get-tuple-element.23.w, bf16[3,768,1024]{2,1,0:T(8,128)(2,1)} %get-tuple-element.28.qkv_in, ...), custom_call_target="tpu_custom_call" | custom-call | tf_op jit(solution)/shard_map/reduce_back/pallas_call | solution.py:1097
  347.2 0.0 copy-start
  347.2 10.2 %fusion.1 = (bf16[590016]{0:T(1024)(128)(2,1)}, f32[590016]{0:T(1024)}, f32[590016]{0:T(1024)}, f32[590016]{0:T(1024)}, f32[590016]{0:T(1024)}) fusion(f32[590016]{0:T(1024)} %param.9, f32[592896]{0:T(1024)} %bitcast.16, s32[]{:T(128)S(6)} %select_n.17, f32[590016]{0:T(1024)} %param.11, f32[590016]{0:T(1024)} %param.10), kind=kLoop, calls=%fused_computation.9 | loop fusion | flops 10030272 | bytes 20060548 | tf_op jit(solution)/shard_map/convert_element_type | solution.py:1206
  357.4 0.0 copy-done
  357.4 1.7 copy.17
  (1 shorter events, 0.0 us)
Async XLA Ops:
  0.6 5.3 %copy-start.1 = (s32[1024]{0:T(1024)S(1)}, s32[1024]{0:T(1024)}, u32[]{:S(2)}) copy-start(s32[1024]{0:T(1024)} %param.7) | copy-start | bytes 12292
  2.5 7.3 %collective-permute-start = (bf16[3072]{0:T(1024)(128)(2,1)S(1)}, bf16[3072]{0:T(1024)(128)(2,1)S(1)}, u32[]{:S(2)}, u32[]{:S(2)}) collective-permute-start(bf16[3072]{0:T(1024)(128)(2,1)S(1)} %slice.8), channel_id=1, source_target_pairs={{0,1},{1,2},{2,3},{3,4},{4,5},{5,6},{6,7},{7,8},{8,9},{9,10},{10,1... | collective-permute-start | bytes 18440 | tf_op jit(solution)/shard_map/ppermute | solution.py:1141
  347.2 10.2 %copy-start = (f32[1024,768]{1,0:T(8,128)S(1)}, f32[1024,768]{1,0:T(8,128)}, u32[]{:S(2)}) copy-start(f32[1024,768]{1,0:T(8,128)} %get-tuple-element.50) | copy-start | bytes 9437188

commit v6 on v5

--- a/solution.py
+++ b/solution.py
@@ -215,8 +215,8 @@
 MESH = pl.DeviceIdType.MESH
 ALL = slice(None)
 HALF = D // 2
-B_ROWS, C_ROWS = 144, 240
-CHUNK = 96
+B_PART, C_PART = 48, 80
+P_PART = 48
 
 
 def place():
@@ -229,340 +229,356 @@
     return (c, i + 1 - 2 * x), (c, i + 2 - 4 * y), (1 - c, i), (c, i + 4), (c, i - 4)
 
 
-def enter(i, c, z, y, x):
-    barrier = pltpu.get_barrier_semaphore()
-    xp, yp, sib, up, down = partners(i, c, z, y, x)
-    for peer in (xp, yp, sib):
-        pl.semaphore_signal(barrier, inc=1, device_id=peer, device_id_type=MESH)
-
-    @pl.when(z > 0)
-    def _():
-        pl.semaphore_signal(barrier, inc=1, device_id=down, device_id_type=MESH)
-
-    @pl.when(z < 3)
-    def _():
-        pl.semaphore_signal(barrier, inc=1, device_id=up, device_id_type=MESH)
-
-    pl.semaphore_wait(barrier, 3 + jnp.minimum(z, 1) + jnp.minimum(3 - z, 1))
-
-
-class Lane:
-    def __init__(self, peer, sends, recvs):
-        self.peer, self.sends, self.recvs = peer, sends, recvs
-
-    def copy(self, ref, n):
-        return pltpu.make_async_remote_copy(
-            src_ref=ref, dst_ref=ref, send_sem=self.sends.at[n], recv_sem=self.recvs.at[n],
-            device_id=self.peer, device_id_type=MESH,
-        )
-
-    def go(self, ref, n):
-        self.copy(ref, n).start()
-
-    def got(self, ref, n):
-        self.copy(ref, n).wait_recv()
-
-    def gone(self, ref, n):
-        self.copy(ref, n).wait_send()
-
-
 def when(cond, fn):
     @pl.when(cond)
     def _():
         fn()
 
 
-def gather_steps(out, tail, result, last, own_sem, out_sem, blk, sems):
+def enter(i, c, z, y, x):
+    barrier = pltpu.get_barrier_semaphore()
+    xp, yp, sib, up, down = partners(i, c, z, y, x)
+
+    def signal(peer):
+        pl.semaphore_signal(barrier, inc=1, device_id=peer, device_id_type=MESH)
+
+    for peer in (xp, yp, sib):
+        signal(peer)
+    when(z > 0, lambda: signal(down))
+    when(z < 3, lambda: signal(up))
+    pl.semaphore_wait(barrier, 3 + jnp.minimum(z, 1) + jnp.minimum(3 - z, 1))
+
+
+def pick(z, values):
+    out = jnp.int32(values[3])
+    for k in (2, 1, 0):
+        out = jnp.where(z == k, jnp.int32(values[k]), out)
+    return out
+
+
+def run_plan(z, words, ops):
+    count = len(words[0])
+    held = [pick(z, [words[k][n] for k in range(4)]) for n in range(count)]
+
+    @pl.loop(0, count)
+    def _(n):
+        word = held[0]
+        for k in range(1, count):
+            word = jnp.where(n == k, held[k], word)
+
+        @pl.loop(0, 3)
+        def _(m):
+            code = jnp.where(m == 0, word, jnp.where(m == 1, word // 256, word // 65536)) % 256
+            kind, e = code // 16, code % 16
+            for k, op in enumerate(ops):
+                when(kind == k, lambda op=op: op(e))
+
+
+def gather_attend_kernel(blk, last, tokens, seg_col, seg_row, result, tail, tokT, qkv, mixb, lse,
+                         held, dist, kn, own_sem, out_sem, pzs, pzr, pfs, pfr, pgs, pgr, p_s, p_r,
+                         b1s, b1r, c1u, c1d, c1r, b2u, b2d, b2r, c2s, c2r, b3s, b3r, c3s, c3r, ss, sr, ts, tr):
     i, c, z, y, x = place()
     xp, yp, sib, up, down = partners(i, c, z, y, x)
-    (sp0z, rp0z, sp0f, rp0f, sp0g, rp0g, ssib0, rsib0, sx, rx, sy, ry, sup, sdown, rz, ssib, rsib,
-     st, rt) = sems
-    lane0z = Lane(up, sp0z, rp0z)
     half = c * HALF
     other = (1 - c) * HALF
-
-    def rows(base, start, size):
-        return pl.ds(pl.multiple_of(base + start, 16), size)
-
-    def p0(k, kind, base, mine):
-        r = rows(base, k * CHUNK, CHUNK)
-        if kind == "z":
-            return out.at[0, y, x, r]
-        if k % 2 == 0:
-            if kind == "f":
-                return out.at[0, y, x if mine else 1 - x, r]
-            return out.at[0, y if mine else 1 - y, ALL, r]
-        if kind == "f":
-            return out.at[0, y if mine else 1 - y, x, r]
-        return out.at[0, ALL, x if mine else 1 - x, r]
-
-    def first(k):
-        return Lane(xp if k % 2 == 0 else yp, sp0f, rp0f)
-
-    def second(k):
-        return Lane(yp if k % 2 == 0 else xp, sp0g, rp0g)
-
-    lane0s = Lane(sib, ssib0, rsib0)
-    lx, ly, ls = Lane(xp, sx, rx), Lane(yp, sy, ry), Lane(sib, ssib, rsib)
-    lup, ldown = Lane(up, sup, rz), Lane(down, sdown, rz)
-
-    def b1(yy, base=half):
-        return out.at[z, yy, x, rows(base, 0, B_ROWS)]
-
-    def b2(zs, xx, base=half):
-        return out.at[zs, ALL, xx, rows(base, 0, B_ROWS)]
-
-    def c1(zs, base=half):
-        return out.at[zs, y, x, rows(base, B_ROWS, C_ROWS)]
-
-    def c2(zs, xx, base=half):
-        return out.at[zs, y, xx, rows(base, B_ROWS, C_ROWS)]
-
-    def c3(zs, yy, base=half):
-        return out.at[zs, yy, ALL, rows(base, B_ROWS, C_ROWS)]
-
-    B, C = 0, 4
-    SB1, SB2, SB3, SC1, SC2, SC3 = 0, 1, 5, 9, 13, 17
-
-    def z_up(ref, n):
-        when(z < 3, lambda: lup.go(ref, n))
-
-    def z_down(ref, n):
-        when(z > 0, lambda: ldown.go(ref, n))
-
-    def z_on(ref, zs, base):
-        when(jnp.logical_and(zs < z, z < 3), lambda: lup.go(ref, base + zs))
-        when(jnp.logical_and(zs > z, z > 0), lambda: ldown.go(ref, base + zs))
-
-    def own(fn):
-        when(z > 0, fn)
-
-    def both(s, fn):
-        when(z - s >= 1, lambda: fn(z - s))
-        when(z + s <= 3, lambda: fn(z + s))
+    local = pltpu.make_async_copy(blk, held.at[z, y, x], own_sem)
+    local.start()
+    enter(i, c, z, y, x)
+
+    def remote(ref, peer, s, r):
+        return pltpu.make_async_remote_copy(
+            src_ref=ref, dst_ref=ref, send_sem=s, recv_sem=r, device_id=peer, device_id_type=MESH
+        )
+
+    def by_parity(k, fn):
+        when(k % 2 == 0, lambda: fn(False))
+        when(k % 2 == 1, lambda: fn(True))
+
+    def rp(k, base):
+        return pl.ds(pl.multiple_of(base + k * P_PART, 16), P_PART)
+
+    def z_ref(k, base=half):
+        return held.at[0, y, x, rp(k, base)]
+
+    def f_ref(k, odd, base=half):
+        if odd:
+            return held.at[0, 1 - y, x, rp(k, base)]
+        return held.at[0, y, 1 - x, rp(k, base)]
+
+    def g_ref(k, odd, mine, base=half):
+        if odd:
+            return held.at[0, ALL, x if mine else 1 - x, rp(k, base)]
+        return held.at[0, y if mine else 1 - y, ALL, rp(k, base)]
+
+    def PZ(k):
+        return remote(z_ref(k), up, pzs.at[k], pzr.at[k])
+
+    def PF(k, odd):
+        return remote(z_ref(k), yp if odd else xp, pfs.at[k], pfr.at[k])
+
+    def PG(k, odd):
+        return remote(g_ref(k, odd, True), xp if odd else yp, pgs.at[k], pgr.at[k])
+
+    def PS(ref, n):
+        return remote(ref, sib, p_s.at[n], p_r.at[n])
+
+    def op_p0z(k):
+        def arrive():
+            PZ(k).wait_recv()
+            PS(z_ref(k), k).start()
+
+        when(z > 0, arrive)
+        when(z < 3, lambda: PZ(k).start())
+        by_parity(k, lambda odd: PF(k, odd).start())
+
+    def op_p0f(k):
+        def turn(odd):
+            PF(k, odd).wait_recv()
+            PG(k, odd).start()
+            PS(f_ref(k, odd), 8 + k).start()
+
+        by_parity(k, turn)
+
+    def op_p0g(k):
+        def turn(odd):
+            PG(k, odd).wait_recv()
+            PS(g_ref(k, odd, False), 16 + k).start()
+
+        by_parity(k, turn)
+
+    split = lambda e: (e // 3 + 1, e % 3)
+
+    def rb(s, base):
+        return pl.ds(pl.multiple_of(base + s * B_PART, 16), B_PART)
+
+    def rc(s, base):
+        return pl.ds(pl.multiple_of(base + 3 * B_PART + s * C_PART, 16), C_PART)
+
+    def b1_ref(s, yy, base=half):
+        return held.at[z, yy, x, rb(s, base)]
+
+    def b2_ref(t, s, xx, base=half):
+        return held.at[t, ALL, xx, rb(s, base)]
+
+    def c1_ref(t, s, base=half):
+        return held.at[t, y, x, rc(s, base)]
+
+    def c2_ref(t, s, xx, base=half):
+        return held.at[t, y, xx, rc(s, base)]
+
+    def c3_ref(t, s, yy, base=half):
+        return held.at[t, yy, ALL, rc(s, base)]
+
+    B1 = lambda s: remote(b1_ref(s, y), yp, b1s.at[s], b1r.at[s])
+    C1U = lambda t, s, e: remote(c1_ref(t, s), up, c1u.at[e], c1r.at[e])
+    C1D = lambda t, s, e: remote(c1_ref(t, s), down, c1d.at[e], c1r.at[e])
+    B2U = lambda t, s, e: remote(b2_ref(t, s, x), up, b2u.at[e], b2r.at[e])
+    B2D = lambda t, s, e: remote(b2_ref(t, s, x), down, b2d.at[e], b2r.at[e])
+    C2 = lambda t, s, e: remote(c2_ref(t, s, x), xp, c2s.at[e], c2r.at[e])
+    B3 = lambda t, s, e: remote(b2_ref(t, s, x), xp, b3s.at[e], b3r.at[e])
+    C3 = lambda t, s, e: remote(c3_ref(t, s, y), yp, c3s.at[e], c3r.at[e])
+    S = lambda ref, n: remote(ref, sib, ss.at[n], sr.at[n])
+
+    def op_own(e):
+        t, s = split(e)
+        B1(s).start()
+        C1D(t, s, e).start()
+
+    def op_ownup(e):
+        t, s = split(e)
+
+        def go():
+            C1U(t, s, e).start()
+            B2U(t, s, e).start()
+
+        when(z < 3, go)
+
+    def op_b1(e):
+        t, s = split(e)
+        B1(s).wait_recv()
+        B2D(t, s, e).start()
+        S(b1_ref(s, 1 - y), 45 + s).start()
+
+    def op_cx(e):
+        t, s = split(e)
+        C2(t, s, e).start()
+
+    def op_bx(e):
+        t, s = split(e)
+        B3(t, s, e).start()
+
+    def op_c1(e):
+        t, s = split(e)
+        C1U(t, s, e).wait_recv()
+        when(jnp.logical_and(t < z, z < 3), lambda: C1U(t, s, e).start())
+        when(jnp.logical_and(t > z, z > 0), lambda: C1D(t, s, e).start())
+        S(c1_ref(t, s), e).start()
+
+    def op_b2(e):
+        t, s = split(e)
+        B2U(t, s, e).wait_recv()
+        when(jnp.logical_and(t < z, z < 3), lambda: B2U(t, s, e).start())
+        when(jnp.logical_and(t > z, z > 0), lambda: B2D(t, s, e).start())
+        S(b2_ref(t, s, x), 9 + e).start()
+
+    def op_c2(e):
+        t, s = split(e)
+        C2(t, s, e).wait_recv()
+        C3(t, s, e).start()
+        S(c2_ref(t, s, 1 - x), 18 + e).start()
+
+    def op_b3(e):
+        t, s = split(e)
+        B3(t, s, e).wait_recv()
+        S(b2_ref(t, s, 1 - x), 27 + e).start()
+
+    def op_c3(e):
+        t, s = split(e)
+        C3(t, s, e).wait_recv()
+        S(c3_ref(t, s, 1 - y), 36 + e).start()
+
+    def op_proj(n):
+        def arrive():
+            @pl.loop(0, 8)
+            def _(k):
+                def got(odd):
+                    PS(f_ref(k, odd, other), 8 + k).wait_recv()
+                    PS(g_ref(k, odd, False, other), 16 + k).wait_recv()
+
+                by_parity(k, got)
+                when(z > 0, lambda: PS(z_ref(k, other), k).wait_recv())
+
+        when(n == 0, arrive)
+
+        @pl.loop(0, 3)
+        def _(t):
+            cols = pl.ds(pl.multiple_of(t * 256, 256), 256)
+            qkv[n, cols] = dot_tn(held[0, n // 2, n % 2, :, cols], tokT[...]).astype(bf16)
+
+    def op_head(h):
+        attend_head(h, dist, kn, qkv, mixb, lse)
 
     line = jnp.logical_and(y == 1, x == 1)
     source = jnp.logical_and(line, z == 3)
-    tz, ty, tx = Lane(down, st, rt), Lane(yp, st, rt), Lane(xp, st, rt)
-
-    def tail_z(at_source):
-        def send():
-            if not at_source:
-                tz.copy(tail, 0).wait_recv()
-            when(z > 0, lambda: tail_copy(down, 0).start())
-            tail_copy(yp, 1).start()
-
-        when(jnp.logical_and(line, source if at_source else jnp.logical_not(source)), send)
-
-    def tail_copy(peer, n):
-        return pltpu.make_async_remote_copy(
-            src_ref=tail, dst_ref=tail, send_sem=st.at[n], recv_sem=rt.at[0],
-            device_id=peer, device_id_type=MESH,
-        )
-
-    def tail_x():
-        def send():
-            when(y == 0, lambda: tail_copy(yp, 1).wait_recv())
-            tail_copy(xp, 2).start()
-
-        when(x == 1, send)
-
-    def tail_end():
-        when(x == 0, lambda: tail_copy(xp, 2).wait_recv())
-        when(x == 1, lambda: tail_copy(xp, 2).wait_send())
-
-        def sent():
-            tail_copy(yp, 1).wait_send()
-            when(z > 0, lambda: tail_copy(down, 0).wait_send())
-
-        when(line, sent)
-
-    def begin():
-        local = pltpu.make_async_copy(blk, out.at[z, y, x], own_sem)
-        local.start()
-        when(source, lambda: tail.__setitem__(Ellipsis, last[...]))
-        local.wait()
-        tail_z(True)
-
-        def at_zero():
-            for k in range(4):
-                lane0z.go(p0(k, "z", half, True), k)
-            for k in range(4):
-                first(k).go(p0(k, "f", half, True), k)
-
-        when(z == 0, at_zero)
-
-        def others():
-            ly.go(b1(y), 4)
-            lx.go(c2(z, x), C + z)
-            ldown.go(c1(z), C + z)
-
-        own(others)
-
-        def pass_on(k):
-            def there():
-                lane0z.got(p0(k, "z", half, True), k)
-                when(z < 3, lambda: lane0z.go(p0(k, "z", half, True), k))
-                lane0s.go(p0(k, "z", half, True), k)
-                first(k).go(p0(k, "f", half, True), k)
-
-            own(there)
-
-        def turn(k):
-            first(k).got(p0(k, "f", half, False), k)
-            second(k).go(p0(k, "g", half, True), k)
-            lane0s.go(p0(k, "f", half, False), 4 + k)
-
-        pass_on(0)
-        pass_on(1)
-        turn(0)
-        pass_on(2)
-        turn(1)
-        pass_on(3)
-        turn(2)
-
-        def own_b():
-            ly.got(b1(1 - y), 4)
-            ls.go(b1(1 - y), SB1)
-            z_up(c1(z), C + z)
-            z_down(b2(z, x), B + z)
-            z_up(b2(z, x), B + z)
-            lx.go(b2(z, x), B + z)
-
-        turn(3)
-        own(own_b)
-        for k in range(4):
-            second(k).got(p0(k, "g", half, False), k)
-            lane0s.go(p0(k, "g", half, False), 8 + k)
-        for k in range(4):
-            own(lambda k=k: lane0s.got(p0(k, "z", other, True), k))
-            lane0s.got(p0(k, "f", other, False), 4 + k)
-            lane0s.got(p0(k, "g", other, False), 8 + k)
-
-    def early_c(zs):
-        lup.got(c1(zs), C + zs)
-        z_on(c1(zs), zs, C)
-        lx.go(c2(zs, x), C + zs)
-        ls.go(c1(zs), SC1 + zs)
-
-    def early_b(zs):
-        lup.got(b2(zs, x), B + zs)
-        z_on(b2(zs, x), zs, B)
-        lx.go(b2(zs, x), B + zs)
-        ls.go(b2(zs, x), SB2 + zs)
-
-    def late(zs):
-        lx.got(c2(zs, 1 - x), C + zs)
-        ly.go(c3(zs, y), zs)
-        ls.go(c2(zs, 1 - x), SC2 + zs)
-
-    def fin(zs):
-        lx.got(b2(zs, 1 - x), B + zs)
-        ls.go(b2(zs, 1 - x), SB3 + zs)
-        ly.got(c3(zs, 1 - y), zs)
-        ls.go(c3(zs, 1 - y), SC3 + zs)
-
-    steps = [
-        lambda: (own(lambda: late(z)), both(1, early_c)),
-        lambda: (both(1, early_b), tail_z(False)),
-        lambda: (both(1, late), both(2, early_c)),
-        lambda: (both(2, early_b), tail_x()),
-        lambda: both(2, late),
-        lambda: (own(lambda: fin(z)), both(3, early_c)),
-        lambda: both(3, early_b),
-        lambda: (both(3, late), both(1, fin)),
-        lambda: both(2, fin),
-        lambda: both(3, fin),
-    ]
-
-    def leave(zs):
-        return pltpu.make_async_copy(out.at[zs], result.at[zs], out_sem.at[zs])
-
-    def sib_got(zs):
-        def own_items():
-            ls.got(b1(1 - y, other), SB1)
-
-        def their_items():
-            ls.got(c1(zs, other), SC1 + zs)
-            ls.got(b2(zs, x, other), SB2 + zs)
-
-        when(zs == z, own_items)
-        when(zs != z, their_items)
-        ls.got(c2(zs, 1 - x, other), SC2 + zs)
-        ls.got(b2(zs, 1 - x, other), SB3 + zs)
-        ls.got(c3(zs, 1 - y, other), SC3 + zs)
-
-    def end():
-        leave(0).start()
-        for zs in range(1, 4):
-            sib_got(zs)
-            leave(zs).start()
-        tail_end()
-        for k in range(4):
-            when(z < 3, lambda: lane0z.gone(p0(k, "z", half, True), k))
-            first(k).gone(p0(k, "f", half, True), k)
-            second(k).gone(p0(k, "g", half, True), k)
-            own(lambda: lane0s.gone(p0(k, "z", half, True), k))
-            lane0s.gone(p0(k, "f", half, False), 4 + k)
-            lane0s.gone(p0(k, "g", half, False), 8 + k)
-
-        def own_sent():
-            ly.gone(b1(y), 4)
-            ls.gone(b1(1 - y), SB1)
-
-        own(own_sent)
-        for zs in range(1, 4):
-            lx.gone(c2(zs, x), C + zs)
-            lx.gone(b2(zs, x), B + zs)
-            ly.gone(c3(zs, y), zs)
-            for ref, base in ((c1(zs), C), (b2(zs, x), B)):
-                when(jnp.logical_and(zs <= z, z < 3), lambda: lup.gone(ref, base + zs))
-                when(jnp.logical_and(zs >= z, z > 0), lambda: ldown.gone(ref, base + zs))
-
-            def theirs():
-                ls.gone(c1(zs), SC1 + zs)
-                ls.gone(b2(zs, x), SB2 + zs)
-
-            when(zs != z, theirs)
-            ls.gone(c2(zs, 1 - x), SC2 + zs)
-            ls.gone(b2(zs, 1 - x), SB3 + zs)
-            ls.gone(c3(zs, 1 - y), SC3 + zs)
-        for zs in range(4):
-            leave(zs).wait()
-
-    return begin, steps, end
-
-
-def gather_attend_kernel(blk, last, tokens, seg_col, seg_row, result, tail, tokT, qkv, mixb, lse,
-                          held, dist, kn, own_sem, out_sem, *sems):
-    i, c, z, y, x = place()
-    if True:
-        enter(i, c, z, y, x)
-    begin, steps, end = gather_steps(held, tail, result, last, own_sem, out_sem, blk, sems)
-    if True:
-        tokT[...] = tokens[...].astype(f32).T.astype(bf16)
-        fill_distance(dist, seg_col, seg_row)
-    if True:
-        begin()
-    if True:
-        project_all(held, tokT, qkv)
-
-    @pl.loop(0, HEADS)
-    def _(h):
-        if True:
-            for n, step in enumerate(steps):
-                when(h == n + 1, step)
-        if True:
-            attend_head(h, dist, kn, qkv, mixb, lse)
-
-    if True:
-        end()
+
+    def T(peer, n):
+        return remote(tail, peer, ts.at[n], tr.at[0])
+
+    def leave(t):
+        return pltpu.make_async_copy(held.at[t], result.at[t], out_sem.at[t])
+
+    def op_other(e):
+        def tail_z():
+            def go():
+                when(z < 3, lambda: T(down, 0).wait_recv())
+                when(z > 0, lambda: T(down, 0).start())
+                T(yp, 1).start()
+
+            when(line, go)
+
+        def tail_x():
+            def go():
+                when(y == 0, lambda: T(yp, 1).wait_recv())
+                T(xp, 2).start()
+
+            when(x == 1, go)
+
+        def out():
+            t = e - 2
+
+            def others():
+                @pl.loop(0, 3)
+                def _(s):
+                    n = (t - 1) * 3 + s
+
+                    def theirs():
+                        S(c1_ref(t, s, other), n).wait_recv()
+                        S(b2_ref(t, s, x, other), 9 + n).wait_recv()
+
+                    when(t != z, theirs)
+                    when(t == z, lambda: S(b1_ref(s, 1 - y, other), 45 + s).wait_recv())
+                    S(c2_ref(t, s, 1 - x, other), 18 + n).wait_recv()
+                    S(b2_ref(t, s, 1 - x, other), 27 + n).wait_recv()
+                    S(c3_ref(t, s, 1 - y, other), 36 + n).wait_recv()
+
+            when(t > 0, others)
+            leave(t).start()
+
+        def prepare():
+            tokT[...] = tokens[...].astype(f32).T.astype(bf16)
+            fill_distance(dist, seg_col, seg_row)
+
+        when(e == 0, tail_z)
+        when(e == 1, tail_x)
+        when(jnp.logical_and(e >= 2, e < 6), out)
+        when(e == 6, prepare)
+
+    when(source, lambda: tail.__setitem__(Ellipsis, last[...]))
+    local.wait()
+    run_plan(z, GATHER_PLAN, [op_p0z, op_p0f, op_p0g, op_own, op_ownup, op_b1, op_bx, op_c1, op_b2, op_c2, op_b3,
+                              op_c3, op_proj, op_head, op_other, op_cx])
+
+    when(x == 0, lambda: T(xp, 2).wait_recv())
+    when(x == 1, lambda: T(xp, 2).wait_send())
+
+    def tail_sent():
+        T(yp, 1).wait_send()
+        when(z > 0, lambda: T(down, 0).wait_send())
+
+    when(line, tail_sent)
+
+    @pl.loop(0, 8)
+    def _(k):
+        def gone(odd):
+            PF(k, odd).wait_send()
+            PG(k, odd).wait_send()
+            PS(f_ref(k, odd), 8 + k).wait_send()
+            PS(g_ref(k, odd, False), 16 + k).wait_send()
+
+        by_parity(k, gone)
+        when(z < 3, lambda: PZ(k).wait_send())
+        when(z > 0, lambda: PS(z_ref(k), k).wait_send())
+
+    @pl.loop(0, 9)
+    def _(e):
+        t, s = split(e)
+        C2(t, s, e).wait_send()
+        B3(t, s, e).wait_send()
+        C3(t, s, e).wait_send()
+
+        def ups():
+            C1U(t, s, e).wait_send()
+            B2U(t, s, e).wait_send()
+
+        def downs():
+            C1D(t, s, e).wait_send()
+            B2D(t, s, e).wait_send()
+
+        when(jnp.logical_and(t <= z, z < 3), ups)
+        when(jnp.logical_and(t >= z, z > 0), downs)
+
+        def mine():
+            B1(s).wait_send()
+            S(b1_ref(s, 1 - y), 45 + s).wait_send()
+
+        def theirs():
+            S(c1_ref(t, s), e).wait_send()
+            S(b2_ref(t, s, x), 9 + e).wait_send()
+
+        when(t == z, mine)
+        when(t != z, theirs)
+        S(c2_ref(t, s, 1 - x), 18 + e).wait_send()
+        S(b2_ref(t, s, 1 - x), 27 + e).wait_send()
+        S(c3_ref(t, s, 1 - y), 36 + e).wait_send()
+
+    for t in range(4):
+        leave(t).wait()
 
 
 def gather_attend(blk, last, tokens, seg):
     Q = pltpu.SemaphoreType.DMA
     any_space = pl.BlockSpec(memory_space=pl.ANY)
-    counts = [4] * 6 + [12, 12, 8, 8, 5, 5, 8, 8, 8, 21, 21, 3, 1]
+    counts = [8] * 6 + [24, 24, 3, 3] + [9] * 12 + [48, 48, 3, 1]
     return pl.pallas_call(
         gather_attend_kernel,
         in_specs=[any_space, VM, VM, VM, VM],
@@ -610,35 +626,36 @@
     ),
 )
 
-
-B_PART, C_PART, PARTS = 48, 80, 3
+GATHER_PLAN = (
+    (
+        131328, 328707, 15075078, 1184016, 1339411, 1470741, 15855639, 2224754, 6324256, 7545379,
+        2369011, 2580865, 12697638, 7635650, 7704976, 16118882, 14868960, 9602000, 13738083, 8688502,
+        11597412, 6653394, 10658225, 7894995, 16316308, 9823154, 6719188, 14001075, 6785159, 9872488,
+        10868404, 11900887, 10016996, 14263990, 14329783, 12114856, 15724517, 15724527,
+    ),
+    (
+        3289392, 5243110, 5308787, 7623170, 1114896, 1209604, 401413, 1253763, 4276231, 7750164,
+        8659478, 1516309, 6381808, 15885041, 6579187, 16184820, 2385285, 16217893, 2586662, 12763584,
+        6721670, 14803192, 10512263, 8966370, 13738344, 10662033, 13865682, 13939091, 9754019, 14918834,
+        9868758, 11851699, 9951397, 11901145, 14345382, 14395318, 12101815, 15724517,
+    ),
+    (
+        3486771, 7754726, 7820628, 7864576, 200706, 296465, 8848658, 1246752, 4392737, 8918084,
+        2233925, 1512816, 15761443, 6550368, 6681700, 16148213, 16316263, 2388328, 8515877, 12592934,
+        7520961, 6393986, 14742114, 14852321, 13734864, 13804464, 11773076, 13936083, 14005397, 14067350,
+        14985141, 10000343, 11065526, 12030425, 10658266, 12096219, 11710949, 15724515,
+    ),
+    (
+        3684150, 5695222, 5805655, 112128, 200706, 1180689, 401413, 467219, 1328966, 1450568,
+        1512819, 15958819, 6776419, 6879479, 2434164, 2524404, 12697639, 8746434, 6644883, 14803189,
+        13689507, 10940528, 7438545, 9957728, 13805491, 9986433, 13890162, 9724546, 13936823, 15055012,
+        9807317, 11833558, 11903191, 14193124, 9623969, 11655856, 11721634, 15724515,
+    ),
+)
+
+
 Q_PART = 96
 COLS = D // 2
-
-
-def pick(z, values):
-    out = jnp.int32(values[3])
-    for k in (2, 1, 0):
-        out = jnp.where(z == k, jnp.int32(values[k]), out)
-    return out
-
-
-def run_plan(z, words, ops):
-    count = len(words[0])
-    held = [pick(z, [words[k][n] for k in range(4)]) for n in range(count)]
-
-    @pl.loop(0, count)
-    def _(n):
-        word = held[0]
-        for k in range(1, count):
-            word = jnp.where(n == k, held[k], word)
-
-        @pl.loop(0, 3)
-        def _(m):
-            code = jnp.where(m == 0, word, jnp.where(m == 1, word // 256, word // 65536)) % 256
-            kind, e = code // 16, code % 16
-            for k, op in enumerate(ops):
-                when(kind == k, lambda op=op: op(e))
 
 
 def reduce_back_kernel(wide, down, w, qkv_in, dO, mixb, lse, tokT, gbranch, first, norm_in, seg_col, seg_row,

time: 365 us -> 342 us (0.937)
  Pallas kernels: 332 us -> 309 us
    pallas_call x1, Pallas kernels: 121 us -> 101 us  [gather_attend(): pl.pallas_call(gather_attend_kernel, in_specs=[any_space, VM, VM, VM, VM]...]
    pallas_call x1, Pallas kernels: 135 us -> 132 us  [reduce_back(): pl.pallas_call(reduce_back_kernel, in_specs=[A, A, A, A, VM, VM, VM, VM,...]
where the time goes in v6:
time: 342 us; the launch traced here: 336 us
  Pallas kernels  309 us (90%)
  other arithmetic  15.5 us (5%)
  local copies, waits for them, and re-layouts  5.08 us (1%)
    pallas_call x1, Pallas kernels, reduce_back(): pl.pallas_call(reduce_back_kernel, in_specs=[A, A, A, A, VM, VM, VM, VM,...  132 us
    pallas_call x1, Pallas kernels, gather_attend(): pl.pallas_call(gather_attend_kernel, in_specs=[any_space, VM, VM, VM, VM]...  101 us
    pallas_call x1, Pallas kernels, feed(): pl.pallas_call(feed_kernel, grid=(n + 12,), in_specs=[pl.BlockSpec((TB, D...  76.1 us
    convert_element_type x1, other arithmetic, local(): master_new.astype(jnp.bfloat16)  10.2 us
  transfers between devices with their start and end apart: 1, of which 1 were waited for; matrix products, arithmetic and copies ran while one was open for 0% of the time, Pallas kernels for 0%

profile of v6, /device:TPU:8, one launch (start us, length us, event | category | flops | bytes accessed | tf_op | source)
XLA Modules:
  0.0 336.0 jit_solution(11292507029760357827)
XLA Ops:
  0.6 0.0 copy-start.1
  0.6 1.8 convert_element_type.11
  2.4 0.1 slice.8
  2.5 3.4 %collective-permute-start = (bf16[3072]{0:T(1024)(128)(2,1)S(1)}, bf16[3072]{0:T(1024)(128)(2,1)S(1)}, u32[]{:S(2)}, u32[]{:S(2)}) collective-permute-start(bf16[3072]{0:T(1024)(128)(2,1)S(1)} %slice.8), channel_id=1, source_target_pairs={{0,1},{1,2},{2,3},{3,4},{4,5},{5,6},{6,7},{7,8},{8,9},{9,10},{10,1... | collective-permute-start | bytes 18440 | tf_op jit(solution)/shard_map/ppermute | solution.py:1158
  5.9 0.0 copy-done.1
  5.9 1.0 copy.14.seg_col
  7.0 0.6 pad.4.last
  7.6 2.2 collective-permute-done
  9.8 1.0 fusion
  10.8 0.5 reshape_reshape.3
  11.3 1.1 reshape.44
  12.4 0.1 copy.13
  12.5 1.2 bitcast_select_fusion.blk
  13.7 101.4 %gather_attend.1 = (bf16[4,2,2,768,768]{4,3,2,1,0:T(8,128)(2,1)}, bf16[16,768]{1,0:T(8,128)(2,1)}, bf16[768,1024]{1,0:T(8,128)(2,1)}, bf16[3,768,1024]{2,1,0:T(8...) custom-call(bf16[768,768]{1,0:T(8,128)(2,1)} %bitcast_select_fusion.blk, bf16[16,768]{1,0:T(8,128)(2,1)} %pad.4.last, ...), custom_call_target="tpu_custom_call" | custom-call | tf_op jit(solution)/shard_map/gather_attend/pallas_call | solution.py:582
  115.1 1.3 slice_convert_fusion.norms
  116.4 76.1 %feed.1 = (bf16[1024,768]{1,0:T(8,128)(2,1)}, f32[1024,768]{1,0:T(8,128)}, bf16[768,1024]{1,0:T(8,128)(2,1)}, bf16[1024,768]{1,0:T(8,128)(2,1)}, f32[4,768]{1,0:...) custom-call(bf16[1024,768]{1,0:T(8,128)(2,1)} %tokens.3, bf16[1024,768]{1,0:T(8,128)(2,1)} %cot.1, ...), custom_call_target="tpu_custom_call" | custom-call | tf_op jit(solution)/shard_map/feed/pallas_call | solution.py:204
  192.6 131.6 %reduce_back.1 = (f32[1024,768]{1,0:T(8,128)}, f32[4632,128]{1,0:T(8,128)}) custom-call(bf16[2,2,2,768,768]{4,3,2,1,0:T(8,128)(2,1)} %bitcast.13, bf16[2,2,768,768]{3,2,1,0:T(8,128)(2,1)} %bitcast.14, bf16[4,2,2,768,768]{4,3,2,1,0:T(8,128)(2,1)} %get-tuple-element.23.w, bf16[3,768,1024]{2,1,0:T(8,128)(2,1)} %get-tuple-element.28.qkv_in, ...), custom_call_target="tpu_custom_call" | custom-call | tf_op jit(solution)/shard_map/reduce_back/pallas_call | solution.py:1114
  324.1 0.0 copy-start
  324.1 10.2 %fusion.1 = (bf16[590016]{0:T(1024)(128)(2,1)}, f32[590016]{0:T(1024)}, f32[590016]{0:T(1024)}, f32[590016]{0:T(1024)}, f32[590016]{0:T(1024)}) fusion(f32[590016]{0:T(1024)} %param.9, f32[592896]{0:T(1024)} %bitcast.16, s32[]{:T(128)S(6)} %select_n.17, f32[590016]{0:T(1024)} %param.11, f32[590016]{0:T(1024)} %param.10), kind=kLoop, calls=%fused_computation.9 | loop fusion | flops 10030272 | bytes 20060548 | tf_op jit(solution)/shard_map/convert_element_type | solution.py:1223
  334.3 0.0 copy-done
  334.3 1.7 copy.17
  (1 shorter events, 0.0 us)
Async XLA Ops:
  0.6 5.3 %copy-start.1 = (s32[1024]{0:T(1024)S(1)}, s32[1024]{0:T(1024)}, u32[]{:S(2)}) copy-start(s32[1024]{0:T(1024)} %param.7) | copy-start | bytes 12292
  2.5 7.3 %collective-permute-start = (bf16[3072]{0:T(1024)(128)(2,1)S(1)}, bf16[3072]{0:T(1024)(128)(2,1)S(1)}, u32[]{:S(2)}, u32[]{:S(2)}) collective-permute-start(bf16[3072]{0:T(1024)(128)(2,1)S(1)} %slice.8), channel_id=1, source_target_pairs={{0,1},{1,2},{2,3},{3,4},{4,5},{5,6},{6,7},{7,8},{8,9},{9,10},{10,1... | collective-permute-start | bytes 18440 | tf_op jit(solution)/shard_map/ppermute | solution.py:1158
  324.1 10.2 %copy-start = (f32[1024,768]{1,0:T(8,128)S(1)}, f32[1024,768]{1,0:T(8,128)}, u32[]{:S(2)}) copy-start(f32[1024,768]{1,0:T(8,128)} %get-tuple-element.50) | copy-start | bytes 9437188

commit v7 on v6

--- a/solution.py
+++ b/solution.py
@@ -55,28 +55,23 @@
             c=pl.ds(pl.multiple_of(t*256,256),256)
             qkv[n,c]=dot_tn(w[0,n//2,n%2,:,c],tokT[...]).astype(bf16)
 
-def attend_head(h,dist,kn,qkv,mixb,lse):
+def attend_head(h,dist,qkv,mixb,lse):
     rows=pl.ds(pl.multiple_of(h*HEAD,HEAD),HEAD)
-    kn[...]=qkv[1,rows].astype(f32).T.astype(bf16)
-    m=slope(h)
-    for b in range(LEN//QB):
-        cols=pl.ds(b*QB,QB)
-        q=qkv[0,rows,cols]*bf16(0.125)
-        s=dot(kn[...],q)-m*dist[:,cols]
-        top=jnp.max(s,0,keepdims=True)
-        e=jnp.exp(s-top)
-        total=jnp.sum(e,0,keepdims=True)
-        o=dot(qkv[2,rows],e.astype(bf16))/total
-        mixb[rows,cols]=o.astype(bf16)
-        lse[h,:,cols]=top+jnp.log(total)
-
-def attend_kernel(tokens,w,seg_col,seg_row,tokT,qkv,mixb,lse,dist,kn):
+    keys=qkv[1,rows].astype(f32).T.astype(bf16)
+    s=dot(keys,qkv[0,rows]*bf16(0.125))-slope(h)*dist[...]
+    top=jnp.max(s,0,keepdims=True)
+    e=jnp.exp(s-top)
+    total=jnp.sum(e,0,keepdims=True)
+    mixb[rows]=(dot(qkv[2,rows],e.astype(bf16))/total).astype(bf16)
+    lse[h]=top+jnp.log(total)
+
+def attend_kernel(tokens,w,seg_col,seg_row,tokT,qkv,mixb,lse,dist):
     tokT[...]=tokens[...].astype(f32).T.astype(bf16)
     fill_distance(dist,seg_col,seg_row)
     project_all(w,tokT,qkv)
     @pl.loop(0,HEADS)
     def _(h):
-        attend_head(h,dist,kn,qkv,mixb,lse)
+        attend_head(h,dist,qkv,mixb,lse)
 
 def attend_shapes():
     S=jax.ShapeDtypeStruct
@@ -86,7 +81,7 @@
     return pl.pallas_call(attend_kernel,grid=(1,),
         in_specs=[VM,pl.BlockSpec((1,2,2,D,D),lambda i:(0,0,0,0,0)),VM,VM],out_specs=[VM]*4,
         out_shape=attend_shapes(),
-        scratch_shapes=[pltpu.VMEM((LEN,LEN),f32),pltpu.VMEM((LEN,HEAD),bf16)],
+        scratch_shapes=[pltpu.VMEM((LEN,LEN),f32)],
         compiler_params=pltpu.CompilerParams(vmem_limit_bytes=58<<20),name="attend")(tokens,w,seg.reshape(LEN,1),seg.reshape(1,LEN))
 
 def attend_back_kernel(w,seg_col,seg_row,tokT,qkv,mixb,lse,dO,first,gbranch,g0,grad_in,dist,kn,vn,p_all,ds_all,dqT,dkT,dvT):
@@ -270,12 +265,26 @@
         def _(m):
             code = jnp.where(m == 0, word, jnp.where(m == 1, word // 256, word // 65536)) % 256
             kind, e = code // 16, code % 16
-            for k, op in enumerate(ops):
-                when(kind == k, lambda op=op: op(e))
+            branch(kind, e, 0, ops)
+
+
+def branch(kind, e, low, ops):
+    if len(ops) == 1:
+        ops[0](e)
+        return
+    half = len(ops) // 2
+
+    def lower():
+        branch(kind, e, low, ops[:half])
+
+    def upper():
+        branch(kind, e, low + half, ops[half:])
+
+    lax.cond(kind < low + half, lower, upper)
 
 
 def gather_attend_kernel(blk, last, tokens, seg_col, seg_row, result, tail, tokT, qkv, mixb, lse,
-                         held, dist, kn, own_sem, out_sem, pzs, pzr, pfs, pfr, pgs, pgr, p_s, p_r,
+                         held, dist, own_sem, out_sem, pzs, pzr, pfs, pfr, pgs, pgr, p_s, p_r,
                          b1s, b1r, c1u, c1d, c1r, b2u, b2d, b2r, c2s, c2r, b3s, b3r, c3s, c3r, ss, sr, ts, tr):
     i, c, z, y, x = place()
     xp, yp, sib, up, down = partners(i, c, z, y, x)
@@ -456,7 +465,7 @@
             qkv[n, cols] = dot_tn(held[0, n // 2, n % 2, :, cols], tokT[...]).astype(bf16)
 
     def op_head(h):
-        attend_head(h, dist, kn, qkv, mixb, lse)
+        attend_head(h, dist, qkv, mixb, lse)
 
     line = jnp.logical_and(y == 1, x == 1)
     source = jnp.logical_and(line, z == 3)
@@ -588,7 +597,7 @@
             *attend_shapes(),
         ],
         scratch_shapes=[
-            pltpu.VMEM((4, 2, 2, D, D), bf16), pltpu.VMEM((LEN, LEN), f32), pltpu.VMEM((LEN, HEAD), bf16),
+            pltpu.VMEM((4, 2, 2, D, D), bf16), pltpu.VMEM((LEN, LEN), f32),
             Q, Q((4,)), *[Q((n,)) for n in counts],
         ],
         compiler_params=pltpu.CompilerParams(
@@ -598,58 +607,58 @@
     )(blk, last, tokens, seg.reshape(LEN, 1), seg.reshape(1, LEN))
 
 
-PLANE_ORDER = (1, 3, 2)
+PLANE_ORDER = (3, 1, 2)
 BACK_PLAN = (
     (
-        14709104, 65761, 422402, 475168, 2192136, 200769, 4334084, 7606533, 7685670, 2639655,
-        8589896, 5255296, 8552726, 4399990, 9454628, 9671313, 3241751, 4531537, 3307544, 3543890,
-        10582358, 10713620, 10517269, 3692343, 8905304, 10638131, 11634052, 8803380, 3526835, 11587925,
-        9745106, 9934485, 10855635, 10987200, 11843009, 12761014, 12895683, 15779782, 15790320,
+        7374723, 460401, 29192, 131366, 2556931, 4593157, 2650951, 4724512, 2192448, 7684376,
+        8397602, 2392705, 4329744, 9605520, 4428581, 7750980, 5650230, 7803479, 5779512, 7869264,
+        10572081, 10713364, 3308053, 10657843, 8082258, 5518644, 8708693, 11568773, 11776689, 9802960,
+        13735830, 10855634, 10928339, 11919527, 12760257, 14792630, 12960963, 15714246, 15724527,
     ),
     (
-        14709104, 65761, 422402, 526112, 1057139, 328707, 4224034, 7672102, 8589863, 2639425,
-        3151488, 4358785, 4748871, 9446435, 9671313, 5273367, 3228453, 4487192, 7934770, 4535969,
-        5339668, 5667747, 6378080, 14825527, 6457109, 8750131, 5736096, 10670132, 13719605, 9744816,
-        9934485, 11776722, 5559123, 12625316, 10928469, 11842983, 12039874, 12895683, 15779782,
+        7374723, 460401, 57352, 7471617, 328707, 2565654, 2627443, 2103412, 4671009, 8487029,
+        2232450, 4727843, 9605520, 7737747, 3543589, 3635008, 1261880, 7881538, 1351984, 7947588,
+        5723811, 8007957, 5265568, 10629938, 14831995, 11568516, 11699889, 5460659, 9802848, 6395798,
+        5518434, 10801205, 12604837, 10987217, 11911873, 11981492, 13878199, 14796228, 15714246,
     ),
     (
-        14709104, 65761, 422402, 526112, 1057139, 262976, 7603490, 1123905, 2572917, 8595474,
-        3151488, 7766657, 2311760, 9539620, 1545106, 4749127, 3217445, 1258104, 5325689, 1324705,
-        4477562, 4553635, 3684256, 8852962, 3383940, 6510213, 13644934, 6599088, 3519441, 5747410,
-        9802853, 12621718, 5816787, 5481892, 12801218, 11904934, 11949492, 12895671, 15779782,
+        7374723, 460401, 57352, 7471617, 328707, 1451814, 1517683, 2170996, 8418584, 2261633,
+        4212259, 9539600, 2397074, 1130823, 4748837, 1193538, 3700535, 3176467, 10571897, 1328035,
+        3228794, 4563025, 8066354, 5722710, 11776177, 8708770, 8815960, 9752754, 9934485, 13746624,
+        13812674, 3384740, 10987060, 11850549, 11974084, 6535109, 13002084, 14767047, 15684948,
     ),
     (
-        14709104, 65761, 422402, 475168, 2192136, 200769, 4334084, 7606533, 2585894, 8595474,
-        3151488, 8552784, 4399990, 9454628, 9671313, 4618007, 3228965, 7870545, 5386823, 4732435,
-        1352057, 8102778, 3684256, 8852962, 3383940, 6718803, 5518470, 11587687, 13723840, 5685681,
-        9721141, 11703957, 12825538, 13882007, 5744036, 10987096, 11847093, 13022916, 15779767,
+        7374723, 460401, 29192, 131366, 2556694, 7537924, 7612439, 2168864, 7684416, 8392738,
+        2327169, 3556162, 2363766, 2462096, 9638546, 4474694, 7812933, 3688467, 7884848, 5320980,
+        10556793, 8016434, 8102816, 8708770, 6719109, 11649200, 9802945, 11704214, 12825538, 13658215,
+        5678500, 13719639, 11904934, 12960948, 13022930, 3393463, 5518419, 13849909, 15720928,
     ),
 )
 
 GATHER_PLAN = (
     (
-        131328, 328707, 15075078, 1184016, 1339411, 1470741, 15855639, 2224754, 6324256, 7545379,
-        2369011, 2580865, 12697638, 7635650, 7704976, 16118882, 14868960, 9602000, 13738083, 8688502,
-        11597412, 6653394, 10658225, 7894995, 16316308, 9823154, 6719188, 14001075, 6785159, 9872488,
-        10868404, 11900887, 10016996, 14263990, 14329783, 12114856, 15724517, 15724527,
+        131328, 328707, 15075078, 1184016, 15757331, 7410964, 1513201, 2224754, 6324256, 7545379,
+        2396403, 2449793, 6455846, 16020625, 12697639, 9601986, 10548597, 11645027, 9687266, 13760118,
+        6594948, 6653394, 10671026, 14940023, 13939604, 16283797, 10716885, 8902246, 11834983, 6850775,
+        10805464, 10869173, 14801636, 14399127, 10987160, 12101815, 15724517, 15724527,
     ),
     (
-        3289392, 5243110, 5308787, 7623170, 1114896, 1209604, 401413, 1253763, 4276231, 7750164,
-        8659478, 1516309, 6381808, 15885041, 6579187, 16184820, 2385285, 16217893, 2586662, 12763584,
-        6721670, 14803192, 10512263, 8966370, 13738344, 10662033, 13865682, 13939091, 9754019, 14918834,
-        9868758, 11851699, 9951397, 11901145, 14345382, 14395318, 12101815, 15724517,
+        3207664, 15086129, 5279744, 5308787, 156000, 7639378, 266243, 10487157, 8586928, 4196113,
+        10568257, 1315446, 1475761, 2196755, 1406752, 16127779, 16053239, 7926517, 6579192, 2253413,
+        6719013, 8857380, 2528871, 12763584, 9672584, 13689448, 13743764, 12046997, 13947794, 13998304,
+        14070691, 11851684, 14263768, 14988706, 14395098, 11708385, 12101859, 15724517,
     ),
     (
-        3486771, 7754726, 7820628, 7864576, 200706, 296465, 8848658, 1246752, 4392737, 8918084,
-        2233925, 1512816, 15761443, 6550368, 6681700, 16148213, 16316263, 2388328, 8515877, 12592934,
-        7520961, 6393986, 14742114, 14852321, 13734864, 13804464, 11773076, 13936083, 14005397, 14067350,
-        14985141, 10000343, 11065526, 12030425, 10658266, 12096219, 11710949, 15724515,
+        16119027, 3486771, 9655270, 5535331, 9721188, 30565, 7902465, 242434, 296611, 8889349,
+        504838, 4460867, 10848325, 1208336, 14988564, 1277974, 2168177, 16183319, 16316401, 6776416,
+        6390120, 7479331, 2237938, 2581122, 2527268, 12763584, 14848406, 9953488, 10015152, 10532562,
+        10933459, 11002325, 14145201, 14202792, 9623969, 14345656, 11721634, 15724515,
     ),
     (
-        3684150, 5695222, 5805655, 112128, 200706, 1180689, 401413, 467219, 1328966, 1450568,
-        1512819, 15958819, 6776419, 6879479, 2434164, 2524404, 12697639, 8746434, 6644883, 14803189,
-        13689507, 10940528, 7438545, 9957728, 13805491, 9986433, 13890162, 9724546, 13936823, 15055012,
-        9807317, 11833558, 11903191, 14193124, 9623969, 11655856, 11721634, 15724515,
+        16316406, 3684150, 9852646, 6772582, 6854488, 11927704, 173569, 12035843, 11011332, 462854,
+        4670994, 15054920, 7541777, 1381142, 2105731, 15931252, 2319348, 2253956, 16086309, 8726308,
+        2528101, 12763584, 10715360, 15757460, 6353265, 13677538, 10781153, 9818465, 13824626, 13870516,
+        9462402, 14988756, 14079377, 14135456, 9623713, 14342577, 11721634, 15724515,
     ),
 )
 
@@ -660,7 +669,7 @@
 
 def reduce_back_kernel(wide, down, w, qkv_in, dO, mixb, lse, tokT, gbranch, first, norm_in, seg_col, seg_row,
                        grad_in, flat_out, own, sl, lc3, lc2, lcz, lczx, lb3, lbz, lbzx, lb1, lf, lg, lz, stage,
-                       dist, p_all, ds_all, wv, kn, vn, qkv, fchunk, flat, nacc, nx, ny, nz, nc,
+                       dist, p_all, ds_all, wv, qkv, fchunk, flat, nacc, nx, ny, nz, nc,
                        own_sem, qkv_sem, w_sem, f_sem, g_sem, o_sem, sib_s, sib_r, st_s, st_r,
                        c3s, c3r, b3s, b3r, c2s, c2r, bus, bur, bds, bdr, cus, cur, cds, cdr, b1s, b1r,
                        fs, fr, gs, gr, zs_, zr_, ns, nr, share_s, share_r, aft_s, aft_r):
@@ -711,7 +720,7 @@
         def _(n):
             k = pl.multiple_of(n * 16, 16)
             a = dst(k)
-            a[...] = (a[...].astype(f32) + src(k)[...].astype(f32)).astype(bf16)
+            a[...] = a[...] + src(k)[...]
 
     r16 = lambda k: pl.ds(k, 16)
     split = lambda e: (e // 3 + 1, e % 3)
@@ -834,23 +843,25 @@
 
     def op_head(h):
         rows = pl.ds(pl.multiple_of(h * HEAD, HEAD), HEAD)
-        kn[...] = qkv[1, rows].astype(f32).T.astype(bf16)
-        vn[...] = qkv[2, rows].astype(f32).T.astype(bf16)
+        keys = qkv[1, rows].astype(f32).T.astype(bf16)
+        values = qkv[2, rows].astype(f32).T.astype(bf16)
         m = slope(h)
+        grad_q = []
         for b in range(LEN // QB):
             cols = pl.ds(b * QB, QB)
-            q = qkv[0, rows, cols] * bf16(0.125)
-            s = dot(kn[...], q) - m * dist[:, cols]
+            do = dO[rows, cols]
+            s = dot(keys, qkv[0, rows, cols] * bf16(0.125)) - m * dist[:, cols]
+            dp = dot(values, do)
+            delta = jnp.sum(do.astype(f32) * mixb[rows, cols].astype(f32), 0, keepdims=True)
             p = jnp.exp(s - lse[h, :, cols])
-            do = dO[rows, cols]
-            delta = jnp.sum(do.astype(f32) * mixb[rows, cols].astype(f32), 0, keepdims=True)
-            dp = dot(vn[...], do)
             p_all[:, cols] = p.astype(bf16)
-            ds_all[:, cols] = (p * (dp - delta)).astype(bf16)
-        grad_q = (dot(qkv[1, rows], ds_all[...]) * 0.125).astype(bf16)
+            ds = (p * (dp - delta)).astype(bf16)
+            ds_all[:, cols] = ds
+            grad_q.append((dot(qkv[1, rows], ds) * 0.125).astype(bf16))
         grad_k = (dot_nt(qkv[0, rows], ds_all[...]) * 0.125).astype(bf16)
         grad_v = dot_nt(dO[rows], p_all[...]).astype(bf16)
-        qkv[0, rows] = grad_q
+        for b in range(LEN // QB):
+            qkv[0, rows, pl.ds(b * QB, QB)] = grad_q[b]
         qkv[1, rows] = grad_k
         qkv[2, rows] = grad_v
 
@@ -1120,7 +1131,7 @@
             V(4, 2, 2, HALF, D), V(4, 2, 2, HALF, D), V(9, 2, C_PART, D), V(9, C_PART, D), V(9, C_PART, D),
             V(3, C_PART, D), V(9, 2, B_PART, D), V(9, 2, B_PART, D), V(3, 2, B_PART, D), V(3, B_PART, D),
             V(8, 2, Q_PART, COLS), V(8, Q_PART, COLS), V(8, Q_PART, COLS), V(8, HALF, COLS),
-            F(LEN, LEN), V(LEN, LEN), V(LEN, LEN), V(D, D), V(LEN, HEAD), V(LEN, HEAD), V(3, D, LEN),
+            F(LEN, LEN), V(LEN, LEN), V(LEN, LEN), V(D, D), V(3, D, LEN),
             F(256, D), F(6 * D + 24, 128), F(4, D), F(4, D), F(4, D), F(4, D), F(4, D),
             Q((4,)), Q, Q((3,)), Q, Q, Q, Q((4,)), Q((4,)), Q((8,)), Q((8,)),
             *[Q((9,))] * 14, Q((3,)), Q((3,)), *[Q((8,))] * 6, Q((4,)), Q((4,)), Q, Q, Q, Q,

time: 342 us -> 309 us (0.904)
  Pallas kernels: 309 us -> 276 us
    pallas_call x1, Pallas kernels: 132 us -> 110 us  [reduce_back(): pl.pallas_call(reduce_back_kernel, in_specs=[A, A, A, A, VM, VM, VM, VM,...]
    pallas_call x1, Pallas kernels: 101 us -> 90 us  [gather_attend(): pl.pallas_call(gather_attend_kernel, in_specs=[any_space, VM, VM, VM, VM]...]
  transfers between devices with their start and end apart: 1 -> 1, of which waited for: 1 -> 1; matrix products, arithmetic and copies ran while one was open for 0% -> 1% of each run, Pallas kernels for 0% -> 0%
where the time goes in v7:
time: 309 us; the launch traced here: 303 us
  Pallas kernels  276 us (89%)
  other arithmetic  15.5 us (5%)
  local copies, waits for them, and re-layouts  5.08 us (2%)
  starting transfers between devices  3.39 us (1%)
    pallas_call x1, Pallas kernels, reduce_back(): pl.pallas_call(reduce_back_kernel, in_specs=[A, A, A, A, VM, VM, VM, VM,...  110 us
    pallas_call x1, Pallas kernels, gather_attend(): pl.pallas_call(gather_attend_kernel, in_specs=[any_space, VM, VM, VM, VM]...  90 us
    pallas_call x1, Pallas kernels, feed(): pl.pallas_call(feed_kernel, grid=(n + 12,), in_specs=[pl.BlockSpec((TB, D...  76 us
    convert_element_type x1, other arithmetic, local(): master_new.astype(jnp.bfloat16)  10.2 us
  transfers between devices with their start and end apart: 1, of which 1 were waited for; matrix products, arithmetic and copies ran while one was open for 1% of the time, Pallas kernels for 0%

profile of v7, /device:TPU:8, one launch (start us, length us, event | category | flops | bytes accessed | tf_op | source)
XLA Modules:
  0.0 303.3 jit_solution(16413724728854513595)
XLA Ops:
  0.6 0.0 copy-start.1
  0.6 1.8 convert_element_type.11
  2.4 0.1 slice.8
  2.5 3.4 %collective-permute-start = (bf16[3072]{0:T(1024)(128)(2,1)S(1)}, bf16[3072]{0:T(1024)(128)(2,1)S(1)}, u32[]{:S(2)}, u32[]{:S(2)}) collective-permute-start(bf16[3072]{0:T(1024)(128)(2,1)S(1)} %slice.8), channel_id=1, source_target_pairs={{0,1},{1,2},{2,3},{3,4},{4,5},{5,6},{6,7},{7,8},{8,9},{9,10},{10,1... | collective-permute-start | bytes 18440 | tf_op jit(solution)/shard_map/ppermute | solution.py:1169
  5.9 0.0 copy-done.1
  5.9 1.0 copy.14.seg_col
  7.0 0.6 pad.4.last
  7.6 2.2 collective-permute-done
  9.8 1.0 fusion
  10.8 0.5 reshape_reshape.3
  11.3 1.1 reshape.44
  12.4 0.1 copy.13
  12.5 1.2 bitcast_select_fusion.blk
  13.7 90.0 %gather_attend.1 = (bf16[4,2,2,768,768]{4,3,2,1,0:T(8,128)(2,1)}, bf16[16,768]{1,0:T(8,128)(2,1)}, bf16[768,1024]{1,0:T(8,128)(2,1)}, bf16[3,768,1024]{2,1,0:T(8...) custom-call(bf16[768,768]{1,0:T(8,128)(2,1)} %bitcast_select_fusion.blk, bf16[16,768]{1,0:T(8,128)(2,1)} %pad.4.last, ...), custom_call_target="tpu_custom_call" | custom-call | tf_op jit(solution)/shard_map/gather_attend/pallas_call | solution.py:591
  103.7 1.3 slice_convert_fusion.norms
  105.1 76.0 %feed.1 = (bf16[1024,768]{1,0:T(8,128)(2,1)}, f32[1024,768]{1,0:T(8,128)}, bf16[768,1024]{1,0:T(8,128)(2,1)}, bf16[1024,768]{1,0:T(8,128)(2,1)}, f32[4,768]{1,0:...) custom-call(bf16[1024,768]{1,0:T(8,128)(2,1)} %tokens.3, bf16[1024,768]{1,0:T(8,128)(2,1)} %cot.1, ...), custom_call_target="tpu_custom_call" | custom-call | tf_op jit(solution)/shard_map/feed/pallas_call | solution.py:199
  181.0 110.3 %reduce_back.1 = (f32[1024,768]{1,0:T(8,128)}, f32[4632,128]{1,0:T(8,128)}) custom-call(bf16[2,2,2,768,768]{4,3,2,1,0:T(8,128)(2,1)} %bitcast.13, bf16[2,2,768,768]{3,2,1,0:T(8,128)(2,1)} %bitcast.14, bf16[4,2,2,768,768]{4,3,2,1,0:T(8,128)(2,1)} %get-tuple-element.23.w, bf16[3,768,1024]{2,1,0:T(8,128)(2,1)} %get-tuple-element.28.qkv_in, ...), custom_call_target="tpu_custom_call" | custom-call | tf_op jit(solution)/shard_map/reduce_back/pallas_call | solution.py:1125
  291.4 0.0 copy-start
  291.4 10.2 %fusion.1 = (bf16[590016]{0:T(1024)(128)(2,1)}, f32[590016]{0:T(1024)}, f32[590016]{0:T(1024)}, f32[590016]{0:T(1024)}, f32[590016]{0:T(1024)}) fusion(f32[590016]{0:T(1024)} %param.9, f32[592896]{0:T(1024)} %bitcast.16, s32[]{:T(128)S(6)} %select_n.17, f32[590016]{0:T(1024)} %param.11, f32[590016]{0:T(1024)} %param.10), kind=kLoop, calls=%fused_computation.9 | loop fusion | flops 10030272 | bytes 20060548 | tf_op jit(solution)/shard_map/convert_element_type | solution.py:1234
  301.6 0.0 copy-done
  301.6 1.7 copy.17
  (1 shorter events, 0.0 us)
Async XLA Ops:
  0.6 5.3 %copy-start.1 = (s32[1024]{0:T(1024)S(1)}, s32[1024]{0:T(1024)}, u32[]{:S(2)}) copy-start(s32[1024]{0:T(1024)} %param.7) | copy-start | bytes 12292
  2.5 7.3 %collective-permute-start = (bf16[3072]{0:T(1024)(128)(2,1)S(1)}, bf16[3072]{0:T(1024)(128)(2,1)S(1)}, u32[]{:S(2)}, u32[]{:S(2)}) collective-permute-start(bf16[3072]{0:T(1024)(128)(2,1)S(1)} %slice.8), channel_id=1, source_target_pairs={{0,1},{1,2},{2,3},{3,4},{4,5},{5,6},{6,7},{7,8},{8,9},{9,10},{10,1... | collective-permute-start | bytes 18440 | tf_op jit(solution)/shard_map/ppermute | solution.py:1169
  291.4 10.2 %copy-start = (f32[1024,768]{1,0:T(8,128)S(1)}, f32[1024,768]{1,0:T(8,128)}, u32[]{:S(2)}) copy-start(f32[1024,768]{1,0:T(8,128)} %get-tuple-element.50) | copy-start | bytes 9437188

commit v8 on v7

--- a/solution.py
+++ b/solution.py
@@ -55,76 +55,86 @@
             c=pl.ds(pl.multiple_of(t*256,256),256)
             qkv[n,c]=dot_tn(w[0,n//2,n%2,:,c],tokT[...]).astype(bf16)
 
-def attend_head(h,dist,qkv,mixb,lse):
+def attend_head(h,dist,qkv,mixb,probs):
     rows=pl.ds(pl.multiple_of(h*HEAD,HEAD),HEAD)
     keys=qkv[1,rows].astype(f32).T.astype(bf16)
     s=dot(keys,qkv[0,rows]*bf16(0.125))-slope(h)*dist[...]
-    top=jnp.max(s,0,keepdims=True)
-    e=jnp.exp(s-top)
-    total=jnp.sum(e,0,keepdims=True)
-    mixb[rows]=(dot(qkv[2,rows],e.astype(bf16))/total).astype(bf16)
-    lse[h]=top+jnp.log(total)
-
-def attend_kernel(tokens,w,seg_col,seg_row,tokT,qkv,mixb,lse,dist):
+    e=jnp.exp(s-jnp.max(s,0,keepdims=True))
+    p=(e*(1.0/jnp.sum(e,0,keepdims=True))).astype(bf16)
+    probs[...]=p
+    mixb[rows]=dot(qkv[2,rows],p).astype(bf16)
+
+def attend_back_head(h,qkv,dO,mixb,probs,ds_all):
+    rows=pl.ds(pl.multiple_of(h*HEAD,HEAD),HEAD)
+    values=qkv[2,rows].astype(f32).T.astype(bf16)
+    grad_q=[]
+    for b in range(LEN//QB):
+        cols=pl.ds(b*QB,QB)
+        do=dO[rows,cols]
+        dp=dot(values,do)
+        delta=jnp.sum(do.astype(f32)*mixb[rows,cols].astype(f32),0,keepdims=True)
+        ds=(probs[:,cols].astype(f32)*(dp-delta)).astype(bf16)
+        ds_all[:,cols]=ds
+        grad_q.append((dot(qkv[1,rows],ds)*0.125).astype(bf16))
+    grad_k=(dot_nt(qkv[0,rows],ds_all[...])*0.125).astype(bf16)
+    grad_v=dot_nt(dO[rows],probs[...]).astype(bf16)
+    for b in range(LEN//QB):
+        qkv[0,rows,pl.ds(b*QB,QB)]=grad_q[b]
+    qkv[1,rows]=grad_k
+    qkv[2,rows]=grad_v
+
+def attend_kernel(tokens,w,seg_col,seg_row,tokT,qkv,mixb,probs_out,dist,probs,sem):
     tokT[...]=tokens[...].astype(f32).T.astype(bf16)
     fill_distance(dist,seg_col,seg_row)
     project_all(w,tokT,qkv)
     @pl.loop(0,HEADS)
     def _(h):
-        attend_head(h,dist,qkv,mixb,lse)
+        attend_head(h,dist,qkv,mixb,probs)
+        move=pltpu.make_async_copy(probs,probs_out.at[h],sem)
+        move.start()
+        move.wait()
 
 def attend_shapes():
     S=jax.ShapeDtypeStruct
-    return [S((D,LEN),bf16),S((3,D,LEN),bf16),S((D,LEN),bf16),S((HEADS,1,LEN),f32)]
+    return [S((D,LEN),bf16),S((3,D,LEN),bf16),S((D,LEN),bf16),S((HEADS,LEN,LEN),bf16)]
+
+ANY=pl.BlockSpec(memory_space=pl.ANY)
 
 def attend(tokens,w,seg):
     return pl.pallas_call(attend_kernel,grid=(1,),
-        in_specs=[VM,pl.BlockSpec((1,2,2,D,D),lambda i:(0,0,0,0,0)),VM,VM],out_specs=[VM]*4,
+        in_specs=[VM,pl.BlockSpec((1,2,2,D,D),lambda i:(0,0,0,0,0)),VM,VM],out_specs=[VM]*3+[ANY],
         out_shape=attend_shapes(),
-        scratch_shapes=[pltpu.VMEM((LEN,LEN),f32)],
+        scratch_shapes=[pltpu.VMEM((LEN,LEN),f32),pltpu.VMEM((LEN,LEN),bf16),pltpu.SemaphoreType.DMA],
         compiler_params=pltpu.CompilerParams(vmem_limit_bytes=58<<20),name="attend")(tokens,w,seg.reshape(LEN,1),seg.reshape(1,LEN))
 
-def attend_back_kernel(w,seg_col,seg_row,tokT,qkv,mixb,lse,dO,first,gbranch,g0,grad_in,dist,kn,vn,p_all,ds_all,dqT,dkT,dvT):
-    fill_distance(dist,seg_col,seg_row)
+def attend_back_kernel(w,tokT,qkv_in,mixb,probs_in,dO,first,gbranch,g0,grad_in,qkv,probs,ds_all,sem,qkv_sem):
+    take=pltpu.make_async_copy(qkv_in,qkv,qkv_sem)
+    take.start()
+    take.wait()
     @pl.loop(0,HEADS)
     def _(h):
-        rows=pl.ds(pl.multiple_of(h*HEAD,HEAD),HEAD)
-        kn[...]=qkv[1,rows].astype(f32).T.astype(bf16)
-        vn[...]=qkv[2,rows].astype(f32).T.astype(bf16)
-        m=slope(h)
-        for b in range(LEN//QB):
-            cols=pl.ds(b*QB,QB)
-            q=qkv[0,rows,cols]*bf16(0.125)
-            s=dot(kn[...],q)-m*dist[:,cols]
-            p=jnp.exp(s-lse[h,:,cols])
-            do=dO[rows,cols]
-            delta=jnp.sum(do.astype(f32)*mixb[rows,cols].astype(f32),0,keepdims=True)
-            dp=dot(vn[...],do)
-            p_all[:,cols]=p.astype(bf16)
-            ds=(p*(dp-delta)).astype(bf16)
-            ds_all[:,cols]=ds
-            dqT[rows,cols]=(dot(qkv[1,rows],ds)*0.125).astype(bf16)
-        dvT[rows]=dot_nt(dO[rows],p_all[...]).astype(bf16)
-        dkT[rows]=(dot_nt(qkv[0,rows],ds_all[...])*0.125).astype(bf16)
+        move=pltpu.make_async_copy(probs_in.at[h],probs,sem)
+        move.start()
+        move.wait()
+        attend_back_head(h,qkv,dO,mixb,probs,ds_all)
     g0[1,1]=dot(mixb[...],gbranch[...]).astype(bf16)
-    for n,g in enumerate((dqT,dkT,dvT)):
-        g0[n//2,n%2]=dot_nt(tokT[...],g[...]).astype(bf16)
+    for n in range(3):
+        g0[n//2,n%2]=dot_nt(tokT[...],qkv[n]).astype(bf16)
     @pl.loop(0,4)
     def _(t):
         c=pl.ds(pl.multiple_of(t*256,256),256)
-        acc=dot(w[0,0,0],dqT[:,c])+dot(w[0,0,1],dkT[:,c])+dot(w[0,1,0],dvT[:,c])
+        acc=dot(w[0,0,0],qkv[0,:,c])+dot(w[0,0,1],qkv[1,:,c])+dot(w[0,1,0],qkv[2,:,c])
         grad_in[c]=first[c]+acc.T
 
-def attend_back(w,seg,tokT,qkv,mixb,lse,dO,first,gbranch):
-    B=lambda: pltpu.VMEM((D,LEN),bf16)
+def attend_back(w,tokT,qkv,mixb,probs,dO,first,gbranch):
     return pl.pallas_call(attend_back_kernel,grid=(1,),
-        in_specs=[pl.BlockSpec((1,2,2,D,D),lambda i:(0,0,0,0,0))]+[VM]*9,out_specs=[VM]*2,
+        in_specs=[pl.BlockSpec((1,2,2,D,D),lambda i:(0,0,0,0,0)),VM,ANY,VM,ANY,VM,VM,VM],out_specs=[VM]*2,
         out_shape=[jax.ShapeDtypeStruct((2,2,D,D),bf16),jax.ShapeDtypeStruct((LEN,D),f32)],
-        scratch_shapes=[pltpu.VMEM((LEN,LEN),f32),pltpu.VMEM((LEN,HEAD),bf16),pltpu.VMEM((LEN,HEAD),bf16),pltpu.VMEM((LEN,LEN),bf16),pltpu.VMEM((LEN,LEN),bf16),B(),B(),B()],
-        compiler_params=pltpu.CompilerParams(vmem_limit_bytes=60<<20),name="attend_back")(w,seg.reshape(LEN,1),seg.reshape(1,LEN),tokT,qkv,mixb,lse,dO,first,gbranch)
+        scratch_shapes=[pltpu.VMEM((3,D,LEN),bf16),pltpu.VMEM((LEN,LEN),bf16),pltpu.VMEM((LEN,LEN),bf16),pltpu.SemaphoreType.DMA,pltpu.SemaphoreType.DMA],
+        compiler_params=pltpu.CompilerParams(vmem_limit_bytes=60<<20),name="attend_back")(w,tokT,qkv,mixb,probs,dO,first,gbranch)
 
 TB=256
-def feed_kernel(tokens,cot,mixb,wo,w1,w2,w3,norms,output,first,dO,gbranch,ng,gdown,gwide,inner,wide,gffn,fa,fb,acc,hid):
+def feed_kernel(tokens,cot,mixb,w,norms,output,first,dO,gbranch,ng,gdown,gwide,inner,wide,gffn,fa,fb,acc,hid,wo,w1,w2,w3,w_sem,wo_sem):
     step=pl.program_id(0)
     gain1=norms[0:1]; shift1=norms[1:2]; gain2=norms[2:3]; shift2=norms[3:4]
     def stats(v):
@@ -133,11 +143,20 @@
         return c*r,r
     def back(e,n,r):
         return r*(e-jnp.mean(e,-1,keepdims=True)-n*jnp.mean(e*n,-1,keepdims=True))
-    W=lambda p,j: (w1,w2)[p-1][0,:,j].reshape(D,D)
-    WD=lambda j: w3[0,j].reshape(D,D)
-    WO=lambda: wo[0,0].reshape(D,D)
+    W=lambda p,j: (w1,w2)[p-1][j].reshape(D,D)
+    WD=lambda j: w3[j].reshape(D,D)
+    WO=lambda: wo[...].reshape(D,D)
+    def load(p,j):
+        source=w.at[p,j] if p==3 else w.at[p,:,j]
+        return pltpu.make_async_copy(source,(w1,w2,w3)[p-1].at[j],w_sem.at[p-1,j])
+    load_out=pltpu.make_async_copy(w.at[0,3],wo,wo_sem)
     @pl.when(step==0)
-    def _(): ng[...]=jnp.zeros_like(ng)
+    def _():
+        load_out.start()
+        for j in range(4):
+            for p in (1,2,3): load(p,j).start()
+        ng[...]=jnp.zeros_like(ng)
+        load_out.wait()
     @pl.when(step<LEN//TB)
     def _():
         rows=pl.ds(pl.multiple_of(step*TB,TB),TB)
@@ -148,6 +167,9 @@
         acc[...]=l1
         @pl.loop(0,4,unroll=2)
         def _(j):
+            @pl.when(step==0)
+            def _():
+                for p in (1,2,3): load(p,j).wait()
             inn=inner[rows]
             ga=dot(inn,W(1,j)); up=dot(inn,W(2,j))
             cum=0.5*(1.0+lax.erf(ga*inv_root_two))
@@ -192,20 +214,19 @@
     last=n-1
     row=lambda i:(jnp.minimum(i,last),0)
     col=lambda i:(0,jnp.minimum(i,last))
-    one=pl.Buffered(1)
     S=jax.ShapeDtypeStruct
     V=lambda s,d=bf16: pltpu.VMEM(s,d)
     clip=lambda v,a,b: jnp.minimum(jnp.maximum(v,a),b)
     return pl.pallas_call(feed_kernel,grid=(n+12,),
         in_specs=[pl.BlockSpec((TB,D),row),pl.BlockSpec((TB,D),row),pl.BlockSpec((D,TB),col),
-            pl.BlockSpec((1,1,4,D//4,D),lambda i:(0,3,0,0,0),pipeline_mode=one),*[pl.BlockSpec((1,4,4,D//4,D),lambda i,p=p:(p,0,0,0,0),pipeline_mode=one) for p in (1,2,3)],pl.BlockSpec((4,D),lambda i:(0,0))],
+            pl.BlockSpec(memory_space=pl.ANY),pl.BlockSpec((4,D),lambda i:(0,0))],
         out_specs=[pl.BlockSpec((TB,D),row),pl.BlockSpec((TB,D),row),pl.BlockSpec((D,TB),col),pl.BlockSpec((TB,D),row),
             pl.BlockSpec((4,D),lambda i:(0,0)),
             pl.BlockSpec((1,D,D),lambda i:(clip(i-n,0,3),0,0)),
             pl.BlockSpec((1,4,1,D//4,D),lambda i:(clip((i-n-4)//4,0,1),0,clip(i-n-4,0,7)%4,0,0))],
         out_shape=[S((LEN,D),bf16),S((LEN,D),f32),S((D,LEN),bf16),S((LEN,D),bf16),S((4,D),f32),S((4,D,D),bf16),S((2,4,4,D//4,D),bf16)],
-        scratch_shapes=[V((LEN,D)),V((8,LEN,D)),V((LEN,D)),V((4,TB,D),f32),V((4,TB,D),f32),V((TB,D),f32),V((4,LEN,D))],
-        compiler_params=pltpu.CompilerParams(vmem_limit_bytes=62<<20),name="feed")(tokens,cot,mixb,*[w.reshape(4,4,4,D//4,D)]*4,norms)
+        scratch_shapes=[V((LEN,D)),V((8,LEN,D)),V((LEN,D)),V((4,TB,D),f32),V((4,TB,D),f32),V((TB,D),f32),V((4,LEN,D)),V((4,D//4,D)),*[V((4,4,D//4,D))]*3,pltpu.SemaphoreType.DMA((3,4)),pltpu.SemaphoreType.DMA],
+        compiler_params=pltpu.CompilerParams(vmem_limit_bytes=62<<20),name="feed")(tokens,cot,mixb,w.reshape(4,4,4,D//4,D),norms)
 
 MESH = pl.DeviceIdType.MESH
 ALL = slice(None)
@@ -283,8 +304,8 @@
     lax.cond(kind < low + half, lower, upper)
 
 
-def gather_attend_kernel(blk, last, tokens, seg_col, seg_row, result, tail, tokT, qkv, mixb, lse,
-                         held, dist, own_sem, out_sem, pzs, pzr, pfs, pfr, pgs, pgr, p_s, p_r,
+def gather_attend_kernel(blk, last, tokens, seg_col, seg_row, result, norms, tokT_out, qkv_out, mixb, probs_out,
+                         held, dist, tail, tokT, qkv, probs, own_sem, out_sem, t_sem, q_sem, p_sem, pzs, pzr, pfs, pfr, pgs, pgr, p_s, p_r,
                          b1s, b1r, c1u, c1d, c1r, b2u, b2d, b2r, c2s, c2r, b3s, b3r, c3s, c3r, ss, sr, ts, tr):
     i, c, z, y, x = place()
     xp, yp, sib, up, down = partners(i, c, z, y, x)
@@ -446,6 +467,14 @@
         C3(t, s, e).wait_recv()
         S(c3_ref(t, s, 1 - y), 36 + e).start()
 
+    def qkv_leaves(n):
+        return pltpu.make_async_copy(qkv.at[n], qkv_out.at[n], q_sem.at[n])
+
+    tokT_leaves = pltpu.make_async_copy(tokT, tokT_out, t_sem)
+
+    def probs_leave(h):
+        return pltpu.make_async_copy(probs.at[h % 2], probs_out.at[h], p_sem.at[h % 2])
+
     def op_proj(n):
         def arrive():
             @pl.loop(0, 8)
@@ -464,8 +493,12 @@
             cols = pl.ds(pl.multiple_of(t * 256, 256), 256)
             qkv[n, cols] = dot_tn(held[0, n // 2, n % 2, :, cols], tokT[...]).astype(bf16)
 
+        qkv_leaves(n).start()
+
     def op_head(h):
-        attend_head(h, dist, qkv, mixb, lse)
+        when(h >= 2, lambda: probs_leave(h - 2).wait())
+        attend_head(h, dist, qkv, mixb, probs.at[h % 2])
+        probs_leave(h).start()
 
     line = jnp.logical_and(y == 1, x == 1)
     source = jnp.logical_and(line, z == 3)
@@ -515,6 +548,7 @@
 
         def prepare():
             tokT[...] = tokens[...].astype(f32).T.astype(bf16)
+            tokT_leaves.start()
             fill_distance(dist, seg_col, seg_row)
 
         when(e == 0, tail_z)
@@ -580,6 +614,12 @@
         S(b2_ref(t, s, 1 - x), 27 + e).wait_send()
         S(c3_ref(t, s, 1 - y), 36 + e).wait_send()
 
+    norms[...] = tail[pl.ds(0, 4)].astype(f32)
+    tokT_leaves.wait()
+    for n in range(3):
+        qkv_leaves(n).wait()
+    for h in (HEADS - 2, HEADS - 1):
+        probs_leave(h).wait()
     for t in range(4):
         leave(t).wait()
 
@@ -591,14 +631,15 @@
     return pl.pallas_call(
         gather_attend_kernel,
         in_specs=[any_space, VM, VM, VM, VM],
-        out_specs=[any_space] + [VM] * 5,
+        out_specs=[any_space, VM, any_space, any_space, VM, any_space],
         out_shape=[
-            jax.ShapeDtypeStruct((4, 2, 2, D, D), bf16), jax.ShapeDtypeStruct((16, D), bf16),
+            jax.ShapeDtypeStruct((4, 2, 2, D, D), bf16), jax.ShapeDtypeStruct((4, D), f32),
             *attend_shapes(),
         ],
         scratch_shapes=[
-            pltpu.VMEM((4, 2, 2, D, D), bf16), pltpu.VMEM((LEN, LEN), f32),
-            Q, Q((4,)), *[Q((n,)) for n in counts],
+            pltpu.VMEM((4, 2, 2, D, D), bf16), pltpu.VMEM((LEN, LEN), f32), pltpu.VMEM((16, D), bf16),
+            pltpu.VMEM((D, LEN), bf16), pltpu.VMEM((3, D, LEN), bf16), pltpu.VMEM((2, LEN, LEN), bf16),
+            Q, Q((4,)), Q, Q((3,)), Q((2,)), *[Q((n,)) for n in counts],
         ],
         compiler_params=pltpu.CompilerParams(
             collective_id=1, has_side_effects=True, vmem_limit_bytes=58 << 20
@@ -607,31 +648,31 @@
     )(blk, last, tokens, seg.reshape(LEN, 1), seg.reshape(1, LEN))
 
 
-PLANE_ORDER = (3, 1, 2)
+PLANE_ORDER = (1, 2, 3)
 BACK_PLAN = (
     (
-        7374723, 460401, 29192, 131366, 2556931, 4593157, 2650951, 4724512, 2192448, 7684376,
-        8397602, 2392705, 4329744, 9605520, 4428581, 7750980, 5650230, 7803479, 5779512, 7869264,
-        10572081, 10713364, 3308053, 10657843, 8082258, 5518644, 8708693, 11568773, 11776689, 9802960,
-        13735830, 10855634, 10928339, 11919527, 12760257, 14792630, 12960963, 15714246, 15724527,
+        7374723, 131328, 263025, 14681376, 4198406, 4261665, 1122930, 7553544, 7619363, 4461092,
+        7685413, 8393510, 5255297, 4592770, 3221366, 1413201, 9605601, 2659143, 3307336, 7870034,
+        3429171, 7935828, 8017205, 8067233, 14853024, 10630788, 8815958, 11622199, 3723443, 13742168,
+        13882034, 9868692, 12632471, 12756388, 10987203, 12891317, 12957622, 15714246, 15724527,
     ),
     (
-        7374723, 460401, 57352, 7471617, 328707, 2565654, 2627443, 2103412, 4671009, 8487029,
-        2232450, 4727843, 9605520, 7737747, 3543589, 3635008, 1261880, 7881538, 1351984, 7947588,
-        5723811, 8007957, 5265568, 10629938, 14831995, 11568516, 11699889, 5460659, 9802848, 6395798,
-        5518434, 10801205, 12604837, 10987217, 11911873, 11981492, 13878199, 14796228, 15714246,
+        7374723, 131328, 254065, 328736, 7475206, 2230049, 7541000, 1209379, 2454820, 1278016,
+        4400705, 8537217, 9467458, 9573521, 4532115, 1406760, 14776390, 4684054, 10557306, 14842696,
+        10688644, 8815968, 5255265, 5321058, 9868692, 5386903, 5452704, 3494964, 10630741, 3684182,
+        10835920, 13743025, 10797400, 12628135, 11708114, 12825794, 13875125, 12960950, 15714246,
     ),
     (
-        7374723, 460401, 57352, 7471617, 328707, 1451814, 1517683, 2170996, 8418584, 2261633,
-        4212259, 9539600, 2397074, 1130823, 4748837, 1193538, 3700535, 3176467, 10571897, 1328035,
-        3228794, 4563025, 8066354, 5722710, 11776177, 8708770, 8815960, 9752754, 9934485, 13746624,
-        13812674, 3384740, 10987060, 11850549, 11974084, 6535109, 13002084, 14767047, 15684948,
+        7374723, 131328, 263025, 14681376, 7475206, 2230049, 7541000, 7611200, 4334657, 8418578,
+        2458241, 1257510, 2573174, 1347984, 7836562, 2634052, 7869776, 1459506, 4600697, 14766497,
+        8016407, 8079156, 1591459, 14836533, 8757380, 13645446, 9713570, 9868600, 11645079, 5488996,
+        6665138, 10801600, 12829349, 13784404, 11839398, 12867253, 11978195, 5752503, 15714136,
     ),
     (
-        7374723, 460401, 29192, 131366, 2556694, 7537924, 7612439, 2168864, 7684416, 8392738,
-        2327169, 3556162, 2363766, 2462096, 9638546, 4474694, 7812933, 3688467, 7884848, 5320980,
-        10556793, 8016434, 8102816, 8708770, 6719109, 11649200, 9802945, 11704214, 12825538, 13658215,
-        5678500, 13719639, 11904934, 12960948, 13022930, 3393463, 5518419, 13849909, 15720928,
+        7374723, 131328, 263025, 14681376, 4198406, 4261665, 533106, 7553553, 7619363, 4461092,
+        7685413, 8552832, 5255206, 9442323, 9578385, 2651795, 3241749, 3307601, 5452626, 3438870,
+        8001364, 10714017, 10519778, 3507845, 14787126, 9802837, 9879985, 11580311, 3654592, 11707600,
+        10867138, 10998438, 11912372, 11933893, 12047302, 4671175, 5650504, 6842214, 15685719,
     ),
 )
 
@@ -639,26 +680,26 @@
     (
         131328, 328707, 15075078, 1184016, 15757331, 7410964, 1513201, 2224754, 6324256, 7545379,
         2396403, 2449793, 6455846, 16020625, 12697639, 9601986, 10548597, 11645027, 9687266, 13760118,
-        6594948, 6653394, 10671026, 14940023, 13939604, 16283797, 10716885, 8902246, 11834983, 6850775,
-        10805464, 10869173, 14801636, 14399127, 10987160, 12101815, 15724517, 15724527,
+        6594948, 10651090, 14922341, 13891447, 16283796, 9819315, 13985414, 8902307, 11822998, 8970455,
+        14182564, 14988709, 11966425, 10019290, 12035803, 12101799, 15724517, 15724527,
     ),
     (
         3207664, 15086129, 5279744, 5308787, 156000, 7639378, 266243, 10487157, 8586928, 4196113,
         10568257, 1315446, 1475761, 2196755, 1406752, 16127779, 16053239, 7926517, 6579192, 2253413,
-        6719013, 8857380, 2528871, 12763584, 9672584, 13689448, 13743764, 12046997, 13947794, 13998304,
-        14070691, 11851684, 14263768, 14988706, 14395098, 11708385, 12101859, 15724517,
+        6719013, 8857380, 2528871, 12763584, 9672584, 13689448, 13743764, 9622165, 14734263, 11785368,
+        14079395, 14136484, 10672293, 14279861, 14801574, 14922407, 12101851, 15724517,
     ),
     (
         16119027, 3486771, 9655270, 5535331, 9721188, 30565, 7902465, 242434, 296611, 8889349,
         504838, 4460867, 10848325, 1208336, 14988564, 1277974, 2168177, 16183319, 16316401, 6776416,
-        6390120, 7479331, 2237938, 2581122, 2527268, 12763584, 14848406, 9953488, 10015152, 10532562,
-        10933459, 11002325, 14145201, 14202792, 9623969, 14345656, 11721634, 15724515,
+        6390120, 7479331, 2237938, 2581122, 2527268, 12763584, 14848406, 9953488, 10015152, 11968722,
+        10933459, 14004705, 11064999, 10606519, 14258904, 10675640, 11721690, 15724515,
     ),
     (
         16316406, 3684150, 9852646, 6772582, 6854488, 11927704, 173569, 12035843, 11011332, 462854,
         4670994, 15054920, 7541777, 1381142, 2105731, 15931252, 2319348, 2253956, 16086309, 8726308,
-        2528101, 12763584, 10715360, 15757460, 6353265, 13677538, 10781153, 9818465, 13824626, 13870516,
-        9462402, 14988756, 14079377, 14135456, 9623713, 14342577, 11721634, 15724515,
+        2528101, 12763584, 10715360, 15757460, 6353265, 13677538, 10781153, 9818465, 13824626, 6455973,
+        9491380, 11899348, 10540516, 10596566, 9623767, 10672561, 11721690, 15724515,
     ),
 )
 
@@ -667,10 +708,10 @@
 COLS = D // 2
 
 
-def reduce_back_kernel(wide, down, w, qkv_in, dO, mixb, lse, tokT, gbranch, first, norm_in, seg_col, seg_row,
+def reduce_back_kernel(wide, down, w, qkv_in, dO_in, mixb_in, probs_in, tokT_in, gbranch_in, first, norm_in,
                        grad_in, flat_out, own, sl, lc3, lc2, lcz, lczx, lb3, lbz, lbzx, lb1, lf, lg, lz, stage,
-                       dist, p_all, ds_all, wv, qkv, fchunk, flat, nacc, nx, ny, nz, nc,
-                       own_sem, qkv_sem, w_sem, f_sem, g_sem, o_sem, sib_s, sib_r, st_s, st_r,
+                       dO, mixb, tokT, gbranch, theirs, probs, ds_all, wv, qkv, fchunk, flat, nacc, nx, ny, nz, nc,
+                       own_sem, in_sem, p_sem, w_sem, f_sem, g_sem, o_sem, sib_s, sib_r, st_s, st_r,
                        c3s, c3r, b3s, b3r, c2s, c2r, bus, bur, bds, bdr, cus, cur, cds, cdr, b1s, b1r,
                        fs, fr, gs, gr, zs_, zr_, ns, nr, share_s, share_r, aft_s, aft_r):
     i, c, z, y, x = place()
@@ -688,16 +729,34 @@
     def local_in(t):
         return pltpu.make_async_copy(planes[t - 1].at[:, :, mine], own.at[t], own_sem.at[t])
 
-    def sib_in(t):
-        return remote(planes[t - 1].at[:, :, other], sl.at[t], sib, sib_s.at[t], sib_r.at[t])
+    def sib_in(t, s, n):
+        k = 2 * ((t - 1) * 3 + s) + n
+        start, size = (s * B_PART, B_PART) if n == 0 else (3 * B_PART + s * C_PART, C_PART)
+        there = pl.ds(pl.multiple_of((1 - c) * HALF + start, 16), size)
+        return remote(planes[t - 1].at[:, :, there], sl.at[t, :, :, pl.ds(start, size)], sib, sib_s.at[k], sib_r.at[k])
 
     for t in PLANE_ORDER:
         local_in(t).start()
-    qkv_copy = pltpu.make_async_copy(qkv_in, qkv, qkv_sem)
-    qkv_copy.start()
+    take = [
+        pltpu.make_async_copy(a, b, in_sem.at[n])
+        for n, (a, b) in enumerate(
+            ((qkv_in, qkv), (dO_in, dO), (mixb_in, mixb), (gbranch_in, gbranch), (tokT_in, tokT))
+        )
+    ]
+    for n in range(3):
+        take[n].start()
+
+    def probs_come(h):
+        return pltpu.make_async_copy(probs_in.at[h], probs.at[h % 2], p_sem.at[h % 2])
+
+    probs_come(0).start()
+    for n in (3, 4):
+        take[n].start()
     enter_more(i, c, z, y, x)
     for t in PLANE_ORDER:
-        sib_in(t).start()
+        for s in range(3):
+            for n in range(2):
+                sib_in(t, s, n).start()
     nacc[...] = norm_in[...]
     NX = remote(nacc, nx, xp, ns.at[0], nr.at[0])
     NY = remote(nacc, ny, yp, ns.at[1], nr.at[1])
@@ -706,8 +765,8 @@
     line = jnp.logical_and(x == 1, y == 1)
     last_line = jnp.logical_and(line, z == 3)
     when(x == 0, lambda: NX.start())
-    fill_distance(dist, seg_col, seg_row)
-    qkv_copy.wait()
+    for move in take:
+        move.wait()
 
     def rb(s, k=0, size=B_PART):
         return pl.ds(pl.multiple_of(s * B_PART + k, 16), size)
@@ -752,15 +811,14 @@
     def op_sum(e):
         t, s = split(e)
 
-        def arrive():
-            for k in (1, 2, 3):
-                def both(k=k):
-                    local_in(k).wait()
-                    sib_in(k).wait_recv()
-
-                when(t == k, both)
-
-        when(s == 0, arrive)
+        for k in (1, 2, 3):
+            when(jnp.logical_and(t == k, s == 0), lambda k=k: local_in(k).wait())
+            for m in range(3):
+                def arrive(k=k, m=m):
+                    for n in range(2):
+                        sib_in(k, m, n).wait_recv()
+
+                when(e == (k - 1) * 3 + m, arrive)
         add_rows(lambda k: own.at[t, :, :, rb(s, k, 16)], lambda k: sl.at[t, :, :, rb(s, k, 16)], B_PART)
         add_rows(lambda k: own.at[t, :, :, rc(s, k, 16)], lambda k: sl.at[t, :, :, rc(s, k, 16)], C_PART)
         C3(t, s, e).start()
@@ -808,9 +866,6 @@
         when(t < z - 1, lambda: BD(t, s, e).start())
         when(t == z, lambda: B1(s).start())
 
-    def res(rows):
-        return dist.at[rows, pl.ds(0, D)]
-
     def op_cz(e):
         t, s = split(e)
         dst = lambda k: own.at[t, y, x, rc(s, k, 16)]
@@ -842,28 +897,9 @@
         add_rows(lambda k: own.at[z, y, x, rb(s, k, 16)], lambda k: lb1.at[s, r16(k)], B_PART)
 
     def op_head(h):
-        rows = pl.ds(pl.multiple_of(h * HEAD, HEAD), HEAD)
-        keys = qkv[1, rows].astype(f32).T.astype(bf16)
-        values = qkv[2, rows].astype(f32).T.astype(bf16)
-        m = slope(h)
-        grad_q = []
-        for b in range(LEN // QB):
-            cols = pl.ds(b * QB, QB)
-            do = dO[rows, cols]
-            s = dot(keys, qkv[0, rows, cols] * bf16(0.125)) - m * dist[:, cols]
-            dp = dot(values, do)
-            delta = jnp.sum(do.astype(f32) * mixb[rows, cols].astype(f32), 0, keepdims=True)
-            p = jnp.exp(s - lse[h, :, cols])
-            p_all[:, cols] = p.astype(bf16)
-            ds = (p * (dp - delta)).astype(bf16)
-            ds_all[:, cols] = ds
-            grad_q.append((dot(qkv[1, rows], ds) * 0.125).astype(bf16))
-        grad_k = (dot_nt(qkv[0, rows], ds_all[...]) * 0.125).astype(bf16)
-        grad_v = dot_nt(dO[rows], p_all[...]).astype(bf16)
-        for b in range(LEN // QB):
-            qkv[0, rows, pl.ds(b * QB, QB)] = grad_q[b]
-        qkv[1, rows] = grad_k
-        qkv[2, rows] = grad_v
+        probs_come(h).wait()
+        when(h < HEADS - 1, lambda: probs_come(h + 1).start())
+        attend_back_head(h, qkv, dO, mixb, probs.at[h % 2], ds_all)
 
     def columns(g):
         return pl.ds(pl.multiple_of(g * COLS, 128), COLS)
@@ -968,7 +1004,7 @@
         return pltpu.make_async_copy(fchunk, grad_in.at[pl.ds(pl.multiple_of(q * 256, 256), 256)], g_sem)
 
     def weight_in(n):
-        target = (p_all.at[pl.ds(0, D), pl.ds(0, D)], ds_all.at[pl.ds(0, D), pl.ds(0, D)], wv)[n]
+        target = (probs.at[0, pl.ds(0, D), pl.ds(0, D)], ds_all.at[pl.ds(0, D), pl.ds(0, D)], wv)[n]
         return pltpu.make_async_copy(w.at[0, n // 2, n % 2], target, w_sem.at[n])
 
     def op_gin(q):
@@ -981,7 +1017,7 @@
         first_in(q).start()
         cols = pl.ds(pl.multiple_of(q * 256, 256), 256)
         d = pl.ds(0, D)
-        acc = dot(p_all[d, d], qkv[0, :, cols]) + dot(ds_all[d, d], qkv[1, :, cols])
+        acc = dot(probs[0, d, d], qkv[0, :, cols]) + dot(ds_all[d, d], qkv[1, :, cols])
         acc = (acc + dot(wv[...], qkv[2, :, cols])).T
         first_in(q).wait()
         fchunk[...] += acc
@@ -1022,10 +1058,25 @@
     run_plan(z, BACK_PLAN, [op_sum, op_c3, op_b3, op_c2, op_bz, op_cz, op_b1, op_head, op_dw, op_sum0, op_f0,
                             op_g0, op_z0, op_gin, op_other])
 
-    half = pl.ds(pl.multiple_of(base, 16), HALF)
-    res(half)[...] = own[z, y, x].astype(f32)
-    share = remote(res(half), res(half), sib, share_s, share_r)
+    spread = jnp.logical_or(z == 1, z == 2)
+
+    def flatten(half, get):
+        def plain():
+            for n in range(6):
+                flat[pl.ds(half * (6 * HALF) + n, HALF, stride=6)] = get(pl.ds(0, HALF), pl.ds(n * 128, 128)).astype(f32)
+
+        def swapped():
+            for n in range(6):
+                for j in range(2):
+                    value = get(pl.ds(j * (D // 4), D // 4), pl.ds(n * 128, 128)).astype(f32)
+                    flat[pl.ds(half * 12 + j * 6 + n, D // 4, stride=24)] = value
+
+        when(jnp.logical_not(spread), plain)
+        when(spread, swapped)
+
+    share = remote(own.at[z, y, x], theirs, sib, share_s, share_r)
     share.start()
+    flatten(c, lambda rows, cols: own[z, y, x, rows, cols])
 
     @pl.loop(0, 9)
     def _(e):
@@ -1059,7 +1110,9 @@
         when(z > 0, lambda: Z0(e, g, k).wait_send())
 
     for t in (1, 2, 3):
-        sib_in(t).wait_send()
+        for s in range(3):
+            for n in range(2):
+                sib_in(t, s, n).wait_send()
     when(x == 0, lambda: NX.wait_send())
     when(jnp.logical_and(x == 1, y == 0), lambda: NY.wait_send())
     when(jnp.logical_and(line, z < 3), lambda: NZ.wait_send())
@@ -1071,33 +1124,26 @@
 
     when(last_line, norm_last)
     grad_out(3).wait()
+    share.wait_recv()
+    flatten(1 - c, lambda rows, cols: theirs[rows, cols])
     share.wait_send()
-    oth = pl.ds(pl.multiple_of((1 - c) * HALF, 16), HALF)
-    remote(res(oth), res(oth), sib, share_s, share_r).wait_recv()
-
-    spread = jnp.logical_or(z == 1, z == 2)
-    for n in range(6):
-        cols = pl.ds(n * 128, 128)
-
-        def plain():
-            flat[pl.ds(n, D, stride=6)] = dist[pl.ds(0, D), cols]
-
-        def swapped():
-            for j in range(4):
-                flat[pl.ds(j * 6 + n, D // 4, stride=24)] = dist[pl.ds(j * (D // 4), D // 4), cols]
-
-        when(jnp.logical_not(spread), plain)
-        when(spread, swapped)
-        when(i == 15, lambda: flat.__setitem__((pl.ds(6 * D + n, 4, stride=6), slice(None)), nacc[:, cols]))
-
-    head_rows, after = pl.ds(0, 24), pl.ds(6 * D, 24)
+    body, head_rows, after = pl.ds(0, 6 * D), pl.ds(0, 24), pl.ds(6 * D, 24)
+    leave = pltpu.make_async_copy(flat.at[body], flat_out.at[body], o_sem.at[0])
+    leave.start()
+
+    def ending():
+        for n in range(6):
+            flat[pl.ds(6 * D + n, 4, stride=6)] = nacc[:, pl.ds(n * 128, 128)]
+
+    when(i == 15, ending)
     give = remote(flat.at[head_rows], flat.at[after], (c, i - 1), aft_s, aft_r)
     when(i > 0, lambda: give.start())
     when(i < 15, lambda: give.wait_recv())
-    leave = pltpu.make_async_copy(flat, flat_out, o_sem)
-    leave.start()
+    leave_after = pltpu.make_async_copy(flat.at[after], flat_out.at[after], o_sem.at[1])
+    leave_after.start()
     when(i > 0, lambda: give.wait_send())
     leave.wait()
+    leave_after.wait()
 
 
 def enter_more(i, c, z, y, x):
@@ -1117,30 +1163,30 @@
     pl.semaphore_wait(barrier, 3 + jnp.minimum(z, 1) + jnp.minimum(3 - z, 1) + more)
 
 
-def reduce_back(wide, down, w, qkv, dO, mixb, lse, tokT, gbranch, first, norms, seg):
+def reduce_back(wide, down, w, qkv, dO, mixb, probs, tokT, gbranch, first, norms):
     Q = pltpu.SemaphoreType.DMA
     V = lambda *s: pltpu.VMEM(s, bf16)
     F = lambda *s: pltpu.VMEM(s, f32)
     A = pl.BlockSpec(memory_space=pl.ANY)
     return pl.pallas_call(
         reduce_back_kernel,
-        in_specs=[A, A, A, A, VM, VM, VM, VM, VM, A, VM, VM, VM],
+        in_specs=[A] * 10 + [VM],
         out_specs=[A, A],
         out_shape=[jax.ShapeDtypeStruct((LEN, D), f32), jax.ShapeDtypeStruct((6 * D + 24, 128), f32)],
         scratch_shapes=[
             V(4, 2, 2, HALF, D), V(4, 2, 2, HALF, D), V(9, 2, C_PART, D), V(9, C_PART, D), V(9, C_PART, D),
             V(3, C_PART, D), V(9, 2, B_PART, D), V(9, 2, B_PART, D), V(3, 2, B_PART, D), V(3, B_PART, D),
             V(8, 2, Q_PART, COLS), V(8, Q_PART, COLS), V(8, Q_PART, COLS), V(8, HALF, COLS),
-            F(LEN, LEN), V(LEN, LEN), V(LEN, LEN), V(D, D), V(3, D, LEN),
+            V(D, LEN), V(D, LEN), V(D, LEN), V(LEN, D), V(HALF, D), V(2, LEN, LEN), V(LEN, LEN), V(D, D), V(3, D, LEN),
             F(256, D), F(6 * D + 24, 128), F(4, D), F(4, D), F(4, D), F(4, D), F(4, D),
-            Q((4,)), Q, Q((3,)), Q, Q, Q, Q((4,)), Q((4,)), Q((8,)), Q((8,)),
+            Q((4,)), Q((5,)), Q((2,)), Q((3,)), Q, Q, Q((2,)), Q((18,)), Q((18,)), Q((8,)), Q((8,)),
             *[Q((9,))] * 14, Q((3,)), Q((3,)), *[Q((8,))] * 6, Q((4,)), Q((4,)), Q, Q, Q, Q,
         ],
         compiler_params=pltpu.CompilerParams(
             collective_id=2, has_side_effects=True, vmem_limit_bytes=62 << 20
         ),
         name="reduce_back",
-    )(wide, down, w, qkv, dO, mixb, lse, tokT, gbranch, first, norms, seg.reshape(LEN, 1), seg.reshape(1, LEN))
+    )(wide, down, w, qkv, dO, mixb, probs, tokT, gbranch, first, norms)
 
 SQUARE = D * D
 TAIL = 4 * D
@@ -1172,8 +1218,7 @@
     if count == 16:
         padded = jnp.pad(last.reshape(4, D), ((0, 12), (0, 0)))
         block = swap_wide(block.reshape(D, D), index)
-        blocks, tail, *attended = gather_attend(block, padded, tokens, segments)
-        norms = tail[:4].astype(f32)
+        blocks, norms, *attended = gather_attend(block, padded, tokens, segments)
     else:
         natural = lax.all_gather(block.reshape(-1, D), "zero", axis=0, tiled=True)
         parts = natural.reshape(4, 4 * D, D)
@@ -1184,19 +1229,19 @@
     return blocks, norms, *attended
 
 
-def back_and_scatter(blocks, segments, tokT, qkv, mixed, log_sum, grad_mixed, first_grad, branch_grad, norm_grads,
+def back_and_scatter(blocks, tokT, qkv, mixed, probs, grad_mixed, first_grad, branch_grad, norm_grads,
                      down_grad, wide_grad):
     count = lax.axis_size("zero")
     index = lax.axis_index("zero")
     if count == 16:
         input_grad, joined = reduce_back(
-            wide_grad, down_grad, blocks, qkv, grad_mixed, mixed, log_sum, tokT, branch_grad, first_grad,
-            norm_grads, segments,
+            wide_grad, down_grad, blocks, qkv, grad_mixed, mixed, probs, tokT, branch_grad, first_grad,
+            norm_grads,
         )
         joined = joined.reshape(-1)
     else:
         square, input_grad = attend_back(
-            blocks, segments, tokT, qkv, mixed, log_sum, grad_mixed, first_grad, branch_grad
+            blocks, tokT, qkv, mixed, probs, grad_mixed, first_grad, branch_grad
         )
         natural = [from_wide(wide_grad[k]).reshape(4 * D, D) for k in (0, 1)]
         natural = jnp.concatenate([square.reshape(4 * D, D), *natural, down_grad.reshape(4 * D, D)])
@@ -1211,12 +1256,12 @@
 
 
 def local(tokens, segments, cotangent, master, moment_one, moment_two):
-    blocks, norms, tokT, qkv, mixed, log_sum = gather_and_attend(master, tokens, segments)
+    blocks, norms, tokT, qkv, mixed, probs = gather_and_attend(master, tokens, segments)
     output, first_grad, grad_mixed, branch_grad, norm_grads, down_grad, wide_grad = feed(
         tokens, cotangent, mixed, blocks, norms
     )
     input_grad, grad_shard = back_and_scatter(
-        blocks, segments, tokT, qkv, mixed, log_sum, grad_mixed, first_grad, branch_grad, norm_grads,
+        blocks, tokT, qkv, mixed, probs, grad_mixed, first_grad, branch_grad, norm_grads,
         down_grad.reshape(2, 2, D, D), wide_grad.reshape(2, 2, 2, D, D),
     )
     grad_shard = grad_shard / (lax.axis_size("zero") * lax.axis_size("dp"))

time: 309 us -> 301 us (0.974)
  Pallas kernels: 276 us -> 270 us
    pallas_call x1, Pallas kernels: 110 us -> 106 us  [reduce_back(): pl.pallas_call(reduce_back_kernel, in_specs=[A] * 10 + [VM], out_specs=[A...]
where the time goes in v8:
time: 301 us; the launch traced here: 296 us
  Pallas kernels  270 us (90%)
  other arithmetic  14.2 us (5%)
  local copies, waits for them, and re-layouts  5.08 us (2%)
  starting transfers between devices  3.39 us (1%)
    pallas_call x1, Pallas kernels, reduce_back(): pl.pallas_call(reduce_back_kernel, in_specs=[A] * 10 + [VM], out_specs=[A...  106 us
    pallas_call x1, Pallas kernels, gather_attend(): pl.pallas_call(gather_attend_kernel, in_specs=[any_space, VM, VM, VM, VM]...  88.1 us
    pallas_call x1, Pallas kernels, feed(): pl.pallas_call(feed_kernel, grid=(n + 12,), in_specs=[pl.BlockSpec((TB, D...  76.4 us
    convert_element_type x1, other arithmetic, local(): master_new.astype(jnp.bfloat16)  10.2 us
  transfers between devices with their start and end apart: 1, of which 1 were waited for; matrix products, arithmetic and copies ran while one was open for 1% of the time, Pallas kernels for 0%

profile of v8, /device:TPU:8, one launch (start us, length us, event | category | flops | bytes accessed | tf_op | source)
XLA Modules:
  0.0 295.7 jit_solution(17530680373176244740)
XLA Ops:
  0.6 0.0 copy-start.1
  0.6 1.8 convert_element_type.8
  2.4 0.1 slice.4
  2.5 3.4 %collective-permute-start = (bf16[3072]{0:T(1024)(128)(2,1)S(1)}, bf16[3072]{0:T(1024)(128)(2,1)S(1)}, u32[]{:S(2)}, u32[]{:S(2)}) collective-permute-start(bf16[3072]{0:T(1024)(128)(2,1)S(1)} %slice.4), channel_id=1, source_target_pairs={{0,1},{1,2},{2,3},{3,4},{4,5},{5,6},{6,7},{7,8},{8,9},{9,10},{10,1... | collective-permute-start | bytes 18440 | tf_op jit(solution)/shard_map/ppermute | solution.py:1215
  5.9 0.0 copy-done.1
  5.9 1.0 copy.14.seg_col
  7.0 0.6 pad.4.last
  7.6 2.2 collective-permute-done
  9.8 1.0 fusion
  10.8 0.5 reshape_reshape.3
  11.3 1.1 reshape.42
  12.4 0.1 copy.13
  12.5 1.2 bitcast_select_fusion.blk
  13.7 88.1 %gather_attend.1 = (bf16[4,2,2,768,768]{4,3,2,1,0:T(8,128)(2,1)}, f32[4,768]{1,0:T(4,128)}, bf16[768,1024]{1,0:T(8,128)(2,1)}, bf16[3,768,1024]{2,1,0:T(8,128)(2...) custom-call(bf16[768,768]{1,0:T(8,128)(2,1)} %bitcast_select_fusion.blk, bf16[16,768]{1,0:T(8,128)(2,1)} %pad.4.last, ...), custom_call_target="tpu_custom_call" | custom-call | tf_op jit(solution)/shard_map/gather_attend/pallas_call | solution.py:631
  101.8 76.4 %feed.1 = (bf16[1024,768]{1,0:T(8,128)(2,1)}, f32[1024,768]{1,0:T(8,128)}, bf16[768,1024]{1,0:T(8,128)(2,1)}, bf16[1024,768]{1,0:T(8,128)(2,1)}, f32[4,768]{1,0:...) custom-call(bf16[1024,768]{1,0:T(8,128)(2,1)} %tokens.3, bf16[1024,768]{1,0:T(8,128)(2,1)} %cot.1, ...), custom_call_target="tpu_custom_call" | custom-call | tf_op jit(solution)/shard_map/feed/pallas_call | solution.py:220
  178.2 105.6 %reduce_back.1 = (f32[1024,768]{1,0:T(8,128)}, f32[4632,128]{1,0:T(8,128)}) custom-call(bf16[2,2,2,768,768]{4,3,2,1,0:T(8,128)(2,1)} %bitcast.10, bf16[2,2,768,768]{3,2,1,0:T(8,128)(2,1)} %bitcast.11, bf16[4,2,2,768,768]{4,3,2,1,0:T(8,128)(2,1)} %get-tuple-element.23.w, bf16[3,768,1024]{2,1,0:T(8,128)(2,1)} %get-tuple-element.28.qkv_in, ...), custom_call_target="tpu_custom_call" | custom-call | tf_op jit(solution)/shard_map/reduce_back/pallas_call | solution.py:1171
  283.8 0.0 copy-start
  283.8 10.2 %fusion.1 = (bf16[590016]{0:T(1024)(128)(2,1)}, f32[590016]{0:T(1024)}, f32[590016]{0:T(1024)}, f32[590016]{0:T(1024)}, f32[590016]{0:T(1024)}) fusion(f32[590016]{0:T(1024)} %param.9, f32[592896]{0:T(1024)} %bitcast.13, s32[]{:T(128)S(6)} %select_n.17, f32[590016]{0:T(1024)} %param.11, f32[590016]{0:T(1024)} %param.10), kind=kLoop, calls=%fused_computation.8 | loop fusion | flops 10030272 | bytes 20060548 | tf_op jit(solution)/shard_map/convert_element_type | solution.py:1279
  294.0 0.0 copy-done
  294.0 1.7 copy.16
  (1 shorter events, 0.0 us)
Async XLA Ops:
  0.6 5.3 %copy-start.1 = (s32[1024]{0:T(1024)S(1)}, s32[1024]{0:T(1024)}, u32[]{:S(2)}) copy-start(s32[1024]{0:T(1024)} %param.7) | copy-start | bytes 12292
  2.5 7.3 %collective-permute-start = (bf16[3072]{0:T(1024)(128)(2,1)S(1)}, bf16[3072]{0:T(1024)(128)(2,1)S(1)}, u32[]{:S(2)}, u32[]{:S(2)}) collective-permute-start(bf16[3072]{0:T(1024)(128)(2,1)S(1)} %slice.4), channel_id=1, source_target_pairs={{0,1},{1,2},{2,3},{3,4},{4,5},{5,6},{6,7},{7,8},{8,9},{9,10},{10,1... | collective-permute-start | bytes 18440 | tf_op jit(solution)/shard_map/ppermute | solution.py:1215
  283.8 10.2 %copy-start = (f32[1024,768]{1,0:T(8,128)S(1)}, f32[1024,768]{1,0:T(8,128)}, u32[]{:S(2)}) copy-start(f32[1024,768]{1,0:T(8,128)} %get-tuple-element.50) | copy-start | bytes 9437188

commit v9 on v8

--- a/solution.py
+++ b/solution.py
@@ -37,14 +37,15 @@
 def slope(h):
     return jnp.exp2(-8.0/HEADS*(jnp.full((1,1),h,jnp.int32).astype(f32)+1.0))
 
-def fill_distance(dist,seg_col,seg_row):
+def fill_distance(dist,seg_row,column):
+    column[...]=jnp.broadcast_to(seg_row[...].astype(f32),(8,LEN)).T
     @pl.loop(0,LEN//128)
     def _(k):
         r=pl.ds(pl.multiple_of(k*128,128),128)
         kk=(lax.broadcasted_iota(jnp.int32,(128,LEN),0)+k*128)
         qq=lax.broadcasted_iota(jnp.int32,(128,LEN),1)
         d=jnp.abs(kk-qq).astype(f32)
-        dist[r]=jnp.where(seg_col[r]==seg_row[...],d,FAR)
+        dist[r]=jnp.where(column[r,0:1]==seg_row[...].astype(f32),d,FAR)
 
 QB=256
 def project_all(w,tokT,qkv):
@@ -83,9 +84,9 @@
     qkv[1,rows]=grad_k
     qkv[2,rows]=grad_v
 
-def attend_kernel(tokens,w,seg_col,seg_row,tokT,qkv,mixb,probs_out,dist,probs,sem):
+def attend_kernel(tokens,w,seg_row,tokT,qkv,mixb,probs_out,dist,column,probs,sem):
     tokT[...]=tokens[...].astype(f32).T.astype(bf16)
-    fill_distance(dist,seg_col,seg_row)
+    fill_distance(dist,seg_row,column)
     project_all(w,tokT,qkv)
     @pl.loop(0,HEADS)
     def _(h):
@@ -102,10 +103,10 @@
 
 def attend(tokens,w,seg):
     return pl.pallas_call(attend_kernel,grid=(1,),
-        in_specs=[VM,pl.BlockSpec((1,2,2,D,D),lambda i:(0,0,0,0,0)),VM,VM],out_specs=[VM]*3+[ANY],
+        in_specs=[VM,pl.BlockSpec((1,2,2,D,D),lambda i:(0,0,0,0,0)),VM],out_specs=[VM]*3+[ANY],
         out_shape=attend_shapes(),
-        scratch_shapes=[pltpu.VMEM((LEN,LEN),f32),pltpu.VMEM((LEN,LEN),bf16),pltpu.SemaphoreType.DMA],
-        compiler_params=pltpu.CompilerParams(vmem_limit_bytes=58<<20),name="attend")(tokens,w,seg.reshape(LEN,1),seg.reshape(1,LEN))
+        scratch_shapes=[pltpu.VMEM((LEN,LEN),f32),pltpu.VMEM((LEN,8),f32),pltpu.VMEM((LEN,LEN),bf16),pltpu.SemaphoreType.DMA],
+        compiler_params=pltpu.CompilerParams(vmem_limit_bytes=58<<20),name="attend")(tokens,w,seg.reshape(1,LEN))
 
 def attend_back_kernel(w,tokT,qkv_in,mixb,probs_in,dO,first,gbranch,g0,grad_in,qkv,probs,ds_all,sem,qkv_sem):
     take=pltpu.make_async_copy(qkv_in,qkv,qkv_sem)
@@ -165,20 +166,26 @@
         l1=n1*gain1+shift1
         inner[rows]=l1.astype(bf16)
         acc[...]=l1
-        @pl.loop(0,4,unroll=2)
-        def _(j):
+        @pl.loop(0,2)
+        def _(n):
+            js=(2*n,2*n+1)
             @pl.when(step==0)
             def _():
-                for p in (1,2,3): load(p,j).wait()
+                for j in js:
+                    for p in (1,2,3): load(p,j).wait()
             inn=inner[rows]
-            ga=dot(inn,W(1,j)); up=dot(inn,W(2,j))
-            cum=0.5*(1.0+lax.erf(ga*inv_root_two))
-            gel=ga*cum
-            fb[j]=gel
-            fa[j]=up*(cum+ga*(jnp.exp(-0.5*ga*ga)*inv_root_tau))
-            h=(gel*up).astype(bf16)
-            hid[j,rows]=h
-            acc[...]+=dot(h,WD(j))
+            sides=[(dot(inn,W(1,j)),dot(inn,W(2,j))) for j in js]
+            total=None
+            for j,(ga,up) in zip(js,sides):
+                cum=0.5*(1.0+lax.erf(ga*inv_root_two))
+                gel=ga*cum
+                fb[j]=gel
+                fa[j]=up*(cum+ga*(jnp.exp(-0.5*ga*ga)*inv_root_tau))
+                h=(gel*up).astype(bf16)
+                hid[j,rows]=h
+                part=dot(h,WD(j))
+                total=part if total is None else total+part
+            acc[...]+=total
         n2,r2=stats(acc[...])
         output[...]=(n2*gain2+shift2).astype(bf16)
         c=cot[...].astype(f32)
@@ -187,12 +194,17 @@
         mid=back(c*gain2,n2,r2)
         gffn[rows]=mid.astype(bf16)
         acc[...]=mid
-        @pl.loop(0,4,unroll=2)
-        def _(j):
-            gh=dot_nt(gffn[rows],WD(j))
-            a=(gh*fa[j]).astype(bf16); b=(gh*fb[j]).astype(bf16)
-            wide[j,rows]=a; wide[4+j,rows]=b
-            acc[...]+=dot_nt(a,W(1,j))+dot_nt(b,W(2,j))
+        @pl.loop(0,2)
+        def _(n):
+            js=(2*n,2*n+1)
+            ghs=[dot_nt(gffn[rows],WD(j)) for j in js]
+            total=None
+            for j,gh in zip(js,ghs):
+                a=(gh*fa[j]).astype(bf16); b=(gh*fb[j]).astype(bf16)
+                wide[j,rows]=a; wide[4+j,rows]=b
+                part=dot_nt(a,W(1,j))+dot_nt(b,W(2,j))
+                total=part if total is None else total+part
+            acc[...]+=total
         gl=acc[...]
         ng[0:1]+=jnp.sum(gl*n1,0,keepdims=True)
         ng[1:2]+=jnp.sum(gl,0,keepdims=True)
@@ -304,15 +316,27 @@
     lax.cond(kind < low + half, lower, upper)
 
 
-def gather_attend_kernel(blk, last, tokens, seg_col, seg_row, result, norms, tokT_out, qkv_out, mixb, probs_out,
-                         held, dist, tail, tokT, qkv, probs, own_sem, out_sem, t_sem, q_sem, p_sem, pzs, pzr, pfs, pfr, pgs, pgr, p_s, p_r,
+def gather_attend_kernel(blk, last, tokens, seg_row, result, norms, tokT_out, qkv_out, mixb, probs_out,
+                         held, dist, column, tail, tokT, qkv, probs, out_sem, t_sem, q_sem, p_sem, pzs, pzr, pfs, pfr, pgs, pgr, p_s, p_r,
                          b1s, b1r, c1u, c1d, c1r, b2u, b2d, b2r, c2s, c2r, b3s, b3r, c3s, c3r, ss, sr, ts, tr):
     i, c, z, y, x = place()
     xp, yp, sib, up, down = partners(i, c, z, y, x)
     half = c * HALF
     other = (1 - c) * HALF
-    local = pltpu.make_async_copy(blk, held.at[z, y, x], own_sem)
-    local.start()
+    spread = jnp.logical_or(z == 1, z == 2)
+
+    def plain():
+        for n in range(6):
+            held[z, y, x, :, pl.ds(n * 128, 128)] = blk[pl.ds(n, D, stride=6)].astype(bf16)
+
+    def swapped():
+        for n in range(6):
+            for j in range(4):
+                value = blk[pl.ds(j * 6 + n, D // 4, stride=24)].astype(bf16)
+                held[z, y, x, pl.ds(j * (D // 4), D // 4), pl.ds(n * 128, 128)] = value
+
+    when(jnp.logical_not(spread), plain)
+    when(spread, swapped)
     enter(i, c, z, y, x)
 
     def remote(ref, peer, s, r):
@@ -549,15 +573,19 @@
         def prepare():
             tokT[...] = tokens[...].astype(f32).T.astype(bf16)
             tokT_leaves.start()
-            fill_distance(dist, seg_col, seg_row)
+            fill_distance(dist, seg_row, column)
 
         when(e == 0, tail_z)
         when(e == 1, tail_x)
         when(jnp.logical_and(e >= 2, e < 6), out)
         when(e == 6, prepare)
 
-    when(source, lambda: tail.__setitem__(Ellipsis, last[...]))
-    local.wait()
+    def norms_here():
+        for n in range(6):
+            tail[pl.ds(0, 4), pl.ds(n * 128, 128)] = last[pl.ds(n, 4, stride=6)].astype(bf16)
+
+    tail[...] = jnp.zeros_like(tail)
+    when(source, norms_here)
     run_plan(z, GATHER_PLAN, [op_p0z, op_p0f, op_p0g, op_own, op_ownup, op_b1, op_bx, op_c1, op_b2, op_c2, op_b3,
                               op_c3, op_proj, op_head, op_other, op_cx])
 
@@ -630,76 +658,77 @@
     counts = [8] * 6 + [24, 24, 3, 3] + [9] * 12 + [48, 48, 3, 1]
     return pl.pallas_call(
         gather_attend_kernel,
-        in_specs=[any_space, VM, VM, VM, VM],
+        in_specs=[VM, VM, VM, VM],
         out_specs=[any_space, VM, any_space, any_space, VM, any_space],
         out_shape=[
             jax.ShapeDtypeStruct((4, 2, 2, D, D), bf16), jax.ShapeDtypeStruct((4, D), f32),
             *attend_shapes(),
         ],
         scratch_shapes=[
-            pltpu.VMEM((4, 2, 2, D, D), bf16), pltpu.VMEM((LEN, LEN), f32), pltpu.VMEM((16, D), bf16),
+            pltpu.VMEM((4, 2, 2, D, D), bf16), pltpu.VMEM((LEN, LEN), f32), pltpu.VMEM((LEN, 8), f32),
+            pltpu.VMEM((16, D), bf16),
             pltpu.VMEM((D, LEN), bf16), pltpu.VMEM((3, D, LEN), bf16), pltpu.VMEM((2, LEN, LEN), bf16),
-            Q, Q((4,)), Q, Q((3,)), Q((2,)), *[Q((n,)) for n in counts],
+            Q((4,)), Q, Q((3,)), Q((2,)), *[Q((n,)) for n in counts],
         ],
         compiler_params=pltpu.CompilerParams(
             collective_id=1, has_side_effects=True, vmem_limit_bytes=58 << 20
         ),
         name="gather_attend",
-    )(blk, last, tokens, seg.reshape(LEN, 1), seg.reshape(1, LEN))
+    )(blk, last, tokens, seg.reshape(1, LEN))
 
 
 PLANE_ORDER = (1, 2, 3)
 BACK_PLAN = (
     (
-        7374723, 131328, 263025, 14681376, 4198406, 4261665, 1122930, 7553544, 7619363, 4461092,
-        7685413, 8393510, 5255297, 4592770, 3221366, 1413201, 9605601, 2659143, 3307336, 7870034,
-        3429171, 7935828, 8017205, 8067233, 14853024, 10630788, 8815958, 11622199, 3723443, 13742168,
-        13882034, 9868692, 12632471, 12756388, 10987203, 12891317, 12957622, 15714246, 15724527,
+        7405680, 291331, 460403, 357748, 532515, 2369408, 4407315, 8484483, 2435092, 71206,
+        7816773, 8525688, 3359796, 3547527, 9442784, 1067094, 3641624, 168519, 9664833, 7999792,
+        5759611, 10585476, 14759989, 10651219, 2232916, 10523856, 9868632, 10768469, 9937841, 13713970,
+        5386672, 12628646, 13870546, 5351347, 11908278, 12961475, 12695492, 15714242, 15724527,
     ),
     (
-        7374723, 131328, 254065, 328736, 7475206, 2230049, 7541000, 1209379, 2454820, 1278016,
-        4400705, 8537217, 9467458, 9573521, 4532115, 1406760, 14776390, 4684054, 10557306, 14842696,
-        10688644, 8815968, 5255265, 5321058, 9868692, 5386903, 5452704, 3494964, 10630741, 3684182,
-        10835920, 13743025, 10797400, 12628135, 11708114, 12825794, 13875125, 12960950, 15714246,
+        33648, 225905, 263795, 329588, 8418784, 1472008, 7807782, 1053816, 8524673, 8026435,
+        2658325, 4624676, 8095489, 14819351, 8750144, 10523175, 9646152, 13637766, 3490887, 9806228,
+        2463286, 3658070, 13801285, 13869731, 5744036, 11644930, 2212148, 11773752, 12629336, 4317618,
+        12760149, 3392422, 12866594, 11952146, 1135557, 12010182, 3327841, 6443600, 15683889,
     ),
     (
-        7374723, 131328, 263025, 14681376, 7475206, 2230049, 7541000, 7611200, 4334657, 8418578,
-        2458241, 1257510, 2573174, 1347984, 7836562, 2634052, 7869776, 1459506, 4600697, 14766497,
-        8016407, 8079156, 1591459, 14836533, 8757380, 13645446, 9713570, 9868600, 11645079, 5488996,
-        6665138, 10801600, 12829349, 13784404, 11839398, 12867253, 11978195, 5752503, 15714136,
+        7405680, 197121, 7631730, 401425, 7701252, 8458880, 489009, 1081975, 4200056, 8855952,
+        9533704, 9580666, 8098594, 14816416, 1541281, 8802437, 9752642, 9840277, 4301362, 9941074,
+        11618344, 3614673, 4662179, 12654770, 14722468, 4596928, 10921938, 377523, 12825875, 12891190,
+        5683126, 12923971, 3692356, 13051334, 4542741, 13850849, 5530675, 5584229, 15688531,
     ),
     (
-        7374723, 131328, 263025, 14681376, 4198406, 4261665, 533106, 7553553, 7619363, 4461092,
-        7685413, 8552832, 5255206, 9442323, 9578385, 2651795, 3241749, 3307601, 5452626, 3438870,
-        8001364, 10714017, 10519778, 3507845, 14787126, 9802837, 9879985, 11580311, 3654592, 11707600,
-        10867138, 10998438, 11912372, 11933893, 12047302, 4671175, 5650504, 6842214, 15685719,
+        7405680, 225793, 7540738, 422944, 7763204, 8601619, 3154181, 2232951, 8471168, 2379906,
+        1131542, 4421667, 9512336, 4277650, 5386873, 10582675, 8062740, 10650850, 3245701, 8868256,
+        3446164, 11645603, 9875649, 9917632, 2598096, 12759973, 10998211, 12891302, 1422600, 13022917,
+        12050483, 5453511, 4605734, 1626647, 5580853, 13850184, 14759782, 5728104, 15685688,
     ),
 )
 
 GATHER_PLAN = (
     (
-        131328, 328707, 15075078, 1184016, 15757331, 7410964, 1513201, 2224754, 6324256, 7545379,
-        2396403, 2449793, 6455846, 16020625, 12697639, 9601986, 10548597, 11645027, 9687266, 13760118,
-        6594948, 10651090, 14922341, 13891447, 16283796, 9819315, 13985414, 8902307, 11822998, 8970455,
-        14182564, 14988709, 11966425, 10019290, 12035803, 12101799, 15724517, 15724527,
+        196870, 1026, 7406867, 7401746, 1050388, 15787542, 9443093, 2494834, 2303104, 9565557,
+        7631858, 2261281, 2127457, 9827248, 8529701, 9630912, 12748737, 16147091, 6788304, 8835793,
+        6330034, 16233847, 13924563, 16287189, 6674082, 14129073, 14182019, 6534048, 14247044, 8955874,
+        10007656, 14345121, 14399159, 14722211, 12101030, 15050980, 15724513, 15724527,
     ),
     (
-        3207664, 15086129, 5279744, 5308787, 156000, 7639378, 266243, 10487157, 8586928, 4196113,
-        10568257, 1315446, 1475761, 2196755, 1406752, 16127779, 16053239, 7926517, 6579192, 2253413,
-        6719013, 8857380, 2528871, 12763584, 9672584, 13689448, 13743764, 9622165, 14734263, 11785368,
-        14079395, 14136484, 10672293, 14279861, 14801574, 14922407, 12101851, 15724517,
+        3273200, 3289330, 5243142, 152067, 7704947, 327684, 1050387, 15941969, 4200210, 1143843,
+        1318933, 7770134, 8910310, 2565186, 7807525, 2225286, 6694646, 9658773, 16236992, 8616069,
+        8966338, 8675986, 14874833, 10596708, 13788564, 6526870, 14013651, 10934230, 14202008, 11755623,
+        10855528, 10729184, 14332633, 14987445, 11000759, 14917794, 15055016, 15724513,
     ),
     (
-        16119027, 3486771, 9655270, 5535331, 9721188, 30565, 7902465, 242434, 296611, 8889349,
-        504838, 4460867, 10848325, 1208336, 14988564, 1277974, 2168177, 16183319, 16316401, 6776416,
-        6390120, 7479331, 2237938, 2581122, 2527268, 12763584, 14848406, 9953488, 10015152, 11968722,
-        10933459, 14004705, 11064999, 10606519, 14258904, 10675640, 11721690, 15724515,
+        3535667, 9647348, 7800565, 7733589, 1442806, 1026, 460049, 4556582, 1184646, 16281976,
+        5444887, 1110408, 1369703, 9782128, 4478104, 8396839, 6694391, 9859732, 2355748, 2171522,
+        15753314, 8503744, 13681249, 14706897, 9556946, 11777426, 13919412, 14002021, 14063459, 14137521,
+        14276790, 10936976, 12049370, 10789544, 15048865, 11576739, 14935218, 15724513,
     ),
     (
-        16316406, 3684150, 9852646, 6772582, 6854488, 11927704, 173569, 12035843, 11011332, 462854,
-        4670994, 15054920, 7541777, 1381142, 2105731, 15931252, 2319348, 2253956, 16086309, 8726308,
-        2528101, 12763584, 10715360, 15757460, 6353265, 13677538, 10781153, 9818465, 13824626, 6455973,
-        9491380, 11899348, 10540516, 10596566, 9623767, 10672561, 11721690, 15724515,
+        16266807, 9976055, 9958998, 419415, 66151, 12059670, 239192, 458769, 1226501, 8721427,
+        2166807, 4617510, 1405255, 2418343, 15738736, 2302705, 16085832, 2487141, 2135656, 12697824,
+        9552528, 7655888, 13820291, 13890709, 13926514, 6521986, 8508914, 11625620, 14049939, 11917219,
+        11821528, 11970656, 9613529, 14867109, 10673060, 11772389, 11706596, 15724515,
     ),
 )
 
@@ -1183,7 +1212,7 @@
             *[Q((9,))] * 14, Q((3,)), Q((3,)), *[Q((8,))] * 6, Q((4,)), Q((4,)), Q, Q, Q, Q,
         ],
         compiler_params=pltpu.CompilerParams(
-            collective_id=2, has_side_effects=True, vmem_limit_bytes=62 << 20
+            collective_id=2, has_side_effects=True, vmem_limit_bytes=55 << 20
         ),
         name="reduce_back",
     )(wide, down, w, qkv, dO, mixb, probs, tokT, gbranch, first, norms)
@@ -1198,33 +1227,26 @@
 
 def to_wide(value):
     return value.reshape(4, D // 4, 4, D).transpose(0, 2, 1, 3).reshape(2, 2, D, D)
-
-
-def swap_wide(block, index):
-    swapped = block.reshape(D // 4, 4, D).transpose(1, 0, 2).reshape(D, D)
-    wide = jnp.logical_and(index >= 4, index < 12)
-    return jnp.where(wide, swapped, block)
 
 
 def gather_and_attend(master, tokens, segments):
     count = lax.axis_size("zero")
     index = lax.axis_index("zero")
     size = 16 * SQUARE // count
-    weights = master.astype(bf16)
-    last = weights[-TAIL:]
+    last = master[-TAIL:]
     before = lax.ppermute(last, "zero", [(k, k + 1) for k in range(count - 1)])
-    joined = jnp.concatenate([before, weights])
+    joined = jnp.concatenate([before, master])
     block = lax.dynamic_slice(joined, (TAIL - TAIL // count * index,), (size,))
     if count == 16:
-        padded = jnp.pad(last.reshape(4, D), ((0, 12), (0, 0)))
-        block = swap_wide(block.reshape(D, D), index)
-        blocks, norms, *attended = gather_attend(block, padded, tokens, segments)
+        block, last = block.reshape(6 * D, 128), last.reshape(24, 128)
+        blocks, norms, *attended = gather_attend(block, last, tokens, segments)
     else:
-        natural = lax.all_gather(block.reshape(-1, D), "zero", axis=0, tiled=True)
+        natural = lax.all_gather(block.astype(bf16).reshape(-1, D), "zero", axis=0, tiled=True)
         parts = natural.reshape(4, 4 * D, D)
         wide = [to_wide(parts[k].reshape(D, FF)) for k in (1, 2)]
         blocks = jnp.stack([parts[0].reshape(2, 2, D, D), *wide, parts[3].reshape(2, 2, D, D)])
-        norms = lax.psum(jnp.where(index == count - 1, last.astype(f32), 0.0), "zero").reshape(4, D)
+        last = last.astype(bf16).astype(f32)
+        norms = lax.psum(jnp.where(index == count - 1, last, 0.0), "zero").reshape(4, D)
         attended = attend(tokens, blocks, segments)
     return blocks, norms, *attended
 

time: 301 us -> 283 us (0.940)
  Pallas kernels: 270 us -> 257 us
    pallas_call x1, Pallas kernels: 106 us -> 97.5 us  [reduce_back(): pl.pallas_call(reduce_back_kernel, in_specs=[A] * 10 + [VM], out_specs=[A...]
    reshape x0 -> x1, other arithmetic: none -> 3.83 us  [gather_and_attend(): block, last = (block.reshape(6 * D, 128), last.reshape(24, 128))]
    pallas_call x1, Pallas kernels: 88.1 us -> 84.5 us  [gather_attend(): pl.pallas_call(gather_attend_kernel, in_specs=[VM, VM, VM, VM], out_specs...]
  transfers between devices with their start and end apart: 1 -> 1, of which waited for: 1 -> 1; matrix products, arithmetic and copies ran while one was open for 1% -> 0% of each run, Pallas kernels for 0% -> 0%
where the time goes in v9:
time: 283 us; the launch traced here: 280 us
  Pallas kernels  257 us (91%)
  other arithmetic  12 us (4%)
  waiting for transfers between devices  3.97 us (1%)
  starting transfers between devices  3.39 us (1%)
  local copies, waits for them, and re-layouts  3.08 us (1%)
    pallas_call x1, Pallas kernels, reduce_back(): pl.pallas_call(reduce_back_kernel, in_specs=[A] * 10 + [VM], out_specs=[A...  97.5 us
    pallas_call x1, Pallas kernels, gather_attend(): pl.pallas_call(gather_attend_kernel, in_specs=[VM, VM, VM, VM], out_specs...  84.5 us
    pallas_call x1, Pallas kernels, feed(): pl.pallas_call(feed_kernel, grid=(n + 12,), in_specs=[pl.BlockSpec((TB, D...  74.5 us
    convert_element_type x1, other arithmetic, local(): master_new.astype(jnp.bfloat16)  8.16 us
  transfers between devices with their start and end apart: 1, of which 1 were waited for; matrix products, arithmetic and copies ran while one was open for 0% of the time, Pallas kernels for 0%

profile of v9, /device:TPU:8, one launch (start us, length us, event | category | flops | bytes accessed | tf_op | source)
XLA Modules:
  0.0 279.7 jit_solution(1529838563539877098)
XLA Ops:
  0.6 1.4 slice_bitcast_fusion
  2.0 3.4 %collective-permute-start = (f32[3072]{0:T(1024)S(1)}, f32[3072]{0:T(1024)S(1)}, u32[]{:S(2)}, u32[]{:S(2)}) collective-permute-start(f32[3072]{0:T(1024)S(1)} %get-tuple-element.43), channel_id=1, source_target_pairs={{0,1},{1,2},{2,3},{3,4},{4,5},{5,6},{6,7},{7,8},{8,9},{9,10},{10,1... | collective-permute-start | bytes 36872 | tf_op jit(solution)/shard_map/ppermute | solution.py:1237
  5.4 4.0 %collective-permute-done = f32[3072]{0:T(1024)S(1)} collective-permute-done((f32[3072]{0:T(1024)S(1)}, f32[3072]{0:T(1024)S(1)}, u32[]{:S(2)}, u32[]{:S(2)}) %collective-permute-start) | collective-permute-done | bytes 12320 | tf_op jit(solution)/shard_map/ppermute | solution.py:1237
  9.4 3.8 %fusion.1.blk = f32[4608,128]{1,0:T(8,128)} fusion(s32[]{:T(128)S(6)} %select_n.6, f32[3072]{0:T(1024)S(1)} %collective-permute-done, f32[590016]{0:T(1024)} %param.9), kind=kLoop, calls=%fused_computation.6 | loop fusion | flops 589824 | bytes 4731652 | tf_op jit(solution)/shard_map/reshape | solution.py:1241
  13.2 84.5 %gather_attend.1 = (bf16[4,2,2,768,768]{4,3,2,1,0:T(8,128)(2,1)}, f32[4,768]{1,0:T(4,128)}, bf16[768,1024]{1,0:T(8,128)(2,1)}, bf16[3,768,1024]{2,1,0:T(8,128)(2...) custom-call(f32[4608,128]{1,0:T(8,128)} %fusion.1.blk, f32[24,128]{1,0:T(8,128)} %get-tuple-element.42.last, ...), custom_call_target="tpu_custom_call" | custom-call | tf_op jit(solution)/shard_map/gather_attend/pallas_call | solution.py:659
  97.8 74.5 %feed.1 = (bf16[1024,768]{1,0:T(8,128)(2,1)}, f32[1024,768]{1,0:T(8,128)}, bf16[768,1024]{1,0:T(8,128)(2,1)}, bf16[1024,768]{1,0:T(8,128)(2,1)}, f32[4,768]{1,0:...) custom-call(bf16[1024,768]{1,0:T(8,128)(2,1)} %tokens.3, bf16[1024,768]{1,0:T(8,128)(2,1)} %cot.1, ...), custom_call_target="tpu_custom_call" | custom-call | tf_op jit(solution)/shard_map/feed/pallas_call | solution.py:232
  172.3 0.0 copy-start
  172.3 0.0 copy-start.2
  172.3 0.0 copy-start.3
  172.3 97.5 %reduce_back.1 = (f32[1024,768]{1,0:T(8,128)}, f32[4632,128]{1,0:T(8,128)}) custom-call(bf16[2,2,2,768,768]{4,3,2,1,0:T(8,128)(2,1)} %bitcast.10, bf16[2,2,768,768]{3,2,1,0:T(8,128)(2,1)} %bitcast.11, bf16[4,2,2,768,768]{4,3,2,1,0:T(8,128)(2,1)} %get-tuple-element.23.w, bf16[3,768,1024]{2,1,0:T(8,128)(2,1)} %get-tuple-element.28.qkv_in, ...), custom_call_target="tpu_custom_call" | custom-call | tf_op jit(solution)/shard_map/reduce_back/pallas_call | solution.py:1200
  269.8 0.0 copy-done
  269.8 0.0 copy-done.2
  269.8 0.0 copy-done.3
  269.8 0.0 copy-start.1
  269.8 8.2 %fusion.2 = (bf16[590016]{0:T(1024)(128)(2,1)}, f32[590016]{0:T(1024)}, f32[590016]{0:T(1024)}, f32[590016]{0:T(1024)}, f32[590016]{0:T(1024)}) fusion(f32[590016]{0:T(1024)S(1)} %copy-done, f32[592896]{0:T(1024)} %bitcast.12, s32[]{:T(128)S(6)} %select_n.7, f32[590016]{0:T(1024)S(1)} %copy-done.2, f32[590016]{0:T(1024)S(1)} %copy-done.3), kind=kLoop, calls=%fused_computation.9 | loop fusion | flops 10030272 | bytes 20060548 | tf_op jit(solution)/shard_map/convert_element_type | solution.py:1301
  278.0 0.0 copy-done.1
  278.0 1.7 copy.14
Async XLA Ops:
  2.0 7.4 %collective-permute-start = (f32[3072]{0:T(1024)S(1)}, f32[3072]{0:T(1024)S(1)}, u32[]{:S(2)}, u32[]{:S(2)}) collective-permute-start(f32[3072]{0:T(1024)S(1)} %get-tuple-element.43), channel_id=1, source_target_pairs={{0,1},{1,2},{2,3},{3,4},{4,5},{5,6},{6,7},{7,8},{8,9},{9,10},{10,1... | collective-permute-start | bytes 36872 | tf_op jit(solution)/shard_map/ppermute | solution.py:1237
  172.3 97.5 %copy-start = (f32[590016]{0:T(1024)S(1)}, f32[590016]{0:T(1024)}, u32[]{:S(2)}) copy-start(f32[590016]{0:T(1024)} %param.9) | copy-start | bytes 7080196
  172.3 97.5 %copy-start.2 = (f32[590016]{0:T(1024)S(1)}, f32[590016]{0:T(1024)}, u32[]{:S(2)}) copy-start(f32[590016]{0:T(1024)} %param.11) | copy-start | bytes 7080196
  172.3 97.5 %copy-start.3 = (f32[590016]{0:T(1024)S(1)}, f32[590016]{0:T(1024)}, u32[]{:S(2)}) copy-start(f32[590016]{0:T(1024)} %param.10) | copy-start | bytes 7080196
  269.8 8.2 %copy-start.1 = (f32[1024,768]{1,0:T(8,128)S(1)}, f32[1024,768]{1,0:T(8,128)}, u32[]{:S(2)}) copy-start(f32[1024,768]{1,0:T(8,128)} %get-tuple-element.52) | copy-start | bytes 9437188

commit v10 on v9

--- a/solution.py
+++ b/solution.py
@@ -316,24 +316,35 @@
     lax.cond(kind < low + half, lower, upper)
 
 
-def gather_attend_kernel(blk, last, tokens, seg_row, result, norms, tokT_out, qkv_out, mixb, probs_out,
-                         held, dist, column, tail, tokT, qkv, probs, out_sem, t_sem, q_sem, p_sem, pzs, pzr, pfs, pfr, pgs, pgr, p_s, p_r,
+def gather_attend_kernel(blk, before, last, tokens_in, seg_row, result, norms, tokT_out, qkv_out, mixb, probs_out,
+                         held, dist, column, tokens, tail, tokT, qkv, probs, tok_sem, out_sem, t_sem, q_sem, p_sem, pzs, pzr, pfs, pfr, pgs, pgr, p_s, p_r,
                          b1s, b1r, c1u, c1d, c1r, b2u, b2d, b2r, c2s, c2r, b3s, b3r, c3s, c3r, ss, sr, ts, tr):
     i, c, z, y, x = place()
     xp, yp, sib, up, down = partners(i, c, z, y, x)
     half = c * HALF
     other = (1 - c) * HALF
+    tokens_come = pltpu.make_async_copy(tokens_in, tokens, tok_sem)
+    tokens_come.start()
     spread = jnp.logical_or(z == 1, z == 2)
 
     def plain():
         for n in range(6):
-            held[z, y, x, :, pl.ds(n * 128, 128)] = blk[pl.ds(n, D, stride=6)].astype(bf16)
+            cols = pl.ds(n * 128, 128)
+            held[z, y, x, :, cols] = blk[pl.ds(n, D, stride=6)].astype(bf16)
+            held[z, y, x, pl.ds(0, 16), cols] = (
+                blk[pl.ds(n, 16, stride=6)] + before[pl.ds(n, 16, stride=6)]
+            ).astype(bf16)
 
     def swapped():
+        top = lax.broadcasted_iota(jnp.int32, (16, 128), 0) == 0
         for n in range(6):
+            cols = pl.ds(n * 128, 128)
             for j in range(4):
                 value = blk[pl.ds(j * 6 + n, D // 4, stride=24)].astype(bf16)
-                held[z, y, x, pl.ds(j * (D // 4), D // 4), pl.ds(n * 128, 128)] = value
+                held[z, y, x, pl.ds(j * (D // 4), D // 4), cols] = value
+                held[z, y, x, pl.ds(j * (D // 4), 16), cols] = (
+                    blk[pl.ds(j * 6 + n, 16, stride=24)] + jnp.where(top, before[pl.ds(j * 6 + n, 1)], 0.0)
+                ).astype(bf16)
 
     when(jnp.logical_not(spread), plain)
     when(spread, swapped)
@@ -571,6 +582,7 @@
             leave(t).start()
 
         def prepare():
+            tokens_come.wait()
             tokT[...] = tokens[...].astype(f32).T.astype(bf16)
             tokT_leaves.start()
             fill_distance(dist, seg_row, column)
@@ -652,13 +664,13 @@
         leave(t).wait()
 
 
-def gather_attend(blk, last, tokens, seg):
+def gather_attend(blk, before, last, tokens, seg):
     Q = pltpu.SemaphoreType.DMA
     any_space = pl.BlockSpec(memory_space=pl.ANY)
     counts = [8] * 6 + [24, 24, 3, 3] + [9] * 12 + [48, 48, 3, 1]
     return pl.pallas_call(
         gather_attend_kernel,
-        in_specs=[VM, VM, VM, VM],
+        in_specs=[VM, VM, VM, any_space, VM],
         out_specs=[any_space, VM, any_space, any_space, VM, any_space],
         out_shape=[
             jax.ShapeDtypeStruct((4, 2, 2, D, D), bf16), jax.ShapeDtypeStruct((4, D), f32),
@@ -666,42 +678,42 @@
         ],
         scratch_shapes=[
             pltpu.VMEM((4, 2, 2, D, D), bf16), pltpu.VMEM((LEN, LEN), f32), pltpu.VMEM((LEN, 8), f32),
-            pltpu.VMEM((16, D), bf16),
+            pltpu.VMEM((LEN, D), bf16), pltpu.VMEM((16, D), bf16),
             pltpu.VMEM((D, LEN), bf16), pltpu.VMEM((3, D, LEN), bf16), pltpu.VMEM((2, LEN, LEN), bf16),
-            Q((4,)), Q, Q((3,)), Q((2,)), *[Q((n,)) for n in counts],
+            Q, Q((4,)), Q, Q((3,)), Q((2,)), *[Q((n,)) for n in counts],
         ],
         compiler_params=pltpu.CompilerParams(
             collective_id=1, has_side_effects=True, vmem_limit_bytes=58 << 20
         ),
         name="gather_attend",
-    )(blk, last, tokens, seg.reshape(1, LEN))
+    )(blk, before, last, tokens, seg.reshape(1, LEN))
 
 
 PLANE_ORDER = (1, 2, 3)
 BACK_PLAN = (
     (
-        7405680, 291331, 460403, 357748, 532515, 2369408, 4407315, 8484483, 2435092, 71206,
-        7816773, 8525688, 3359796, 3547527, 9442784, 1067094, 3641624, 168519, 9664833, 7999792,
-        5759611, 10585476, 14759989, 10651219, 2232916, 10523856, 9868632, 10768469, 9937841, 13713970,
-        5386672, 12628646, 13870546, 5351347, 11908278, 12961475, 12695492, 15714242, 15724527,
+        7405680, 7471873, 7570180, 488454, 2295925, 2573089, 8393537, 2364545, 345894, 8525430,
+        4728834, 7807120, 1523782, 4487222, 2237712, 9574545, 7943987, 8860689, 5667415, 4579349,
+        3167099, 3252242, 8665314, 8804485, 9655458, 10589234, 9818165, 9852385, 10699442, 11554980,
+        13816215, 5354322, 11642306, 11839398, 11981761, 12892096, 11912135, 15713989, 15724527,
     ),
     (
-        33648, 225905, 263795, 329588, 8418784, 1472008, 7807782, 1053816, 8524673, 8026435,
-        2658325, 4624676, 8095489, 14819351, 8750144, 10523175, 9646152, 13637766, 3490887, 9806228,
-        2463286, 3658070, 13801285, 13869731, 5744036, 11644930, 2212148, 11773752, 12629336, 4317618,
-        12760149, 3392422, 12866594, 11952146, 1135557, 12010182, 3327841, 6443600, 15683889,
+        7405680, 7471873, 422660, 7671924, 526198, 8422163, 8880769, 364579, 3182967, 7874194,
+        2376465, 1447731, 2430073, 2587514, 3642338, 4671016, 165025, 8773684, 8794440, 13645336,
+        9802784, 4478870, 5644962, 1417379, 13711511, 10821952, 11707602, 11617624, 14790849, 10900672,
+        12727635, 10990421, 12891331, 11878977, 6296261, 11978679, 13878864, 6435425, 15684177,
     ),
     (
-        7405680, 197121, 7631730, 401425, 7701252, 8458880, 489009, 1081975, 4200056, 8855952,
-        9533704, 9580666, 8098594, 14816416, 1541281, 8802437, 9752642, 9840277, 4301362, 9941074,
-        11618344, 3614673, 4662179, 12654770, 14722468, 4596928, 10921938, 377523, 12825875, 12891190,
-        5683126, 12923971, 3692356, 13051334, 4542741, 13850849, 5530675, 5584229, 15688531,
+        65648, 7565937, 7603728, 8585991, 554464, 8851840, 2502785, 1472130, 161680, 7870353,
+        3219833, 2627706, 10588737, 9634976, 14819963, 8750112, 13665872, 4232210, 2376354, 13735207,
+        9934407, 10703281, 3658310, 10855617, 12628146, 12727828, 10987095, 377779, 1291336, 3720260,
+        12957111, 3298851, 11941063, 2475587, 1399009, 13845842, 5452644, 3499363, 15684948,
     ),
     (
-        7405680, 225793, 7540738, 422944, 7763204, 8601619, 3154181, 2232951, 8471168, 2379906,
-        1131542, 4421667, 9512336, 4277650, 5386873, 10582675, 8062740, 10650850, 3245701, 8868256,
-        3446164, 11645603, 9875649, 9917632, 2598096, 12759973, 10998211, 12891302, 1422600, 13022917,
-        12050483, 5453511, 4605734, 1626647, 5580853, 13850184, 14759782, 5728104, 15685688,
+        65648, 7471985, 7602803, 328739, 8397173, 4395393, 8615456, 1278480, 409892, 9539652,
+        7807525, 4231698, 7947640, 3380017, 1331248, 8102266, 4383392, 8750087, 10637702, 9744775,
+        10692245, 9879728, 2594753, 12759602, 10866771, 11736484, 11839427, 14722756, 12956951, 12006664,
+        4601031, 13022742, 13718087, 1626708, 5589032, 6698963, 5715681, 3692135, 15689816,
     ),
 )
 
@@ -779,8 +791,6 @@
         return pltpu.make_async_copy(probs_in.at[h], probs.at[h % 2], p_sem.at[h % 2])
 
     probs_come(0).start()
-    for n in (3, 4):
-        take[n].start()
     enter_more(i, c, z, y, x)
     for t in PLANE_ORDER:
         for s in range(3):
@@ -794,8 +804,6 @@
     line = jnp.logical_and(x == 1, y == 1)
     last_line = jnp.logical_and(line, z == 3)
     when(x == 0, lambda: NX.start())
-    for move in take:
-        move.wait()
 
     def rb(s, k=0, size=B_PART):
         return pl.ds(pl.multiple_of(s * B_PART + k, 16), size)
@@ -926,6 +934,18 @@
         add_rows(lambda k: own.at[z, y, x, rb(s, k, 16)], lambda k: lb1.at[s, r16(k)], B_PART)
 
     def op_head(h):
+        def operands():
+            for n in range(3):
+                take[n].wait()
+            for n in (3, 4):
+                take[n].start()
+
+        def late_operands():
+            for n in (3, 4):
+                take[n].wait()
+
+        when(h == 0, operands)
+        when(h == 2, late_operands)
         probs_come(h).wait()
         when(h < HEADS - 1, lambda: probs_come(h + 1).start())
         attend_back_head(h, qkv, dO, mixb, probs.at[h % 2], ds_all)
@@ -1234,13 +1254,17 @@
     index = lax.axis_index("zero")
     size = 16 * SQUARE // count
     last = master[-TAIL:]
-    before = lax.ppermute(last, "zero", [(k, k + 1) for k in range(count - 1)])
-    joined = jnp.concatenate([before, master])
-    block = lax.dynamic_slice(joined, (TAIL - TAIL // count * index,), (size,))
+    step = TAIL // count
+    zeros = jnp.zeros((TAIL,), f32)
+    ending = lax.dynamic_slice(jnp.concatenate([last, zeros]), (TAIL - step * (index + 1),), (TAIL,))
+    before = lax.ppermute(ending, "zero", [(k, k + 1) for k in range(count - 1)])
+    block = lax.dynamic_slice(jnp.concatenate([zeros, master]), (TAIL - step * index,), (size,))
     if count == 16:
+        before = jnp.pad(before.reshape(24, 128), ((0, 72), (0, 0)))
         block, last = block.reshape(6 * D, 128), last.reshape(24, 128)
-        blocks, norms, *attended = gather_attend(block, last, tokens, segments)
+        blocks, norms, *attended = gather_attend(block, before, last, tokens, segments)
     else:
+        block = jnp.concatenate([block[:TAIL] + before, block[TAIL:]])
         natural = lax.all_gather(block.astype(bf16).reshape(-1, D), "zero", axis=0, tiled=True)
         parts = natural.reshape(4, 4 * D, D)
         wide = [to_wide(parts[k].reshape(D, FF)) for k in (1, 2)]

time: 283 us -> 279 us (0.986)
  local copies, waits for them, and re-layouts: 3.08 us -> 7.62 us
  other arithmetic: 12 us -> 8.16 us
  waiting for transfers between devices: 3.97 us -> 0.14 us
    reshape x1 -> x2, local copies, waits for them, and re-layouts: 1.39 us -> 5.23 us  [gather_and_attend(): block, last = (block.reshape(6 * D, 128), last.reshape(24, 128))]
    reshape x1 -> x0, other arithmetic: 3.83 us -> none  [gather_and_attend(): block, last = (block.reshape(6 * D, 128), last.reshape(24, 128))]
    ppermute x1, waiting for transfers between devices: 3.97 us -> 0.14 us  [gather_and_attend(): lax.ppermute(ending, 'zero', [(k, k + 1) for k in range(count - 1)])]
  transfers between devices with their start and end apart: 1 -> 1, of which waited for: 1 -> 1; matrix products, arithmetic and copies ran while one was open for 0% -> 1% of each run, Pallas kernels for 0% -> 0%
where the time goes in v10:
time: 279 us; the launch traced here: 275 us
  Pallas kernels  255 us (91%)
  other arithmetic  8.16 us (3%)
  local copies, waits for them, and re-layouts  7.62 us (3%)
  starting transfers between devices  3.39 us (1%)
    pallas_call x1, Pallas kernels, reduce_back(): pl.pallas_call(reduce_back_kernel, in_specs=[A] * 10 + [VM], out_specs=[A...  95 us
    pallas_call x1, Pallas kernels, gather_attend(): pl.pallas_call(gather_attend_kernel, in_specs=[VM, VM, VM, any_space, VM]...  85.9 us
    pallas_call x1, Pallas kernels, feed(): pl.pallas_call(feed_kernel, grid=(n + 12,), in_specs=[pl.BlockSpec((TB, D...  74.5 us
    convert_element_type x1, other arithmetic, local(): master_new.astype(jnp.bfloat16)  8.16 us
  transfers between devices with their start and end apart: 1, of which 1 were waited for; matrix products, arithmetic and copies ran while one was open for 1% of the time, Pallas kernels for 0%

profile of v10, /device:TPU:8, one launch (start us, length us, event | category | flops | bytes accessed | tf_op | source)
XLA Modules:
  0.0 275.5 jit_solution(4745066635716183802)
XLA Ops:
  0.6 1.4 slice_bitcast_fusion
  2.0 0.1 pad_dynamic-slice_fusion.1
  2.1 3.4 %collective-permute-start = (f32[3072]{0:T(1024)S(1)}, f32[3072]{0:T(1024)S(1)}, u32[]{:S(2)}, u32[]{:S(2)}) collective-permute-start(f32[3072]{0:T(1024)S(1)} %pad_dynamic-slice_fusion.1), channel_id=1, source_target_pairs={{0,1},{1,2},{2,3},{3,4},{4,5},{5,6},{6,7},{7,8},{8,9},{9,10},{10,1... | collective-permute-start | bytes 36872 | tf_op jit(solution)/shard_map/ppermute | solution.py:1260
  5.5 3.8 %fusion.blk = f32[4608,128]{1,0:T(8,128)} fusion(s32[]{:T(128)S(6)} %select_n.9, f32[590016]{0:T(1024)} %param.9), kind=kLoop, calls=%fused_computation.4 | loop fusion | bytes 4719364 | tf_op jit(solution)/shard_map/reshape | solution.py:1264
  9.3 0.1 collective-permute-done
  9.5 0.6 pad.6.before
  10.1 85.9 %gather_attend.1 = (bf16[4,2,2,768,768]{4,3,2,1,0:T(8,128)(2,1)}, f32[4,768]{1,0:T(4,128)}, bf16[768,1024]{1,0:T(8,128)(2,1)}, bf16[3,768,1024]{2,1,0:T(8,128)(2...) custom-call(f32[4608,128]{1,0:T(8,128)} %fusion.blk, f32[96,128]{1,0:T(8,128)} %pad.6.before, ...), custom_call_target="tpu_custom_call" | custom-call | tf_op jit(solution)/shard_map/gather_attend/pallas_call | solution.py:671
  96.0 74.5 %feed.1 = (bf16[1024,768]{1,0:T(8,128)(2,1)}, f32[1024,768]{1,0:T(8,128)}, bf16[768,1024]{1,0:T(8,128)(2,1)}, bf16[1024,768]{1,0:T(8,128)(2,1)}, f32[4,768]{1,0:...) custom-call(bf16[1024,768]{1,0:T(8,128)(2,1)} %tokens.1, bf16[1024,768]{1,0:T(8,128)(2,1)} %cot.1, ...), custom_call_target="tpu_custom_call" | custom-call | tf_op jit(solution)/shard_map/feed/pallas_call | solution.py:232
  170.6 0.0 copy-start
  170.6 0.0 copy-start.2
  170.6 0.0 copy-start.3
  170.6 95.0 %reduce_back.1 = (f32[1024,768]{1,0:T(8,128)}, f32[4632,128]{1,0:T(8,128)}) custom-call(bf16[2,2,2,768,768]{4,3,2,1,0:T(8,128)(2,1)} %bitcast.11, bf16[2,2,768,768]{3,2,1,0:T(8,128)(2,1)} %bitcast.12, bf16[4,2,2,768,768]{4,3,2,1,0:T(8,128)(2,1)} %get-tuple-element.23.w, bf16[3,768,1024]{2,1,0:T(8,128)(2,1)} %get-tuple-element.28.qkv_in, ...), custom_call_target="tpu_custom_call" | custom-call | tf_op jit(solution)/shard_map/reduce_back/pallas_call | solution.py:1220
  265.6 0.0 copy-done
  265.6 0.0 copy-done.2
  265.6 0.0 copy-done.3
  265.6 0.0 copy-start.1
  265.6 8.2 %fusion.1 = (bf16[590016]{0:T(1024)(128)(2,1)}, f32[590016]{0:T(1024)}, f32[590016]{0:T(1024)}, f32[590016]{0:T(1024)}, f32[590016]{0:T(1024)}) fusion(f32[590016]{0:T(1024)S(1)} %copy-done, f32[592896]{0:T(1024)} %bitcast.13, s32[]{:T(128)S(6)} %select_n.11, f32[590016]{0:T(1024)S(1)} %copy-done.2, f32[590016]{0:T(1024)S(1)} %copy-done.3), kind=kLoop, calls=%fused_computation.8 | loop fusion | flops 10030272 | bytes 20060548 | tf_op jit(solution)/shard_map/convert_element_type | solution.py:1325
  273.8 0.0 copy-done.1
  273.8 1.7 copy.14
Async XLA Ops:
  2.1 7.4 %collective-permute-start = (f32[3072]{0:T(1024)S(1)}, f32[3072]{0:T(1024)S(1)}, u32[]{:S(2)}, u32[]{:S(2)}) collective-permute-start(f32[3072]{0:T(1024)S(1)} %pad_dynamic-slice_fusion.1), channel_id=1, source_target_pairs={{0,1},{1,2},{2,3},{3,4},{4,5},{5,6},{6,7},{7,8},{8,9},{9,10},{10,1... | collective-permute-start | bytes 36872 | tf_op jit(solution)/shard_map/ppermute | solution.py:1260
  170.6 95.0 %copy-start = (f32[590016]{0:T(1024)S(1)}, f32[590016]{0:T(1024)}, u32[]{:S(2)}) copy-start(f32[590016]{0:T(1024)} %param.9) | copy-start | bytes 7080196
  170.6 95.0 %copy-start.2 = (f32[590016]{0:T(1024)S(1)}, f32[590016]{0:T(1024)}, u32[]{:S(2)}) copy-start(f32[590016]{0:T(1024)} %param.11) | copy-start | bytes 7080196
  170.6 95.0 %copy-start.3 = (f32[590016]{0:T(1024)S(1)}, f32[590016]{0:T(1024)}, u32[]{:S(2)}) copy-start(f32[590016]{0:T(1024)} %param.10) | copy-start | bytes 7080196
  265.6 8.2 %copy-start.1 = (f32[1024,768]{1,0:T(8,128)S(1)}, f32[1024,768]{1,0:T(8,128)}, u32[]{:S(2)}) copy-start(f32[1024,768]{1,0:T(8,128)} %get-tuple-element.52) | copy-start | bytes 9437188

commit v11 on v10

--- a/solution.py
+++ b/solution.py
@@ -233,10 +233,10 @@
         in_specs=[pl.BlockSpec((TB,D),row),pl.BlockSpec((TB,D),row),pl.BlockSpec((D,TB),col),
             pl.BlockSpec(memory_space=pl.ANY),pl.BlockSpec((4,D),lambda i:(0,0))],
         out_specs=[pl.BlockSpec((TB,D),row),pl.BlockSpec((TB,D),row),pl.BlockSpec((D,TB),col),pl.BlockSpec((TB,D),row),
-            pl.BlockSpec((4,D),lambda i:(0,0)),
+            pl.BlockSpec((8,D),lambda i:(0,0)),
             pl.BlockSpec((1,D,D),lambda i:(clip(i-n,0,3),0,0)),
             pl.BlockSpec((1,4,1,D//4,D),lambda i:(clip((i-n-4)//4,0,1),0,clip(i-n-4,0,7)%4,0,0))],
-        out_shape=[S((LEN,D),bf16),S((LEN,D),f32),S((D,LEN),bf16),S((LEN,D),bf16),S((4,D),f32),S((4,D,D),bf16),S((2,4,4,D//4,D),bf16)],
+        out_shape=[S((LEN,D),bf16),S((LEN,D),f32),S((D,LEN),bf16),S((LEN,D),bf16),S((8,D),f32),S((4,D,D),bf16),S((2,4,4,D//4,D),bf16)],
         scratch_shapes=[V((LEN,D)),V((8,LEN,D)),V((LEN,D)),V((4,TB,D),f32),V((4,TB,D),f32),V((TB,D),f32),V((4,LEN,D)),V((4,D//4,D)),*[V((4,4,D//4,D))]*3,pltpu.SemaphoreType.DMA((3,4)),pltpu.SemaphoreType.DMA],
         compiler_params=pltpu.CompilerParams(vmem_limit_bytes=62<<20),name="feed")(tokens,cot,mixb,w.reshape(4,4,4,D//4,D),norms)
 
@@ -1182,7 +1182,7 @@
 
     def ending():
         for n in range(6):
-            flat[pl.ds(6 * D + n, 4, stride=6)] = nacc[:, pl.ds(n * 128, 128)]
+            flat[pl.ds(6 * D + n, 8, stride=6)] = nacc[:, pl.ds(n * 128, 128)]
 
     when(i == 15, ending)
     give = remote(flat.at[head_rows], flat.at[after], (c, i - 1), aft_s, aft_r)
@@ -1227,7 +1227,7 @@
             V(3, C_PART, D), V(9, 2, B_PART, D), V(9, 2, B_PART, D), V(3, 2, B_PART, D), V(3, B_PART, D),
             V(8, 2, Q_PART, COLS), V(8, Q_PART, COLS), V(8, Q_PART, COLS), V(8, HALF, COLS),
             V(D, LEN), V(D, LEN), V(D, LEN), V(LEN, D), V(HALF, D), V(2, LEN, LEN), V(LEN, LEN), V(D, D), V(3, D, LEN),
-            F(256, D), F(6 * D + 24, 128), F(4, D), F(4, D), F(4, D), F(4, D), F(4, D),
+            F(256, D), F(6 * D + 64, 128), F(8, D), F(8, D), F(8, D), F(8, D), F(8, D),
             Q((4,)), Q((5,)), Q((2,)), Q((3,)), Q, Q, Q((2,)), Q((18,)), Q((18,)), Q((8,)), Q((8,)),
             *[Q((9,))] * 14, Q((3,)), Q((3,)), *[Q((8,))] * 6, Q((4,)), Q((4,)), Q, Q, Q, Q,
         ],
@@ -1260,8 +1260,8 @@
     before = lax.ppermute(ending, "zero", [(k, k + 1) for k in range(count - 1)])
     block = lax.dynamic_slice(jnp.concatenate([zeros, master]), (TAIL - step * index,), (size,))
     if count == 16:
-        before = jnp.pad(before.reshape(24, 128), ((0, 72), (0, 0)))
-        block, last = block.reshape(6 * D, 128), last.reshape(24, 128)
+        before = jnp.pad(before.reshape(24, 128), ((0, 104), (0, 0)))
+        block, last = block.reshape(6 * D, 128), jnp.pad(last.reshape(24, 128), ((0, 40), (0, 0)))
         blocks, norms, *attended = gather_attend(block, before, last, tokens, segments)
     else:
         block = jnp.concatenate([block[:TAIL] + before, block[TAIL:]])
@@ -1293,7 +1293,7 @@
         natural = jnp.concatenate([square.reshape(4 * D, D), *natural, down_grad.reshape(4 * D, D)])
         block = lax.psum_scatter(natural, "zero", scatter_dimension=0, tiled=True)
         block = lax.psum(block.astype(f32), "dp")
-        tail = lax.psum(norm_grads, ("dp", "zero"))
+        tail = lax.psum(norm_grads[:4], ("dp", "zero"))
         flat = block.reshape(-1)
         after = lax.ppermute(flat[:TAIL], "zero", [(k + 1, k) for k in range(count - 1)])
         joined = jnp.concatenate([flat, jnp.where(index == count - 1, tail.reshape(-1), after)])

time: 279 us -> 279 us (level)
  transfers between devices with their start and end apart: 1 -> 1, of which waited for: 1 -> 0; matrix products, arithmetic and copies ran while one was open for 1% -> 2% of each run, Pallas kernels for 0% -> 0%
where the time goes in v11:
time: 279 us; the launch traced here: 276 us
  Pallas kernels  256 us (92%)
  other arithmetic  8.16 us (3%)
  local copies, waits for them, and re-layouts  7.64 us (3%)
  starting transfers between devices  3.39 us (1%)
    pallas_call x1, Pallas kernels, reduce_back(): pl.pallas_call(reduce_back_kernel, in_specs=[A] * 10 + [VM], out_specs=[A...  95 us
    pallas_call x1, Pallas kernels, gather_attend(): pl.pallas_call(gather_attend_kernel, in_specs=[VM, VM, VM, any_space, VM]...  86.1 us
    pallas_call x1, Pallas kernels, feed(): pl.pallas_call(feed_kernel, grid=(n + 12,), in_specs=[pl.BlockSpec((TB, D...  74.5 us
    convert_element_type x1, other arithmetic, local(): master_new.astype(jnp.bfloat16)  8.16 us
  transfers between devices with their start and end apart: 1, of which 0 were waited for; matrix products, arithmetic and copies ran while one was open for 2% of the time, Pallas kernels for 0%

profile of v11, /device:TPU:8, one launch (start us, length us, event | category | flops | bytes accessed | tf_op | source)
XLA Modules:
  0.0 275.5 jit_solution(9191319930591479961)
XLA Ops:
  0.6 0.8 slice_bitcast_fusion
  1.4 0.1 pad_dynamic-slice_fusion.1
  1.5 3.4 %collective-permute-start = (f32[3072]{0:T(1024)S(1)}, f32[3072]{0:T(1024)S(1)}, u32[]{:S(2)}, u32[]{:S(2)}) collective-permute-start(f32[3072]{0:T(1024)S(1)} %pad_dynamic-slice_fusion.1), channel_id=1, source_target_pairs={{0,1},{1,2},{2,3},{3,4},{4,5},{5,6},{6,7},{7,8},{8,9},{9,10},{10,1... | collective-permute-start | bytes 36872 | tf_op jit(solution)/shard_map/ppermute | solution.py:1260
  4.9 3.8 %fusion.blk = f32[4608,128]{1,0:T(8,128)} fusion(s32[]{:T(128)S(6)} %select_n.9, f32[590016]{0:T(1024)} %param.9), kind=kLoop, calls=%fused_computation.4 | loop fusion | bytes 4719364 | tf_op jit(solution)/shard_map/reshape | solution.py:1264
  8.7 0.6 pad.11.last
  9.4 0.0 collective-permute-done
  9.4 0.6 pad.10.before
  10.0 86.1 %gather_attend.1 = (bf16[4,2,2,768,768]{4,3,2,1,0:T(8,128)(2,1)}, f32[4,768]{1,0:T(4,128)}, bf16[768,1024]{1,0:T(8,128)(2,1)}, bf16[3,768,1024]{2,1,0:T(8,128)(2...) custom-call(f32[4608,128]{1,0:T(8,128)} %fusion.blk, f32[128,128]{1,0:T(8,128)} %pad.10.before, ...), custom_call_target="tpu_custom_call" | custom-call | tf_op jit(solution)/shard_map/gather_attend/pallas_call | solution.py:671
  96.1 74.5 %feed.1 = (bf16[1024,768]{1,0:T(8,128)(2,1)}, f32[1024,768]{1,0:T(8,128)}, bf16[768,1024]{1,0:T(8,128)(2,1)}, bf16[1024,768]{1,0:T(8,128)(2,1)}, f32[8,768]{1,0:...) custom-call(bf16[1024,768]{1,0:T(8,128)(2,1)} %tokens.1, bf16[1024,768]{1,0:T(8,128)(2,1)} %cot.1, ...), custom_call_target="tpu_custom_call" | custom-call | tf_op jit(solution)/shard_map/feed/pallas_call | solution.py:232
  170.6 0.0 copy-start
  170.6 0.0 copy-start.2
  170.6 0.0 copy-start.3
  170.6 95.0 %reduce_back.1 = (f32[1024,768]{1,0:T(8,128)}, f32[4632,128]{1,0:T(8,128)}) custom-call(bf16[2,2,2,768,768]{4,3,2,1,0:T(8,128)(2,1)} %bitcast.11, bf16[2,2,768,768]{3,2,1,0:T(8,128)(2,1)} %bitcast.12, bf16[4,2,2,768,768]{4,3,2,1,0:T(8,128)(2,1)} %get-tuple-element.23.w, bf16[3,768,1024]{2,1,0:T(8,128)(2,1)} %get-tuple-element.28.qkv_in, ...), custom_call_target="tpu_custom_call" | custom-call | tf_op jit(solution)/shard_map/reduce_back/pallas_call | solution.py:1220
  265.6 0.0 copy-done
  265.6 0.0 copy-done.2
  265.6 0.0 copy-done.3
  265.7 0.0 copy-start.1
  265.7 8.2 %fusion.1 = (bf16[590016]{0:T(1024)(128)(2,1)}, f32[590016]{0:T(1024)}, f32[590016]{0:T(1024)}, f32[590016]{0:T(1024)}, f32[590016]{0:T(1024)}) fusion(f32[590016]{0:T(1024)S(1)} %copy-done, f32[592896]{0:T(1024)} %bitcast.13, s32[]{:T(128)S(6)} %select_n.11, f32[590016]{0:T(1024)S(1)} %copy-done.2, f32[590016]{0:T(1024)S(1)} %copy-done.3), kind=kLoop, calls=%fused_computation.8 | loop fusion | flops 10030272 | bytes 20060548 | tf_op jit(solution)/shard_map/convert_element_type | solution.py:1325
  273.8 0.0 copy-done.1
  273.8 1.7 copy.14
Async XLA Ops:
  1.5 7.9 %collective-permute-start = (f32[3072]{0:T(1024)S(1)}, f32[3072]{0:T(1024)S(1)}, u32[]{:S(2)}, u32[]{:S(2)}) collective-permute-start(f32[3072]{0:T(1024)S(1)} %pad_dynamic-slice_fusion.1), channel_id=1, source_target_pairs={{0,1},{1,2},{2,3},{3,4},{4,5},{5,6},{6,7},{7,8},{8,9},{9,10},{10,1... | collective-permute-start | bytes 36872 | tf_op jit(solution)/shard_map/ppermute | solution.py:1260
  170.6 95.1 %copy-start = (f32[590016]{0:T(1024)S(1)}, f32[590016]{0:T(1024)}, u32[]{:S(2)}) copy-start(f32[590016]{0:T(1024)} %param.9) | copy-start | bytes 7080196
  170.6 95.1 %copy-start.2 = (f32[590016]{0:T(1024)S(1)}, f32[590016]{0:T(1024)}, u32[]{:S(2)}) copy-start(f32[590016]{0:T(1024)} %param.11) | copy-start | bytes 7080196
  170.6 95.1 %copy-start.3 = (f32[590016]{0:T(1024)S(1)}, f32[590016]{0:T(1024)}, u32[]{:S(2)}) copy-start(f32[590016]{0:T(1024)} %param.10) | copy-start | bytes 7080196
  265.7 8.2 %copy-start.1 = (f32[1024,768]{1,0:T(8,128)S(1)}, f32[1024,768]{1,0:T(8,128)}, u32[]{:S(2)}) copy-start(f32[1024,768]{1,0:T(8,128)} %get-tuple-element.52) | copy-start | bytes 9437188

commit v12 on v11

--- a/solution.py
+++ b/solution.py
@@ -1127,6 +1127,12 @@
     share.start()
     flatten(c, lambda rows, cols: own[z, y, x, rows, cols])
 
+    def leave(half, n):
+        rows = pl.ds(pl.multiple_of(half * (6 * HALF), 8), 6 * HALF)
+        return pltpu.make_async_copy(flat.at[rows], flat_out.at[rows], o_sem.at[n])
+
+    when(jnp.logical_not(spread), lambda: leave(c, 0).start())
+
     @pl.loop(0, 9)
     def _(e):
         t, s = split(e)
@@ -1176,9 +1182,9 @@
     share.wait_recv()
     flatten(1 - c, lambda rows, cols: theirs[rows, cols])
     share.wait_send()
-    body, head_rows, after = pl.ds(0, 6 * D), pl.ds(0, 24), pl.ds(6 * D, 24)
-    leave = pltpu.make_async_copy(flat.at[body], flat_out.at[body], o_sem.at[0])
-    leave.start()
+    head_rows, after = pl.ds(0, 24), pl.ds(6 * D, 24)
+    when(spread, lambda: leave(c, 0).start())
+    leave(1 - c, 2).start()
 
     def ending():
         for n in range(6):
@@ -1191,7 +1197,8 @@
     leave_after = pltpu.make_async_copy(flat.at[after], flat_out.at[after], o_sem.at[1])
     leave_after.start()
     when(i > 0, lambda: give.wait_send())
-    leave.wait()
+    leave(c, 0).wait()
+    leave(1 - c, 2).wait()
     leave_after.wait()
 
 
@@ -1228,7 +1235,7 @@
             V(8, 2, Q_PART, COLS), V(8, Q_PART, COLS), V(8, Q_PART, COLS), V(8, HALF, COLS),
             V(D, LEN), V(D, LEN), V(D, LEN), V(LEN, D), V(HALF, D), V(2, LEN, LEN), V(LEN, LEN), V(D, D), V(3, D, LEN),
             F(256, D), F(6 * D + 64, 128), F(8, D), F(8, D), F(8, D), F(8, D), F(8, D),
-            Q((4,)), Q((5,)), Q((2,)), Q((3,)), Q, Q, Q((2,)), Q((18,)), Q((18,)), Q((8,)), Q((8,)),
+            Q((4,)), Q((5,)), Q((2,)), Q((3,)), Q, Q, Q((3,)), Q((18,)), Q((18,)), Q((8,)), Q((8,)),
             *[Q((9,))] * 14, Q((3,)), Q((3,)), *[Q((8,))] * 6, Q((4,)), Q((4,)), Q, Q, Q, Q,
         ],
         compiler_params=pltpu.CompilerParams(

time: 279 us -> 279 us (level)
  no operation moved by 1% of the time
where the time goes in v12:
time: 279 us; the launch traced here: 276 us
  Pallas kernels  256 us (92%)
  other arithmetic  8.16 us (3%)
  local copies, waits for them, and re-layouts  7.64 us (3%)
  starting transfers between devices  3.39 us (1%)
    pallas_call x1, Pallas kernels, reduce_back(): pl.pallas_call(reduce_back_kernel, in_specs=[A] * 10 + [VM], out_specs=[A...  95 us
    pallas_call x1, Pallas kernels, gather_attend(): pl.pallas_call(gather_attend_kernel, in_specs=[VM, VM, VM, any_space, VM]...  86.1 us
    pallas_call x1, Pallas kernels, feed(): pl.pallas_call(feed_kernel, grid=(n + 12,), in_specs=[pl.BlockSpec((TB, D...  74.5 us
    convert_element_type x1, other arithmetic, local(): master_new.astype(jnp.bfloat16)  8.16 us
  transfers between devices with their start and end apart: 1, of which 0 were waited for; matrix products, arithmetic and copies ran while one was open for 2% of the time, Pallas kernels for 0%

profile of v12, /device:TPU:8, one launch (start us, length us, event | category | flops | bytes accessed | tf_op | source)
XLA Modules:
  0.0 275.5 jit_solution(6643709394629656530)
XLA Ops:
  0.6 0.8 slice_bitcast_fusion
  1.4 0.1 pad_dynamic-slice_fusion.1
  1.5 3.4 %collective-permute-start = (f32[3072]{0:T(1024)S(1)}, f32[3072]{0:T(1024)S(1)}, u32[]{:S(2)}, u32[]{:S(2)}) collective-permute-start(f32[3072]{0:T(1024)S(1)} %pad_dynamic-slice_fusion.1), channel_id=1, source_target_pairs={{0,1},{1,2},{2,3},{3,4},{4,5},{5,6},{6,7},{7,8},{8,9},{9,10},{10,1... | collective-permute-start | bytes 36872 | tf_op jit(solution)/shard_map/ppermute | solution.py:1267
  4.9 3.8 %fusion.blk = f32[4608,128]{1,0:T(8,128)} fusion(s32[]{:T(128)S(6)} %select_n.9, f32[590016]{0:T(1024)} %param.9), kind=kLoop, calls=%fused_computation.4 | loop fusion | bytes 4719364 | tf_op jit(solution)/shard_map/reshape | solution.py:1271
  8.7 0.6 pad.11.last
  9.4 0.0 collective-permute-done
  9.4 0.6 pad.10.before
  10.0 86.1 %gather_attend.1 = (bf16[4,2,2,768,768]{4,3,2,1,0:T(8,128)(2,1)}, f32[4,768]{1,0:T(4,128)}, bf16[768,1024]{1,0:T(8,128)(2,1)}, bf16[3,768,1024]{2,1,0:T(8,128)(2...) custom-call(f32[4608,128]{1,0:T(8,128)} %fusion.blk, f32[128,128]{1,0:T(8,128)} %pad.10.before, ...), custom_call_target="tpu_custom_call" | custom-call | tf_op jit(solution)/shard_map/gather_attend/pallas_call | solution.py:671
  96.1 74.5 %feed.1 = (bf16[1024,768]{1,0:T(8,128)(2,1)}, f32[1024,768]{1,0:T(8,128)}, bf16[768,1024]{1,0:T(8,128)(2,1)}, bf16[1024,768]{1,0:T(8,128)(2,1)}, f32[8,768]{1,0:...) custom-call(bf16[1024,768]{1,0:T(8,128)(2,1)} %tokens.1, bf16[1024,768]{1,0:T(8,128)(2,1)} %cot.1, ...), custom_call_target="tpu_custom_call" | custom-call | tf_op jit(solution)/shard_map/feed/pallas_call | solution.py:232
  170.6 0.0 copy-start
  170.6 0.0 copy-start.2
  170.6 0.0 copy-start.3
  170.6 95.0 %reduce_back.1 = (f32[1024,768]{1,0:T(8,128)}, f32[4632,128]{1,0:T(8,128)}) custom-call(bf16[2,2,2,768,768]{4,3,2,1,0:T(8,128)(2,1)} %bitcast.11, bf16[2,2,768,768]{3,2,1,0:T(8,128)(2,1)} %bitcast.12, bf16[4,2,2,768,768]{4,3,2,1,0:T(8,128)(2,1)} %get-tuple-element.23.w, bf16[3,768,1024]{2,1,0:T(8,128)(2,1)} %get-tuple-element.28.qkv_in, ...), custom_call_target="tpu_custom_call" | custom-call | tf_op jit(solution)/shard_map/reduce_back/pallas_call | solution.py:1227
  265.6 0.0 copy-done
  265.6 0.0 copy-done.2
  265.7 0.0 copy-done.3
  265.7 0.0 copy-start.1
  265.7 8.2 %fusion.1 = (bf16[590016]{0:T(1024)(128)(2,1)}, f32[590016]{0:T(1024)}, f32[590016]{0:T(1024)}, f32[590016]{0:T(1024)}, f32[590016]{0:T(1024)}) fusion(f32[590016]{0:T(1024)S(1)} %copy-done, f32[592896]{0:T(1024)} %bitcast.13, s32[]{:T(128)S(6)} %select_n.11, f32[590016]{0:T(1024)S(1)} %copy-done.2, f32[590016]{0:T(1024)S(1)} %copy-done.3), kind=kLoop, calls=%fused_computation.8 | loop fusion | flops 10030272 | bytes 20060548 | tf_op jit(solution)/shard_map/convert_element_type | solution.py:1332
  273.8 0.0 copy-done.1
  273.8 1.7 copy.14
Async XLA Ops:
  1.5 7.9 %collective-permute-start = (f32[3072]{0:T(1024)S(1)}, f32[3072]{0:T(1024)S(1)}, u32[]{:S(2)}, u32[]{:S(2)}) collective-permute-start(f32[3072]{0:T(1024)S(1)} %pad_dynamic-slice_fusion.1), channel_id=1, source_target_pairs={{0,1},{1,2},{2,3},{3,4},{4,5},{5,6},{6,7},{7,8},{8,9},{9,10},{10,1... | collective-permute-start | bytes 36872 | tf_op jit(solution)/shard_map/ppermute | solution.py:1267
  170.6 95.1 %copy-start = (f32[590016]{0:T(1024)S(1)}, f32[590016]{0:T(1024)}, u32[]{:S(2)}) copy-start(f32[590016]{0:T(1024)} %param.9) | copy-start | bytes 7080196
  170.6 95.1 %copy-start.2 = (f32[590016]{0:T(1024)S(1)}, f32[590016]{0:T(1024)}, u32[]{:S(2)}) copy-start(f32[590016]{0:T(1024)} %param.11) | copy-start | bytes 7080196
  170.6 95.1 %copy-start.3 = (f32[590016]{0:T(1024)S(1)}, f32[590016]{0:T(1024)}, u32[]{:S(2)}) copy-start(f32[590016]{0:T(1024)} %param.10) | copy-start | bytes 7080196
  265.7 8.2 %copy-start.1 = (f32[1024,768]{1,0:T(8,128)S(1)}, f32[1024,768]{1,0:T(8,128)}, u32[]{:S(2)}) copy-start(f32[1024,768]{1,0:T(8,128)} %get-tuple-element.52) | copy-start | bytes 9437188
